TPU v7x, 256 devices: a whole 4x4x8 slice. The times are simulated.
256 devices in a mesh: row: 8 (over y, core), col: 16 (over z, x_hi), slab: 2 (over x_lo).
Axes of the slice: x: 4 (x_hi: 2, x_lo: 2; x = x_hi * 2 + x_lo), y: 4, z: 8, core: 2. Of those that a mesh axis runs over, the one named last changes fastest.
Arguments:
- feats: bfloat16 [65536, 256], P(('slab', 'col', 'row')), parts along dimension 0, may hold values from -6 to 6
- weight: bfloat16 [256, 256], replicated, may hold values from -0.375 to 0.375
- bias: float32 [256], replicated, may hold values from -4 to 4
- grad_out: bfloat16 [65536, 256], P(('slab', 'row', 'col')), parts along dimension 0, may hold values from -20 to 20
- tile_vals: bfloat16 [16, 16, 192, 128, 128], P(('slab', 'row'), 'col'), parts along dimension 0, may hold values from 0 to 1, as said below
- tile_rows: int32 [16, 16, 192], P(('slab', 'row'), 'col'), parts along dimension 0, may hold values from 0 to 31, as said below
- tile_cols: int32 [16, 16, 192], P(('slab', 'row'), 'col'), parts along dimension 0, may hold values from 0 to 15, as said below
- tile_count: int32 [16, 16], P(('slab', 'row'), 'col'), parts along dimension 0, may hold values from 1 to 192, as said below
Outputs:
- hidden_out: bfloat16 [65536, 256], P(('slab', 'row', 'col')), parts along dimension 0
- grad_feats: bfloat16 [65536, 256], P(('slab', 'col', 'row')), parts along dimension 0
- grad_weight: float32 [512, 256], P('slab'), parts along dimension 0
- grad_bias: float32 [512], P('slab'), parts along dimension 0
There are 2 independent parts, one for each index of `slab`. A program takes and returns all parts, laid end to end along the dimension named above; an argument that names none is the same for every part. Nothing has to cross between parts.
Inputs may be any that keep to these rules, and one draw needn't show every extreme that they name: `tile_count`: each block's live tile count; some block has exactly 192 in every draw. `tile_rows`: tile rows within a block; positions of a block's tiles may repeat. `tile_cols`: tile columns within a block. `tile_vals`: nonnegative edge weights.
All inputs are finite; a program needn't handle non-finite values.
Results may differ from a plain program's by a relative error of at most 0.023.
Values may be sent and summed in bfloat16 or wider, within the bound.
No kernel may reach another device: no remote copies, remote signals or barrier semaphores. Data moves between devices by JAX's collectives and lax.ppermute only.
A program may use at most 128 MiB of HBM per device.

v0:
```python
import math

import jax
import jax.numpy as jnp
from jax import lax
from jax.sharding import PartitionSpec as P

TB = 32


def forward_tiles(values, where_rows, where_cols, live_count, source, out_tiles):
    tile_size = values.shape[-1]
    feature_width = source.shape[-1]
    source_tiles = source.reshape(-1, tile_size, feature_width)

    def forward_accumulate(batch_index, running):
        first_slot = batch_index * TB
        tile_block = lax.dynamic_slice_in_dim(values, first_slot, TB, 0)
        slot_rows = lax.dynamic_slice_in_dim(where_rows, first_slot, TB, 0)
        slot_cols = lax.dynamic_slice_in_dim(where_cols, first_slot, TB, 0)
        live_mask = (first_slot + jnp.arange(TB, dtype=jnp.int32) < live_count).astype(jnp.float32)
        picked = jnp.take(source_tiles, slot_cols, axis=0)
        product = jnp.einsum("tmn,tnh->tmh", tile_block, picked, preferred_element_type=jnp.float32)
        return running.at[slot_rows].add(product * live_mask[:, None, None])

    batches = (live_count + TB - 1) // TB
    running = lax.fori_loop(
        0,
        batches,
        forward_accumulate,
        jnp.zeros((out_tiles, tile_size, feature_width), jnp.float32),
    )
    return running.reshape(out_tiles * tile_size, feature_width)


def backward_tiles(values, where_rows, where_cols, live_count, source, out_tiles):
    tile_size = values.shape[-1]
    feature_width = source.shape[-1]
    source_tiles = source.reshape(-1, tile_size, feature_width)

    def backward_accumulate(batch_index, running):
        first_slot = batch_index * TB
        tile_block = lax.dynamic_slice_in_dim(values, first_slot, TB, 0)
        slot_rows = lax.dynamic_slice_in_dim(where_rows, first_slot, TB, 0)
        slot_cols = lax.dynamic_slice_in_dim(where_cols, first_slot, TB, 0)
        live_mask = (first_slot + jnp.arange(TB, dtype=jnp.int32) < live_count).astype(jnp.float32)
        picked = jnp.take(source_tiles, slot_rows, axis=0)
        product = jnp.einsum("tmn,tmh->tnh", tile_block, picked, preferred_element_type=jnp.float32)
        return running.at[slot_cols].add(product * live_mask[:, None, None])

    batches = (live_count + TB - 1) // TB
    running = lax.fori_loop(
        0,
        batches,
        backward_accumulate,
        jnp.zeros((out_tiles, tile_size, feature_width), jnp.float32),
    )
    return running.reshape(out_tiles * tile_size, feature_width)


def activate(summed, bias, given):
    pre_act = summed + bias[None, :]
    gate_value = jax.nn.sigmoid(pre_act)
    hidden_vals = (pre_act * gate_value).astype(jnp.bfloat16)
    slope = gate_value * (1.0 + pre_act * (1.0 - gate_value))
    grad_vals = (given.astype(jnp.float32) * slope).astype(jnp.bfloat16)
    return (hidden_vals, grad_vals)


def per_device(feats, weight, bias, grad_out, tile_vals, tile_rows, tile_cols, tile_count):
    row_count = lax.axis_size("row")
    col_count = lax.axis_size("col")
    shard_rows = feats.shape[0]
    tile_size = tile_vals.shape[-1]
    values = tile_vals[0, 0]
    where_rows = tile_rows[0, 0]
    where_cols = tile_cols[0, 0]
    live_count = tile_count[0, 0]
    row_tiles = shard_rows * col_count // tile_size
    col_tiles = shard_rows * row_count // tile_size
    projected = jnp.dot(feats, weight, preferred_element_type=jnp.float32).astype(jnp.bfloat16)
    source = lax.all_gather(projected, "row", axis=0, tiled=True)
    partial_value = forward_tiles(values, where_rows, where_cols, live_count, source, row_tiles)
    summed = lax.psum_scatter(
        partial_value.astype(jnp.bfloat16), "col", scatter_dimension=0, tiled=True
    ).astype(jnp.float32)
    hidden_out, own_grad = activate(summed, bias, grad_out)
    grad_block = lax.all_gather(own_grad, "col", axis=0, tiled=True)
    back_terms = backward_tiles(values, where_rows, where_cols, live_count, grad_block, col_tiles)
    column_total = lax.psum_scatter(
        back_terms.astype(jnp.bfloat16), "row", scatter_dimension=0, tiled=True
    )
    grad_feats = lax.dot_general(
        column_total, weight, (((1,), (1,)), ((), ())), preferred_element_type=jnp.float32
    ).astype(jnp.bfloat16)
    local_weight = lax.dot_general(
        feats, column_total, (((0,), (0,)), ((), ())), preferred_element_type=jnp.float32
    )
    local_bias = jnp.sum(own_grad.astype(jnp.float32), axis=0)
    grad_weight, grad_bias = lax.psum((local_weight, local_bias), ("row", "col"))
    grad_scale = 1.0 / math.sqrt(shard_rows * row_count * col_count)
    return (hidden_out, grad_feats, grad_weight * grad_scale, grad_bias * grad_scale)


def solution(mesh):
    in_specs = (
        P(("slab", "col", "row"), None),
        P(),
        P(),
        P(("slab", "row", "col"), None),
        P(("slab", "row"), "col", None, None, None),
        P(("slab", "row"), "col", None),
        P(("slab", "row"), "col", None),
        P(("slab", "row"), "col"),
    )
    out_specs = (
        P(("slab", "row", "col"), None),
        P(("slab", "col", "row"), None),
        P("slab", None),
        P("slab"),
    )
    return jax.shard_map(
        per_device, mesh=mesh, in_specs=in_specs, out_specs=out_specs, check_vma=False
    )
```

profile of v0, /device:TPU:1, one launch (start us, length us, event | category | flops | bytes accessed | tf_op | source)
XLA Modules:
  0.0 1987.6 jit_solution(14323019574529804268)
XLA Ops:
  10.6 30.1 %all-gather.3.cloned.1.call-done = bf16[2048,256]{1,0:T(8,128)(2,1)} async-done(((bf16[256,256]{1,0:T(8,128)(2,1)}), bf16[2048,256]{1,0:T(8,128)(2,1)}) %all-gather.3.cloned.1.call-update) | async-done | bytes 1048592 | tf_op jit(solution)/shard_map/all_gather | solution.py:82
  43.1 61.6 %while.20 = (s32[]{:T(128)}, f32[32,128,256]{2,1,0:T(8,128)}, s32[]{:T(128)}, s32[192]{0:T(256)S(1)}, bf16[192,128,128]{2,1,0:T(8,128)(2,1)}, /*index=5*/s32[192...) while((s32[]{:T(128)}, f32[32,128,256]{2,1,0:T(8,128)}, ...), condition=%wide.region_2.3_spmd, body=%wide.region_0.2_spmd.sunk | while | flops 271582592 | bytes 24122744 | solution.py:27
  44.6 4.0 convolution_multiply_fusion.4
  48.6 9.9 scatter_fusion
  59.9 4.0 convolution_multiply_fusion.4
  64.0 10.0 scatter_fusion
  75.3 4.0 convolution_multiply_fusion.4
  79.4 10.1 scatter_fusion
  90.9 4.0 convolution_multiply_fusion.4
  94.9 9.9 scatter_fusion
  108.7 232.6 %reduce-scatter.3.cloned.1.call-done = bf16[256,256]{1,0:T(8,128)(2,1)} async-done(((bf16[4096,256]{1,0:T(8,128)(2,1)}), bf16[256,256]{1,0:T(8,128)(2,1)}) %reduce-scatter.3.cloned.1.call-update) | async-done | bytes 131088 | tf_op jit(solution)/shard_map/reduce_scatter | solution.py:84
  343.1 8.6 copy.12
  351.8 77.7 %all-gather.5.cloned.1.call-done = bf16[4096,256]{1,0:T(8,128)(2,1)} async-done(((bf16[256,256]{1,0:T(8,128)(2,1)}), bf16[4096,256]{1,0:T(8,128)(2,1)}) %all-gather.5.cloned.1.call-update) | async-done | bytes 2097168 | tf_op jit(solution)/shard_map/all_gather | solution.py:88
  429.7 62.6 %while.21 = (s32[]{:T(128)}, f32[16,128,256]{2,1,0:T(8,128)S(1)}, s32[]{:T(128)}, s32[192]{0:T(256)S(1)}, bf16[192,128,128]{1,2,0:T(8,128)(2,1)}, /*index=5*/s32...) while((s32[]{:T(128)}, f32[16,128,256]{2,1,0:T(8,128)S(1)}, ...), condition=%wide.region_6.7_spmd, body=%wide.region_4.6_spmd.sunk | while | flops 271582592 | bytes 24122744 | solution.py:52
  434.0 4.7 convolution_multiply_fusion.5
  438.8 6.5 scatter_fusion.1
  449.7 4.7 convolution_multiply_fusion.5
  454.5 6.5 scatter_fusion.1
  465.3 4.7 convolution_multiply_fusion.5
  470.1 6.5 scatter_fusion.1
  481.0 4.7 convolution_multiply_fusion.5
  485.8 6.5 scatter_fusion.1
  493.5 326.8 %psum.15 = f32[256]{0:T(256)S(1)} all-reduce(f32[256]{0:T(256)S(1)} %get-tuple-element.140), channel_id=1, replica_groups=mesh['row'=8,'col'=16,'slab'=2] {'row','col'}, use_global_device_ids=true, to_apply=%region_10.11 | all-reduce | flops 256 | bytes 2048 | tf_op jit(solution)/shard_map/psum | solution.py:100
  824.5 1154.7 %all-reduce.2.cloned.1.call-done = f32[256,256]{0,1:T(8,128)} async-done(((f32[256,256]{0,1:T(8,128)}), f32[256,256]{0,1:T(8,128)}) %all-reduce.2.cloned.1.call-update) | async-done | bytes 262160 | tf_op jit(solution)/shard_map/psum | solution.py:100
  (68 shorter events, 41.8 us)
Async XLA Ops:
  7.2 0.9 copy-start
  7.2 33.5 %all-gather.3.cloned.1.call-start = ((), (), s32[]{:S(2)}) async-start(), calls=%async_computation.2 | async-start | bytes 1179648 | tf_op jit(solution)/shard_map/all_gather | solution.py:82
  9.8 331.5 %reduce-scatter.3.cloned.1.call-start = ((), (), s32[]{:S(2)}) async-start(), calls=%async_computation.3 | async-start | bytes 2228224 | tf_op jit(solution)/shard_map/reduce_scatter | solution.py:84
  40.6 2.5 copy-start.1
  40.6 2.5 copy-start.4
  40.7 2.5 copy-start.5
  108.6 232.7 %copy-start.3 = (bf16[256,256]{1,0:T(8,128)(2,1)S(1)}, bf16[256,256]{1,0:T(8,128)(2,1)}, u32[]{:S(2)}) copy-start(bf16[256,256]{1,0:T(8,128)(2,1)} %param.15) | copy-start | bytes 393220
  108.6 232.7 %copy-start.6 = (f32[256]{0:T(256)S(1)}, f32[256]{0:T(256)}, u32[]{:S(2)}) copy-start(f32[256]{0:T(256)} %param.14) | copy-start | bytes 3076
  108.6 320.9 %all-gather.5.cloned.1.call-start = ((), (), s32[]{:S(2)}) async-start(), calls=%async_computation.4 | async-start | bytes 2228224 | tf_op jit(solution)/shard_map/all_gather | solution.py:88
  343.1 477.2 %reduce-scatter.5.cloned.1.call-start = ((), (), s32[]{:S(2)}) async-start(), calls=%async_computation.5 | async-start | bytes 1179648 | tf_op jit(solution)/shard_map/reduce_scatter | solution.py:90
  492.3 330.4 %copy-start.2 = (bf16[256,256]{1,0:T(8,128)(2,1)S(1)}, bf16[256,256]{1,0:T(8,128)(2,1)}, u32[]{:S(2)}) copy-start(bf16[256,256]{1,0:T(8,128)(2,1)} %param.13) | copy-start | bytes 393220
  493.4 1485.8 %all-reduce.2.cloned.1.call-start = ((), (), s32[]{:S(2)}) async-start(), calls=%async_computation.6 | async-start | bytes 524288 | tf_op jit(solution)/shard_map/psum | solution.py:100
Sparse Core Ops, SparseCore 0:
  10.4 30.1 all-gather.2
  108.7 232.5 reduce-scatter.2
  344.5 84.9 all-gather.4
  493.5 63.9 reduce-scatter.4
  822.3 1156.9 all-reduce.1
where the time goes:
time: 1990 us
  waiting for transfers between devices  1500 us (75%)
  blocking collectives  327 us (16%)
  other arithmetic  80.4 us (4%)
  matrix products  40 us (2%)
  local copies, waits for them, and re-layouts  30.1 us (2%)
    psum x1, waiting for transfers between devices, per_device(): lax.psum((local_weight, local_bias), ('row', 'col'))  1150 us
    psum x1, blocking collectives, per_device(): lax.psum((local_weight, local_bias), ('row', 'col'))  327 us
    reduce_scatter x1, waiting for transfers between devices, per_device(): lax.psum_scatter(partial_value.astype(jnp.bfloat16), 'col', scatter_dimen...  233 us
    all_gather x1, waiting for transfers between devices, per_device(): grad_block = lax.all_gather(own_grad, 'col', axis=0, tiled=True)  77.7 us
    scatter-add x4, other arithmetic, forward_accumulate(): return running.at[slot_rows].add(product * live_mask[:, None, None])  39.8 us
  transfers between devices with their start and end apart: 5, of which 4 were waited for; matrix products, arithmetic and copies ran while one was open for 1% of the time, Pallas kernels for 0%

commit v1 on v0

v1 whole, which is shorter than its diff:
```python
import functools
import math

import jax
import jax.numpy as jnp
from jax import lax
from jax.experimental import pallas as pl
from jax.experimental.pallas import tpu as pltpu
from jax.sharding import PartitionSpec as P

TILE = 128
UNROLL = 8
NY = 4
NZ = 8
F32 = jnp.float32
BF16 = jnp.bfloat16
LIMIT = pltpu.CompilerParams(vmem_limit_bytes=32 * 2**20)


def vmem():
    return pl.BlockSpec(memory_space=pltpu.VMEM)


def smem():
    return pl.BlockSpec(memory_space=pltpu.SMEM)


def shape(rows, dtype):
    return jax.ShapeDtypeStruct((rows, 256), dtype)


def call(body, name, out_shape, args, scalars=0, scratch=(), flops=0, moved=0):
    return pl.pallas_call(
        body,
        name=name,
        out_shape=out_shape,
        in_specs=[smem()] * scalars + [vmem()] * (len(args) - scalars),
        out_specs=jax.tree.map(lambda _: vmem(), out_shape),
        scratch_shapes=scratch,
        compiler_params=LIMIT,
        cost_estimate=pl.CostEstimate(flops=flops, bytes_accessed=moved, transcendentals=0),
    )(*args)


def to_core(a):
    return lax.ppermute(a, "row", [(i, i ^ 1) for i in range(2 * NY)])


def to_y(a, step):
    return lax.ppermute(a, "row", [(i, (i + 2 * step) % (2 * NY)) for i in range(2 * NY)])


def to_x(a):
    return lax.ppermute(a, "col", [(i, i ^ 1) for i in range(2 * NZ)])


def to_z(a, step):
    return lax.ppermute(a, "col", [(i, (i + 2 * step) % (2 * NZ)) for i in range(2 * NZ)])


def flip_z(a, bit):
    return lax.ppermute(a, "col", [(i, i ^ (2 * bit)) for i in range(2 * NZ)])


def gather_row(own):
    got = {(0, 0): own}
    for step in (1, -1, 2):
        got[(-step) % NY, 0] = to_y(own, step)
    got[0, 1] = to_core(own)
    for dy in (1, 3, 2):
        got[dy, 1] = to_core(got[dy, 0])
    return got


def gather_col(own):
    got = {(0, 0): own}
    got[0, 1] = to_x(own)
    for step in (1, -1, 2, -2, 4):
        got[(-step) % NZ, 0] = to_z(own, step)
    got[3, 0] = to_z(got[2, 0], -1)
    got[5, 0] = to_z(got[6, 0], 1)
    for dz in (1, 7, 2, 6, 4):
        got[dz, 1] = to_x(got[dz, 0])
    got[3, 1] = to_z(got[0, 1], -3)
    got[5, 1] = to_z(got[0, 1], 3)
    return got


def place(ref, total, first, dtype):
    for half in range(2):
        ref[half * TILE : (half + 1) * TILE] = total[2 * first + half].astype(dtype)


def forward_body(rows, cols, count, vals, *rest):
    blocks, outs, (source, total) = rest[:8], rest[8:-2], rest[-2:]
    for k in range(8):
        for half in range(2):
            source[2 * k + half] = blocks[k][half * TILE : (half + 1) * TILE]
    total[...] = jnp.zeros_like(total)
    live = count[0]

    def batch(i, carry):
        terms = []
        for u in range(UNROLL):
            t = i * UNROLL + u
            terms.append(jnp.dot(vals[t], source[cols[t]], preferred_element_type=F32))
        for u in range(UNROLL):
            t = i * UNROLL + u
            r = jnp.where(t < live, rows[t], 32)
            total[r] = total[r] + terms[u]
        return carry

    lax.fori_loop(0, (live + UNROLL - 1) // UNROLL, batch, 0)
    own, kept, up, down, over, far_up, far_down = outs
    place(own, total, 0, F32)
    for n, (dz, dx) in enumerate(((0, 1), (1, 0), (7, 0), (2, 0), (6, 0), (4, 0))):
        place(kept.at[n], total, 2 * dz + dx, F32)
    place(up, total, 2 * 3, BF16)
    place(down, total, 2 * 5, BF16)
    for n, dz in enumerate((1, 7, 2, 6, 4)):
        place(over.at[n], total, 2 * dz + 1, BF16)
    place(far_up, total, 2 * 3 + 1, BF16)
    place(far_down, total, 2 * 5 + 1, BF16)


def relay_body(kept, up, down, over, far_up, far_down, *outs):
    def wide(ref):
        return ref[...].astype(F32)

    outs[0][...] = (kept[0] + wide(far_up) + wide(far_down)).astype(BF16)
    outs[1][...] = (kept[1] + wide(over.at[0])).astype(BF16)
    outs[2][...] = (kept[2] + wide(over.at[1])).astype(BF16)
    outs[3][...] = (kept[3] + wide(over.at[2]) + wide(up)).astype(BF16)
    outs[4][...] = (kept[4] + wide(over.at[3]) + wide(down)).astype(BF16)
    outs[5][...] = (kept[5] + wide(over.at[4])).astype(BF16)


def activate_body(own, a, b, c, d, e, f, weight, bias, given, hidden, grad, high, low):
    summed = own[...]
    for ref in (a, b, c, d, e, f):
        summed = summed + ref[...].astype(F32)
    top = summed.astype(BF16)
    rest = (summed - top.astype(F32)).astype(BF16)
    high[...] = top
    low[...] = rest
    pre_act = (
        jnp.dot(top, weight[...], preferred_element_type=F32)
        + jnp.dot(rest, weight[...], preferred_element_type=F32)
        + bias[...]
    )
    gate_value = jax.nn.sigmoid(pre_act)
    hidden[...] = (pre_act * gate_value).astype(BF16)
    slope = gate_value * (1.0 + pre_act * (1.0 - gate_value))
    grad[...] = (given[...].astype(F32) * slope).astype(BF16)


def terms_body(order, high, low, grad, kept, sent, whole):
    g = grad[...]
    dims = (((0,), (0,)), ((), ()))
    whole[...] = lax.dot_general(high[...], g, dims, preferred_element_type=F32) + lax.dot_general(
        low[...], g, dims, preferred_element_type=F32
    )
    sums = jnp.sum(g.astype(F32), axis=0, keepdims=True)
    for dy in range(NY):
        for dc, ref in enumerate((kept, sent)):
            first = pl.multiple_of(order[2 * dy + dc] * 32, 32)
            ref[dy, 0:32] = whole[pl.ds(first, 32)]
            ref[dy, 32:40] = jnp.broadcast_to(sums, (8, 256))


def backward_body(rows, cols, count, vals, *rest):
    blocks, outs, (source, total) = rest[:16], rest[16:-2], rest[-2:]
    for k in range(16):
        for half in range(2):
            source[2 * k + half] = blocks[k][half * TILE : (half + 1) * TILE]
    total[...] = jnp.zeros_like(total)
    live = count[0]

    def batch(i, carry):
        terms = []
        for u in range(UNROLL):
            t = i * UNROLL + u
            terms.append(
                lax.dot_general(
                    vals[t], source[rows[t]], (((0,), (0,)), ((), ())), preferred_element_type=F32
                )
            )
        for u in range(UNROLL):
            t = i * UNROLL + u
            c = jnp.where(t < live, cols[t], 16)
            total[c] = total[c] + terms[u]
        return carry

    lax.fori_loop(0, (live + UNROLL - 1) // UNROLL, batch, 0)
    own, kept, core, over = outs
    place(own, total, 0, F32)
    for n, dy in enumerate((1, 2, 3)):
        place(kept.at[n], total, 2 * dy, F32)
        place(over.at[n], total, 2 * dy + 1, BF16)
    place(core, total, 1, BF16)


def back_relay_body(kept, over, *outs):
    for n in range(3):
        outs[n][...] = (kept[n] + over[n].astype(F32)).astype(BF16)


def finish_body(own, a, b, c, d, weight, out):
    back = own[...]
    for ref in (a, b, c, d):
        back = back + ref[...].astype(F32)
    out[...] = lax.dot_general(
        back.astype(BF16), weight[...], (((1,), (1,)), ((), ())), preferred_element_type=F32
    ).astype(BF16)


def assemble_body(scale, order, same, other, weight, bias):
    for dy in range(NY):
        for dc, ref in enumerate((same, other)):
            first = pl.multiple_of(order[2 * dy + dc] * 32, 32)
            weight[pl.ds(first, 32)] = ref[dy, 0:32] * scale
    bias[...] = same[0, 32:40] * scale


def sum_terms(kept, sent, order, scale):
    mine = kept + to_core(sent)
    piece = mine[0]
    for step in (1, 3, 2):
        piece = piece + to_y(mine[step], step)
    piece = piece + to_x(piece)
    for bit in (1, 2, 4):
        piece = piece + flip_z(piece, bit)
    parts = [piece, None, None, None]
    for step in (1, 3, 2):
        parts[(-step) % NY] = to_y(piece, step)
    same = jnp.stack(parts)
    other = to_core(same)
    return call(
        functools.partial(assemble_body, scale),
        "assemble",
        (shape(256, F32), shape(8, F32)),
        (order, same, other),
        scalars=1,
    )


def per_device(feats, weight, bias, grad_out, tile_vals, tile_rows, tile_cols, tile_count):
    shard = feats.shape[0]
    scale = 1.0 / math.sqrt(shard * 2 * NY * 2 * NZ)
    vals = tile_vals[0, 0]
    count = tile_count[0]
    row, col = lax.axis_index("row"), lax.axis_index("col")
    y, core, z, x = row // 2, row % 2, col // 2, col % 2
    owner_row, owner_col = tile_rows[0, 0] // 2, tile_cols[0, 0] // 2
    rel_z = (owner_row // 2 - z) % NZ
    rel_x = (owner_row + x) % 2
    rows = (rel_z * 2 + rel_x) * 2 + tile_rows[0, 0] % 2
    rel_y = (owner_col // 2 - y) % NY
    rel_c = (owner_col + core) % 2
    cols = (rel_y * 2 + rel_c) * 2 + tile_cols[0, 0] % 2
    steps = jnp.arange(2 * NY, dtype=jnp.int32)
    order = (steps // 2 + y) % NY * 2 + (steps + core) % 2

    source = gather_row(feats)
    work = 2 * 192 * TILE * TILE * 256
    own, kept, up, down, over, far_up, far_down = call(
        forward_body,
        "forward_tiles",
        (
            shape(shard, F32),
            jax.ShapeDtypeStruct((6, shard, 256), F32),
            shape(shard, BF16),
            shape(shard, BF16),
            jax.ShapeDtypeStruct((5, shard, 256), BF16),
            shape(shard, BF16),
            shape(shard, BF16),
        ),
        (rows, cols, count, vals, *[source[k // 2, k % 2] for k in range(8)]),
        scalars=3,
        scratch=(pltpu.VMEM((16, TILE, 256), BF16), pltpu.VMEM((33, TILE, 256), F32)),
        flops=work,
        moved=16 * 2**20,
    )
    over = to_x(over)
    far_up, far_down = to_z(far_up, 3), to_z(far_down, -3)
    up, down = to_z(up, 1), to_z(down, -1)
    sends = call(
        relay_body,
        "relay",
        tuple(shape(shard, BF16) for _ in range(6)),
        (kept, up, down, over, far_up, far_down),
        moved=4 * 2**20,
    )
    got = [to_x(sends[0])] + [to_z(a, s) for a, s in zip(sends[1:], (1, -1, 2, -2, 4))]
    hidden_out, own_grad, high, low = call(
        activate_body,
        "activate",
        tuple(shape(shard, BF16) for _ in range(4)),
        (own, *got, weight, bias[None, :], grad_out),
        flops=4 * 256**3,
        moved=2 * 2**20,
    )
    grads = gather_col(own_grad)
    kept_terms, sent_terms = call(
        terms_body,
        "weight_terms",
        (jax.ShapeDtypeStruct((NY, 40, 256), F32), jax.ShapeDtypeStruct((NY, 40, 256), F32)),
        (order, high, low, own_grad),
        scalars=1,
        scratch=(pltpu.VMEM((256, 256), F32),),
        flops=4 * 256**3,
        moved=2**20,
    )
    grad_weight, grad_bias = sum_terms(kept_terms, sent_terms, order, scale)
    own, kept, same, over = call(
        backward_body,
        "backward_tiles",
        (
            shape(shard, F32),
            jax.ShapeDtypeStruct((3, shard, 256), F32),
            shape(shard, BF16),
            jax.ShapeDtypeStruct((3, shard, 256), BF16),
        ),
        (rows, cols, count, vals, *[grads[k // 2, k % 2] for k in range(16)]),
        scalars=3,
        scratch=(pltpu.VMEM((32, TILE, 256), BF16), pltpu.VMEM((17, TILE, 256), F32)),
        flops=work,
        moved=16 * 2**20,
    )
    over = to_core(over)
    same = to_core(same)
    sends = call(
        back_relay_body,
        "back_relay",
        tuple(shape(shard, BF16) for _ in range(3)),
        (kept, over),
        moved=2**20,
    )
    got = [to_y(a, s) for a, s in zip(sends, (1, 2, 3))]
    grad_feats = call(
        finish_body,
        "finish",
        shape(shard, BF16),
        (own, same, *got, weight),
        flops=2 * 256**3,
        moved=2**20,
    )
    return (hidden_out, grad_feats, grad_weight, grad_bias[0])


def solution(mesh):
    in_specs = (
        P(("slab", "col", "row"), None),
        P(),
        P(),
        P(("slab", "row", "col"), None),
        P(("slab", "row"), "col", None, None, None),
        P(("slab", "row"), "col", None),
        P(("slab", "row"), "col", None),
        P(("slab", "row"), "col"),
    )
    out_specs = (
        P(("slab", "row", "col"), None),
        P(("slab", "col", "row"), None),
        P("slab", None),
        P("slab"),
    )
    return jax.shard_map(
        per_device, mesh=mesh, in_specs=in_specs, out_specs=out_specs, check_vma=False
    )
```

time: 1990 us -> 164 us (0.08)
  waiting for transfers between devices: 1500 us -> 42.5 us
  blocking collectives: 327 us -> 0 us
  starting transfers between devices: 0.21 us -> 105 us
  other arithmetic: 80.4 us -> 0.82 us
  matrix products: 40 us -> 0 us
  local copies, waits for them, and re-layouts: 30.1 us -> 4.27 us
    psum x1 -> x0, waiting for transfers between devices: 1150 us -> none  [per_device(): lax.psum((local_weight, local_bias), ('row', 'col'))]
    psum x1 -> x0, blocking collectives: 327 us -> none  [per_device(): lax.psum((local_weight, local_bias), ('row', 'col'))]
    reduce_scatter x2 -> x0, waiting for transfers between devices: 233 us -> none  [the longest x1 233 us: per_device(): lax.psum_scatter(partial_value.astype(jnp.bfloat16), 'col', scatter_dimen...]
    all_gather x2 -> x0, waiting for transfers between devices: 108 us -> none  [the longest x1 77.7 us: per_device(): grad_block = lax.all_gather(own_grad, 'col', axis=0, tiled=True)]
    ppermute x0 -> x50, starting transfers between devices: none -> 105 us  [the longest x18 40.7 us: to_z(): lax.ppermute(a, 'col', [(i, (i + 2 * step) % (2 * NZ)) for i in range(2 *...]
    scatter-add x8 -> x0, other arithmetic: 65.7 us -> none  [the longest x4 39.8 us: forward_accumulate(): return running.at[slot_rows].add(product * live_mask[:, None, None])]
    ppermute x0 -> x50, waiting for transfers between devices: none -> 42.5 us  [the longest x18 18.1 us: to_z(): lax.ppermute(a, 'col', [(i, (i + 2 * step) % (2 * NZ)) for i in range(2 *...]
    dot_general x11 -> x0, matrix products: 40 us -> none  [the longest x4 18.9 us: backward_accumulate(): jnp.einsum('tmn,tmh->tnh', tile_block, picked, preferred_element_type=jnp...]
  transfers between devices with their start and end apart: 5 -> 50, of which waited for: 4 -> 17; matrix products, arithmetic and copies ran while one was open for 1% -> 1% of each run, Pallas kernels for 0% -> 3%
where the time goes in v1:
time: 164 us; the launch traced here: 163 us
  starting transfers between devices  105 us (64%)
  waiting for transfers between devices  42.5 us (26%)
  Pallas kernels  8.91 us (5%)
  local copies, waits for them, and re-layouts  4.27 us (3%)
    ppermute x18, starting transfers between devices, to_z(): lax.ppermute(a, 'col', [(i, (i + 2 * step) % (2 * NZ)) for i in range(2 *...  40.7 us
    ppermute x8, starting transfers between devices, to_core(): return lax.ppermute(a, 'row', [(i, i ^ 1) for i in range(2 * NY)])  26.1 us
    ppermute x9, starting transfers between devices, to_x(): return lax.ppermute(a, 'col', [(i, i ^ 1) for i in range(2 * NZ)])  20 us
    ppermute x18, waiting for transfers between devices, to_z(): lax.ppermute(a, 'col', [(i, (i + 2 * step) % (2 * NZ)) for i in range(2 *...  18.1 us
    ppermute x12, starting transfers between devices, to_y(): lax.ppermute(a, 'row', [(i, (i + 2 * step) % (2 * NY)) for i in range(2 *...  15.4 us
    ppermute x3, waiting for transfers between devices, flip_z(): return lax.ppermute(a, 'col', [(i, i ^ 2 * bit) for i in range(2 * NZ)])  11.4 us
    pallas_call x8, Pallas kernels, call(): pl.pallas_call(body, name=name, out_shape=out_shape, in_specs=[smem()] *...  8.91 us
    ppermute x12, waiting for transfers between devices, to_y(): lax.ppermute(a, 'row', [(i, (i + 2 * step) % (2 * NY)) for i in range(2 *...  6.39 us
  transfers between devices with their start and end apart: 50, of which 17 were waited for; matrix products, arithmetic and copies ran while one was open for 1% of the time, Pallas kernels for 3%

profile of v1, /device:TPU:1, one launch (start us, length us, event | category | flops | bytes accessed | tf_op | source)
XLA Modules:
  0.0 162.7 jit_solution(9120651601785362616)
XLA Ops:
  0.6 3.8 %collective-permute-start.3 = (bf16[256,256]{1,0:T(8,128)(2,1)}, bf16[256,256]{1,0:T(8,128)(2,1)S(1)}, u32[]{:S(2)}, u32[]{:S(2)}) collective-permute-start(bf16[256,256]{1,0:T(8,128)(2,1)} %rest_0_.1), channel_id=1, source_target_pairs={{0,128},{32,160},{64,192},{96,224},{128,0},{160,32},{192,64},{224,... | collective-permute-start | bytes 393224 | tf_op jit(solution)/shard_map/ppermute | solution.py:50
  8.1 3.3 %collective-permute-start.4 = (bf16[256,256]{1,0:T(8,128)(2,1)S(1)}, bf16[256,256]{1,0:T(8,128)(2,1)S(1)}, u32[]{:S(2)}, u32[]{:S(2)}) collective-permute-start(bf16[256,256]{1,0:T(8,128)(2,1)S(1)} %collective-permute-done.3.rest_4_), channel_id=1, source_target_pairs={{0,32},{32,0},{64,96},{96,64},{128,160},{160,128},{192,224},{224,1... | collective-permute-start | bytes 393224 | tf_op jit(solution)/shard_map/ppermute | solution.py:46
  14.7 2.8 %copy-done = bf16[1,1,192,128,128]{4,3,2,1,0:T(8,128)(2,1)S(1)} copy-done((bf16[1,1,192,128,128]{4,3,2,1,0:T(8,128)(2,1)S(1)}, bf16[1,1,192,128,128]{4,3,2,1,0:T(8,128)(2,1)}, u32[]{:S(2)}) %copy-start) | copy-done | bytes 6291480
  22.1 8.3 %collective-permute-start.7 = (bf16[256,256]{1,0:T(8,128)(2,1)S(1)}, bf16[256,256]{1,0:T(8,128)(2,1)S(1)}, u32[]{:S(2)}, u32[]{:S(2)}) collective-permute-start(bf16[256,256]{1,0:T(8,128)(2,1)S(1)} %get-tuple-element.34), channel_id=1, source_target_pairs={{0,4},{2,6},{4,8},{6,10},{8,12},{10,14},{12,16},{14,18},{16,20},{1... | collective-permute-start | bytes 393224 | tf_op jit(solution)/shard_map/ppermute | solution.py:58
  31.4 3.1 %collective-permute-start.10 = (bf16[256,256]{1,0:T(8,128)(2,1)S(1)}, bf16[256,256]{1,0:T(8,128)(2,1)S(1)}, u32[]{:S(2)}, u32[]{:S(2)}) collective-permute-start(bf16[256,256]{1,0:T(8,128)(2,1)S(1)} %get-tuple-element.37), channel_id=1, source_target_pairs={{0,12},{2,14},{4,16},{6,18},{8,20},{10,22},{12,24},{14,26},{16,28}... | collective-permute-start | bytes 393224 | tf_op jit(solution)/shard_map/ppermute | solution.py:58
  35.8 6.8 %collective-permute-done.10.far_up = bf16[256,256]{1,0:T(8,128)(2,1)S(1)} collective-permute-done((bf16[256,256]{1,0:T(8,128)(2,1)S(1)}, bf16[256,256]{1,0:T(8,128)(2,1)S(1)}, u32[]{:S(2)}, u32[]{:S(2)}) %collective-permute-start.10) | collective-permute-done | bytes 131104 | tf_op jit(solution)/shard_map/ppermute | solution.py:58
  42.9 4.0 %collective-permute-start.12 = (bf16[256,256]{1,0:T(8,128)(2,1)S(1)}, bf16[256,256]{1,0:T(8,128)(2,1)S(1)}, u32[]{:S(2)}, u32[]{:S(2)}) collective-permute-start(bf16[256,256]{1,0:T(8,128)(2,1)S(1)} %get-tuple-element.39), channel_id=1, source_target_pairs={{0,2},{2,0},{4,6},{6,4},{8,10},{10,8},{12,14},{14,12},{16,18},{18,... | collective-permute-start | bytes 393224 | tf_op jit(solution)/shard_map/ppermute | solution.py:54
  47.0 2.6 %collective-permute-start.14 = (bf16[256,256]{1,0:T(8,128)(2,1)S(1)}, bf16[256,256]{1,0:T(8,128)(2,1)S(1)}, u32[]{:S(2)}, u32[]{:S(2)}) collective-permute-start(bf16[256,256]{1,0:T(8,128)(2,1)S(1)} %get-tuple-element.41), channel_id=1, source_target_pairs={{0,28},{2,30},{4,0},{6,2},{8,4},{10,6},{12,8},{14,10},{16,12},{18,... | collective-permute-start | bytes 393224 | tf_op jit(solution)/shard_map/ppermute | solution.py:58
  53.2 4.9 %collective-permute-start.17 = (bf16[256,256]{1,0:T(8,128)(2,1)S(1)}, bf16[256,256]{1,0:T(8,128)(2,1)S(1)}, u32[]{:S(2)}, u32[]{:S(2)}) collective-permute-start(bf16[256,256]{1,0:T(8,128)(2,1)S(1)} %get-tuple-element.44), channel_id=1, source_target_pairs={{0,16},{2,18},{4,20},{6,22},{8,24},{10,26},{12,28},{14,30},{16,0},... | collective-permute-start | bytes 393224 | tf_op jit(solution)/shard_map/ppermute | solution.py:58
  58.0 4.5 %collective-permute-done.16.e = bf16[256,256]{1,0:T(8,128)(2,1)S(1)} collective-permute-done((bf16[256,256]{1,0:T(8,128)(2,1)S(1)}, bf16[256,256]{1,0:T(8,128)(2,1)S(1)}, u32[]{:S(2)}, u32[]{:S(2)}) %collective-permute-start.16) | collective-permute-done | bytes 131104 | tf_op jit(solution)/shard_map/ppermute | solution.py:58
  66.7 4.2 %collective-permute-start.38 = (f32[4,40,256]{2,1,0:T(8,128)S(1)}, f32[4,40,256]{2,1,0:T(8,128)S(1)}, u32[]{:S(2)}, u32[]{:S(2)}) collective-permute-start(f32[4,40,256]{2,1,0:T(8,128)S(1)} %get-tuple-element.57), channel_id=1, source_target_pairs={{0,32},{32,0},{64,96},{96,64},{128,160},{160,128},{192,224},{224,1... | collective-permute-start | bytes 491528 | tf_op jit(solution)/shard_map/ppermute | solution.py:46
  73.0 3.0 %collective-permute-start.25 = (bf16[256,256]{1,0:T(8,128)(2,1)S(1)}, bf16[256,256]{1,0:T(8,128)(2,1)S(1)}, u32[]{:S(2)}, u32[]{:S(2)}) collective-permute-start(bf16[256,256]{1,0:T(8,128)(2,1)S(1)} %get-tuple-element.46.rest_0_.grad), channel_id=1, source_target_pairs={{0,16},{2,18},{4,20},{6,22},{8,24},{10,26},{12,28},{14,30},{16,0},... | collective-permute-start | bytes 393224 | tf_op jit(solution)/shard_map/ppermute | solution.py:58
  76.0 2.7 %collective-permute-start.21 = (bf16[256,256]{1,0:T(8,128)(2,1)S(1)}, bf16[256,256]{1,0:T(8,128)(2,1)S(1)}, u32[]{:S(2)}, u32[]{:S(2)}) collective-permute-start(bf16[256,256]{1,0:T(8,128)(2,1)S(1)} %get-tuple-element.46.rest_0_.grad), channel_id=1, source_target_pairs={{0,24},{2,26},{4,28},{6,30},{8,0},{10,2},{12,4},{14,6},{16,8},{18,... | collective-permute-start | bytes 393224 | tf_op jit(solution)/shard_map/ppermute | solution.py:58
  78.7 5.7 %collective-permute-start.18 = (bf16[256,256]{1,0:T(8,128)(2,1)S(1)}, bf16[256,256]{1,0:T(8,128)(2,1)S(1)}, u32[]{:S(2)}, u32[]{:S(2)}) collective-permute-start(bf16[256,256]{1,0:T(8,128)(2,1)S(1)} %get-tuple-element.46.rest_0_.grad), channel_id=1, source_target_pairs={{0,2},{2,0},{4,6},{6,4},{8,10},{10,8},{12,14},{14,12},{16,18},{18,... | collective-permute-start | bytes 393224 | tf_op jit(solution)/shard_map/ppermute | solution.py:54
  87.0 3.5 %collective-permute-done.21.rest_4_ = bf16[256,256]{1,0:T(8,128)(2,1)S(1)} collective-permute-done((bf16[256,256]{1,0:T(8,128)(2,1)S(1)}, bf16[256,256]{1,0:T(8,128)(2,1)S(1)}, u32[]{:S(2)}, u32[]{:S(2)}) %collective-permute-start.21) | collective-permute-done | bytes 131104 | tf_op jit(solution)/shard_map/ppermute | solution.py:58
  98.7 4.3 %collective-permute-start.24 = (bf16[256,256]{1,0:T(8,128)(2,1)S(1)}, bf16[256,256]{1,0:T(8,128)(2,1)S(1)}, u32[]{:S(2)}, u32[]{:S(2)}) collective-permute-start(bf16[256,256]{1,0:T(8,128)(2,1)S(1)} %collective-permute-done.18.rest_1_), channel_id=1, source_target_pairs={{0,20},{2,22},{4,24},{6,26},{8,28},{10,30},{12,0},{14,2},{16,4},{1... | collective-permute-start | bytes 393224 | tf_op jit(solution)/shard_map/ppermute | solution.py:58
  103.8 2.9 %collective-permute-start.39 = (f32[40,256]{1,0:T(8,128)S(1)}, f32[40,256]{1,0:T(8,128)S(1)}, u32[]{:S(2)}, u32[]{:S(2)}) collective-permute-start(f32[40,256]{1,0:T(8,128)S(1)} %get-tuple-element.60), channel_id=1, source_target_pairs={{0,64},{32,96},{64,128},{96,160},{128,192},{160,224},{192,0},{224,... | collective-permute-start | bytes 122888 | tf_op jit(solution)/shard_map/ppermute | solution.py:50
  113.6 9.1 %collective-permute-start.34 = (bf16[3,256,256]{2,1,0:T(8,128)(2,1)S(1)}, bf16[3,256,256]{2,1,0:T(8,128)(2,1)S(1)}, u32[]{:S(2)}, u32[]{:S(2)}) collective-permute-start(bf16[3,256,256]{2,1,0:T(8,128)(2,1)S(1)} %get-tuple-element.50), channel_id=1, source_target_pairs={{0,32},{32,0},{64,96},{96,64},{128,160},{160,128},{192,224},{224,1... | collective-permute-start | bytes 1179656 | tf_op jit(solution)/shard_map/ppermute | solution.py:46
  122.8 4.3 %collective-permute-done.42 = f32[40,256]{1,0:T(8,128)S(1)} collective-permute-done((f32[40,256]{1,0:T(8,128)S(1)}, f32[40,256]{1,0:T(8,128)S(1)}, u32[]{:S(2)}, u32[]{:S(2)}) %collective-permute-start.42) | collective-permute-done | bytes 40992 | tf_op jit(solution)/shard_map/ppermute | solution.py:54
  127.1 2.8 %collective-permute-done.43 = f32[40,256]{1,0:T(8,128)S(1)} collective-permute-done((f32[40,256]{1,0:T(8,128)S(1)}, f32[40,256]{1,0:T(8,128)S(1)}, u32[]{:S(2)}, u32[]{:S(2)}) %collective-permute-start.43) | collective-permute-done | bytes 40992 | tf_op jit(solution)/shard_map/ppermute | solution.py:62
  130.0 3.9 %collective-permute-done.44 = f32[40,256]{1,0:T(8,128)S(1)} collective-permute-done((f32[40,256]{1,0:T(8,128)S(1)}, f32[40,256]{1,0:T(8,128)S(1)}, u32[]{:S(2)}, u32[]{:S(2)}) %collective-permute-start.44) | collective-permute-done | bytes 40992 | tf_op jit(solution)/shard_map/ppermute | solution.py:62
  136.4 4.7 %collective-permute-done.45 = f32[40,256]{1,0:T(8,128)S(1)} collective-permute-done((f32[40,256]{1,0:T(8,128)S(1)}, f32[40,256]{1,0:T(8,128)S(1)}, u32[]{:S(2)}, u32[]{:S(2)}) %collective-permute-start.45) | collective-permute-done | bytes 40992 | tf_op jit(solution)/shard_map/ppermute | solution.py:62
  146.2 6.0 %collective-permute-start.49 = (f32[4,40,256]{2,1,0:T(8,128)S(1)}, f32[4,40,256]{2,1,0:T(8,128)S(1)}, u32[]{:S(2)}, u32[]{:S(2)}) collective-permute-start(f32[4,40,256]{2,1,0:T(8,128)S(1)} %pad_maximum_fusion.same), channel_id=1, source_target_pairs={{0,32},{32,0},{64,96},{96,64},{128,160},{160,128},{192,224},{224,1... | collective-permute-start | bytes 491528 | tf_op jit(solution)/shard_map/ppermute | solution.py:46
  158.4 3.4 %collective-permute-done.36.c = bf16[256,256]{1,0:T(8,128)(2,1)S(1)} collective-permute-done((bf16[256,256]{1,0:T(8,128)(2,1)S(1)}, bf16[256,256]{1,0:T(8,128)(2,1)S(1)}, u32[]{:S(2)}, u32[]{:S(2)}) %collective-permute-start.36) | collective-permute-done | bytes 131104 | tf_op jit(solution)/shard_map/ppermute | solution.py:50
  (107 shorter events, 56.2 us)
Async XLA Ops:
  20.7 21.9 %collective-permute-start.9 = (bf16[5,256,256]{2,1,0:T(8,128)(2,1)S(1)}, bf16[5,256,256]{2,1,0:T(8,128)(2,1)S(1)}, u32[]{:S(2)}, u32[]{:S(2)}) collective-permute-start(bf16[5,256,256]{2,1,0:T(8,128)(2,1)S(1)} %get-tuple-element.36), channel_id=1, source_target_pairs={{0,2},{2,0},{4,6},{6,4},{8,10},{10,8},{12,14},{14,12},{16,18},{18,... | collective-permute-start | bytes 1966088 | tf_op jit(solution)/shard_map/ppermute | solution.py:54
  22.1 13.7 %collective-permute-start.7 = (bf16[256,256]{1,0:T(8,128)(2,1)S(1)}, bf16[256,256]{1,0:T(8,128)(2,1)S(1)}, u32[]{:S(2)}, u32[]{:S(2)}) collective-permute-start(bf16[256,256]{1,0:T(8,128)(2,1)S(1)} %get-tuple-element.34), channel_id=1, source_target_pairs={{0,4},{2,6},{4,8},{6,10},{8,12},{10,14},{12,16},{14,18},{16,20},{1... | collective-permute-start | bytes 393224 | tf_op jit(solution)/shard_map/ppermute | solution.py:58
  31.4 11.3 %collective-permute-start.10 = (bf16[256,256]{1,0:T(8,128)(2,1)S(1)}, bf16[256,256]{1,0:T(8,128)(2,1)S(1)}, u32[]{:S(2)}, u32[]{:S(2)}) collective-permute-start(bf16[256,256]{1,0:T(8,128)(2,1)S(1)} %get-tuple-element.37), channel_id=1, source_target_pairs={{0,12},{2,14},{4,16},{6,18},{8,20},{10,22},{12,24},{14,26},{16,28}... | collective-permute-start | bytes 393224 | tf_op jit(solution)/shard_map/ppermute | solution.py:58
  42.9 10.3 %collective-permute-start.12 = (bf16[256,256]{1,0:T(8,128)(2,1)S(1)}, bf16[256,256]{1,0:T(8,128)(2,1)S(1)}, u32[]{:S(2)}, u32[]{:S(2)}) collective-permute-start(bf16[256,256]{1,0:T(8,128)(2,1)S(1)} %get-tuple-element.39), channel_id=1, source_target_pairs={{0,2},{2,0},{4,6},{6,4},{8,10},{10,8},{12,14},{14,12},{16,18},{18,... | collective-permute-start | bytes 393224 | tf_op jit(solution)/shard_map/ppermute | solution.py:54
  46.9 11.1 %collective-permute-start.13 = (bf16[256,256]{1,0:T(8,128)(2,1)S(1)}, bf16[256,256]{1,0:T(8,128)(2,1)S(1)}, u32[]{:S(2)}, u32[]{:S(2)}) collective-permute-start(bf16[256,256]{1,0:T(8,128)(2,1)S(1)} %get-tuple-element.40), channel_id=1, source_target_pairs={{0,4},{2,6},{4,8},{6,10},{8,12},{10,14},{12,16},{14,18},{16,20},{1... | collective-permute-start | bytes 393224 | tf_op jit(solution)/shard_map/ppermute | solution.py:58
  47.0 11.1 %collective-permute-start.14 = (bf16[256,256]{1,0:T(8,128)(2,1)S(1)}, bf16[256,256]{1,0:T(8,128)(2,1)S(1)}, u32[]{:S(2)}, u32[]{:S(2)}) collective-permute-start(bf16[256,256]{1,0:T(8,128)(2,1)S(1)} %get-tuple-element.41), channel_id=1, source_target_pairs={{0,28},{2,30},{4,0},{6,2},{8,4},{10,6},{12,8},{14,10},{16,12},{18,... | collective-permute-start | bytes 393224 | tf_op jit(solution)/shard_map/ppermute | solution.py:58
  51.4 11.2 %collective-permute-start.16 = (bf16[256,256]{1,0:T(8,128)(2,1)S(1)}, bf16[256,256]{1,0:T(8,128)(2,1)S(1)}, u32[]{:S(2)}, u32[]{:S(2)}) collective-permute-start(bf16[256,256]{1,0:T(8,128)(2,1)S(1)} %get-tuple-element.43), channel_id=1, source_target_pairs={{0,24},{2,26},{4,28},{6,30},{8,0},{10,2},{12,4},{14,6},{16,8},{18,... | collective-permute-start | bytes 393224 | tf_op jit(solution)/shard_map/ppermute | solution.py:58
  53.2 9.4 %collective-permute-start.17 = (bf16[256,256]{1,0:T(8,128)(2,1)S(1)}, bf16[256,256]{1,0:T(8,128)(2,1)S(1)}, u32[]{:S(2)}, u32[]{:S(2)}) collective-permute-start(bf16[256,256]{1,0:T(8,128)(2,1)S(1)} %get-tuple-element.44), channel_id=1, source_target_pairs={{0,16},{2,18},{4,20},{6,22},{8,24},{10,26},{12,28},{14,30},{16,0},... | collective-permute-start | bytes 393224 | tf_op jit(solution)/shard_map/ppermute | solution.py:58
  63.5 15.1 %collective-permute-start.31 = (bf16[256,256]{1,0:T(8,128)(2,1)S(1)}, bf16[256,256]{1,0:T(8,128)(2,1)S(1)}, u32[]{:S(2)}, u32[]{:S(2)}) collective-permute-start(bf16[256,256]{1,0:T(8,128)(2,1)S(1)} %get-tuple-element.46.rest_0_.grad), channel_id=1, source_target_pairs={{0,4},{2,6},{4,8},{6,10},{8,12},{10,14},{12,16},{14,18},{16,20},{1... | collective-permute-start | bytes 393224 | tf_op jit(solution)/shard_map/ppermute | solution.py:58
  66.7 27.0 %collective-permute-start.38 = (f32[4,40,256]{2,1,0:T(8,128)S(1)}, f32[4,40,256]{2,1,0:T(8,128)S(1)}, u32[]{:S(2)}, u32[]{:S(2)}) collective-permute-start(f32[4,40,256]{2,1,0:T(8,128)S(1)} %get-tuple-element.57), channel_id=1, source_target_pairs={{0,32},{32,0},{64,96},{96,64},{128,160},{160,128},{192,224},{224,1... | collective-permute-start | bytes 491528 | tf_op jit(solution)/shard_map/ppermute | solution.py:46
  73.0 12.7 %collective-permute-start.25 = (bf16[256,256]{1,0:T(8,128)(2,1)S(1)}, bf16[256,256]{1,0:T(8,128)(2,1)S(1)}, u32[]{:S(2)}, u32[]{:S(2)}) collective-permute-start(bf16[256,256]{1,0:T(8,128)(2,1)S(1)} %get-tuple-element.46.rest_0_.grad), channel_id=1, source_target_pairs={{0,16},{2,18},{4,20},{6,22},{8,24},{10,26},{12,28},{14,30},{16,0},... | collective-permute-start | bytes 393224 | tf_op jit(solution)/shard_map/ppermute | solution.py:58
  76.0 14.5 %collective-permute-start.21 = (bf16[256,256]{1,0:T(8,128)(2,1)S(1)}, bf16[256,256]{1,0:T(8,128)(2,1)S(1)}, u32[]{:S(2)}, u32[]{:S(2)}) collective-permute-start(bf16[256,256]{1,0:T(8,128)(2,1)S(1)} %get-tuple-element.46.rest_0_.grad), channel_id=1, source_target_pairs={{0,24},{2,26},{4,28},{6,30},{8,0},{10,2},{12,4},{14,6},{16,8},{18,... | collective-permute-start | bytes 393224 | tf_op jit(solution)/shard_map/ppermute | solution.py:58
  78.7 14.1 %collective-permute-start.19 = (bf16[256,256]{1,0:T(8,128)(2,1)S(1)}, bf16[256,256]{1,0:T(8,128)(2,1)S(1)}, u32[]{:S(2)}, u32[]{:S(2)}) collective-permute-start(bf16[256,256]{1,0:T(8,128)(2,1)S(1)} %get-tuple-element.46.rest_0_.grad), channel_id=1, source_target_pairs={{0,28},{2,30},{4,0},{6,2},{8,4},{10,6},{12,8},{14,10},{16,12},{18,... | collective-permute-start | bytes 393224 | tf_op jit(solution)/shard_map/ppermute | solution.py:58
  78.7 17.2 %collective-permute-start.18 = (bf16[256,256]{1,0:T(8,128)(2,1)S(1)}, bf16[256,256]{1,0:T(8,128)(2,1)S(1)}, u32[]{:S(2)}, u32[]{:S(2)}) collective-permute-start(bf16[256,256]{1,0:T(8,128)(2,1)S(1)} %get-tuple-element.46.rest_0_.grad), channel_id=1, source_target_pairs={{0,2},{2,0},{4,6},{6,4},{8,10},{10,8},{12,14},{14,12},{16,18},{18,... | collective-permute-start | bytes 393224 | tf_op jit(solution)/shard_map/ppermute | solution.py:54
  85.6 10.7 %collective-permute-start.32 = (bf16[256,256]{1,0:T(8,128)(2,1)S(1)}, bf16[256,256]{1,0:T(8,128)(2,1)S(1)}, u32[]{:S(2)}, u32[]{:S(2)}) collective-permute-start(bf16[256,256]{1,0:T(8,128)(2,1)S(1)} %collective-permute-done.31.rest_14_), channel_id=1, source_target_pairs={{0,2},{2,0},{4,6},{6,4},{8,10},{10,8},{12,14},{14,12},{16,18},{18,... | collective-permute-start | bytes 393224 | tf_op jit(solution)/shard_map/ppermute | solution.py:54
  93.6 9.4 %collective-permute-start.26 = (bf16[256,256]{1,0:T(8,128)(2,1)S(1)}, bf16[256,256]{1,0:T(8,128)(2,1)S(1)}, u32[]{:S(2)}, u32[]{:S(2)}) collective-permute-start(bf16[256,256]{1,0:T(8,128)(2,1)S(1)} %collective-permute-done.25.rest_8_), channel_id=1, source_target_pairs={{0,2},{2,0},{4,6},{6,4},{8,10},{10,8},{12,14},{14,12},{16,18},{18,... | collective-permute-start | bytes 393224 | tf_op jit(solution)/shard_map/ppermute | solution.py:54
  96.3 10.4 %collective-permute-start.22 = (bf16[256,256]{1,0:T(8,128)(2,1)S(1)}, bf16[256,256]{1,0:T(8,128)(2,1)S(1)}, u32[]{:S(2)}, u32[]{:S(2)}) collective-permute-start(bf16[256,256]{1,0:T(8,128)(2,1)S(1)} %collective-permute-done.21.rest_4_), channel_id=1, source_target_pairs={{0,2},{2,0},{4,6},{6,4},{8,10},{10,8},{12,14},{14,12},{16,18},{18,... | collective-permute-start | bytes 393224 | tf_op jit(solution)/shard_map/ppermute | solution.py:54
  98.5 12.7 %collective-permute-start.29 = (bf16[256,256]{1,0:T(8,128)(2,1)S(1)}, bf16[256,256]{1,0:T(8,128)(2,1)S(1)}, u32[]{:S(2)}, u32[]{:S(2)}) collective-permute-start(bf16[256,256]{1,0:T(8,128)(2,1)S(1)} %collective-permute-done.18.rest_1_), channel_id=1, source_target_pairs={{0,12},{2,14},{4,16},{6,18},{8,20},{10,22},{12,24},{14,26},{16,28}... | collective-permute-start | bytes 393224 | tf_op jit(solution)/shard_map/ppermute | solution.py:58
  98.7 12.6 %collective-permute-start.24 = (bf16[256,256]{1,0:T(8,128)(2,1)S(1)}, bf16[256,256]{1,0:T(8,128)(2,1)S(1)}, u32[]{:S(2)}, u32[]{:S(2)}) collective-permute-start(bf16[256,256]{1,0:T(8,128)(2,1)S(1)} %collective-permute-done.18.rest_1_), channel_id=1, source_target_pairs={{0,20},{2,22},{4,24},{6,26},{8,28},{10,30},{12,0},{14,2},{16,4},{1... | collective-permute-start | bytes 393224 | tf_op jit(solution)/shard_map/ppermute | solution.py:58
  103.8 18.9 %collective-permute-start.39 = (f32[40,256]{1,0:T(8,128)S(1)}, f32[40,256]{1,0:T(8,128)S(1)}, u32[]{:S(2)}, u32[]{:S(2)}) collective-permute-start(f32[40,256]{1,0:T(8,128)S(1)} %get-tuple-element.60), channel_id=1, source_target_pairs={{0,64},{32,96},{64,128},{96,160},{128,192},{160,224},{192,0},{224,... | collective-permute-start | bytes 122888 | tf_op jit(solution)/shard_map/ppermute | solution.py:50
  106.7 15.9 %collective-permute-start.41 = (f32[40,256]{1,0:T(8,128)S(1)}, f32[40,256]{1,0:T(8,128)S(1)}, u32[]{:S(2)}, u32[]{:S(2)}) collective-permute-start(f32[40,256]{1,0:T(8,128)S(1)} %get-tuple-element.61), channel_id=1, source_target_pairs={{0,128},{32,160},{64,192},{96,224},{128,0},{160,32},{192,64},{224,... | collective-permute-start | bytes 122888 | tf_op jit(solution)/shard_map/ppermute | solution.py:50
  108.6 14.0 %collective-permute-start.40 = (f32[40,256]{1,0:T(8,128)S(1)}, f32[40,256]{1,0:T(8,128)S(1)}, u32[]{:S(2)}, u32[]{:S(2)}) collective-permute-start(f32[40,256]{1,0:T(8,128)S(1)} %get-tuple-element.62), channel_id=1, source_target_pairs={{0,192},{32,224},{64,0},{96,32},{128,64},{160,96},{192,128},{224,1... | collective-permute-start | bytes 122888 | tf_op jit(solution)/shard_map/ppermute | solution.py:50
  113.6 38.7 %collective-permute-start.34 = (bf16[3,256,256]{2,1,0:T(8,128)(2,1)S(1)}, bf16[3,256,256]{2,1,0:T(8,128)(2,1)S(1)}, u32[]{:S(2)}, u32[]{:S(2)}) collective-permute-start(bf16[3,256,256]{2,1,0:T(8,128)(2,1)S(1)} %get-tuple-element.50), channel_id=1, source_target_pairs={{0,32},{32,0},{64,96},{96,64},{128,160},{160,128},{192,224},{224,1... | collective-permute-start | bytes 1179656 | tf_op jit(solution)/shard_map/ppermute | solution.py:46
  146.2 10.1 %collective-permute-start.49 = (f32[4,40,256]{2,1,0:T(8,128)S(1)}, f32[4,40,256]{2,1,0:T(8,128)S(1)}, u32[]{:S(2)}, u32[]{:S(2)}) collective-permute-start(f32[4,40,256]{2,1,0:T(8,128)S(1)} %pad_maximum_fusion.same), channel_id=1, source_target_pairs={{0,32},{32,0},{64,96},{96,64},{128,160},{160,128},{192,224},{224,1... | collective-permute-start | bytes 491528 | tf_op jit(solution)/shard_map/ppermute | solution.py:46
  (32 other events, 403.6 us)

commit v2 on v0

v2 whole, which is shorter than its diff:
```python
import functools
import math

import jax
import jax.numpy as jnp
from jax import lax
from jax.experimental import pallas as pl
from jax.experimental.pallas import tpu as pltpu
from jax.sharding import PartitionSpec as P

TILE = 128
UNROLL = 8
ORDER = (
    ((0, 0), (0, 1), (1, 0), (7, 0)),
    ((1, 1), (7, 1), (2, 0), (6, 0)),
    ((2, 1), (6, 1), (3, 0), (5, 0)),
    ((3, 1), (5, 1), (4, 0), (4, 1)),
)
NY = 4
NZ = 8
F32 = jnp.float32
BF16 = jnp.bfloat16
LIMIT = pltpu.CompilerParams(vmem_limit_bytes=32 * 2**20)


def vmem():
    return pl.BlockSpec(memory_space=pltpu.VMEM)


def smem():
    return pl.BlockSpec(memory_space=pltpu.SMEM)


def shape(rows, dtype):
    return jax.ShapeDtypeStruct((rows, 256), dtype)


def call(body, name, out_shape, args, scalars=0, scratch=(), flops=0, moved=0, specs=None):
    return pl.pallas_call(
        body,
        name=name,
        out_shape=out_shape,
        in_specs=specs or [smem()] * scalars + [vmem()] * (len(args) - scalars),
        out_specs=jax.tree.map(lambda _: vmem(), out_shape),
        scratch_shapes=scratch,
        compiler_params=LIMIT,
        cost_estimate=pl.CostEstimate(flops=flops, bytes_accessed=moved, transcendentals=0),
    )(*args)


def to_core(a):
    return lax.ppermute(a, "row", [(i, i ^ 1) for i in range(2 * NY)])


def to_y(a, step):
    return lax.ppermute(a, "row", [(i, (i + 2 * step) % (2 * NY)) for i in range(2 * NY)])


def to_x(a):
    return lax.ppermute(a, "col", [(i, i ^ 1) for i in range(2 * NZ)])


def to_z(a, step):
    return lax.ppermute(a, "col", [(i, (i + 2 * step) % (2 * NZ)) for i in range(2 * NZ)])


def gather_row(own):
    got = {(0, 0): own}
    for step in (1, -1, 2):
        got[(-step) % NY, 0] = to_y(own, step)
    got[0, 1] = to_core(own)
    for dy in (1, 3, 2):
        got[dy, 1] = to_core(got[dy, 0])
    return got


def load_body(source, out, sem):
    copy = pltpu.make_async_copy(source, out, sem)
    copy.start()
    copy.wait()


def collect_body(*refs):
    blocks, out = refs[:-1], refs[-1]
    for k, block in enumerate(blocks):
        for half in range(2):
            out[2 * k + half] = block[half * TILE : (half + 1) * TILE]


def place(ref, total, first, dtype):
    for half in range(2):
        ref[half * TILE : (half + 1) * TILE] = total[2 * first + half].astype(dtype)


def add_tiles(group, starts, order, to_slot, product, total, dummy):
    first, last = starts[group], starts[group + 1]

    def batch(i, carry):
        slots = [first + i * UNROLL + u for u in range(UNROLL)]
        safe = [jnp.minimum(t, 191) for t in slots]
        terms = [product(order[t], t) for t in safe]
        for slot, t, term in zip(slots, safe, terms):
            place_at = jnp.where(slot < last, to_slot(t), dummy)
            total[place_at] = total[place_at] + term
        return carry

    lax.fori_loop(0, (last - first + UNROLL - 1) // UNROLL, batch, 0)


def forward_body(group, starts, order, rows, cols, vals, source, *rest):
    outs, total = rest[:-1], rest[-1]
    total[...] = jnp.zeros_like(total)
    add_tiles(
        group,
        starts,
        order,
        lambda t: jnp.clip(rows[t] - 8 * group, 0, 7),
        lambda tile, t: jnp.dot(vals[tile], source[cols[t]], preferred_element_type=F32),
        total,
        8,
    )
    if group == 3:
        far, over, kept = outs
        place(far, total, 3, BF16)
        place(over.at[0], total, 0, BF16)
        place(over.at[1], total, 1, BF16)
        place(kept, total, 2, F32)
    elif group:
        over, kept = outs
        for n in range(2):
            place(over.at[n], total, n, BF16)
            place(kept.at[n], total, 2 + n, F32)
    else:
        own, over, kept = outs
        place(own, total, 0, F32)
        place(over, total, 1, BF16)
        for n in range(2):
            place(kept.at[n], total, 2 + n, F32)


def wide(ref):
    return ref[...].astype(F32)


def split_body(kept, got, low, high):
    total = (kept[...] + wide(got)).astype(BF16)
    low[...] = total[0:TILE]
    high[...] = total[TILE : 2 * TILE]


def relay_half_body(kept, over, up, down, up_out, down_out):
    top, rest = slice(0, TILE), slice(TILE, 2 * TILE)
    up_out[top] = (kept[0, top] + wide(over.at[0, top]) + wide(up)).astype(BF16)
    up_out[rest] = (kept[0, rest] + wide(over.at[0, rest])).astype(BF16)
    down_out[top] = (kept[1, top] + wide(over.at[1, top])).astype(BF16)
    down_out[rest] = (kept[1, rest] + wide(over.at[1, rest]) + wide(down)).astype(BF16)


def relay_body(kept, over, up, down, up_out, down_out):
    up_out[...] = (kept[0] + wide(over.at[0]) + wide(up)).astype(BF16)
    down_out[...] = (kept[1] + wide(over.at[1]) + wide(down)).astype(BF16)


def activate_body(own, over, up, down, weight, bias, given, hidden, grad, message):
    summed = own[...] + wide(over) + wide(up) + wide(down)
    top = summed.astype(BF16)
    rest = (summed - top.astype(F32)).astype(BF16)
    pre_act = (
        jnp.dot(top, weight[...], preferred_element_type=F32)
        + jnp.dot(rest, weight[...], preferred_element_type=F32)
        + bias[...]
    )
    gate_value = jax.nn.sigmoid(pre_act)
    hidden[...] = (pre_act * gate_value).astype(BF16)
    slope = gate_value * (1.0 + pre_act * (1.0 - gate_value))
    result = (given[...].astype(F32) * slope).astype(BF16)
    grad[...] = result
    message[0:256] = result
    message[256:512] = top


def terms_body(z, *refs):
    own, ups, downs, far_grad, far_sum, out, grads, sums = (
        refs[0],
        refs[1:4],
        refs[4:7],
        refs[7],
        refs[8],
        refs[9],
        refs[10],
        refs[11],
    )
    blocks = {0: own, 7: ups[0], 6: ups[1], 5: ups[2], 1: downs[0], 2: downs[1], 3: downs[2]}
    for dz in range(NZ):
        at = (z[0] + dz) % NZ
        if dz == 4:
            grads[at] = far_grad[...]
            sums[at] = far_sum[...]
        else:
            grads[at] = blocks[dz][0:256]
            sums[at] = blocks[dz][256:512]
    total = jnp.zeros((256, 256), F32)
    column = jnp.zeros((1, 256), F32)
    for k in range(NZ):
        total = total + lax.dot_general(
            sums[k], grads[k], (((0,), (0,)), ((), ())), preferred_element_type=F32
        )
        column = column + jnp.sum(grads[k].astype(F32), axis=0, keepdims=True)
    out[0:256] = total
    out[256:264] = jnp.broadcast_to(column, (8, 256))


def backward_body(group, starts, order, rows, cols, vals, *rest):
    count = 4 if group == 0 else 3 if group < 3 else 3
    blocks, rest = rest[:count], rest[count:]
    if group:
        before, rest = rest[0], rest[1:]
    if group == 3:
        own, kept, over, source, total = rest
    else:
        total, source = rest
    n = 0
    for block, size in zip(blocks, (1, 1, 1, 1) if group == 0 else (2, 1, 1)):
        for half in range(2 * size):
            source[n] = block[half * TILE : (half + 1) * TILE]
            n += 1
    if group:
        total[...] = before[...]
    else:
        total[...] = jnp.zeros_like(total)
    add_tiles(
        group,
        starts,
        order,
        lambda t: cols[t],
        lambda tile, t: lax.dot_general(
            vals[tile],
            source[jnp.clip(rows[t] - 8 * group, 0, 7)],
            (((0,), (0,)), ((), ())),
            preferred_element_type=F32,
        ),
        total,
        16,
    )
    if group == 3:
        place(own, total, 0, F32)
        for k, dy in enumerate((1, 2, 3)):
            place(kept.at[k], total, 2 * dy, F32)
            place(over.at[k], total, 2 * dy + 1, BF16)
        place(over.at[3], total, 1, BF16)


def back_relay_body(kept, over, mine, other, out_a, out_b, out_c, own_terms):
    terms = (mine[...] + other[...]).astype(BF16)
    own_terms[0:256] = terms[0:256]
    own_terms[256:272] = jnp.broadcast_to(terms[256:257], (16, 256))
    for k, out in enumerate((out_a, out_b, out_c)):
        out[0:256] = (kept[k] + over[k].astype(F32)).astype(BF16)
        out[256:512] = terms[0:256]
        out[512:528] = jnp.broadcast_to(terms[256:257], (16, 256))


def finish_body(scale, own, over, a, b, c, terms, weight, out, grad_weight, grad_bias):
    back = own[...] + over[3].astype(F32)
    for ref in (a, b, c):
        back = back + ref[0:256].astype(F32)
    out[...] = lax.dot_general(
        back.astype(BF16), weight[...], (((1,), (1,)), ((), ())), preferred_element_type=F32
    ).astype(BF16)
    total = (wide(terms) + b[256:528].astype(F32)) + (
        a[256:528].astype(F32) + c[256:528].astype(F32)
    )
    grad_weight[...] = total[0:256] * scale
    grad_bias[...] = total[256:264] * scale


def per_device(feats, weight, bias, grad_out, tile_vals, tile_rows, tile_cols, tile_count):
    shard = feats.shape[0]
    scale = 1.0 / math.sqrt(shard * 2 * NY * 2 * NZ)
    row, col = lax.axis_index("row"), lax.axis_index("col")
    y, core, z, x = row // 2, row % 2, col // 2, col % 2
    owner_row, owner_col = tile_rows[0, 0] // 2, tile_cols[0, 0] // 2
    where = (owner_row // 2 - z) % NZ * 2 + (owner_row + x) % 2
    ranks = [0] * (2 * NZ)
    for rank, (dz, dx) in enumerate(sum(ORDER, ())):
        ranks[dz * 2 + dx] = rank
    rank = sum(jnp.where(where == k, r, 0) for k, r in enumerate(ranks))
    rows = rank * 2 + tile_rows[0, 0] % 2
    rel_y = (owner_col // 2 - y) % NY
    cols = (rel_y * 2 + (owner_col + core) % 2) * 2 + tile_cols[0, 0] % 2
    slots = jnp.arange(rows.shape[0], dtype=jnp.int32)
    live = slots < tile_count[0, 0]
    key = jnp.where(live, rank // 4, 4) * rows.shape[0] + slots
    position = jnp.sum((key[None, :] < key[:, None]).astype(jnp.int32), axis=1)
    chosen = position[None, :] == slots[:, None]
    order, rows, cols = (
        jnp.sum(jnp.where(chosen, a[None, :], 0), axis=1) for a in (slots, rows, cols)
    )
    groups = jnp.arange(8, dtype=jnp.int32)
    starts = jnp.sum((key[None, :] < groups[:, None] * rows.shape[0]).astype(jnp.int32), axis=1)
    plan = (starts, order, rows, cols)

    tiles = tile_vals[0, 0]
    vals = call(
        load_body,
        "load_tiles",
        jax.ShapeDtypeStruct(tiles.shape, BF16),
        (tiles,),
        scratch=(pltpu.SemaphoreType.DMA,),
        moved=2 * tiles.size * 2,
        specs=[pl.BlockSpec(memory_space=pl.ANY)],
    )
    gathered = gather_row(feats)
    source = call(
        collect_body,
        "collect",
        jax.ShapeDtypeStruct((16, TILE, 256), BF16),
        tuple(gathered[k // 2, k % 2] for k in range(8)),
        moved=2**21,
    )
    work = 2 * 48 * TILE * TILE * 256

    one, two = shape(shard, F32), jax.ShapeDtypeStruct((2, shard, 256), F32)
    one16, two16 = shape(shard, BF16), jax.ShapeDtypeStruct((2, shard, 256), BF16)

    def forward(group, outs):
        return call(
            functools.partial(forward_body, group),
            f"forward_{group}",
            outs,
            (*plan, vals, source),
            scalars=4,
            scratch=(pltpu.VMEM((9, TILE, 256), F32),),
            flops=work,
            moved=4 * 2**20,
        )

    far, over3, kept4 = forward(3, (one16, two16, one))
    far, over3 = to_x(far), to_x(over3)
    over2, kept3 = forward(2, (two16, two))
    low, high = call(
        split_body, "split", (shape(TILE, BF16), shape(TILE, BF16)), (kept4, far), moved=2**19
    )
    over2 = to_x(over2)
    up, down = to_z(low, 1), to_z(high, -1)
    over1, kept2 = forward(1, (two16, two))
    over1 = to_x(over1)
    up, down = call(
        relay_half_body, "relay_3", (one16, one16), (kept3, over3, up, down), moved=2**20
    )
    up, down = to_z(up, 1), to_z(down, -1)
    own, over0, kept1 = forward(0, (one, one16, two))
    over0 = to_x(over0)
    up, down = call(relay_body, "relay_2", (one16, one16), (kept2, over2, up, down), moved=2**20)
    up, down = to_z(up, 1), to_z(down, -1)
    up, down = call(relay_body, "relay_1", (one16, one16), (kept1, over1, up, down), moved=2**20)
    up, down = to_z(up, 1), to_z(down, -1)
    hidden_out, grad, message = call(
        activate_body,
        "activate",
        (one16, one16, shape(2 * shard, BF16)),
        (own, over0, up, down, weight, bias[None, :], grad_out),
        flops=4 * 256**3,
        moved=2 * 2**20,
    )

    def backward(group, blocks, before, outs):
        return call(
            functools.partial(backward_body, group),
            f"backward_{group}",
            outs,
            (*plan, vals, *blocks, *before),
            scalars=4,
            scratch=(pltpu.VMEM((8, TILE, 256), BF16),)
            + ((pltpu.VMEM((17, TILE, 256), F32),) if group == 3 else ()),
            flops=work,
            moved=6 * 2**20,
        )

    running = jax.ShapeDtypeStruct((17, TILE, 256), F32)
    over = to_x(grad)
    up, down = to_z(message, 1), to_z(message, -1)
    ups, downs = [up], [down]
    blocks, before = (grad, over, down, up), ()
    for group in (0, 1, 2):
        over = to_x(jnp.concatenate([downs[-1][:shard], ups[-1][:shard]]))
        if group < 2:
            up, down = to_z(ups[-1], 1), to_z(downs[-1], -1)
        else:
            up, down = to_z(ups[-1][:shard], 1), to_z(downs[-1][shard:], -1)
        total = backward(group, blocks, before, running)
        up, down, total = lax.optimization_barrier((up, down, total))
        ups.append(up)
        downs.append(down)
        blocks, before = (over, down, up), (total,)
    far_grad, far_sum = ups.pop(), downs.pop()
    far_over = to_x(far_grad)
    terms = call(
        terms_body,
        "weight_terms",
        shape(264, F32),
        (z[None], message, *ups, *downs, far_grad, far_sum),
        scalars=1,
        scratch=(pltpu.VMEM((NZ, 256, 256), BF16), pltpu.VMEM((NZ, 256, 256), BF16)),
        flops=2 * 2048 * 256 * 256,
        moved=4 * 2**20,
    )
    terms = terms + to_x(terms)
    own, kept, over = backward(
        3,
        (over, far_grad, far_over),
        (total,),
        (
            one,
            jax.ShapeDtypeStruct((3, shard, 256), F32),
            jax.ShapeDtypeStruct((4, shard, 256), BF16),
        ),
    )
    over, other = to_core(over), to_core(terms)
    *sends, terms = call(
        back_relay_body,
        "back_relay",
        (*[shape(528, BF16)] * 3, shape(272, BF16)),
        (kept, over, terms, other),
        moved=2 * 2**20,
    )
    got = [to_y(a, s) for a, s in zip(sends, (1, 2, 3))]
    grad_feats, grad_weight, grad_bias = call(
        functools.partial(finish_body, scale),
        "finish",
        (one16, shape(256, F32), shape(8, F32)),
        (own, over, *got, terms, weight),
        flops=2 * 256**3,
        moved=2 * 2**20,
    )
    return (hidden_out, grad_feats, grad_weight, grad_bias[0])


def solution(mesh):
    in_specs = (
        P(("slab", "col", "row"), None),
        P(),
        P(),
        P(("slab", "row", "col"), None),
        P(("slab", "row"), "col", None, None, None),
        P(("slab", "row"), "col", None),
        P(("slab", "row"), "col", None),
        P(("slab", "row"), "col"),
    )
    out_specs = (
        P(("slab", "row", "col"), None),
        P(("slab", "col", "row"), None),
        P("slab", None),
        P("slab"),
    )
    return jax.shard_map(
        per_device, mesh=mesh, in_specs=in_specs, out_specs=out_specs, check_vma=False
    )
```

time: 1990 us -> 134 us (0.07)
  waiting for transfers between devices: 1500 us -> 36.1 us
  blocking collectives: 327 us -> 0 us
  other arithmetic: 80.4 us -> 1.43 us
  starting transfers between devices: 0.21 us -> 71.8 us
  matrix products: 40 us -> 0 us
  local copies, waits for them, and re-layouts: 30.1 us -> 3.64 us
    psum x1 -> x0, waiting for transfers between devices: 1150 us -> none  [per_device(): lax.psum((local_weight, local_bias), ('row', 'col'))]
    psum x1 -> x0, blocking collectives: 327 us -> none  [per_device(): lax.psum((local_weight, local_bias), ('row', 'col'))]
    reduce_scatter x2 -> x0, waiting for transfers between devices: 233 us -> none  [the longest x1 233 us: per_device(): lax.psum_scatter(partial_value.astype(jnp.bfloat16), 'col', scatter_dimen...]
    all_gather x2 -> x0, waiting for transfers between devices: 108 us -> none  [the longest x1 77.7 us: per_device(): grad_block = lax.all_gather(own_grad, 'col', axis=0, tiled=True)]
    ppermute x0 -> x39, starting transfers between devices: none -> 71.8 us  [the longest x16 28.1 us: to_z(): lax.ppermute(a, 'col', [(i, (i + 2 * step) % (2 * NZ)) for i in range(2 *...]
    scatter-add x8 -> x0, other arithmetic: 65.7 us -> none  [the longest x4 39.8 us: forward_accumulate(): return running.at[slot_rows].add(product * live_mask[:, None, None])]
    dot_general x11 -> x0, matrix products: 40 us -> none  [the longest x4 18.9 us: backward_accumulate(): jnp.einsum('tmn,tmh->tnh', tile_block, picked, preferred_element_type=jnp...]
    ppermute x0 -> x39, waiting for transfers between devices: none -> 36.1 us  [the longest x11 12.7 us: to_x(): return lax.ppermute(a, 'col', [(i, i ^ 1) for i in range(2 * NZ)])]
  transfers between devices with their start and end apart: 5 -> 39, of which waited for: 4 -> 15; matrix products, arithmetic and copies ran while one was open for 1% -> 1% of each run, Pallas kernels for 0% -> 12%
where the time goes in v2:
time: 134 us
  starting transfers between devices  71.8 us (54%)
  waiting for transfers between devices  36.1 us (27%)
  Pallas kernels  19.1 us (14%)
  local copies, waits for them, and re-layouts  3.64 us (3%)
  between operations  1.66 us (1%)
  other arithmetic  1.43 us (1%)
    ppermute x16, starting transfers between devices, to_z(): lax.ppermute(a, 'col', [(i, (i + 2 * step) % (2 * NZ)) for i in range(2 *...  28.1 us
    pallas_call x18, Pallas kernels, call(): pl.pallas_call(body, name=name, out_shape=out_shape, in_specs=specs or [s...  19.1 us
    ppermute x6, starting transfers between devices, to_core(): return lax.ppermute(a, 'row', [(i, i ^ 1) for i in range(2 * NY)])  17.1 us
    ppermute x11, starting transfers between devices, to_x(): return lax.ppermute(a, 'col', [(i, i ^ 1) for i in range(2 * NZ)])  13.3 us
    ppermute x6, starting transfers between devices, to_y(): lax.ppermute(a, 'row', [(i, (i + 2 * step) % (2 * NY)) for i in range(2 *...  13.2 us
    ppermute x11, waiting for transfers between devices, to_x(): return lax.ppermute(a, 'col', [(i, i ^ 1) for i in range(2 * NZ)])  12.7 us
    ppermute x6, waiting for transfers between devices, to_y(): lax.ppermute(a, 'row', [(i, (i + 2 * step) % (2 * NY)) for i in range(2 *...  11.1 us
    ppermute x16, waiting for transfers between devices, to_z(): lax.ppermute(a, 'col', [(i, (i + 2 * step) % (2 * NZ)) for i in range(2 *...  11.1 us
  transfers between devices with their start and end apart: 39, of which 15 were waited for; matrix products, arithmetic and copies ran while one was open for 1% of the time, Pallas kernels for 12%

profile of v2, /device:TPU:1, one launch (start us, length us, event | category | flops | bytes accessed | tf_op | source)
XLA Modules:
  0.0 133.8 jit_solution(8192064691028465364)
XLA Ops:
  0.6 3.8 %collective-permute-start.3 = (bf16[256,256]{1,0:T(8,128)(2,1)}, bf16[256,256]{1,0:T(8,128)(2,1)S(1)}, u32[]{:S(2)}, u32[]{:S(2)}) collective-permute-start(bf16[256,256]{1,0:T(8,128)(2,1)} %refs_0_.1), channel_id=1, source_target_pairs={{0,128},{32,160},{64,192},{96,224},{128,0},{160,32},{192,64},{224,... | collective-permute-start | bytes 393224 | tf_op jit(solution)/shard_map/ppermute | solution.py:56
  14.0 2.8 %copy-done = bf16[1,1,192,128,128]{4,3,2,1,0:T(8,128)(2,1)S(1)} copy-done((bf16[1,1,192,128,128]{4,3,2,1,0:T(8,128)(2,1)S(1)}, bf16[1,1,192,128,128]{4,3,2,1,0:T(8,128)(2,1)}, u32[]{:S(2)}) %copy-start) | copy-done | bytes 6291480
  19.4 2.5 %collective-permute-start.10 = (bf16[2,256,256]{2,1,0:T(8,128)(2,1)S(1)}, bf16[2,256,256]{2,1,0:T(8,128)(2,1)S(1)}, u32[]{:S(2)}, u32[]{:S(2)}) collective-permute-start(bf16[2,256,256]{2,1,0:T(8,128)(2,1)S(1)} %get-tuple-element.51), channel_id=1, source_target_pairs={{0,2},{2,0},{4,6},{6,4},{8,10},{10,8},{12,14},{14,12},{16,18},{18,... | collective-permute-start | bytes 786440 | tf_op jit(solution)/shard_map/ppermute | solution.py:60
  26.0 5.9 %collective-permute-done.11.got = bf16[256,256]{1,0:T(8,128)(2,1)S(1)} collective-permute-done((bf16[256,256]{1,0:T(8,128)(2,1)S(1)}, bf16[256,256]{1,0:T(8,128)(2,1)S(1)}, u32[]{:S(2)}, u32[]{:S(2)}) %collective-permute-start.11) | collective-permute-done | bytes 131104 | tf_op jit(solution)/shard_map/ppermute | solution.py:60
  32.4 6.3 %collective-permute-start.13 = (bf16[128,256]{1,0:T(8,128)(2,1)S(1)}, bf16[128,256]{1,0:T(8,128)(2,1)S(1)}, u32[]{:S(2)}, u32[]{:S(2)}) collective-permute-start(bf16[128,256]{1,0:T(8,128)(2,1)S(1)} %get-tuple-element.55), channel_id=1, source_target_pairs={{0,28},{2,30},{4,0},{6,2},{8,4},{10,6},{12,8},{14,10},{16,12},{18,... | collective-permute-start | bytes 196616 | tf_op jit(solution)/shard_map/ppermute | solution.py:64
  38.8 2.3 %collective-permute-done.12.up = bf16[128,256]{1,0:T(8,128)(2,1)S(1)} collective-permute-done((bf16[128,256]{1,0:T(8,128)(2,1)S(1)}, bf16[128,256]{1,0:T(8,128)(2,1)S(1)}, u32[]{:S(2)}, u32[]{:S(2)}) %collective-permute-start.12) | collective-permute-done | bytes 65568 | tf_op jit(solution)/shard_map/ppermute | solution.py:64
  41.3 2.9 %collective-permute-start.15 = (bf16[256,256]{1,0:T(8,128)(2,1)S(1)}, bf16[256,256]{1,0:T(8,128)(2,1)S(1)}, u32[]{:S(2)}, u32[]{:S(2)}) collective-permute-start(bf16[256,256]{1,0:T(8,128)(2,1)S(1)} %get-tuple-element.57), channel_id=1, source_target_pairs={{0,28},{2,30},{4,0},{6,2},{8,4},{10,6},{12,8},{14,10},{16,12},{18,... | collective-permute-start | bytes 393224 | tf_op jit(solution)/shard_map/ppermute | solution.py:64
  48.1 2.4 %collective-permute-start.17 = (bf16[256,256]{1,0:T(8,128)(2,1)S(1)}, bf16[256,256]{1,0:T(8,128)(2,1)S(1)}, u32[]{:S(2)}, u32[]{:S(2)}) collective-permute-start(bf16[256,256]{1,0:T(8,128)(2,1)S(1)} %get-tuple-element.59), channel_id=1, source_target_pairs={{0,28},{2,30},{4,0},{6,2},{8,4},{10,6},{12,8},{14,10},{16,12},{18,... | collective-permute-start | bytes 393224 | tf_op jit(solution)/shard_map/ppermute | solution.py:64
  56.0 2.6 %collective-permute-start.19 = (bf16[256,256]{1,0:T(8,128)(2,1)S(1)}, bf16[256,256]{1,0:T(8,128)(2,1)S(1)}, u32[]{:S(2)}, u32[]{:S(2)}) collective-permute-start(bf16[256,256]{1,0:T(8,128)(2,1)S(1)} %get-tuple-element.61), channel_id=1, source_target_pairs={{0,28},{2,30},{4,0},{6,2},{8,4},{10,6},{12,8},{14,10},{16,12},{18,... | collective-permute-start | bytes 393224 | tf_op jit(solution)/shard_map/ppermute | solution.py:64
  58.6 2.9 %collective-permute-done.18.up = bf16[256,256]{1,0:T(8,128)(2,1)S(1)} collective-permute-done((bf16[256,256]{1,0:T(8,128)(2,1)S(1)}, bf16[256,256]{1,0:T(8,128)(2,1)S(1)}, u32[]{:S(2)}, u32[]{:S(2)}) %collective-permute-start.18) | collective-permute-done | bytes 131104 | tf_op jit(solution)/shard_map/ppermute | solution.py:64
  62.4 2.2 %collective-permute-start.22 = (bf16[512,256]{1,0:T(8,128)(2,1)S(1)}, bf16[512,256]{1,0:T(8,128)(2,1)S(1)}, u32[]{:S(2)}, u32[]{:S(2)}) collective-permute-start(bf16[512,256]{1,0:T(8,128)(2,1)S(1)} %get-tuple-element.63.refs_0_), channel_id=1, source_target_pairs={{0,28},{2,30},{4,0},{6,2},{8,4},{10,6},{12,8},{14,10},{16,12},{18,... | collective-permute-start | bytes 786440 | tf_op jit(solution)/shard_map/ppermute | solution.py:64
  64.6 3.3 %collective-permute-done.22.rest_2_.refs_4_ = bf16[512,256]{1,0:T(8,128)(2,1)S(1)} collective-permute-done((bf16[512,256]{1,0:T(8,128)(2,1)S(1)}, bf16[512,256]{1,0:T(8,128)(2,1)S(1)}, u32[]{:S(2)}, u32[]{:S(2)}) %collective-permute-start.22) | collective-permute-done | bytes 262176 | tf_op jit(solution)/shard_map/ppermute | solution.py:64
  67.9 3.5 %collective-permute-start.23 = (bf16[512,256]{1,0:T(8,128)(2,1)S(1)}, bf16[512,256]{1,0:T(8,128)(2,1)S(1)}, u32[]{:S(2)}, u32[]{:S(2)}) collective-permute-start(bf16[512,256]{1,0:T(8,128)(2,1)S(1)} %collective-permute-done.22.rest_2_.refs_4_), channel_id=1, source_target_pairs={{0,28},{2,30},{4,0},{6,2},{8,4},{10,6},{12,8},{14,10},{16,12},{18,... | collective-permute-start | bytes 786440 | tf_op jit(solution)/shard_map/ppermute | solution.py:64
  71.5 3.0 %collective-permute-start.27 = (bf16[512,256]{1,0:T(8,128)(2,1)S(1)}, bf16[512,256]{1,0:T(8,128)(2,1)S(1)}, u32[]{:S(2)}, u32[]{:S(2)}) collective-permute-start(bf16[512,256]{1,0:T(8,128)(2,1)S(1)} %pad_maximum_fusion), channel_id=1, source_target_pairs={{0,2},{2,0},{4,6},{6,4},{8,10},{10,8},{12,14},{14,12},{16,18},{18,... | collective-permute-start | bytes 786440 | tf_op jit(solution)/shard_map/ppermute | solution.py:60
  74.5 2.2 %collective-permute-done.24.rest_1_ = bf16[256,256]{1,0:T(8,128)(2,1)S(1)} collective-permute-done((bf16[256,256]{1,0:T(8,128)(2,1)S(1)}, bf16[256,256]{1,0:T(8,128)(2,1)S(1)}, u32[]{:S(2)}, u32[]{:S(2)}) %collective-permute-start.24) | collective-permute-done | bytes 131104 | tf_op jit(solution)/shard_map/ppermute | solution.py:60
  76.7 2.1 %backward_0.1.rest_3_ = f32[17,128,256]{2,1,0:T(8,128)S(1)} custom-call(s32[8]{0:T(128)S(1)} %convert_reduce_fusion.1.starts, s32[192]{0:T(256)S(1)} %get-tuple-element.86.order, s32[192]{0:T(256)S(1)} %get-tuple-element.85.rows, s32[192]{0:T(256)S(1)} %get-tuple-element.84.cols, bf16[192,128,128]{2,1,0:T(8,128)(2,1)S(1)} %load_tiles.1.vals, ...), custom_call_target="tpu_custom_call" | custom-call | flops 402653184 | bytes 6291456 | tf_op jit(solution)/shard_map/backward_0/pallas_call | solution.py:39
  79.0 3.8 %collective-permute-start.26 = (bf16[512,256]{1,0:T(8,128)(2,1)S(1)}, bf16[512,256]{1,0:T(8,128)(2,1)S(1)}, u32[]{:S(2)}, u32[]{:S(2)}) collective-permute-start(bf16[512,256]{1,0:T(8,128)(2,1)S(1)} %collective-permute-done.23.rest_1_.refs_5_), channel_id=1, source_target_pairs={{0,28},{2,30},{4,0},{6,2},{8,4},{10,6},{12,8},{14,10},{16,12},{18,... | collective-permute-start | bytes 786440 | tf_op jit(solution)/shard_map/ppermute | solution.py:64
  82.9 2.1 %backward_1.1.rest_3_ = f32[17,128,256]{2,1,0:T(8,128)S(1)} custom-call(s32[8]{0:T(128)S(1)} %convert_reduce_fusion.1.starts, s32[192]{0:T(256)S(1)} %get-tuple-element.86.order, s32[192]{0:T(256)S(1)} %get-tuple-element.85.rows, s32[192]{0:T(256)S(1)} %get-tuple-element.84.cols, bf16[192,128,128]{2,1,0:T(8,128)(2,1)S(1)} %load_tiles.1.vals, ...), custom_call_target="tpu_custom_call" | custom-call | flops 402653184 | bytes 6291456 | tf_op jit(solution)/shard_map/backward_1/pallas_call | solution.py:39
  86.7 2.9 %collective-permute-start.30 = (bf16[256,256]{1,0:T(8,128)(2,1)S(1)}, bf16[256,256]{1,0:T(8,128)(2,1)S(1)}, u32[]{:S(2)}, u32[]{:S(2)}) collective-permute-start(bf16[256,256]{1,0:T(8,128)(2,1)S(1)} %get-tuple-element.89), channel_id=1, source_target_pairs={{0,28},{2,30},{4,0},{6,2},{8,4},{10,6},{12,8},{14,10},{16,12},{18,... | collective-permute-start | bytes 393224 | tf_op jit(solution)/shard_map/ppermute | solution.py:64
  92.7 3.2 %collective-permute-start.32 = (bf16[256,256]{1,0:T(8,128)(2,1)S(1)}, bf16[256,256]{1,0:T(8,128)(2,1)S(1)}, u32[]{:S(2)}, u32[]{:S(2)}) collective-permute-start(bf16[256,256]{1,0:T(8,128)(2,1)S(1)} %collective-permute-done.29.rest_1_.refs_7_), channel_id=1, source_target_pairs={{0,2},{2,0},{4,6},{6,4},{8,10},{10,8},{12,14},{14,12},{16,18},{18,... | collective-permute-start | bytes 393224 | tf_op jit(solution)/shard_map/ppermute | solution.py:60
  100.9 9.0 %collective-permute-start.33 = (bf16[4,256,256]{2,1,0:T(8,128)(2,1)S(1)}, bf16[4,256,256]{2,1,0:T(8,128)(2,1)S(1)}, u32[]{:S(2)}, u32[]{:S(2)}) collective-permute-start(bf16[4,256,256]{2,1,0:T(8,128)(2,1)S(1)} %get-tuple-element.74), channel_id=1, source_target_pairs={{0,32},{32,0},{64,96},{96,64},{128,160},{160,128},{192,224},{224,1... | collective-permute-start | bytes 1572872 | tf_op jit(solution)/shard_map/ppermute | solution.py:52
  110.0 2.7 %collective-permute-start.35 = (f32[264,256]{1,0:T(8,128)S(1)}, f32[264,256]{1,0:T(8,128)S(1)}, u32[]{:S(2)}, u32[]{:S(2)}) collective-permute-start(f32[264,256]{1,0:T(8,128)S(1)} %add.420.mine), channel_id=1, source_target_pairs={{0,32},{32,0},{64,96},{96,64},{128,160},{160,128},{192,224},{224,1... | collective-permute-start | bytes 811016 | tf_op jit(solution)/shard_map/ppermute | solution.py:52
  114.0 4.3 %collective-permute-start.36 = (bf16[528,256]{1,0:T(8,128)(2,1)S(1)}, bf16[528,256]{1,0:T(8,128)(2,1)S(1)}, u32[]{:S(2)}, u32[]{:S(2)}) collective-permute-start(bf16[528,256]{1,0:T(8,128)(2,1)S(1)} %get-tuple-element.77), channel_id=1, source_target_pairs={{0,64},{32,96},{64,128},{96,160},{128,192},{160,224},{192,0},{224,... | collective-permute-start | bytes 811016 | tf_op jit(solution)/shard_map/ppermute | solution.py:56
  123.8 8.4 %collective-permute-done.37.b = bf16[528,256]{1,0:T(8,128)(2,1)S(1)} collective-permute-done((bf16[528,256]{1,0:T(8,128)(2,1)S(1)}, bf16[528,256]{1,0:T(8,128)(2,1)S(1)}, u32[]{:S(2)}, u32[]{:S(2)}) %collective-permute-start.37) | collective-permute-done | bytes 270368 | tf_op jit(solution)/shard_map/ppermute | solution.py:56
  (99 shorter events, 44.9 us)
Async XLA Ops:
  0.6 8.2 %collective-permute-start.3 = (bf16[256,256]{1,0:T(8,128)(2,1)}, bf16[256,256]{1,0:T(8,128)(2,1)S(1)}, u32[]{:S(2)}, u32[]{:S(2)}) collective-permute-start(bf16[256,256]{1,0:T(8,128)(2,1)} %refs_0_.1), channel_id=1, source_target_pairs={{0,128},{32,160},{64,192},{96,224},{128,0},{160,32},{192,64},{224,... | collective-permute-start | bytes 393224 | tf_op jit(solution)/shard_map/ppermute | solution.py:56
  5.2 12.2 %collective-permute-start = (bf16[256,256]{1,0:T(8,128)(2,1)}, bf16[256,256]{1,0:T(8,128)(2,1)S(1)}, u32[]{:S(2)}, u32[]{:S(2)}) collective-permute-start(bf16[256,256]{1,0:T(8,128)(2,1)} %refs_0_.1), channel_id=1, source_target_pairs={{0,32},{32,0},{64,96},{96,64},{128,160},{160,128},{192,224},{224,1... | collective-permute-start | bytes 393224 | tf_op jit(solution)/shard_map/ppermute | solution.py:52
  8.8 8.7 %collective-permute-start.4 = (bf16[256,256]{1,0:T(8,128)(2,1)S(1)}, bf16[256,256]{1,0:T(8,128)(2,1)S(1)}, u32[]{:S(2)}, u32[]{:S(2)}) collective-permute-start(bf16[256,256]{1,0:T(8,128)(2,1)S(1)} %collective-permute-done.3.refs_4_), channel_id=1, source_target_pairs={{0,32},{32,0},{64,96},{96,64},{128,160},{160,128},{192,224},{224,1... | collective-permute-start | bytes 393224 | tf_op jit(solution)/shard_map/ppermute | solution.py:52
  19.4 21.7 %collective-permute-start.10 = (bf16[2,256,256]{2,1,0:T(8,128)(2,1)S(1)}, bf16[2,256,256]{2,1,0:T(8,128)(2,1)S(1)}, u32[]{:S(2)}, u32[]{:S(2)}) collective-permute-start(bf16[2,256,256]{2,1,0:T(8,128)(2,1)S(1)} %get-tuple-element.51), channel_id=1, source_target_pairs={{0,2},{2,0},{4,6},{6,4},{8,10},{10,8},{12,14},{14,12},{16,18},{18,... | collective-permute-start | bytes 786440 | tf_op jit(solution)/shard_map/ppermute | solution.py:60
  21.9 10.0 %collective-permute-start.11 = (bf16[256,256]{1,0:T(8,128)(2,1)S(1)}, bf16[256,256]{1,0:T(8,128)(2,1)S(1)}, u32[]{:S(2)}, u32[]{:S(2)}) collective-permute-start(bf16[256,256]{1,0:T(8,128)(2,1)S(1)} %get-tuple-element.53), channel_id=1, source_target_pairs={{0,2},{2,0},{4,6},{6,4},{8,10},{10,8},{12,14},{14,12},{16,18},{18,... | collective-permute-start | bytes 393224 | tf_op jit(solution)/shard_map/ppermute | solution.py:60
  24.4 21.8 %collective-permute-start.9 = (bf16[2,256,256]{2,1,0:T(8,128)(2,1)S(1)}, bf16[2,256,256]{2,1,0:T(8,128)(2,1)S(1)}, u32[]{:S(2)}, u32[]{:S(2)}) collective-permute-start(bf16[2,256,256]{2,1,0:T(8,128)(2,1)S(1)} %get-tuple-element.49), channel_id=1, source_target_pairs={{0,2},{2,0},{4,6},{6,4},{8,10},{10,8},{12,14},{14,12},{16,18},{18,... | collective-permute-start | bytes 786440 | tf_op jit(solution)/shard_map/ppermute | solution.py:60
  32.0 9.1 %collective-permute-start.12 = (bf16[128,256]{1,0:T(8,128)(2,1)S(1)}, bf16[128,256]{1,0:T(8,128)(2,1)S(1)}, u32[]{:S(2)}, u32[]{:S(2)}) collective-permute-start(bf16[128,256]{1,0:T(8,128)(2,1)S(1)} %get-tuple-element.54), channel_id=1, source_target_pairs={{0,4},{2,6},{4,8},{6,10},{8,12},{10,14},{12,16},{14,18},{16,20},{1... | collective-permute-start | bytes 196616 | tf_op jit(solution)/shard_map/ppermute | solution.py:64
  32.4 8.7 %collective-permute-start.13 = (bf16[128,256]{1,0:T(8,128)(2,1)S(1)}, bf16[128,256]{1,0:T(8,128)(2,1)S(1)}, u32[]{:S(2)}, u32[]{:S(2)}) collective-permute-start(bf16[128,256]{1,0:T(8,128)(2,1)S(1)} %get-tuple-element.55), channel_id=1, source_target_pairs={{0,28},{2,30},{4,0},{6,2},{8,4},{10,6},{12,8},{14,10},{16,12},{18,... | collective-permute-start | bytes 196616 | tf_op jit(solution)/shard_map/ppermute | solution.py:64
  46.1 9.6 %collective-permute-start.8 = (bf16[2,256,256]{2,1,0:T(8,128)(2,1)S(1)}, bf16[2,256,256]{2,1,0:T(8,128)(2,1)S(1)}, u32[]{:S(2)}, u32[]{:S(2)}) collective-permute-start(bf16[2,256,256]{2,1,0:T(8,128)(2,1)S(1)} %get-tuple-element.47), channel_id=1, source_target_pairs={{0,2},{2,0},{4,6},{6,4},{8,10},{10,8},{12,14},{14,12},{16,18},{18,... | collective-permute-start | bytes 786440 | tf_op jit(solution)/shard_map/ppermute | solution.py:60
  47.5 8.2 %collective-permute-start.16 = (bf16[256,256]{1,0:T(8,128)(2,1)S(1)}, bf16[256,256]{1,0:T(8,128)(2,1)S(1)}, u32[]{:S(2)}, u32[]{:S(2)}) collective-permute-start(bf16[256,256]{1,0:T(8,128)(2,1)S(1)} %get-tuple-element.58), channel_id=1, source_target_pairs={{0,4},{2,6},{4,8},{6,10},{8,12},{10,14},{12,16},{14,18},{16,20},{1... | collective-permute-start | bytes 393224 | tf_op jit(solution)/shard_map/ppermute | solution.py:64
  48.1 7.6 %collective-permute-start.17 = (bf16[256,256]{1,0:T(8,128)(2,1)S(1)}, bf16[256,256]{1,0:T(8,128)(2,1)S(1)}, u32[]{:S(2)}, u32[]{:S(2)}) collective-permute-start(bf16[256,256]{1,0:T(8,128)(2,1)S(1)} %get-tuple-element.59), channel_id=1, source_target_pairs={{0,28},{2,30},{4,0},{6,2},{8,4},{10,6},{12,8},{14,10},{16,12},{18,... | collective-permute-start | bytes 393224 | tf_op jit(solution)/shard_map/ppermute | solution.py:64
  64.6 6.8 %collective-permute-start.20 = (bf16[512,256]{1,0:T(8,128)(2,1)S(1)}, bf16[512,256]{1,0:T(8,128)(2,1)S(1)}, u32[]{:S(2)}, u32[]{:S(2)}) collective-permute-start(bf16[512,256]{1,0:T(8,128)(2,1)S(1)} %get-tuple-element.63.refs_0_), channel_id=1, source_target_pairs={{0,4},{2,6},{4,8},{6,10},{8,12},{10,14},{12,16},{14,18},{16,20},{1... | collective-permute-start | bytes 786440 | tf_op jit(solution)/shard_map/ppermute | solution.py:64
  67.9 11.0 %collective-permute-start.23 = (bf16[512,256]{1,0:T(8,128)(2,1)S(1)}, bf16[512,256]{1,0:T(8,128)(2,1)S(1)}, u32[]{:S(2)}, u32[]{:S(2)}) collective-permute-start(bf16[512,256]{1,0:T(8,128)(2,1)S(1)} %collective-permute-done.22.rest_2_.refs_4_), channel_id=1, source_target_pairs={{0,28},{2,30},{4,0},{6,2},{8,4},{10,6},{12,8},{14,10},{16,12},{18,... | collective-permute-start | bytes 786440 | tf_op jit(solution)/shard_map/ppermute | solution.py:64
  71.4 7.5 %collective-permute-start.21 = (bf16[512,256]{1,0:T(8,128)(2,1)S(1)}, bf16[512,256]{1,0:T(8,128)(2,1)S(1)}, u32[]{:S(2)}, u32[]{:S(2)}) collective-permute-start(bf16[512,256]{1,0:T(8,128)(2,1)S(1)} %collective-permute-done.20.rest_3_.refs_1_), channel_id=1, source_target_pairs={{0,4},{2,6},{4,8},{6,10},{8,12},{10,14},{12,16},{14,18},{16,20},{1... | collective-permute-start | bytes 786440 | tf_op jit(solution)/shard_map/ppermute | solution.py:64
  71.5 11.4 %collective-permute-start.27 = (bf16[512,256]{1,0:T(8,128)(2,1)S(1)}, bf16[512,256]{1,0:T(8,128)(2,1)S(1)}, u32[]{:S(2)}, u32[]{:S(2)}) collective-permute-start(bf16[512,256]{1,0:T(8,128)(2,1)S(1)} %pad_maximum_fusion), channel_id=1, source_target_pairs={{0,2},{2,0},{4,6},{6,4},{8,10},{10,8},{12,14},{14,12},{16,18},{18,... | collective-permute-start | bytes 786440 | tf_op jit(solution)/shard_map/ppermute | solution.py:60
  78.9 7.5 %collective-permute-start.25 = (bf16[512,256]{1,0:T(8,128)(2,1)S(1)}, bf16[512,256]{1,0:T(8,128)(2,1)S(1)}, u32[]{:S(2)}, u32[]{:S(2)}) collective-permute-start(bf16[512,256]{1,0:T(8,128)(2,1)S(1)} %collective-permute-done.21.rest_2_.refs_2_), channel_id=1, source_target_pairs={{0,4},{2,6},{4,8},{6,10},{8,12},{10,14},{12,16},{14,18},{16,20},{1... | collective-permute-start | bytes 786440 | tf_op jit(solution)/shard_map/ppermute | solution.py:64
  79.0 7.5 %collective-permute-start.26 = (bf16[512,256]{1,0:T(8,128)(2,1)S(1)}, bf16[512,256]{1,0:T(8,128)(2,1)S(1)}, u32[]{:S(2)}, u32[]{:S(2)}) collective-permute-start(bf16[512,256]{1,0:T(8,128)(2,1)S(1)} %collective-permute-done.23.rest_1_.refs_5_), channel_id=1, source_target_pairs={{0,28},{2,30},{4,0},{6,2},{8,4},{10,6},{12,8},{14,10},{16,12},{18,... | collective-permute-start | bytes 786440 | tf_op jit(solution)/shard_map/ppermute | solution.py:64
  82.8 7.7 %collective-permute-start.31 = (bf16[512,256]{1,0:T(8,128)(2,1)S(1)}, bf16[512,256]{1,0:T(8,128)(2,1)S(1)}, u32[]{:S(2)}, u32[]{:S(2)}) collective-permute-start(bf16[512,256]{1,0:T(8,128)(2,1)S(1)} %pad_maximum_fusion.2), channel_id=1, source_target_pairs={{0,2},{2,0},{4,6},{6,4},{8,10},{10,8},{12,14},{14,12},{16,18},{18,... | collective-permute-start | bytes 786440 | tf_op jit(solution)/shard_map/ppermute | solution.py:60
  89.6 8.0 %collective-permute-start.28 = (bf16[512,256]{1,0:T(8,128)(2,1)S(1)}, bf16[512,256]{1,0:T(8,128)(2,1)S(1)}, u32[]{:S(2)}, u32[]{:S(2)}) collective-permute-start(bf16[512,256]{1,0:T(8,128)(2,1)S(1)} %pad_maximum_fusion.1), channel_id=1, source_target_pairs={{0,2},{2,0},{4,6},{6,4},{8,10},{10,8},{12,14},{14,12},{16,18},{18,... | collective-permute-start | bytes 786440 | tf_op jit(solution)/shard_map/ppermute | solution.py:60
  96.5 13.5 %collective-permute-start.34 = (f32[264,256]{1,0:T(8,128)S(1)}, f32[264,256]{1,0:T(8,128)S(1)}, u32[]{:S(2)}, u32[]{:S(2)}) collective-permute-start(f32[264,256]{1,0:T(8,128)S(1)} %weight_terms.1), channel_id=1, source_target_pairs={{0,2},{2,0},{4,6},{6,4},{8,10},{10,8},{12,14},{14,12},{16,18},{18,... | collective-permute-start | bytes 811016 | tf_op jit(solution)/shard_map/ppermute | solution.py:60
  100.9 13.0 %collective-permute-start.33 = (bf16[4,256,256]{2,1,0:T(8,128)(2,1)S(1)}, bf16[4,256,256]{2,1,0:T(8,128)(2,1)S(1)}, u32[]{:S(2)}, u32[]{:S(2)}) collective-permute-start(bf16[4,256,256]{2,1,0:T(8,128)(2,1)S(1)} %get-tuple-element.74), channel_id=1, source_target_pairs={{0,32},{32,0},{64,96},{96,64},{128,160},{160,128},{192,224},{224,1... | collective-permute-start | bytes 1572872 | tf_op jit(solution)/shard_map/ppermute | solution.py:52
  114.0 9.8 %collective-permute-start.36 = (bf16[528,256]{1,0:T(8,128)(2,1)S(1)}, bf16[528,256]{1,0:T(8,128)(2,1)S(1)}, u32[]{:S(2)}, u32[]{:S(2)}) collective-permute-start(bf16[528,256]{1,0:T(8,128)(2,1)S(1)} %get-tuple-element.77), channel_id=1, source_target_pairs={{0,64},{32,96},{64,128},{96,160},{128,192},{160,224},{192,0},{224,... | collective-permute-start | bytes 811016 | tf_op jit(solution)/shard_map/ppermute | solution.py:56
  118.3 13.9 %collective-permute-start.37 = (bf16[528,256]{1,0:T(8,128)(2,1)S(1)}, bf16[528,256]{1,0:T(8,128)(2,1)S(1)}, u32[]{:S(2)}, u32[]{:S(2)}) collective-permute-start(bf16[528,256]{1,0:T(8,128)(2,1)S(1)} %get-tuple-element.78), channel_id=1, source_target_pairs={{0,128},{32,160},{64,192},{96,224},{128,0},{160,32},{192,64},{224,... | collective-permute-start | bytes 811016 | tf_op jit(solution)/shard_map/ppermute | solution.py:56
  120.0 12.2 %collective-permute-start.38 = (bf16[528,256]{1,0:T(8,128)(2,1)S(1)}, bf16[528,256]{1,0:T(8,128)(2,1)S(1)}, u32[]{:S(2)}, u32[]{:S(2)}) collective-permute-start(bf16[528,256]{1,0:T(8,128)(2,1)S(1)} %get-tuple-element.79), channel_id=1, source_target_pairs={{0,192},{32,224},{64,0},{96,32},{128,64},{160,96},{192,128},{224,1... | collective-permute-start | bytes 811016 | tf_op jit(solution)/shard_map/ppermute | solution.py:56
  (20 other events, 130.6 us)

commit v3 on v2

--- a/solution.py
+++ b/solution.py
@@ -9,13 +9,16 @@
 from jax.sharding import PartitionSpec as P
 
 TILE = 128
-UNROLL = 8
+UNROLL = 16
 ORDER = (
-    ((0, 0), (0, 1), (1, 0), (7, 0)),
-    ((1, 1), (7, 1), (2, 0), (6, 0)),
-    ((2, 1), (6, 1), (3, 0), (5, 0)),
-    ((3, 1), (5, 1), (4, 0), (4, 1)),
+    ((0, 0), (0, 1)),
+    ((1, 1), (7, 1), (1, 0), (7, 0)),
+    ((2, 1), (6, 1), (2, 0), (6, 0)),
+    ((3, 1), (5, 1), (3, 0), (5, 0)),
+    ((4, 0), (4, 1)),
 )
+FIRST = (0, 2, 6, 10, 14)
+LAST = 4
 NY = 4
 NZ = 8
 F32 = jnp.float32
@@ -64,16 +67,6 @@
     return lax.ppermute(a, "col", [(i, (i + 2 * step) % (2 * NZ)) for i in range(2 * NZ)])
 
 
-def gather_row(own):
-    got = {(0, 0): own}
-    for step in (1, -1, 2):
-        got[(-step) % NY, 0] = to_y(own, step)
-    got[0, 1] = to_core(own)
-    for dy in (1, 3, 2):
-        got[dy, 1] = to_core(got[dy, 0])
-    return got
-
-
 def load_body(source, out, sem):
     copy = pltpu.make_async_copy(source, out, sem)
     copy.start()
@@ -109,32 +102,25 @@
 
 def forward_body(group, starts, order, rows, cols, vals, source, *rest):
     outs, total = rest[:-1], rest[-1]
+    size = 2 * len(ORDER[group])
     total[...] = jnp.zeros_like(total)
     add_tiles(
         group,
         starts,
         order,
-        lambda t: jnp.clip(rows[t] - 8 * group, 0, 7),
+        lambda t: jnp.clip(rows[t] - 2 * FIRST[group], 0, size - 1),
         lambda tile, t: jnp.dot(vals[tile], source[cols[t]], preferred_element_type=F32),
         total,
-        8,
-    )
-    if group == 3:
-        far, over, kept = outs
-        place(far, total, 3, BF16)
-        place(over.at[0], total, 0, BF16)
-        place(over.at[1], total, 1, BF16)
-        place(kept, total, 2, F32)
-    elif group:
+        size,
+    )
+    if group in (0, LAST):
+        kept, over = outs
+        place(kept, total, 0, F32)
+        place(over, total, 1, BF16)
+    else:
         over, kept = outs
         for n in range(2):
             place(over.at[n], total, n, BF16)
-            place(kept.at[n], total, 2 + n, F32)
-    else:
-        own, over, kept = outs
-        place(own, total, 0, F32)
-        place(over, total, 1, BF16)
-        for n in range(2):
             place(kept.at[n], total, 2 + n, F32)
 
 
@@ -206,21 +192,21 @@
             sums[k], grads[k], (((0,), (0,)), ((), ())), preferred_element_type=F32
         )
         column = column + jnp.sum(grads[k].astype(F32), axis=0, keepdims=True)
-    out[0:256] = total
-    out[256:264] = jnp.broadcast_to(column, (8, 256))
+    out[0:256] = total.astype(BF16)
+    out[256:272] = jnp.broadcast_to(column.astype(BF16), (16, 256))
 
 
 def backward_body(group, starts, order, rows, cols, vals, *rest):
-    count = 4 if group == 0 else 3 if group < 3 else 3
-    blocks, rest = rest[:count], rest[count:]
+    sizes = (1, 1) if group in (0, LAST) else (2, 1, 1)
+    blocks, rest = rest[: len(sizes)], rest[len(sizes) :]
     if group:
         before, rest = rest[0], rest[1:]
-    if group == 3:
+    if group == LAST:
         own, kept, over, source, total = rest
     else:
         total, source = rest
     n = 0
-    for block, size in zip(blocks, (1, 1, 1, 1) if group == 0 else (2, 1, 1)):
+    for block, size in zip(blocks, sizes):
         for half in range(2 * size):
             source[n] = block[half * TILE : (half + 1) * TILE]
             n += 1
@@ -235,14 +221,14 @@
         lambda t: cols[t],
         lambda tile, t: lax.dot_general(
             vals[tile],
-            source[jnp.clip(rows[t] - 8 * group, 0, 7)],
+            source[jnp.clip(rows[t] - 2 * FIRST[group], 0, n - 1)],
             (((0,), (0,)), ((), ())),
             preferred_element_type=F32,
         ),
         total,
         16,
     )
-    if group == 3:
+    if group == LAST:
         place(own, total, 0, F32)
         for k, dy in enumerate((1, 2, 3)):
             place(kept.at[k], total, 2 * dy, F32)
@@ -250,28 +236,23 @@
         place(over.at[3], total, 1, BF16)
 
 
-def back_relay_body(kept, over, mine, other, out_a, out_b, out_c, own_terms):
-    terms = (mine[...] + other[...]).astype(BF16)
-    own_terms[0:256] = terms[0:256]
-    own_terms[256:272] = jnp.broadcast_to(terms[256:257], (16, 256))
+def back_relay_body(kept, over, out_a, out_b, out_c):
     for k, out in enumerate((out_a, out_b, out_c)):
-        out[0:256] = (kept[k] + over[k].astype(F32)).astype(BF16)
-        out[256:512] = terms[0:256]
-        out[512:528] = jnp.broadcast_to(terms[256:257], (16, 256))
-
-
-def finish_body(scale, own, over, a, b, c, terms, weight, out, grad_weight, grad_bias):
-    back = own[...] + over[3].astype(F32)
-    for ref in (a, b, c):
-        back = back + ref[0:256].astype(F32)
+        out[...] = (kept[k] + over[k].astype(F32)).astype(BF16)
+
+
+def sum_terms_body(own, a, b, c, out):
+    out[...] = (wide(own) + wide(b)) + (wide(a) + wide(c))
+
+
+def finish_body(scale, own, over, a, b, c, mine, other, weight, out, grad_weight, grad_bias):
+    back = own[...] + over[3].astype(F32) + wide(a) + wide(b) + wide(c)
     out[...] = lax.dot_general(
         back.astype(BF16), weight[...], (((1,), (1,)), ((), ())), preferred_element_type=F32
     ).astype(BF16)
-    total = (wide(terms) + b[256:528].astype(F32)) + (
-        a[256:528].astype(F32) + c[256:528].astype(F32)
-    )
+    total = mine[...] + other[...]
     grad_weight[...] = total[0:256] * scale
-    grad_bias[...] = total[256:264] * scale
+    grad_bias[...] = total[256:257] * scale
 
 
 def per_device(feats, weight, bias, grad_out, tile_vals, tile_rows, tile_cols, tile_count):
@@ -285,12 +266,13 @@
     for rank, (dz, dx) in enumerate(sum(ORDER, ())):
         ranks[dz * 2 + dx] = rank
     rank = sum(jnp.where(where == k, r, 0) for k, r in enumerate(ranks))
+    group = sum((rank >= f).astype(jnp.int32) for f in FIRST[1:])
     rows = rank * 2 + tile_rows[0, 0] % 2
     rel_y = (owner_col // 2 - y) % NY
     cols = (rel_y * 2 + (owner_col + core) % 2) * 2 + tile_cols[0, 0] % 2
     slots = jnp.arange(rows.shape[0], dtype=jnp.int32)
     live = slots < tile_count[0, 0]
-    key = jnp.where(live, rank // 4, 4) * rows.shape[0] + slots
+    key = jnp.where(live, group, LAST + 1) * rows.shape[0] + slots
     position = jnp.sum((key[None, :] < key[:, None]).astype(jnp.int32), axis=1)
     chosen = position[None, :] == slots[:, None]
     order, rows, cols = (
@@ -308,9 +290,15 @@
         (tiles,),
         scratch=(pltpu.SemaphoreType.DMA,),
         moved=2 * tiles.size * 2,
-        specs=[pl.BlockSpec(memory_space=pl.ANY)],
-    )
-    gathered = gather_row(feats)
+        specs=[pl.BlockSpec(memory_space=pltpu.HBM)],
+    )
+    gathered = {(0, 0): feats, (0, 1): to_core(feats)}
+    steps = (1, -1, 2)
+    arrived = [to_y(feats, step) for step in steps]
+    arrived, vals, plan = lax.optimization_barrier((arrived, vals, plan))
+    for step, block in zip(steps, arrived):
+        gathered[(-step) % NY, 0] = block
+        gathered[(-step) % NY, 1] = to_core(block)
     source = call(
         collect_body,
         "collect",
@@ -323,36 +311,41 @@
     one, two = shape(shard, F32), jax.ShapeDtypeStruct((2, shard, 256), F32)
     one16, two16 = shape(shard, BF16), jax.ShapeDtypeStruct((2, shard, 256), BF16)
 
-    def forward(group, outs):
+    def forward(group, outs, source):
         return call(
             functools.partial(forward_body, group),
             f"forward_{group}",
             outs,
             (*plan, vals, source),
             scalars=4,
-            scratch=(pltpu.VMEM((9, TILE, 256), F32),),
-            flops=work,
-            moved=4 * 2**20,
+            scratch=(pltpu.VMEM((2 * len(ORDER[group]) + 1, TILE, 256), F32),),
+            flops=0,
+            moved=0,
         )
 
-    far, over3, kept4 = forward(3, (one16, two16, one))
-    far, over3 = to_x(far), to_x(over3)
-    over2, kept3 = forward(2, (two16, two))
+    kept4, far = forward(4, (one, one16), source)
+    far, kept4, source = lax.optimization_barrier((far, kept4, source))
+    far = to_x(far)
+    over3, kept3 = forward(3, (two16, two), source)
+    over3 = to_x(over3)
     low, high = call(
         split_body, "split", (shape(TILE, BF16), shape(TILE, BF16)), (kept4, far), moved=2**19
     )
+    up, down = to_z(low, 1), to_z(high, -1)
+    low, source = lax.optimization_barrier((low, source))
+    over2, kept2 = forward(2, (two16, two), source)
+    over2, up, down = lax.optimization_barrier((over2, up, down))
     over2 = to_x(over2)
-    up, down = to_z(low, 1), to_z(high, -1)
-    over1, kept2 = forward(1, (two16, two))
-    over1 = to_x(over1)
     up, down = call(
         relay_half_body, "relay_3", (one16, one16), (kept3, over3, up, down), moved=2**20
     )
     up, down = to_z(up, 1), to_z(down, -1)
-    own, over0, kept1 = forward(0, (one, one16, two))
-    over0 = to_x(over0)
+    over1, kept1 = forward(1, (two16, two), source)
+    over1 = to_x(over1)
     up, down = call(relay_body, "relay_2", (one16, one16), (kept2, over2, up, down), moved=2**20)
     up, down = to_z(up, 1), to_z(down, -1)
+    own, over0 = forward(0, (one, one16), source)
+    over0 = to_x(over0)
     up, down = call(relay_body, "relay_1", (one16, one16), (kept1, over1, up, down), moved=2**20)
     up, down = to_z(up, 1), to_z(down, -1)
     hidden_out, grad, message = call(
@@ -372,16 +365,17 @@
             (*plan, vals, *blocks, *before),
             scalars=4,
             scratch=(pltpu.VMEM((8, TILE, 256), BF16),)
-            + ((pltpu.VMEM((17, TILE, 256), F32),) if group == 3 else ()),
-            flops=work,
-            moved=6 * 2**20,
+            + ((pltpu.VMEM((17, TILE, 256), F32),) if group == LAST else ()),
+            flops=0,
+            moved=0,
         )
 
     running = jax.ShapeDtypeStruct((17, TILE, 256), F32)
     over = to_x(grad)
     up, down = to_z(message, 1), to_z(message, -1)
+    up, down, over = lax.optimization_barrier((up, down, over))
     ups, downs = [up], [down]
-    blocks, before = (grad, over, down, up), ()
+    blocks, before = (grad, over), ()
     for group in (0, 1, 2):
         over = to_x(jnp.concatenate([downs[-1][:shard], ups[-1][:shard]]))
         if group < 2:
@@ -390,25 +384,30 @@
             up, down = to_z(ups[-1][:shard], 1), to_z(downs[-1][shard:], -1)
         total = backward(group, blocks, before, running)
         up, down, total = lax.optimization_barrier((up, down, total))
+        blocks, before = (over, downs[-1], ups[-1]), (total,)
         ups.append(up)
         downs.append(down)
-        blocks, before = (over, down, up), (total,)
     far_grad, far_sum = ups.pop(), downs.pop()
     far_over = to_x(far_grad)
+    total = backward(3, blocks, before, running)
+    total, far_sum = lax.optimization_barrier((total, far_sum))
     terms = call(
         terms_body,
         "weight_terms",
-        shape(264, F32),
+        shape(272, BF16),
         (z[None], message, *ups, *downs, far_grad, far_sum),
         scalars=1,
         scratch=(pltpu.VMEM((NZ, 256, 256), BF16), pltpu.VMEM((NZ, 256, 256), BF16)),
         flops=2 * 2048 * 256 * 256,
-        moved=4 * 2**20,
-    )
-    terms = terms + to_x(terms)
+        moved=0,
+    )
+    moved_terms = [to_y(terms, s) for s in (1, 2, 3)]
+    terms = call(
+        sum_terms_body, "sum_terms", shape(272, F32), (terms, *moved_terms), moved=2**20
+    )
     own, kept, over = backward(
-        3,
-        (over, far_grad, far_over),
+        4,
+        (far_grad, far_over),
         (total,),
         (
             one,
@@ -416,24 +415,24 @@
             jax.ShapeDtypeStruct((4, shard, 256), BF16),
         ),
     )
-    over, other = to_core(over), to_core(terms)
-    *sends, terms = call(
-        back_relay_body,
-        "back_relay",
-        (*[shape(528, BF16)] * 3, shape(272, BF16)),
-        (kept, over, terms, other),
-        moved=2 * 2**20,
+    over = to_core(over)
+    across = to_x(terms)
+    sends = call(
+        back_relay_body, "back_relay", (one16, one16, one16), (kept, over), moved=2 * 2**20
     )
     got = [to_y(a, s) for a, s in zip(sends, (1, 2, 3))]
+    across, _ = lax.optimization_barrier((across, sends[0]))
+    terms = terms + across
+    other = to_core(terms)
     grad_feats, grad_weight, grad_bias = call(
         functools.partial(finish_body, scale),
         "finish",
-        (one16, shape(256, F32), shape(8, F32)),
-        (own, over, *got, terms, weight),
+        (one16, shape(256, F32), shape(1, F32)),
+        (own, over, *got, terms, other, weight),
         flops=2 * 256**3,
         moved=2 * 2**20,
     )
-    return (hidden_out, grad_feats, grad_weight, grad_bias[0])
+    return (hidden_out, grad_feats, grad_weight, grad_bias.reshape(256))
 
 
 def solution(mesh):

time: 134 us -> 141 us (1.052)
  waiting for transfers between devices: 36.1 us -> 48.1 us
  Pallas kernels: 19.1 us -> 13.7 us
  starting transfers between devices: 71.8 us -> 73.3 us
    ppermute x11, starting transfers between devices: 13.3 us -> 20.1 us  [to_x(): return lax.ppermute(a, 'col', [(i, i ^ 1) for i in range(2 * NZ)])]
    ppermute x11, waiting for transfers between devices: 12.7 us -> 19.4 us  [to_x(): return lax.ppermute(a, 'col', [(i, i ^ 1) for i in range(2 * NZ)])]
    ppermute x6 -> x9, waiting for transfers between devices: 11.1 us -> 16.9 us  [to_y(): lax.ppermute(a, 'row', [(i, (i + 2 * step) % (2 * NY)) for i in range(2 *...]
    pallas_call x18 -> x21, Pallas kernels: 19.1 us -> 13.7 us  [call(): pl.pallas_call(body, name=name, out_shape=out_shape, in_specs=specs or [s...]
    ppermute x6 -> x9, starting transfers between devices: 13.2 us -> 10.8 us  [to_y(): lax.ppermute(a, 'row', [(i, (i + 2 * step) % (2 * NY)) for i in range(2 *...]
    ppermute x16, starting transfers between devices: 28.1 us -> 25.9 us  [to_z(): lax.ppermute(a, 'col', [(i, (i + 2 * step) % (2 * NZ)) for i in range(2 *...]
  transfers between devices with their start and end apart: 39 -> 42, of which waited for: 15 -> 23; matrix products, arithmetic and copies ran while one was open for 1% -> 1% of each run, Pallas kernels for 12% -> 7%
where the time goes in v3:
time: 141 us
  starting transfers between devices  73.3 us (52%)
  waiting for transfers between devices  48.1 us (34%)
  Pallas kernels  13.7 us (10%)
  local copies, waits for them, and re-layouts  2.88 us (2%)
  between operations  1.64 us (1%)
  other arithmetic  1.43 us (1%)
    ppermute x16, starting transfers between devices, to_z(): lax.ppermute(a, 'col', [(i, (i + 2 * step) % (2 * NZ)) for i in range(2 *...  25.9 us
    ppermute x11, starting transfers between devices, to_x(): return lax.ppermute(a, 'col', [(i, i ^ 1) for i in range(2 * NZ)])  20.1 us
    ppermute x11, waiting for transfers between devices, to_x(): return lax.ppermute(a, 'col', [(i, i ^ 1) for i in range(2 * NZ)])  19.4 us
    ppermute x9, waiting for transfers between devices, to_y(): lax.ppermute(a, 'row', [(i, (i + 2 * step) % (2 * NY)) for i in range(2 *...  16.9 us
    ppermute x6, starting transfers between devices, to_core(): return lax.ppermute(a, 'row', [(i, i ^ 1) for i in range(2 * NY)])  16.5 us
    pallas_call x21, Pallas kernels, call(): pl.pallas_call(body, name=name, out_shape=out_shape, in_specs=specs or [s...  13.7 us
    ppermute x16, waiting for transfers between devices, to_z(): lax.ppermute(a, 'col', [(i, (i + 2 * step) % (2 * NZ)) for i in range(2 *...  10.8 us
    ppermute x9, starting transfers between devices, to_y(): lax.ppermute(a, 'row', [(i, (i + 2 * step) % (2 * NY)) for i in range(2 *...  10.8 us
  transfers between devices with their start and end apart: 42, of which 23 were waited for; matrix products, arithmetic and copies ran while one was open for 1% of the time, Pallas kernels for 7%

profile of v3, /device:TPU:1, one launch (start us, length us, event | category | flops | bytes accessed | tf_op | source)
XLA Modules:
  0.0 141.0 jit_solution(15316501058827160987)
XLA Ops:
  0.6 3.8 %collective-permute-start.2 = (bf16[256,256]{1,0:T(8,128)(2,1)}, bf16[256,256]{1,0:T(8,128)(2,1)S(1)}, u32[]{:S(2)}, u32[]{:S(2)}) collective-permute-start(bf16[256,256]{1,0:T(8,128)(2,1)} %refs_0_.1), channel_id=1, source_target_pairs={{0,128},{32,160},{64,192},{96,224},{128,0},{160,32},{192,64},{224,... | collective-permute-start | bytes 393224 | tf_op jit(solution)/shard_map/ppermute | solution.py:59
  9.2 2.8 %copy-done = bf16[1,1,192,128,128]{4,3,2,1,0:T(8,128)(2,1)S(1)} copy-done((bf16[1,1,192,128,128]{4,3,2,1,0:T(8,128)(2,1)S(1)}, bf16[1,1,192,128,128]{4,3,2,1,0:T(8,128)(2,1)}, u32[]{:S(2)}) %copy-start) | copy-done | bytes 6291480
  16.0 2.7 %collective-permute-start.7 = (bf16[256,256]{1,0:T(8,128)(2,1)S(1)}, bf16[256,256]{1,0:T(8,128)(2,1)S(1)}, u32[]{:S(2)}, u32[]{:S(2)}) collective-permute-start(bf16[256,256]{1,0:T(8,128)(2,1)S(1)} %get-tuple-element.75), channel_id=1, source_target_pairs={{0,2},{2,0},{4,6},{6,4},{8,10},{10,8},{12,14},{14,12},{16,18},{18,... | collective-permute-start | bytes 393224 | tf_op jit(solution)/shard_map/ppermute | solution.py:63
  21.4 6.1 %collective-permute-start.11 = (bf16[128,256]{1,0:T(8,128)(2,1)S(1)}, bf16[128,256]{1,0:T(8,128)(2,1)S(1)}, u32[]{:S(2)}, u32[]{:S(2)}) collective-permute-start(bf16[128,256]{1,0:T(8,128)(2,1)S(1)} %get-tuple-element.85), channel_id=1, source_target_pairs={{0,28},{2,30},{4,0},{6,2},{8,4},{10,6},{12,8},{14,10},{16,12},{18,... | collective-permute-start | bytes 196616 | tf_op jit(solution)/shard_map/ppermute | solution.py:67
  28.9 3.0 %collective-permute-done.10.up = bf16[128,256]{1,0:T(8,128)(2,1)S(1)} collective-permute-done((bf16[128,256]{1,0:T(8,128)(2,1)S(1)}, bf16[128,256]{1,0:T(8,128)(2,1)S(1)}, u32[]{:S(2)}, u32[]{:S(2)}) %collective-permute-start.10) | collective-permute-done | bytes 65568 | tf_op jit(solution)/shard_map/ppermute | solution.py:67
  31.9 3.2 %collective-permute-start.12 = (bf16[2,256,256]{2,1,0:T(8,128)(2,1)S(1)}, bf16[2,256,256]{2,1,0:T(8,128)(2,1)S(1)}, u32[]{:S(2)}, u32[]{:S(2)}) collective-permute-start(bf16[2,256,256]{2,1,0:T(8,128)(2,1)S(1)} %get-tuple-element.86), channel_id=1, source_target_pairs={{0,2},{2,0},{4,6},{6,4},{8,10},{10,8},{12,14},{14,12},{16,18},{18,... | collective-permute-start | bytes 786440 | tf_op jit(solution)/shard_map/ppermute | solution.py:63
  35.3 2.7 %collective-permute-start.15 = (bf16[256,256]{1,0:T(8,128)(2,1)S(1)}, bf16[256,256]{1,0:T(8,128)(2,1)S(1)}, u32[]{:S(2)}, u32[]{:S(2)}) collective-permute-start(bf16[256,256]{1,0:T(8,128)(2,1)S(1)} %get-tuple-element.92), channel_id=1, source_target_pairs={{0,28},{2,30},{4,0},{6,2},{8,4},{10,6},{12,8},{14,10},{16,12},{18,... | collective-permute-start | bytes 393224 | tf_op jit(solution)/shard_map/ppermute | solution.py:67
  40.8 2.6 %collective-permute-start.17 = (bf16[256,256]{1,0:T(8,128)(2,1)S(1)}, bf16[256,256]{1,0:T(8,128)(2,1)S(1)}, u32[]{:S(2)}, u32[]{:S(2)}) collective-permute-start(bf16[256,256]{1,0:T(8,128)(2,1)S(1)} %get-tuple-element.94), channel_id=1, source_target_pairs={{0,28},{2,30},{4,0},{6,2},{8,4},{10,6},{12,8},{14,10},{16,12},{18,... | collective-permute-start | bytes 393224 | tf_op jit(solution)/shard_map/ppermute | solution.py:67
  46.6 2.7 %collective-permute-start.19 = (bf16[256,256]{1,0:T(8,128)(2,1)S(1)}, bf16[256,256]{1,0:T(8,128)(2,1)S(1)}, u32[]{:S(2)}, u32[]{:S(2)}) collective-permute-start(bf16[256,256]{1,0:T(8,128)(2,1)S(1)} %get-tuple-element.96), channel_id=1, source_target_pairs={{0,28},{2,30},{4,0},{6,2},{8,4},{10,6},{12,8},{14,10},{16,12},{18,... | collective-permute-start | bytes 393224 | tf_op jit(solution)/shard_map/ppermute | solution.py:67
  53.1 2.8 %collective-permute-start.21 = (bf16[512,256]{1,0:T(8,128)(2,1)S(1)}, bf16[512,256]{1,0:T(8,128)(2,1)S(1)}, u32[]{:S(2)}, u32[]{:S(2)}) collective-permute-start(bf16[512,256]{1,0:T(8,128)(2,1)S(1)} %get-tuple-element.98.refs_0_), channel_id=1, source_target_pairs={{0,28},{2,30},{4,0},{6,2},{8,4},{10,6},{12,8},{14,10},{16,12},{18,... | collective-permute-start | bytes 786440 | tf_op jit(solution)/shard_map/ppermute | solution.py:67
  58.0 3.1 %collective-permute-done.22.rest_1_ = bf16[256,256]{1,0:T(8,128)(2,1)S(1)} collective-permute-done((bf16[256,256]{1,0:T(8,128)(2,1)S(1)}, bf16[256,256]{1,0:T(8,128)(2,1)S(1)}, u32[]{:S(2)}, u32[]{:S(2)}) %collective-permute-start.22) | collective-permute-done | bytes 131104 | tf_op jit(solution)/shard_map/ppermute | solution.py:63
  62.3 2.7 %collective-permute-start.24 = (bf16[512,256]{1,0:T(8,128)(2,1)S(1)}, bf16[512,256]{1,0:T(8,128)(2,1)S(1)}, u32[]{:S(2)}, u32[]{:S(2)}) collective-permute-start(bf16[512,256]{1,0:T(8,128)(2,1)S(1)} %collective-permute-done.21.rest_1_.refs_4_), channel_id=1, source_target_pairs={{0,28},{2,30},{4,0},{6,2},{8,4},{10,6},{12,8},{14,10},{16,12},{18,... | collective-permute-start | bytes 786440 | tf_op jit(solution)/shard_map/ppermute | solution.py:67
  70.5 3.4 %collective-permute-start.26 = (bf16[512,256]{1,0:T(8,128)(2,1)S(1)}, bf16[512,256]{1,0:T(8,128)(2,1)S(1)}, u32[]{:S(2)}, u32[]{:S(2)}) collective-permute-start(bf16[512,256]{1,0:T(8,128)(2,1)S(1)} %collective-permute-done.24.rest_1_.refs_5_), channel_id=1, source_target_pairs={{0,28},{2,30},{4,0},{6,2},{8,4},{10,6},{12,8},{14,10},{16,12},{18,... | collective-permute-start | bytes 786440 | tf_op jit(solution)/shard_map/ppermute | solution.py:67
  78.4 3.1 %collective-permute-start.32 = (bf16[512,256]{1,0:T(8,128)(2,1)S(1)}, bf16[512,256]{1,0:T(8,128)(2,1)S(1)}, u32[]{:S(2)}, u32[]{:S(2)}) collective-permute-start(bf16[512,256]{1,0:T(8,128)(2,1)S(1)} %pad_maximum_fusion.2), channel_id=1, source_target_pairs={{0,2},{2,0},{4,6},{6,4},{8,10},{10,8},{12,14},{14,12},{16,18},{18,... | collective-permute-start | bytes 786440 | tf_op jit(solution)/shard_map/ppermute | solution.py:63
  81.4 2.7 %collective-permute-start.29 = (bf16[256,256]{1,0:T(8,128)(2,1)S(1)}, bf16[256,256]{1,0:T(8,128)(2,1)S(1)}, u32[]{:S(2)}, u32[]{:S(2)}) collective-permute-start(bf16[256,256]{1,0:T(8,128)(2,1)S(1)} %get-tuple-element.130), channel_id=1, source_target_pairs={{0,28},{2,30},{4,0},{6,2},{8,4},{10,6},{12,8},{14,10},{16,12},{18,... | collective-permute-start | bytes 393224 | tf_op jit(solution)/shard_map/ppermute | solution.py:67
  85.4 2.6 %collective-permute-done.28.rest_0_.refs_7_ = bf16[256,256]{1,0:T(8,128)(2,1)S(1)} collective-permute-done((bf16[256,256]{1,0:T(8,128)(2,1)S(1)}, bf16[256,256]{1,0:T(8,128)(2,1)S(1)}, u32[]{:S(2)}, u32[]{:S(2)}) %collective-permute-start.28) | collective-permute-done | bytes 131104 | tf_op jit(solution)/shard_map/ppermute | solution.py:67
  88.8 4.5 %collective-permute-done.31.rest_1_ = bf16[256,256]{1,0:T(8,128)(2,1)S(1)} collective-permute-done((bf16[256,256]{1,0:T(8,128)(2,1)S(1)}, bf16[256,256]{1,0:T(8,128)(2,1)S(1)}, u32[]{:S(2)}, u32[]{:S(2)}) %collective-permute-start.31) | collective-permute-done | bytes 131104 | tf_op jit(solution)/shard_map/ppermute | solution.py:63
  94.2 12.1 %collective-permute-start.33 = (bf16[4,256,256]{2,1,0:T(8,128)(2,1)S(1)}, bf16[4,256,256]{2,1,0:T(8,128)(2,1)S(1)}, u32[]{:S(2)}, u32[]{:S(2)}) collective-permute-start(bf16[4,256,256]{2,1,0:T(8,128)(2,1)S(1)} %get-tuple-element.114), channel_id=1, source_target_pairs={{0,32},{32,0},{64,96},{96,64},{128,160},{160,128},{192,224},{224,1... | collective-permute-start | bytes 1572872 | tf_op jit(solution)/shard_map/ppermute | solution.py:55
  106.9 2.6 %collective-permute-start.39 = (bf16[272,256]{1,0:T(8,128)(2,1)S(1)}, bf16[272,256]{1,0:T(8,128)(2,1)S(1)}, u32[]{:S(2)}, u32[]{:S(2)}) collective-permute-start(bf16[272,256]{1,0:T(8,128)(2,1)S(1)} %weight_terms.1.own), channel_id=1, source_target_pairs={{0,192},{32,224},{64,0},{96,32},{128,64},{160,96},{192,128},{224,1... | collective-permute-start | bytes 417800 | tf_op jit(solution)/shard_map/ppermute | solution.py:59
  110.5 4.9 %collective-permute-done.39.c = bf16[272,256]{1,0:T(8,128)(2,1)S(1)} collective-permute-done((bf16[272,256]{1,0:T(8,128)(2,1)S(1)}, bf16[272,256]{1,0:T(8,128)(2,1)S(1)}, u32[]{:S(2)}, u32[]{:S(2)}) %collective-permute-start.39) | collective-permute-done | bytes 139296 | tf_op jit(solution)/shard_map/ppermute | solution.py:59
  116.0 3.5 %collective-permute-done.37.a = bf16[272,256]{1,0:T(8,128)(2,1)S(1)} collective-permute-done((bf16[272,256]{1,0:T(8,128)(2,1)S(1)}, bf16[272,256]{1,0:T(8,128)(2,1)S(1)}, u32[]{:S(2)}, u32[]{:S(2)}) %collective-permute-start.37) | collective-permute-done | bytes 139296 | tf_op jit(solution)/shard_map/ppermute | solution.py:59
  120.2 8.7 %collective-permute-done.40 = f32[272,256]{1,0:T(8,128)S(1)} collective-permute-done((f32[272,256]{1,0:T(8,128)S(1)}, f32[272,256]{1,0:T(8,128)S(1)}, u32[]{:S(2)}, u32[]{:S(2)}) %collective-permute-start.40) | collective-permute-done | bytes 278560 | tf_op jit(solution)/shard_map/ppermute | solution.py:63
  132.2 4.8 %collective-permute-done.35.b = bf16[256,256]{1,0:T(8,128)(2,1)S(1)} collective-permute-done((bf16[256,256]{1,0:T(8,128)(2,1)S(1)}, bf16[256,256]{1,0:T(8,128)(2,1)S(1)}, u32[]{:S(2)}, u32[]{:S(2)}) %collective-permute-start.35) | collective-permute-done | bytes 131104 | tf_op jit(solution)/shard_map/ppermute | solution.py:59
  137.1 3.0 %collective-permute-done.34.a = bf16[256,256]{1,0:T(8,128)(2,1)S(1)} collective-permute-done((bf16[256,256]{1,0:T(8,128)(2,1)S(1)}, bf16[256,256]{1,0:T(8,128)(2,1)S(1)}, u32[]{:S(2)}, u32[]{:S(2)}) %collective-permute-start.34) | collective-permute-done | bytes 131104 | tf_op jit(solution)/shard_map/ppermute | solution.py:59
  (107 shorter events, 45.3 us)
Async XLA Ops:
  0.6 12.1 %collective-permute-start.2 = (bf16[256,256]{1,0:T(8,128)(2,1)}, bf16[256,256]{1,0:T(8,128)(2,1)S(1)}, u32[]{:S(2)}, u32[]{:S(2)}) collective-permute-start(bf16[256,256]{1,0:T(8,128)(2,1)} %refs_0_.1), channel_id=1, source_target_pairs={{0,128},{32,160},{64,192},{96,224},{128,0},{160,32},{192,64},{224,... | collective-permute-start | bytes 393224 | tf_op jit(solution)/shard_map/ppermute | solution.py:59
  4.5 8.2 %collective-permute-start.1 = (bf16[256,256]{1,0:T(8,128)(2,1)}, bf16[256,256]{1,0:T(8,128)(2,1)S(1)}, u32[]{:S(2)}, u32[]{:S(2)}) collective-permute-start(bf16[256,256]{1,0:T(8,128)(2,1)} %refs_0_.1), channel_id=1, source_target_pairs={{0,192},{32,224},{64,0},{96,32},{128,64},{160,96},{192,128},{224,1... | collective-permute-start | bytes 393224 | tf_op jit(solution)/shard_map/ppermute | solution.py:59
  5.2 7.5 %collective-permute-start = (bf16[256,256]{1,0:T(8,128)(2,1)}, bf16[256,256]{1,0:T(8,128)(2,1)S(1)}, u32[]{:S(2)}, u32[]{:S(2)}) collective-permute-start(bf16[256,256]{1,0:T(8,128)(2,1)} %refs_0_.1), channel_id=1, source_target_pairs={{0,64},{32,96},{64,128},{96,160},{128,192},{160,224},{192,0},{224,... | collective-permute-start | bytes 393224 | tf_op jit(solution)/shard_map/ppermute | solution.py:59
  5.9 8.3 %collective-permute-start.3 = (bf16[256,256]{1,0:T(8,128)(2,1)}, bf16[256,256]{1,0:T(8,128)(2,1)S(1)}, u32[]{:S(2)}, u32[]{:S(2)}) collective-permute-start(bf16[256,256]{1,0:T(8,128)(2,1)} %refs_0_.1), channel_id=1, source_target_pairs={{0,32},{32,0},{64,96},{96,64},{128,160},{160,128},{192,224},{224,1... | collective-permute-start | bytes 393224 | tf_op jit(solution)/shard_map/ppermute | solution.py:55
  19.4 15.7 %collective-permute-start.13 = (bf16[2,256,256]{2,1,0:T(8,128)(2,1)S(1)}, bf16[2,256,256]{2,1,0:T(8,128)(2,1)S(1)}, u32[]{:S(2)}, u32[]{:S(2)}) collective-permute-start(bf16[2,256,256]{2,1,0:T(8,128)(2,1)S(1)} %get-tuple-element.88), channel_id=1, source_target_pairs={{0,2},{2,0},{4,6},{6,4},{8,10},{10,8},{12,14},{14,12},{16,18},{18,... | collective-permute-start | bytes 786440 | tf_op jit(solution)/shard_map/ppermute | solution.py:63
  21.4 7.4 %collective-permute-start.11 = (bf16[128,256]{1,0:T(8,128)(2,1)S(1)}, bf16[128,256]{1,0:T(8,128)(2,1)S(1)}, u32[]{:S(2)}, u32[]{:S(2)}) collective-permute-start(bf16[128,256]{1,0:T(8,128)(2,1)S(1)} %get-tuple-element.85), channel_id=1, source_target_pairs={{0,28},{2,30},{4,0},{6,2},{8,4},{10,6},{12,8},{14,10},{16,12},{18,... | collective-permute-start | bytes 196616 | tf_op jit(solution)/shard_map/ppermute | solution.py:67
  31.9 8.7 %collective-permute-start.12 = (bf16[2,256,256]{2,1,0:T(8,128)(2,1)S(1)}, bf16[2,256,256]{2,1,0:T(8,128)(2,1)S(1)}, u32[]{:S(2)}, u32[]{:S(2)}) collective-permute-start(bf16[2,256,256]{2,1,0:T(8,128)(2,1)S(1)} %get-tuple-element.86), channel_id=1, source_target_pairs={{0,2},{2,0},{4,6},{6,4},{8,10},{10,8},{12,14},{14,12},{16,18},{18,... | collective-permute-start | bytes 786440 | tf_op jit(solution)/shard_map/ppermute | solution.py:63
  39.1 7.3 %collective-permute-start.9 = (bf16[2,256,256]{2,1,0:T(8,128)(2,1)S(1)}, bf16[2,256,256]{2,1,0:T(8,128)(2,1)S(1)}, u32[]{:S(2)}, u32[]{:S(2)}) collective-permute-start(bf16[2,256,256]{2,1,0:T(8,128)(2,1)S(1)} %get-tuple-element.82), channel_id=1, source_target_pairs={{0,2},{2,0},{4,6},{6,4},{8,10},{10,8},{12,14},{14,12},{16,18},{18,... | collective-permute-start | bytes 786440 | tf_op jit(solution)/shard_map/ppermute | solution.py:63
  44.5 7.1 %collective-permute-start.8 = (bf16[256,256]{1,0:T(8,128)(2,1)S(1)}, bf16[256,256]{1,0:T(8,128)(2,1)S(1)}, u32[]{:S(2)}, u32[]{:S(2)}) collective-permute-start(bf16[256,256]{1,0:T(8,128)(2,1)S(1)} %get-tuple-element.80), channel_id=1, source_target_pairs={{0,2},{2,0},{4,6},{6,4},{8,10},{10,8},{12,14},{14,12},{16,18},{18,... | collective-permute-start | bytes 393224 | tf_op jit(solution)/shard_map/ppermute | solution.py:63
  53.1 8.1 %collective-permute-start.21 = (bf16[512,256]{1,0:T(8,128)(2,1)S(1)}, bf16[512,256]{1,0:T(8,128)(2,1)S(1)}, u32[]{:S(2)}, u32[]{:S(2)}) collective-permute-start(bf16[512,256]{1,0:T(8,128)(2,1)S(1)} %get-tuple-element.98.refs_0_), channel_id=1, source_target_pairs={{0,28},{2,30},{4,0},{6,2},{8,4},{10,6},{12,8},{14,10},{16,12},{18,... | collective-permute-start | bytes 786440 | tf_op jit(solution)/shard_map/ppermute | solution.py:67
  62.3 8.2 %collective-permute-start.24 = (bf16[512,256]{1,0:T(8,128)(2,1)S(1)}, bf16[512,256]{1,0:T(8,128)(2,1)S(1)}, u32[]{:S(2)}, u32[]{:S(2)}) collective-permute-start(bf16[512,256]{1,0:T(8,128)(2,1)S(1)} %collective-permute-done.21.rest_1_.refs_4_), channel_id=1, source_target_pairs={{0,28},{2,30},{4,0},{6,2},{8,4},{10,6},{12,8},{14,10},{16,12},{18,... | collective-permute-start | bytes 786440 | tf_op jit(solution)/shard_map/ppermute | solution.py:67
  65.0 11.5 %collective-permute-start.27 = (bf16[512,256]{1,0:T(8,128)(2,1)S(1)}, bf16[512,256]{1,0:T(8,128)(2,1)S(1)}, u32[]{:S(2)}, u32[]{:S(2)}) collective-permute-start(bf16[512,256]{1,0:T(8,128)(2,1)S(1)} %pad_maximum_fusion), channel_id=1, source_target_pairs={{0,2},{2,0},{4,6},{6,4},{8,10},{10,8},{12,14},{14,12},{16,18},{18,... | collective-permute-start | bytes 786440 | tf_op jit(solution)/shard_map/ppermute | solution.py:63
  70.5 7.8 %collective-permute-start.25 = (bf16[512,256]{1,0:T(8,128)(2,1)S(1)}, bf16[512,256]{1,0:T(8,128)(2,1)S(1)}, u32[]{:S(2)}, u32[]{:S(2)}) collective-permute-start(bf16[512,256]{1,0:T(8,128)(2,1)S(1)} %collective-permute-done.23.rest_2_.refs_2_), channel_id=1, source_target_pairs={{0,4},{2,6},{4,8},{6,10},{8,12},{10,14},{12,16},{14,18},{16,20},{1... | collective-permute-start | bytes 786440 | tf_op jit(solution)/shard_map/ppermute | solution.py:67
  70.5 7.8 %collective-permute-start.26 = (bf16[512,256]{1,0:T(8,128)(2,1)S(1)}, bf16[512,256]{1,0:T(8,128)(2,1)S(1)}, u32[]{:S(2)}, u32[]{:S(2)}) collective-permute-start(bf16[512,256]{1,0:T(8,128)(2,1)S(1)} %collective-permute-done.24.rest_1_.refs_5_), channel_id=1, source_target_pairs={{0,28},{2,30},{4,0},{6,2},{8,4},{10,6},{12,8},{14,10},{16,12},{18,... | collective-permute-start | bytes 786440 | tf_op jit(solution)/shard_map/ppermute | solution.py:67
  74.0 10.1 %collective-permute-start.30 = (bf16[512,256]{1,0:T(8,128)(2,1)S(1)}, bf16[512,256]{1,0:T(8,128)(2,1)S(1)}, u32[]{:S(2)}, u32[]{:S(2)}) collective-permute-start(bf16[512,256]{1,0:T(8,128)(2,1)S(1)} %pad_maximum_fusion.1), channel_id=1, source_target_pairs={{0,2},{2,0},{4,6},{6,4},{8,10},{10,8},{12,14},{14,12},{16,18},{18,... | collective-permute-start | bytes 786440 | tf_op jit(solution)/shard_map/ppermute | solution.py:63
  78.4 9.6 %collective-permute-start.32 = (bf16[512,256]{1,0:T(8,128)(2,1)S(1)}, bf16[512,256]{1,0:T(8,128)(2,1)S(1)}, u32[]{:S(2)}, u32[]{:S(2)}) collective-permute-start(bf16[512,256]{1,0:T(8,128)(2,1)S(1)} %pad_maximum_fusion.2), channel_id=1, source_target_pairs={{0,2},{2,0},{4,6},{6,4},{8,10},{10,8},{12,14},{14,12},{16,18},{18,... | collective-permute-start | bytes 786440 | tf_op jit(solution)/shard_map/ppermute | solution.py:63
  81.4 6.5 %collective-permute-start.28 = (bf16[256,256]{1,0:T(8,128)(2,1)S(1)}, bf16[256,256]{1,0:T(8,128)(2,1)S(1)}, u32[]{:S(2)}, u32[]{:S(2)}) collective-permute-start(bf16[256,256]{1,0:T(8,128)(2,1)S(1)} %slice.24), channel_id=1, source_target_pairs={{0,4},{2,6},{4,8},{6,10},{8,12},{10,14},{12,16},{14,18},{16,20},{1... | collective-permute-start | bytes 393224 | tf_op jit(solution)/shard_map/ppermute | solution.py:67
  94.2 25.9 %collective-permute-start.33 = (bf16[4,256,256]{2,1,0:T(8,128)(2,1)S(1)}, bf16[4,256,256]{2,1,0:T(8,128)(2,1)S(1)}, u32[]{:S(2)}, u32[]{:S(2)}) collective-permute-start(bf16[4,256,256]{2,1,0:T(8,128)(2,1)S(1)} %get-tuple-element.114), channel_id=1, source_target_pairs={{0,32},{32,0},{64,96},{96,64},{128,160},{160,128},{192,224},{224,1... | collective-permute-start | bytes 1572872 | tf_op jit(solution)/shard_map/ppermute | solution.py:55
  106.9 8.5 %collective-permute-start.39 = (bf16[272,256]{1,0:T(8,128)(2,1)S(1)}, bf16[272,256]{1,0:T(8,128)(2,1)S(1)}, u32[]{:S(2)}, u32[]{:S(2)}) collective-permute-start(bf16[272,256]{1,0:T(8,128)(2,1)S(1)} %weight_terms.1.own), channel_id=1, source_target_pairs={{0,192},{32,224},{64,0},{96,32},{128,64},{160,96},{192,128},{224,1... | collective-permute-start | bytes 417800 | tf_op jit(solution)/shard_map/ppermute | solution.py:59
  109.8 9.8 %collective-permute-start.37 = (bf16[272,256]{1,0:T(8,128)(2,1)S(1)}, bf16[272,256]{1,0:T(8,128)(2,1)S(1)}, u32[]{:S(2)}, u32[]{:S(2)}) collective-permute-start(bf16[272,256]{1,0:T(8,128)(2,1)S(1)} %weight_terms.1.own), channel_id=1, source_target_pairs={{0,64},{32,96},{64,128},{96,160},{128,192},{160,224},{192,0},{224,... | collective-permute-start | bytes 417800 | tf_op jit(solution)/shard_map/ppermute | solution.py:59
  119.6 9.3 %collective-permute-start.40 = (f32[272,256]{1,0:T(8,128)S(1)}, f32[272,256]{1,0:T(8,128)S(1)}, u32[]{:S(2)}, u32[]{:S(2)}) collective-permute-start(f32[272,256]{1,0:T(8,128)S(1)} %sum_terms.1), channel_id=1, source_target_pairs={{0,2},{2,0},{4,6},{6,4},{8,10},{10,8},{12,14},{14,12},{16,18},{18,... | collective-permute-start | bytes 835592 | tf_op jit(solution)/shard_map/ppermute | solution.py:63
  128.9 11.2 %collective-permute-start.41 = (f32[272,256]{1,0:T(8,128)S(1)}, f32[272,256]{1,0:T(8,128)S(1)}, u32[]{:S(2)}, u32[]{:S(2)}) collective-permute-start(f32[272,256]{1,0:T(8,128)S(1)} %add.447.mine), channel_id=1, source_target_pairs={{0,32},{32,0},{64,96},{96,64},{128,160},{160,128},{192,224},{224,1... | collective-permute-start | bytes 835592 | tf_op jit(solution)/shard_map/ppermute | solution.py:55
  130.4 6.6 %collective-permute-start.35 = (bf16[256,256]{1,0:T(8,128)(2,1)S(1)}, bf16[256,256]{1,0:T(8,128)(2,1)S(1)}, u32[]{:S(2)}, u32[]{:S(2)}) collective-permute-start(bf16[256,256]{1,0:T(8,128)(2,1)S(1)} %get-tuple-element.117), channel_id=1, source_target_pairs={{0,128},{32,160},{64,192},{96,224},{128,0},{160,32},{192,64},{224,... | collective-permute-start | bytes 393224 | tf_op jit(solution)/shard_map/ppermute | solution.py:59
  131.3 8.8 %collective-permute-start.34 = (bf16[256,256]{1,0:T(8,128)(2,1)S(1)}, bf16[256,256]{1,0:T(8,128)(2,1)S(1)}, u32[]{:S(2)}, u32[]{:S(2)}) collective-permute-start(bf16[256,256]{1,0:T(8,128)(2,1)S(1)} %get-tuple-element.116), channel_id=1, source_target_pairs={{0,64},{32,96},{64,128},{96,160},{128,192},{160,224},{192,0},{224,... | collective-permute-start | bytes 393224 | tf_op jit(solution)/shard_map/ppermute | solution.py:59
  (23 other events, 130.6 us)

commit v4 on v3

v4 whole, which is shorter than its diff:
```python
import functools
import math

import jax
import jax.numpy as jnp
from jax import lax
from jax.experimental import pallas as pl
from jax.experimental.pallas import tpu as pltpu
from jax.sharding import PartitionSpec as P

TILE = 128
UNROLL = 16
ORDER = (
    ((0, 0), (1, 0)),
    ((7, 0), (6, 0), (0, 1), (1, 1)),
    ((2, 0), (3, 0), (7, 1), (6, 1)),
    ((5, 0), (4, 0), (2, 1), (3, 1)),
    ((5, 1), (4, 1)),
)
FIRST = (0, 2, 6, 10, 14)
LAST = 4
NY = 4
NZ = 8
F32 = jnp.float32
BF16 = jnp.bfloat16
LIMIT = pltpu.CompilerParams(vmem_limit_bytes=32 * 2**20)


def vmem():
    return pl.BlockSpec(memory_space=pltpu.VMEM)


def smem():
    return pl.BlockSpec(memory_space=pltpu.SMEM)


def shape(rows, dtype):
    return jax.ShapeDtypeStruct((rows, 256), dtype)


def call(body, name, out_shape, args, scalars=0, scratch=(), flops=0, moved=0, specs=None):
    return pl.pallas_call(
        body,
        name=name,
        out_shape=out_shape,
        in_specs=specs or [smem()] * scalars + [vmem()] * (len(args) - scalars),
        out_specs=jax.tree.map(lambda _: vmem(), out_shape),
        scratch_shapes=scratch,
        compiler_params=LIMIT,
        cost_estimate=pl.CostEstimate(flops=flops, bytes_accessed=moved, transcendentals=0),
    )(*args)


def to_core(a):
    return lax.ppermute(a, "row", [(i, i ^ 1) for i in range(2 * NY)])


def to_y(a, step):
    return lax.ppermute(a, "row", [(i, (i + 2 * step) % (2 * NY)) for i in range(2 * NY)])


def to_x(a):
    return lax.ppermute(a, "col", [(i, i ^ 1) for i in range(2 * NZ)])


def swap_z(a, side):
    pairs = []
    for row in range(2 * NY):
        for col in range(2 * NZ):
            z, x = divmod(col, 2)
            step = side if (z + row) % 2 == 0 else -side
            pairs.append((row * 2 * NZ + col, row * 2 * NZ + (z + step) % NZ * 2 + x))
    return lax.ppermute(a, ("row", "col"), pairs)


def flip_z(a, bit):
    return lax.ppermute(a, "col", [(i, i ^ (2 * bit)) for i in range(2 * NZ)])


def load_body(source, out, sem):
    copy = pltpu.make_async_copy(source, out, sem)
    copy.start()
    copy.wait()


def collect_body(*refs):
    blocks, out = refs[:-1], refs[-1]
    for k, block in enumerate(blocks):
        for half in range(2):
            out[2 * k + half] = block[half * TILE : (half + 1) * TILE]


def place(ref, total, first, dtype):
    for half in range(2):
        ref[half * TILE : (half + 1) * TILE] = total[2 * first + half].astype(dtype)


def add_tiles(group, starts, order, to_slot, product, total, dummy):
    first, last = starts[group], starts[group + 1]

    def batch(i, carry):
        slots = [first + i * UNROLL + u for u in range(UNROLL)]
        safe = [jnp.minimum(t, 191) for t in slots]
        terms = [product(order[t], t) for t in safe]
        for slot, t, term in zip(slots, safe, terms):
            place_at = jnp.where(slot < last, to_slot(t), dummy)
            total[place_at] = total[place_at] + term
        return carry

    lax.fori_loop(0, (last - first + UNROLL - 1) // UNROLL, batch, 0)


def forward_body(group, starts, order, rows, cols, vals, source, *rest):
    outs, total = rest[:-1], rest[-1]
    size = 2 * len(ORDER[group])
    total[...] = jnp.zeros_like(total)
    add_tiles(
        group,
        starts,
        order,
        lambda t: jnp.clip(rows[t] - 2 * FIRST[group], 0, size - 1),
        lambda tile, t: jnp.dot(vals[tile], source[cols[t]], preferred_element_type=F32),
        total,
        size,
    )
    outs = list(outs)
    if group < LAST:
        kept = outs.pop(0)
        for n in range(2):
            place(kept.at[n], total, n, F32)
    if group:
        over = outs.pop(0)
        for n in range(2):
            place(over.at[n], total, size // 2 - 2 + n, BF16)


def wide(ref):
    return ref[...].astype(F32)


def relay_first_body(kept, over, out):
    out[...] = (kept[...] + wide(over)).astype(BF16)


def relay_body(kept, over, got, out):
    out[...] = (kept[...] + wide(over) + wide(got)).astype(BF16)


def relay_last_body(kept, over, got, own, out):
    own[...] = kept[0] + wide(over.at[0]) + wide(got.at[0])
    out[...] = (kept[1] + wide(over.at[1]) + wide(got.at[1])).astype(BF16)


def activate_body(own, got, weight, bias, given, hidden, grad, high, low):
    summed = own[...] + wide(got)
    top = summed.astype(BF16)
    rest = (summed - top.astype(F32)).astype(BF16)
    high[...] = top
    low[...] = rest
    pre_act = (
        jnp.dot(top, weight[...], preferred_element_type=F32)
        + jnp.dot(rest, weight[...], preferred_element_type=F32)
        + bias[...]
    )
    gate_value = jax.nn.sigmoid(pre_act)
    hidden[...] = (pre_act * gate_value).astype(BF16)
    slope = gate_value * (1.0 + pre_act * (1.0 - gate_value))
    grad[...] = (given[...].astype(F32) * slope).astype(BF16)


def terms_body(core, high, low, grad, kept, sent, whole):
    g = grad[...]
    dims = (((0,), (0,)), ((), ()))
    whole[...] = lax.dot_general(high[...], g, dims, preferred_element_type=F32) + lax.dot_general(
        low[...], g, dims, preferred_element_type=F32
    )
    column = jnp.sum(g.astype(F32), axis=0, keepdims=True)
    for ref, half in ((kept, core[0]), (sent, 1 - core[0])):
        ref[0:128] = whole[pl.ds(pl.multiple_of(half * 128, 128), 128)]
        ref[128:136] = jnp.broadcast_to(column, (8, 256))


def backward_body(group, starts, order, rows, cols, vals, *rest):
    count = 1 if group in (0, LAST) else 2
    blocks, rest = rest[:count], rest[count:]
    if group:
        before, rest = rest[0], rest[1:]
    if group == LAST:
        own, kept, over, source, total = rest
    else:
        total, source = rest
    n = 0
    for block in blocks:
        for half in range(4):
            source[n] = block[half // 2, half % 2 * TILE : (half % 2 + 1) * TILE]
            n += 1
    if group:
        total[...] = before[...]
    else:
        total[...] = jnp.zeros_like(total)
    add_tiles(
        group,
        starts,
        order,
        lambda t: cols[t],
        lambda tile, t: lax.dot_general(
            vals[tile],
            source[jnp.clip(rows[t] - 2 * FIRST[group], 0, n - 1)],
            (((0,), (0,)), ((), ())),
            preferred_element_type=F32,
        ),
        total,
        16,
    )
    if group == LAST:
        place(own, total, 0, F32)
        for k, dy in enumerate((1, 2, 3)):
            place(kept.at[k], total, 2 * dy, F32)
            place(over.at[k], total, 2 * dy + 1, BF16)
        place(over.at[3], total, 1, BF16)


def back_relay_body(kept, over, terms, out_a, out_b, out_c, mine):
    mine[0:128] = terms[0:128].astype(BF16)
    mine[128:144] = jnp.broadcast_to(terms[128:129], (16, 256)).astype(BF16)
    for k, out in enumerate((out_a, out_b, out_c)):
        out[0:256] = (kept[k] + over[k].astype(F32)).astype(BF16)
        out[256:400] = mine[...]


def sum_terms_body(scale, own, a, b, c, out):
    total = (wide(own) + b[256:400].astype(F32)) + (
        a[256:400].astype(F32) + c[256:400].astype(F32)
    )
    out[...] = total[0:136] * scale


def finish_body(own, over, a, b, c, weight, out):
    back = own[...] + over[3].astype(F32)
    for ref in (a, b, c):
        back = back + ref[0:256].astype(F32)
    out[...] = lax.dot_general(
        back.astype(BF16), weight[...], (((1,), (1,)), ((), ())), preferred_element_type=F32
    ).astype(BF16)


def assemble_body(core, mine, other, weight, bias):
    for ref, half in ((mine, core[0]), (other, 1 - core[0])):
        weight[pl.ds(pl.multiple_of(half * 128, 128), 128)] = ref[0:128]
    bias[...] = mine[128:129]


def per_device(feats, weight, bias, grad_out, tile_vals, tile_rows, tile_cols, tile_count):
    shard = feats.shape[0]
    scale = 1.0 / math.sqrt(shard * 2 * NY * 2 * NZ)
    row, col = lax.axis_index("row"), lax.axis_index("col")
    y, core, z, x = row // 2, row % 2, col // 2, col % 2
    owner_row, owner_col = tile_rows[0, 0] // 2, tile_cols[0, 0] // 2
    toward = 1 - 2 * ((z + core) % 2)
    where = (owner_row // 2 - z) * toward % NZ * 2 + (owner_row + x) % 2
    ranks = [0] * (2 * NZ)
    for rank, (dz, dx) in enumerate(sum(ORDER, ())):
        ranks[dz * 2 + dx] = rank
    rank = sum(jnp.where(where == k, r, 0) for k, r in enumerate(ranks))
    group = sum((rank >= f).astype(jnp.int32) for f in FIRST[1:])
    rows = rank * 2 + tile_rows[0, 0] % 2
    rel_y = (owner_col // 2 - y) % NY
    cols = (rel_y * 2 + (owner_col + core) % 2) * 2 + tile_cols[0, 0] % 2
    slots = jnp.arange(rows.shape[0], dtype=jnp.int32)
    live = slots < tile_count[0, 0]
    key = jnp.where(live, group, LAST + 1) * rows.shape[0] + slots
    position = jnp.sum((key[None, :] < key[:, None]).astype(jnp.int32), axis=1)
    chosen = position[None, :] == slots[:, None]
    order, rows, cols = (
        jnp.sum(jnp.where(chosen, a[None, :], 0), axis=1) for a in (slots, rows, cols)
    )
    groups = jnp.arange(8, dtype=jnp.int32)
    starts = jnp.sum((key[None, :] < groups[:, None] * rows.shape[0]).astype(jnp.int32), axis=1)
    plan = (starts, order, rows, cols)

    tiles = tile_vals[0, 0]
    vals = call(
        load_body,
        "load_tiles",
        jax.ShapeDtypeStruct(tiles.shape, BF16),
        (tiles,),
        scratch=(pltpu.SemaphoreType.DMA,),
        moved=2 * tiles.size * 2,
        specs=[pl.BlockSpec(memory_space=pltpu.HBM)],
    )
    gathered = {(0, 0): feats, (0, 1): to_core(feats)}
    steps = (1, -1, 2)
    arrived = [to_y(feats, step) for step in steps]
    arrived, vals, plan = lax.optimization_barrier((arrived, vals, plan))
    for step, block in zip(steps, arrived):
        gathered[(-step) % NY, 0] = block
        gathered[(-step) % NY, 1] = to_core(block)
    source = call(
        collect_body,
        "collect",
        jax.ShapeDtypeStruct((16, TILE, 256), BF16),
        tuple(gathered[k // 2, k % 2] for k in range(8)),
        moved=2**21,
    )
    work = 2 * 48 * TILE * TILE * 256

    one, two = shape(shard, F32), jax.ShapeDtypeStruct((2, shard, 256), F32)
    one16, two16 = shape(shard, BF16), jax.ShapeDtypeStruct((2, shard, 256), BF16)
    half = shape(136, F32)

    def forward(group, outs, source):
        return call(
            functools.partial(forward_body, group),
            f"forward_{group}",
            outs,
            (*plan, vals, source),
            scalars=4,
            scratch=(pltpu.VMEM((2 * len(ORDER[group]) + 1, TILE, 256), F32),),
            flops=0,
            moved=0,
        )

    def relay(body, name, outs, *args):
        return call(body, name, outs, args, moved=2**20)

    (over_a,) = forward(4, (two16,), source)
    over_a, source = lax.optimization_barrier((over_a, source))
    over_a = to_x(over_a)
    kept_a, over_b = forward(3, (two, two16), source)
    over_b = to_x(over_b)
    moving = relay(relay_first_body, "relay_first", two16, kept_a, over_a)
    moving, source = lax.optimization_barrier((moving, source))
    moving = swap_z(moving, -1)
    kept_b, over_c = forward(2, (two, two16), source)
    over_c = to_x(over_c)
    moving = relay(relay_body, "relay_b", two16, kept_b, over_b, moving)
    moving, source = lax.optimization_barrier((moving, source))
    moving = swap_z(moving, 1)
    kept_c, over_d = forward(1, (two, two16), source)
    over_d = to_x(over_d)
    moving = relay(relay_body, "relay_c", two16, kept_c, over_c, moving)
    moving, source = lax.optimization_barrier((moving, source))
    moving = swap_z(moving, -1)
    (kept_d,) = forward(0, (two,), source)
    own, moving = relay(relay_last_body, "relay_last", (one, one16), kept_d, over_d, moving)
    moving = swap_z(moving, 1)
    hidden_out, grad, high, low = call(
        activate_body,
        "activate",
        (one16, one16, one16, one16),
        (own, moving, weight, bias[None, :], grad_out),
        flops=4 * 256**3,
        moved=2 * 2**20,
    )

    def backward(group, blocks, before, outs):
        return call(
            functools.partial(backward_body, group),
            f"backward_{group}",
            outs,
            (*plan, vals, *blocks, *before),
            scalars=4,
            scratch=(pltpu.VMEM((8, TILE, 256), BF16),)
            + ((pltpu.VMEM((17, TILE, 256), F32),) if group == LAST else ()),
            flops=0,
            moved=0,
        )

    running = jax.ShapeDtypeStruct((17, TILE, 256), F32)
    barrier = lax.optimization_barrier
    first = swap_z(grad, 1)
    kept, sent = call(
        terms_body,
        "weight_terms",
        (half, half),
        (core[None], high, low, grad),
        scalars=1,
        scratch=(pltpu.VMEM((256, 256), F32),),
        flops=4 * 256**3,
        moved=2**20,
    )
    terms = kept + to_core(sent)
    terms, _ = barrier((terms, first))
    pair_d = jnp.stack([grad, first])
    pair_c = swap_z(pair_d, -1)
    over_d = to_x(pair_d)
    terms = terms + to_x(terms)
    total = backward(0, (pair_d,), (), running)
    pair_c, total, terms = barrier((pair_c, total, terms))
    pair_b = swap_z(pair_c, 1)
    over_c = to_x(pair_c)
    terms = terms + flip_z(terms, 1)
    total = backward(1, (pair_c, over_d), (total,), running)
    pair_b, total, terms = barrier((pair_b, total, terms))
    pair_a = swap_z(pair_b, -1)
    over_b = to_x(pair_b)
    terms = terms + flip_z(terms, 2)
    total = backward(2, (pair_b, over_c), (total,), running)
    pair_a, total, terms = barrier((pair_a, total, terms))
    over_a = to_x(pair_a)
    terms = terms + flip_z(terms, 4)
    total = backward(3, (pair_a, over_b), (total,), running)
    over_a, total, terms = barrier((over_a, total, terms))
    own, kept, over = backward(
        4,
        (over_a,),
        (total,),
        (
            one,
            jax.ShapeDtypeStruct((3, shard, 256), F32),
            jax.ShapeDtypeStruct((4, shard, 256), BF16),
        ),
    )
    over = to_core(over)
    *sends, mine = call(
        back_relay_body,
        "back_relay",
        (*[shape(400, BF16)] * 3, shape(144, BF16)),
        (kept, over, terms),
        moved=2 * 2**20,
    )
    got = [to_y(a, s) for a, s in zip(sends, (1, 2, 3))]
    mine = call(
        functools.partial(sum_terms_body, scale), "sum_terms", half, (mine, *got), moved=2**19
    )
    other = to_core(mine)
    grad_feats = call(
        finish_body,
        "finish",
        one16,
        (own, over, *got, weight),
        flops=2 * 256**3,
        moved=2 * 2**20,
    )
    grad_weight, grad_bias = call(
        assemble_body,
        "assemble",
        (shape(256, F32), shape(1, F32)),
        (core[None], mine, other),
        scalars=1,
        moved=2**19,
    )
    return (hidden_out, grad_feats, grad_weight, grad_bias.reshape(256))


def solution(mesh):
    in_specs = (
        P(("slab", "col", "row"), None),
        P(),
        P(),
        P(("slab", "row", "col"), None),
        P(("slab", "row"), "col", None, None, None),
        P(("slab", "row"), "col", None),
        P(("slab", "row"), "col", None),
        P(("slab", "row"), "col"),
    )
    out_specs = (
        P(("slab", "row", "col"), None),
        P(("slab", "col", "row"), None),
        P("slab", None),
        P("slab"),
    )
    return jax.shard_map(
        per_device, mesh=mesh, in_specs=in_specs, out_specs=out_specs, check_vma=False
    )
```

time: 141 us -> 132 us (0.936)
  waiting for transfers between devices: 48.1 us -> 30.8 us
  starting transfers between devices: 73.3 us -> 77.3 us
  Pallas kernels: 13.7 us -> 17.6 us
    ppermute x11 -> x9, waiting for transfers between devices: 19.4 us -> 10.2 us  [to_x(): return lax.ppermute(a, 'col', [(i, i ^ 1) for i in range(2 * NZ)])]
    ppermute x9 -> x6, waiting for transfers between devices: 16.9 us -> 7.83 us  [to_y(): lax.ppermute(a, 'row', [(i, (i + 2 * step) % (2 * NY)) for i in range(2 *...]
    ppermute x6 -> x7, starting transfers between devices: 16.5 us -> 23.6 us  [to_core(): return lax.ppermute(a, 'row', [(i, i ^ 1) for i in range(2 * NY)])]
    ppermute x16 -> x11, starting transfers between devices: 25.9 us -> 20.9 us  [the longest x8 16.4 us: swap_z(): return lax.ppermute(a, ('row', 'col'), pairs)]
    pallas_call x21 -> x22, Pallas kernels: 13.7 us -> 17.6 us  [call(): pl.pallas_call(body, name=name, out_shape=out_shape, in_specs=specs or [s...]
    ppermute x11 -> x9, starting transfers between devices: 20.1 us -> 23 us  [to_x(): return lax.ppermute(a, 'col', [(i, i ^ 1) for i in range(2 * NZ)])]
    ppermute x6 -> x7, waiting for transfers between devices: 1.03 us -> 2.66 us  [to_core(): return lax.ppermute(a, 'row', [(i, i ^ 1) for i in range(2 * NY)])]
    ppermute x9 -> x6, starting transfers between devices: 10.8 us -> 9.74 us  [to_y(): lax.ppermute(a, 'row', [(i, (i + 2 * step) % (2 * NY)) for i in range(2 *...]
  transfers between devices with their start and end apart: 42 -> 33, of which waited for: 23 -> 15; matrix products, arithmetic and copies ran while one was open for 1% -> 1% of each run, Pallas kernels for 7% -> 10%
where the time goes in v4:
time: 132 us
  starting transfers between devices  77.3 us (59%)
  waiting for transfers between devices  30.8 us (23%)
  Pallas kernels  17.6 us (13%)
  local copies, waits for them, and re-layouts  2.81 us (2%)
  between operations  1.57 us (1%)
  other arithmetic  1.46 us (1%)
    ppermute x7, starting transfers between devices, to_core(): return lax.ppermute(a, 'row', [(i, i ^ 1) for i in range(2 * NY)])  23.6 us
    ppermute x9, starting transfers between devices, to_x(): return lax.ppermute(a, 'col', [(i, i ^ 1) for i in range(2 * NZ)])  23 us
    pallas_call x22, Pallas kernels, call(): pl.pallas_call(body, name=name, out_shape=out_shape, in_specs=specs or [s...  17.6 us
    ppermute x8, starting transfers between devices, swap_z(): return lax.ppermute(a, ('row', 'col'), pairs)  16.4 us
    ppermute x9, waiting for transfers between devices, to_x(): return lax.ppermute(a, 'col', [(i, i ^ 1) for i in range(2 * NZ)])  10.2 us
    ppermute x6, starting transfers between devices, to_y(): lax.ppermute(a, 'row', [(i, (i + 2 * step) % (2 * NY)) for i in range(2 *...  9.74 us
    ppermute x6, waiting for transfers between devices, to_y(): lax.ppermute(a, 'row', [(i, (i + 2 * step) % (2 * NY)) for i in range(2 *...  7.83 us
    ppermute x3, waiting for transfers between devices, flip_z(): return lax.ppermute(a, 'col', [(i, i ^ 2 * bit) for i in range(2 * NZ)])  6.88 us
  transfers between devices with their start and end apart: 33, of which 15 were waited for; matrix products, arithmetic and copies ran while one was open for 1% of the time, Pallas kernels for 10%

profile of v4, /device:TPU:1, one launch (start us, length us, event | category | flops | bytes accessed | tf_op | source)
XLA Modules:
  0.0 131.5 jit_solution(13741544919679072879)
XLA Ops:
  0.6 3.8 %collective-permute-start.2 = (bf16[256,256]{1,0:T(8,128)(2,1)}, bf16[256,256]{1,0:T(8,128)(2,1)S(1)}, u32[]{:S(2)}, u32[]{:S(2)}) collective-permute-start(bf16[256,256]{1,0:T(8,128)(2,1)} %refs_0_.1), channel_id=1, source_target_pairs={{0,128},{32,160},{64,192},{96,224},{128,0},{160,32},{192,64},{224,... | collective-permute-start | bytes 393224 | tf_op jit(solution)/shard_map/ppermute | solution.py:59
  9.2 2.8 %copy-done = bf16[1,1,192,128,128]{4,3,2,1,0:T(8,128)(2,1)S(1)} copy-done((bf16[1,1,192,128,128]{4,3,2,1,0:T(8,128)(2,1)S(1)}, bf16[1,1,192,128,128]{4,3,2,1,0:T(8,128)(2,1)}, u32[]{:S(2)}) %copy-start) | copy-done | bytes 6291480
  16.4 2.3 %collective-permute-start.7 = (bf16[2,256,256]{2,1,0:T(8,128)(2,1)S(1)}, bf16[2,256,256]{2,1,0:T(8,128)(2,1)S(1)}, u32[]{:S(2)}, u32[]{:S(2)}) collective-permute-start(bf16[2,256,256]{2,1,0:T(8,128)(2,1)S(1)} %forward_4.1), channel_id=1, source_target_pairs={{0,2},{2,0},{4,6},{6,4},{8,10},{10,8},{12,14},{14,12},{16,18},{18,... | collective-permute-start | bytes 786440 | tf_op jit(solution)/shard_map/ppermute | solution.py:63
  21.2 4.4 %collective-permute-done.7.over = bf16[2,256,256]{2,1,0:T(8,128)(2,1)S(1)} collective-permute-done((bf16[2,256,256]{2,1,0:T(8,128)(2,1)S(1)}, bf16[2,256,256]{2,1,0:T(8,128)(2,1)S(1)}, u32[]{:S(2)}, u32[]{:S(2)}) %collective-permute-start.7) | collective-permute-done | bytes 262176 | tf_op jit(solution)/shard_map/ppermute | solution.py:63
  28.1 4.1 %collective-permute-start.10 = (bf16[2,256,256]{2,1,0:T(8,128)(2,1)S(1)}, bf16[2,256,256]{2,1,0:T(8,128)(2,1)S(1)}, u32[]{:S(2)}, u32[]{:S(2)}) collective-permute-start(bf16[2,256,256]{2,1,0:T(8,128)(2,1)S(1)} %get-tuple-element.73), channel_id=1, source_target_pairs={{0,2},{2,0},{4,6},{6,4},{8,10},{10,8},{12,14},{14,12},{16,18},{18,... | collective-permute-start | bytes 786440 | tf_op jit(solution)/shard_map/ppermute | solution.py:63
  32.3 4.3 %collective-permute-start.11 = (bf16[2,256,256]{2,1,0:T(8,128)(2,1)S(1)}, bf16[2,256,256]{2,1,0:T(8,128)(2,1)S(1)}, u32[]{:S(2)}, u32[]{:S(2)}) collective-permute-start(bf16[2,256,256]{2,1,0:T(8,128)(2,1)S(1)} %relay_b.1), channel_id=1, source_target_pairs={{0,4},{2,6},{4,0},{6,2},{8,12},{10,14},{12,8},{14,10},{16,20},{18,... | collective-permute-start | bytes 786440 | tf_op jit(solution)/shard_map/ppermute | solution.py:73
  38.2 2.9 %collective-permute-start.12 = (bf16[2,256,256]{2,1,0:T(8,128)(2,1)S(1)}, bf16[2,256,256]{2,1,0:T(8,128)(2,1)S(1)}, u32[]{:S(2)}, u32[]{:S(2)}) collective-permute-start(bf16[2,256,256]{2,1,0:T(8,128)(2,1)S(1)} %get-tuple-element.76), channel_id=1, source_target_pairs={{0,2},{2,0},{4,6},{6,4},{8,10},{10,8},{12,14},{14,12},{16,18},{18,... | collective-permute-start | bytes 786440 | tf_op jit(solution)/shard_map/ppermute | solution.py:63
  42.4 4.6 %collective-permute-done.12.over = bf16[2,256,256]{2,1,0:T(8,128)(2,1)S(1)} collective-permute-done((bf16[2,256,256]{2,1,0:T(8,128)(2,1)S(1)}, bf16[2,256,256]{2,1,0:T(8,128)(2,1)S(1)}, u32[]{:S(2)}, u32[]{:S(2)}) %collective-permute-start.12) | collective-permute-done | bytes 262176 | tf_op jit(solution)/shard_map/ppermute | solution.py:63
  47.1 2.3 %collective-permute-start.14 = (bf16[256,256]{1,0:T(8,128)(2,1)S(1)}, bf16[256,256]{1,0:T(8,128)(2,1)S(1)}, u32[]{:S(2)}, u32[]{:S(2)}) collective-permute-start(bf16[256,256]{1,0:T(8,128)(2,1)S(1)} %get-tuple-element.79), channel_id=1, source_target_pairs={{0,4},{2,6},{4,0},{6,2},{8,12},{10,14},{12,8},{14,10},{16,20},{18,... | collective-permute-start | bytes 393224 | tf_op jit(solution)/shard_map/ppermute | solution.py:73
  49.4 3.2 %collective-permute-done.14.got = bf16[256,256]{1,0:T(8,128)(2,1)S(1)} collective-permute-done((bf16[256,256]{1,0:T(8,128)(2,1)S(1)}, bf16[256,256]{1,0:T(8,128)(2,1)S(1)}, u32[]{:S(2)}, u32[]{:S(2)}) %collective-permute-start.14) | collective-permute-done | bytes 131104 | tf_op jit(solution)/shard_map/ppermute | solution.py:73
  53.5 2.5 %collective-permute-start.15 = (bf16[256,256]{1,0:T(8,128)(2,1)S(1)}, bf16[256,256]{1,0:T(8,128)(2,1)S(1)}, u32[]{:S(2)}, u32[]{:S(2)}) collective-permute-start(bf16[256,256]{1,0:T(8,128)(2,1)S(1)} %get-tuple-element.81.grad), channel_id=1, source_target_pairs={{0,4},{2,6},{4,0},{6,2},{8,12},{10,14},{12,8},{14,10},{16,20},{18,... | collective-permute-start | bytes 393224 | tf_op jit(solution)/shard_map/ppermute | solution.py:73
  56.3 2.3 %collective-permute-start.17 = (f32[136,256]{1,0:T(8,128)S(1)}, f32[136,256]{1,0:T(8,128)S(1)}, u32[]{:S(2)}, u32[]{:S(2)}) collective-permute-start(f32[136,256]{1,0:T(8,128)S(1)} %get-tuple-element.85), channel_id=1, source_target_pairs={{0,32},{32,0},{64,96},{96,64},{128,160},{160,128},{192,224},{224,1... | collective-permute-start | bytes 417800 | tf_op jit(solution)/shard_map/ppermute | solution.py:55
  60.5 3.9 %collective-permute-start.18 = (f32[136,256]{1,0:T(8,128)S(1)}, f32[136,256]{1,0:T(8,128)S(1)}, u32[]{:S(2)}, u32[]{:S(2)}) collective-permute-start(f32[136,256]{1,0:T(8,128)S(1)} %add.467), channel_id=1, source_target_pairs={{0,2},{2,0},{4,6},{6,4},{8,10},{10,8},{12,14},{14,12},{16,18},{18,... | collective-permute-start | bytes 417800 | tf_op jit(solution)/shard_map/ppermute | solution.py:63
  66.9 3.5 %collective-permute-start.19 = (bf16[2,256,256]{2,1,0:T(8,128)(2,1)S(1)}, bf16[2,256,256]{2,1,0:T(8,128)(2,1)S(1)}, u32[]{:S(2)}, u32[]{:S(2)}) collective-permute-start(bf16[2,256,256]{2,1,0:T(8,128)(2,1)S(1)} %collective-permute-done.16.rest_0_), channel_id=1, source_target_pairs={{0,4},{2,6},{4,0},{6,2},{8,12},{10,14},{12,8},{14,10},{16,20},{18,... | collective-permute-start | bytes 786440 | tf_op jit(solution)/shard_map/ppermute | solution.py:73
  70.4 3.0 %collective-permute-start.23 = (bf16[2,256,256]{2,1,0:T(8,128)(2,1)S(1)}, bf16[2,256,256]{2,1,0:T(8,128)(2,1)S(1)}, u32[]{:S(2)}, u32[]{:S(2)}) collective-permute-start(bf16[2,256,256]{2,1,0:T(8,128)(2,1)S(1)} %collective-permute-done.16.rest_0_), channel_id=1, source_target_pairs={{0,2},{2,0},{4,6},{6,4},{8,10},{10,8},{12,14},{14,12},{16,18},{18,... | collective-permute-start | bytes 786440 | tf_op jit(solution)/shard_map/ppermute | solution.py:63
  76.1 3.3 %collective-permute-start.26 = (bf16[2,256,256]{2,1,0:T(8,128)(2,1)S(1)}, bf16[2,256,256]{2,1,0:T(8,128)(2,1)S(1)}, u32[]{:S(2)}, u32[]{:S(2)}) collective-permute-start(bf16[2,256,256]{2,1,0:T(8,128)(2,1)S(1)} %collective-permute-done.19.rest_0_), channel_id=1, source_target_pairs={{0,2},{2,0},{4,6},{6,4},{8,10},{10,8},{12,14},{14,12},{16,18},{18,... | collective-permute-start | bytes 786440 | tf_op jit(solution)/shard_map/ppermute | solution.py:63
  80.7 3.9 %collective-permute-done.24 = f32[136,256]{1,0:T(8,128)S(1)} collective-permute-done((f32[136,256]{1,0:T(8,128)S(1)}, f32[136,256]{1,0:T(8,128)S(1)}, u32[]{:S(2)}, u32[]{:S(2)}) %collective-permute-start.24) | collective-permute-done | bytes 139296 | tf_op jit(solution)/shard_map/ppermute | solution.py:77
  84.7 2.6 %collective-permute-start.25 = (bf16[2,256,256]{2,1,0:T(8,128)(2,1)S(1)}, bf16[2,256,256]{2,1,0:T(8,128)(2,1)S(1)}, u32[]{:S(2)}, u32[]{:S(2)}) collective-permute-start(bf16[2,256,256]{2,1,0:T(8,128)(2,1)S(1)} %collective-permute-done.22.rest_0_), channel_id=1, source_target_pairs={{0,2},{2,0},{4,6},{6,4},{8,10},{10,8},{12,14},{14,12},{16,18},{18,... | collective-permute-start | bytes 786440 | tf_op jit(solution)/shard_map/ppermute | solution.py:63
  87.3 4.1 %collective-permute-start.27 = (f32[136,256]{1,0:T(8,128)S(1)}, f32[136,256]{1,0:T(8,128)S(1)}, u32[]{:S(2)}, u32[]{:S(2)}) collective-permute-start(f32[136,256]{1,0:T(8,128)S(1)} %add.470), channel_id=1, source_target_pairs={{0,16},{2,18},{4,20},{6,22},{8,24},{10,26},{12,28},{14,30},{16,0},... | collective-permute-start | bytes 417800 | tf_op jit(solution)/shard_map/ppermute | solution.py:77
  93.2 3.0 %collective-permute-done.27 = f32[136,256]{1,0:T(8,128)S(1)} collective-permute-done((f32[136,256]{1,0:T(8,128)S(1)}, f32[136,256]{1,0:T(8,128)S(1)}, u32[]{:S(2)}, u32[]{:S(2)}) %collective-permute-start.27) | collective-permute-done | bytes 139296 | tf_op jit(solution)/shard_map/ppermute | solution.py:77
  97.5 16.7 %collective-permute-start.28 = (bf16[4,256,256]{2,1,0:T(8,128)(2,1)S(1)}, bf16[4,256,256]{2,1,0:T(8,128)(2,1)S(1)}, u32[]{:S(2)}, u32[]{:S(2)}) collective-permute-start(bf16[4,256,256]{2,1,0:T(8,128)(2,1)S(1)} %get-tuple-element.99), channel_id=1, source_target_pairs={{0,32},{32,0},{64,96},{96,64},{128,160},{160,128},{192,224},{224,1... | collective-permute-start | bytes 1572872 | tf_op jit(solution)/shard_map/ppermute | solution.py:55
  116.6 2.2 %collective-permute-start.30 = (bf16[400,256]{1,0:T(8,128)(2,1)S(1)}, bf16[400,256]{1,0:T(8,128)(2,1)S(1)}, u32[]{:S(2)}, u32[]{:S(2)}) collective-permute-start(bf16[400,256]{1,0:T(8,128)(2,1)S(1)} %get-tuple-element.103), channel_id=1, source_target_pairs={{0,128},{32,160},{64,192},{96,224},{128,0},{160,32},{192,64},{224,... | collective-permute-start | bytes 614408 | tf_op jit(solution)/shard_map/ppermute | solution.py:59
  120.3 3.1 %collective-permute-done.29.a = bf16[400,256]{1,0:T(8,128)(2,1)S(1)} collective-permute-done((bf16[400,256]{1,0:T(8,128)(2,1)S(1)}, bf16[400,256]{1,0:T(8,128)(2,1)S(1)}, u32[]{:S(2)}, u32[]{:S(2)}) %collective-permute-start.29) | collective-permute-done | bytes 204832 | tf_op jit(solution)/shard_map/ppermute | solution.py:59
  123.5 4.6 %collective-permute-done.30.b = bf16[400,256]{1,0:T(8,128)(2,1)S(1)} collective-permute-done((bf16[400,256]{1,0:T(8,128)(2,1)S(1)}, bf16[400,256]{1,0:T(8,128)(2,1)S(1)}, u32[]{:S(2)}, u32[]{:S(2)}) %collective-permute-start.30) | collective-permute-done | bytes 204832 | tf_op jit(solution)/shard_map/ppermute | solution.py:59
  (86 shorter events, 36.6 us)
Async XLA Ops:
  0.6 12.0 %collective-permute-start.2 = (bf16[256,256]{1,0:T(8,128)(2,1)}, bf16[256,256]{1,0:T(8,128)(2,1)S(1)}, u32[]{:S(2)}, u32[]{:S(2)}) collective-permute-start(bf16[256,256]{1,0:T(8,128)(2,1)} %refs_0_.1), channel_id=1, source_target_pairs={{0,128},{32,160},{64,192},{96,224},{128,0},{160,32},{192,64},{224,... | collective-permute-start | bytes 393224 | tf_op jit(solution)/shard_map/ppermute | solution.py:59
  4.5 8.2 %collective-permute-start.1 = (bf16[256,256]{1,0:T(8,128)(2,1)}, bf16[256,256]{1,0:T(8,128)(2,1)S(1)}, u32[]{:S(2)}, u32[]{:S(2)}) collective-permute-start(bf16[256,256]{1,0:T(8,128)(2,1)} %refs_0_.1), channel_id=1, source_target_pairs={{0,192},{32,224},{64,0},{96,32},{128,64},{160,96},{192,128},{224,1... | collective-permute-start | bytes 393224 | tf_op jit(solution)/shard_map/ppermute | solution.py:59
  5.2 7.5 %collective-permute-start = (bf16[256,256]{1,0:T(8,128)(2,1)}, bf16[256,256]{1,0:T(8,128)(2,1)S(1)}, u32[]{:S(2)}, u32[]{:S(2)}) collective-permute-start(bf16[256,256]{1,0:T(8,128)(2,1)} %refs_0_.1), channel_id=1, source_target_pairs={{0,64},{32,96},{64,128},{96,160},{128,192},{160,224},{192,0},{224,... | collective-permute-start | bytes 393224 | tf_op jit(solution)/shard_map/ppermute | solution.py:59
  5.9 8.3 %collective-permute-start.3 = (bf16[256,256]{1,0:T(8,128)(2,1)}, bf16[256,256]{1,0:T(8,128)(2,1)S(1)}, u32[]{:S(2)}, u32[]{:S(2)}) collective-permute-start(bf16[256,256]{1,0:T(8,128)(2,1)} %refs_0_.1), channel_id=1, source_target_pairs={{0,32},{32,0},{64,96},{96,64},{128,160},{160,128},{192,224},{224,1... | collective-permute-start | bytes 393224 | tf_op jit(solution)/shard_map/ppermute | solution.py:55
  16.4 9.2 %collective-permute-start.7 = (bf16[2,256,256]{2,1,0:T(8,128)(2,1)S(1)}, bf16[2,256,256]{2,1,0:T(8,128)(2,1)S(1)}, u32[]{:S(2)}, u32[]{:S(2)}) collective-permute-start(bf16[2,256,256]{2,1,0:T(8,128)(2,1)S(1)} %forward_4.1), channel_id=1, source_target_pairs={{0,2},{2,0},{4,6},{6,4},{8,10},{10,8},{12,14},{14,12},{16,18},{18,... | collective-permute-start | bytes 786440 | tf_op jit(solution)/shard_map/ppermute | solution.py:63
  20.3 11.9 %collective-permute-start.8 = (bf16[2,256,256]{2,1,0:T(8,128)(2,1)S(1)}, bf16[2,256,256]{2,1,0:T(8,128)(2,1)S(1)}, u32[]{:S(2)}, u32[]{:S(2)}) collective-permute-start(bf16[2,256,256]{2,1,0:T(8,128)(2,1)S(1)} %get-tuple-element.69), channel_id=1, source_target_pairs={{0,2},{2,0},{4,6},{6,4},{8,10},{10,8},{12,14},{14,12},{16,18},{18,... | collective-permute-start | bytes 786440 | tf_op jit(solution)/shard_map/ppermute | solution.py:63
  25.6 6.6 %collective-permute-start.9 = (bf16[2,256,256]{2,1,0:T(8,128)(2,1)S(1)}, bf16[2,256,256]{2,1,0:T(8,128)(2,1)S(1)}, u32[]{:S(2)}, u32[]{:S(2)}) collective-permute-start(bf16[2,256,256]{2,1,0:T(8,128)(2,1)S(1)} %relay_first.1), channel_id=1, source_target_pairs={{0,28},{2,30},{4,8},{6,10},{8,4},{10,6},{12,16},{14,18},{16,12},{1... | collective-permute-start | bytes 786440 | tf_op jit(solution)/shard_map/ppermute | solution.py:73
  28.1 13.0 %collective-permute-start.10 = (bf16[2,256,256]{2,1,0:T(8,128)(2,1)S(1)}, bf16[2,256,256]{2,1,0:T(8,128)(2,1)S(1)}, u32[]{:S(2)}, u32[]{:S(2)}) collective-permute-start(bf16[2,256,256]{2,1,0:T(8,128)(2,1)S(1)} %get-tuple-element.73), channel_id=1, source_target_pairs={{0,2},{2,0},{4,6},{6,4},{8,10},{10,8},{12,14},{14,12},{16,18},{18,... | collective-permute-start | bytes 786440 | tf_op jit(solution)/shard_map/ppermute | solution.py:63
  32.3 8.8 %collective-permute-start.11 = (bf16[2,256,256]{2,1,0:T(8,128)(2,1)S(1)}, bf16[2,256,256]{2,1,0:T(8,128)(2,1)S(1)}, u32[]{:S(2)}, u32[]{:S(2)}) collective-permute-start(bf16[2,256,256]{2,1,0:T(8,128)(2,1)S(1)} %relay_b.1), channel_id=1, source_target_pairs={{0,4},{2,6},{4,0},{6,2},{8,12},{10,14},{12,8},{14,10},{16,20},{18,... | collective-permute-start | bytes 786440 | tf_op jit(solution)/shard_map/ppermute | solution.py:73
  38.2 8.8 %collective-permute-start.12 = (bf16[2,256,256]{2,1,0:T(8,128)(2,1)S(1)}, bf16[2,256,256]{2,1,0:T(8,128)(2,1)S(1)}, u32[]{:S(2)}, u32[]{:S(2)}) collective-permute-start(bf16[2,256,256]{2,1,0:T(8,128)(2,1)S(1)} %get-tuple-element.76), channel_id=1, source_target_pairs={{0,2},{2,0},{4,6},{6,4},{8,10},{10,8},{12,14},{14,12},{16,18},{18,... | collective-permute-start | bytes 786440 | tf_op jit(solution)/shard_map/ppermute | solution.py:63
  58.7 8.2 %collective-permute-start.16 = (bf16[2,256,256]{2,1,0:T(8,128)(2,1)S(1)}, bf16[2,256,256]{2,1,0:T(8,128)(2,1)S(1)}, u32[]{:S(2)}, u32[]{:S(2)}) collective-permute-start(bf16[2,256,256]{2,1,0:T(8,128)(2,1)S(1)} %pad_maximum_fusion.rest_0_), channel_id=1, source_target_pairs={{0,28},{2,30},{4,8},{6,10},{8,4},{10,6},{12,16},{14,18},{16,12},{1... | collective-permute-start | bytes 786440 | tf_op jit(solution)/shard_map/ppermute | solution.py:73
  60.5 6.3 %collective-permute-start.18 = (f32[136,256]{1,0:T(8,128)S(1)}, f32[136,256]{1,0:T(8,128)S(1)}, u32[]{:S(2)}, u32[]{:S(2)}) collective-permute-start(f32[136,256]{1,0:T(8,128)S(1)} %add.467), channel_id=1, source_target_pairs={{0,2},{2,0},{4,6},{6,4},{8,10},{10,8},{12,14},{14,12},{16,18},{18,... | collective-permute-start | bytes 417800 | tf_op jit(solution)/shard_map/ppermute | solution.py:63
  64.4 8.9 %collective-permute-start.20 = (bf16[2,256,256]{2,1,0:T(8,128)(2,1)S(1)}, bf16[2,256,256]{2,1,0:T(8,128)(2,1)S(1)}, u32[]{:S(2)}, u32[]{:S(2)}) collective-permute-start(bf16[2,256,256]{2,1,0:T(8,128)(2,1)S(1)} %pad_maximum_fusion.rest_0_), channel_id=1, source_target_pairs={{0,2},{2,0},{4,6},{6,4},{8,10},{10,8},{12,14},{14,12},{16,18},{18,... | collective-permute-start | bytes 786440 | tf_op jit(solution)/shard_map/ppermute | solution.py:63
  66.9 8.2 %collective-permute-start.19 = (bf16[2,256,256]{2,1,0:T(8,128)(2,1)S(1)}, bf16[2,256,256]{2,1,0:T(8,128)(2,1)S(1)}, u32[]{:S(2)}, u32[]{:S(2)}) collective-permute-start(bf16[2,256,256]{2,1,0:T(8,128)(2,1)S(1)} %collective-permute-done.16.rest_0_), channel_id=1, source_target_pairs={{0,4},{2,6},{4,0},{6,2},{8,12},{10,14},{12,8},{14,10},{16,20},{18,... | collective-permute-start | bytes 786440 | tf_op jit(solution)/shard_map/ppermute | solution.py:73
  70.4 9.1 %collective-permute-start.23 = (bf16[2,256,256]{2,1,0:T(8,128)(2,1)S(1)}, bf16[2,256,256]{2,1,0:T(8,128)(2,1)S(1)}, u32[]{:S(2)}, u32[]{:S(2)}) collective-permute-start(bf16[2,256,256]{2,1,0:T(8,128)(2,1)S(1)} %collective-permute-done.16.rest_0_), channel_id=1, source_target_pairs={{0,2},{2,0},{4,6},{6,4},{8,10},{10,8},{12,14},{14,12},{16,18},{18,... | collective-permute-start | bytes 786440 | tf_op jit(solution)/shard_map/ppermute | solution.py:63
  75.1 9.5 %collective-permute-start.22 = (bf16[2,256,256]{2,1,0:T(8,128)(2,1)S(1)}, bf16[2,256,256]{2,1,0:T(8,128)(2,1)S(1)}, u32[]{:S(2)}, u32[]{:S(2)}) collective-permute-start(bf16[2,256,256]{2,1,0:T(8,128)(2,1)S(1)} %collective-permute-done.19.rest_0_), channel_id=1, source_target_pairs={{0,28},{2,30},{4,8},{6,10},{8,4},{10,6},{12,16},{14,18},{16,12},{1... | collective-permute-start | bytes 786440 | tf_op jit(solution)/shard_map/ppermute | solution.py:73
  75.7 8.9 %collective-permute-start.24 = (f32[136,256]{1,0:T(8,128)S(1)}, f32[136,256]{1,0:T(8,128)S(1)}, u32[]{:S(2)}, u32[]{:S(2)}) collective-permute-start(f32[136,256]{1,0:T(8,128)S(1)} %add.469), channel_id=1, source_target_pairs={{0,8},{2,10},{4,12},{6,14},{8,0},{10,2},{12,4},{14,6},{16,24},{18,... | collective-permute-start | bytes 417800 | tf_op jit(solution)/shard_map/ppermute | solution.py:77
  76.1 15.3 %collective-permute-start.26 = (bf16[2,256,256]{2,1,0:T(8,128)(2,1)S(1)}, bf16[2,256,256]{2,1,0:T(8,128)(2,1)S(1)}, u32[]{:S(2)}, u32[]{:S(2)}) collective-permute-start(bf16[2,256,256]{2,1,0:T(8,128)(2,1)S(1)} %collective-permute-done.19.rest_0_), channel_id=1, source_target_pairs={{0,2},{2,0},{4,6},{6,4},{8,10},{10,8},{12,14},{14,12},{16,18},{18,... | collective-permute-start | bytes 786440 | tf_op jit(solution)/shard_map/ppermute | solution.py:63
  84.7 11.5 %collective-permute-start.25 = (bf16[2,256,256]{2,1,0:T(8,128)(2,1)S(1)}, bf16[2,256,256]{2,1,0:T(8,128)(2,1)S(1)}, u32[]{:S(2)}, u32[]{:S(2)}) collective-permute-start(bf16[2,256,256]{2,1,0:T(8,128)(2,1)S(1)} %collective-permute-done.22.rest_0_), channel_id=1, source_target_pairs={{0,2},{2,0},{4,6},{6,4},{8,10},{10,8},{12,14},{14,12},{16,18},{18,... | collective-permute-start | bytes 786440 | tf_op jit(solution)/shard_map/ppermute | solution.py:63
  87.3 8.8 %collective-permute-start.27 = (f32[136,256]{1,0:T(8,128)S(1)}, f32[136,256]{1,0:T(8,128)S(1)}, u32[]{:S(2)}, u32[]{:S(2)}) collective-permute-start(f32[136,256]{1,0:T(8,128)S(1)} %add.470), channel_id=1, source_target_pairs={{0,16},{2,18},{4,20},{6,22},{8,24},{10,26},{12,28},{14,30},{16,0},... | collective-permute-start | bytes 417800 | tf_op jit(solution)/shard_map/ppermute | solution.py:77
  97.5 18.2 %collective-permute-start.28 = (bf16[4,256,256]{2,1,0:T(8,128)(2,1)S(1)}, bf16[4,256,256]{2,1,0:T(8,128)(2,1)S(1)}, u32[]{:S(2)}, u32[]{:S(2)}) collective-permute-start(bf16[4,256,256]{2,1,0:T(8,128)(2,1)S(1)} %get-tuple-element.99), channel_id=1, source_target_pairs={{0,32},{32,0},{64,96},{96,64},{128,160},{160,128},{192,224},{224,1... | collective-permute-start | bytes 1572872 | tf_op jit(solution)/shard_map/ppermute | solution.py:55
  115.9 7.6 %collective-permute-start.29 = (bf16[400,256]{1,0:T(8,128)(2,1)S(1)}, bf16[400,256]{1,0:T(8,128)(2,1)S(1)}, u32[]{:S(2)}, u32[]{:S(2)}) collective-permute-start(bf16[400,256]{1,0:T(8,128)(2,1)S(1)} %get-tuple-element.102), channel_id=1, source_target_pairs={{0,64},{32,96},{64,128},{96,160},{128,192},{160,224},{192,0},{224,... | collective-permute-start | bytes 614408 | tf_op jit(solution)/shard_map/ppermute | solution.py:59
  116.6 11.4 %collective-permute-start.30 = (bf16[400,256]{1,0:T(8,128)(2,1)S(1)}, bf16[400,256]{1,0:T(8,128)(2,1)S(1)}, u32[]{:S(2)}, u32[]{:S(2)}) collective-permute-start(bf16[400,256]{1,0:T(8,128)(2,1)S(1)} %get-tuple-element.103), channel_id=1, source_target_pairs={{0,128},{32,160},{64,192},{96,224},{128,0},{160,32},{192,64},{224,... | collective-permute-start | bytes 614408 | tf_op jit(solution)/shard_map/ppermute | solution.py:59
  118.8 9.3 %collective-permute-start.31 = (bf16[400,256]{1,0:T(8,128)(2,1)S(1)}, bf16[400,256]{1,0:T(8,128)(2,1)S(1)}, u32[]{:S(2)}, u32[]{:S(2)}) collective-permute-start(bf16[400,256]{1,0:T(8,128)(2,1)S(1)} %get-tuple-element.104), channel_id=1, source_target_pairs={{0,192},{32,224},{64,0},{96,32},{128,64},{160,96},{192,128},{224,1... | collective-permute-start | bytes 614408 | tf_op jit(solution)/shard_map/ppermute | solution.py:59
  (14 other events, 72.9 us)

commit v5 on v4

--- a/solution.py
+++ b/solution.py
@@ -12,13 +12,12 @@
 UNROLL = 16
 ORDER = (
     ((0, 0), (1, 0)),
-    ((7, 0), (6, 0), (0, 1), (1, 1)),
-    ((2, 0), (3, 0), (7, 1), (6, 1)),
-    ((5, 0), (4, 0), (2, 1), (3, 1)),
-    ((5, 1), (4, 1)),
+    ((7, 0), (6, 0), (7, 1), (6, 1), (0, 1), (1, 1)),
+    ((2, 0), (3, 0), (2, 1), (3, 1)),
+    ((5, 0), (4, 0), (5, 1), (4, 1)),
 )
-FIRST = (0, 2, 6, 10, 14)
-LAST = 4
+FIRST = (0, 2, 8, 12)
+LAST = 3
 NY = 4
 NZ = 8
 F32 = jnp.float32
@@ -63,13 +62,14 @@
     return lax.ppermute(a, "col", [(i, i ^ 1) for i in range(2 * NZ)])
 
 
-def swap_z(a, side):
+def swap_z(a, side, across=0):
     pairs = []
     for row in range(2 * NY):
         for col in range(2 * NZ):
             z, x = divmod(col, 2)
             step = side if (z + row) % 2 == 0 else -side
-            pairs.append((row * 2 * NZ + col, row * 2 * NZ + (z + step) % NZ * 2 + x))
+            to = (z + step) % NZ * 2 + (x + across) % 2
+            pairs.append((row * 2 * NZ + col, row * 2 * NZ + to))
     return lax.ppermute(a, ("row", "col"), pairs)
 
 
@@ -123,32 +123,22 @@
         total,
         size,
     )
-    outs = list(outs)
-    if group < LAST:
-        kept = outs.pop(0)
+    for k, out in enumerate(outs):
         for n in range(2):
-            place(kept.at[n], total, n, F32)
-    if group:
-        over = outs.pop(0)
-        for n in range(2):
-            place(over.at[n], total, size // 2 - 2 + n, BF16)
+            place(out.at[n], total, 2 * k + n, F32 if k == 0 and group < LAST else BF16)
 
 
 def wide(ref):
     return ref[...].astype(F32)
 
 
-def relay_first_body(kept, over, out):
-    out[...] = (kept[...] + wide(over)).astype(BF16)
-
-
-def relay_body(kept, over, got, out):
-    out[...] = (kept[...] + wide(over) + wide(got)).astype(BF16)
-
-
-def relay_last_body(kept, over, got, own, out):
-    own[...] = kept[0] + wide(over.at[0]) + wide(got.at[0])
-    out[...] = (kept[1] + wide(over.at[1]) + wide(got.at[1])).astype(BF16)
+def relay_body(kept, got, over, out):
+    out[...] = (kept[...] + wide(got) + wide(over)).astype(BF16)
+
+
+def relay_last_body(kept, got, over, near, own, out):
+    own[...] = kept[0] + wide(got.at[0]) + wide(over.at[0]) + wide(near.at[0])
+    out[...] = (kept[1] + wide(got.at[1]) + wide(over.at[1]) + wide(near.at[1])).astype(BF16)
 
 
 def activate_body(own, got, weight, bias, given, hidden, grad, high, low):
@@ -176,12 +166,16 @@
     )
     column = jnp.sum(g.astype(F32), axis=0, keepdims=True)
     for ref, half in ((kept, core[0]), (sent, 1 - core[0])):
-        ref[0:128] = whole[pl.ds(pl.multiple_of(half * 128, 128), 128)]
-        ref[128:136] = jnp.broadcast_to(column, (8, 256))
+        ref[0:128] = whole[pl.ds(pl.multiple_of(half * 128, 128), 128)].astype(BF16)
+        ref[128:144] = jnp.broadcast_to(column, (16, 256)).astype(BF16)
+
+
+def add_terms_body(mine, other, out):
+    out[...] = (wide(mine) + wide(other)).astype(BF16)
 
 
 def backward_body(group, starts, order, rows, cols, vals, *rest):
-    count = 1 if group in (0, LAST) else 2
+    count = (1, 3, 2, 2)[group]
     blocks, rest = rest[:count], rest[count:]
     if group:
         before, rest = rest[0], rest[1:]
@@ -220,12 +214,10 @@
         place(over.at[3], total, 1, BF16)
 
 
-def back_relay_body(kept, over, terms, out_a, out_b, out_c, mine):
-    mine[0:128] = terms[0:128].astype(BF16)
-    mine[128:144] = jnp.broadcast_to(terms[128:129], (16, 256)).astype(BF16)
+def back_relay_body(kept, over, terms, out_a, out_b, out_c):
     for k, out in enumerate((out_a, out_b, out_c)):
         out[0:256] = (kept[k] + over[k].astype(F32)).astype(BF16)
-        out[256:400] = mine[...]
+        out[256:400] = terms[...]
 
 
 def sum_terms_body(scale, own, a, b, c, out):
@@ -306,7 +298,7 @@
 
     one, two = shape(shard, F32), jax.ShapeDtypeStruct((2, shard, 256), F32)
     one16, two16 = shape(shard, BF16), jax.ShapeDtypeStruct((2, shard, 256), BF16)
-    half = shape(136, F32)
+    half = shape(144, BF16)
 
     def forward(group, outs, source):
         return call(
@@ -323,26 +315,22 @@
     def relay(body, name, outs, *args):
         return call(body, name, outs, args, moved=2**20)
 
-    (over_a,) = forward(4, (two16,), source)
-    over_a, source = lax.optimization_barrier((over_a, source))
-    over_a = to_x(over_a)
-    kept_a, over_b = forward(3, (two, two16), source)
-    over_b = to_x(over_b)
-    moving = relay(relay_first_body, "relay_first", two16, kept_a, over_a)
-    moving, source = lax.optimization_barrier((moving, source))
-    moving = swap_z(moving, -1)
-    kept_b, over_c = forward(2, (two, two16), source)
-    over_c = to_x(over_c)
-    moving = relay(relay_body, "relay_b", two16, kept_b, over_b, moving)
-    moving, source = lax.optimization_barrier((moving, source))
-    moving = swap_z(moving, 1)
-    kept_c, over_d = forward(1, (two, two16), source)
-    over_d = to_x(over_d)
-    moving = relay(relay_body, "relay_c", two16, kept_c, over_c, moving)
-    moving, source = lax.optimization_barrier((moving, source))
-    moving = swap_z(moving, -1)
-    (kept_d,) = forward(0, (two,), source)
-    own, moving = relay(relay_last_body, "relay_last", (one, one16), kept_d, over_d, moving)
+    barrier = lax.optimization_barrier
+    moving, over = forward(3, (two16, two16), source)
+    moving, over, source = barrier((moving, over, source))
+    moving, over = swap_z(moving, -1), swap_z(over, -1, 1)
+    kept, next_over = forward(2, (two, two16), source)
+    next_over = swap_z(next_over, 1, 1)
+    moving = relay(relay_body, "relay_2", two16, kept, moving, over)
+    moving, source = barrier((moving, source))
+    moving, over = swap_z(moving, 1), next_over
+    kept, next_over, near = forward(1, (two, two16, two16), source)
+    next_over, near = swap_z(next_over, -1, 1), to_x(near)
+    moving = relay(relay_body, "relay_1", two16, kept, moving, over)
+    moving, source = barrier((moving, source))
+    moving, over = swap_z(moving, -1), next_over
+    (kept,) = forward(0, (two,), source)
+    own, moving = relay(relay_last_body, "relay_0", (one, one16), kept, moving, over, near)
     moving = swap_z(moving, 1)
     hidden_out, grad, high, low = call(
         activate_body,
@@ -360,16 +348,23 @@
             outs,
             (*plan, vals, *blocks, *before),
             scalars=4,
-            scratch=(pltpu.VMEM((8, TILE, 256), BF16),)
+            scratch=(pltpu.VMEM((2 * len(ORDER[group]), TILE, 256), BF16),)
             + ((pltpu.VMEM((17, TILE, 256), F32),) if group == LAST else ()),
             flops=0,
             moved=0,
         )
 
     running = jax.ShapeDtypeStruct((17, TILE, 256), F32)
-    barrier = lax.optimization_barrier
+    last = (
+        one,
+        jax.ShapeDtypeStruct((3, shard, 256), F32),
+        jax.ShapeDtypeStruct((4, shard, 256), BF16),
+    )
+    def add_terms(mine, other):
+        return call(add_terms_body, "add_terms", half, (mine, other), moved=2**18)
+
     first = swap_z(grad, 1)
-    kept, sent = call(
+    terms, sent = call(
         terms_body,
         "weight_terms",
         (half, half),
@@ -379,49 +374,42 @@
         flops=4 * 256**3,
         moved=2**20,
     )
-    terms = kept + to_core(sent)
-    terms, _ = barrier((terms, first))
+    terms = add_terms(terms, to_core(sent))
+    terms, first = barrier((terms, first))
     pair_d = jnp.stack([grad, first])
-    pair_c = swap_z(pair_d, -1)
-    over_d = to_x(pair_d)
-    terms = terms + to_x(terms)
+    pair, over, near = swap_z(pair_d, -1), swap_z(pair_d, -1, 1), to_x(pair_d)
+    moved_terms = to_x(terms)
     total = backward(0, (pair_d,), (), running)
-    pair_c, total, terms = barrier((pair_c, total, terms))
-    pair_b = swap_z(pair_c, 1)
-    over_c = to_x(pair_c)
-    terms = terms + flip_z(terms, 1)
-    total = backward(1, (pair_c, over_d), (total,), running)
-    pair_b, total, terms = barrier((pair_b, total, terms))
-    pair_a = swap_z(pair_b, -1)
-    over_b = to_x(pair_b)
-    terms = terms + flip_z(terms, 2)
-    total = backward(2, (pair_b, over_c), (total,), running)
-    pair_a, total, terms = barrier((pair_a, total, terms))
-    over_a = to_x(pair_a)
-    terms = terms + flip_z(terms, 4)
-    total = backward(3, (pair_a, over_b), (total,), running)
-    over_a, total, terms = barrier((over_a, total, terms))
-    own, kept, over = backward(
-        4,
-        (over_a,),
-        (total,),
-        (
-            one,
-            jax.ShapeDtypeStruct((3, shard, 256), F32),
-            jax.ShapeDtypeStruct((4, shard, 256), BF16),
-        ),
-    )
+    pair, over, total, moved_terms = barrier((pair, over, total, moved_terms))
+    blocks = (pair, over, near)
+    for group, way, bit in ((1, 1, 1), (2, -1, 2)):
+        next_pair, over = swap_z(pair, way), swap_z(pair, way, 1)
+        terms = add_terms(terms, moved_terms)
+        terms, blocks, total = barrier((terms, blocks, total))
+        moved_terms = flip_z(terms, bit)
+        total = backward(group, blocks, (total,), running)
+        pair, over, total, moved_terms = barrier((next_pair, over, total, moved_terms))
+        blocks = (pair, over)
+    terms = add_terms(terms, moved_terms)
+    terms, blocks, total = barrier((terms, blocks, total))
+    moved_terms = flip_z(terms, 4)
+    own, kept, over = backward(LAST, blocks, (total,), last)
+    terms = add_terms(terms, moved_terms)
     over = to_core(over)
-    *sends, mine = call(
+    sends = call(
         back_relay_body,
         "back_relay",
-        (*[shape(400, BF16)] * 3, shape(144, BF16)),
+        (shape(400, BF16),) * 3,
         (kept, over, terms),
         moved=2 * 2**20,
     )
     got = [to_y(a, s) for a, s in zip(sends, (1, 2, 3))]
     mine = call(
-        functools.partial(sum_terms_body, scale), "sum_terms", half, (mine, *got), moved=2**19
+        functools.partial(sum_terms_body, scale),
+        "sum_terms",
+        shape(136, F32),
+        (terms, *got),
+        moved=2**19,
     )
     other = to_core(mine)
     grad_feats = call(

time: 132 us -> 135 us (1.023)
  waiting for transfers between devices: 30.8 us -> 46.2 us
  starting transfers between devices: 77.3 us -> 69.3 us
  Pallas kernels: 17.6 us -> 13.6 us
    ppermute x8 -> x14, starting transfers between devices: 16.4 us -> 41.7 us  [swap_z(): return lax.ppermute(a, ('row', 'col'), pairs)]
    ppermute x9 -> x3, starting transfers between devices: 23 us -> 5.04 us  [to_x(): return lax.ppermute(a, 'col', [(i, i ^ 1) for i in range(2 * NZ)])]
    ppermute x7, starting transfers between devices: 23.6 us -> 8.82 us  [to_core(): return lax.ppermute(a, 'row', [(i, i ^ 1) for i in range(2 * NY)])]
    ppermute x8 -> x14, waiting for transfers between devices: 3.19 us -> 10.5 us  [swap_z(): return lax.ppermute(a, ('row', 'col'), pairs)]
    ppermute x3, waiting for transfers between devices: 6.88 us -> 13.1 us  [flip_z(): return lax.ppermute(a, 'col', [(i, i ^ 2 * bit) for i in range(2 * NZ)])]
    pallas_call x22 -> x24, Pallas kernels: 17.6 us -> 13.6 us  [call(): pl.pallas_call(body, name=name, out_shape=out_shape, in_specs=specs or [s...]
    ppermute x9 -> x3, waiting for transfers between devices: 10.2 us -> 11.6 us  [to_x(): return lax.ppermute(a, 'col', [(i, i ^ 1) for i in range(2 * NZ)])]
  transfers between devices with their start and end apart: 33 -> 33, of which waited for: 15 -> 20; matrix products, arithmetic and copies ran while one was open for 1% -> 1% of each run, Pallas kernels for 10% -> 7%
where the time goes in v5:
time: 135 us
  starting transfers between devices  69.3 us (51%)
  waiting for transfers between devices  46.2 us (34%)
  Pallas kernels  13.6 us (10%)
  local copies, waits for them, and re-layouts  2.81 us (2%)
  between operations  1.56 us (1%)
  other arithmetic  1.36 us (1%)
    ppermute x14, starting transfers between devices, swap_z(): return lax.ppermute(a, ('row', 'col'), pairs)  41.7 us
    pallas_call x24, Pallas kernels, call(): pl.pallas_call(body, name=name, out_shape=out_shape, in_specs=specs or [s...  13.6 us
    ppermute x3, waiting for transfers between devices, flip_z(): return lax.ppermute(a, 'col', [(i, i ^ 2 * bit) for i in range(2 * NZ)])  13.1 us
    ppermute x3, waiting for transfers between devices, to_x(): return lax.ppermute(a, 'col', [(i, i ^ 1) for i in range(2 * NZ)])  11.6 us
    ppermute x14, waiting for transfers between devices, swap_z(): return lax.ppermute(a, ('row', 'col'), pairs)  10.5 us
    ppermute x6, starting transfers between devices, to_y(): lax.ppermute(a, 'row', [(i, (i + 2 * step) % (2 * NY)) for i in range(2 *...  10.5 us
    ppermute x7, starting transfers between devices, to_core(): return lax.ppermute(a, 'row', [(i, i ^ 1) for i in range(2 * NY)])  8.82 us
    ppermute x6, waiting for transfers between devices, to_y(): lax.ppermute(a, 'row', [(i, (i + 2 * step) % (2 * NY)) for i in range(2 *...  8.61 us
  transfers between devices with their start and end apart: 33, of which 20 were waited for; matrix products, arithmetic and copies ran while one was open for 1% of the time, Pallas kernels for 7%

profile of v5, /device:TPU:1, one launch (start us, length us, event | category | flops | bytes accessed | tf_op | source)
XLA Modules:
  0.0 134.8 jit_solution(3190338022615489215)
XLA Ops:
  0.6 3.8 %collective-permute-start.2 = (bf16[256,256]{1,0:T(8,128)(2,1)}, bf16[256,256]{1,0:T(8,128)(2,1)S(1)}, u32[]{:S(2)}, u32[]{:S(2)}) collective-permute-start(bf16[256,256]{1,0:T(8,128)(2,1)} %refs_0_.1), channel_id=1, source_target_pairs={{0,128},{32,160},{64,192},{96,224},{128,0},{160,32},{192,64},{224,... | collective-permute-start | bytes 393224 | tf_op jit(solution)/shard_map/ppermute | solution.py:58
  9.2 2.8 %copy-done = bf16[1,1,192,128,128]{4,3,2,1,0:T(8,128)(2,1)S(1)} copy-done((bf16[1,1,192,128,128]{4,3,2,1,0:T(8,128)(2,1)S(1)}, bf16[1,1,192,128,128]{4,3,2,1,0:T(8,128)(2,1)}, u32[]{:S(2)}) %copy-start) | copy-done | bytes 6291480
  16.5 2.5 %collective-permute-start.7 = (bf16[2,256,256]{2,1,0:T(8,128)(2,1)S(1)}, bf16[2,256,256]{2,1,0:T(8,128)(2,1)S(1)}, u32[]{:S(2)}, u32[]{:S(2)}) collective-permute-start(bf16[2,256,256]{2,1,0:T(8,128)(2,1)S(1)} %get-tuple-element.81), channel_id=1, source_target_pairs={{0,28},{2,30},{4,8},{6,10},{8,4},{10,6},{12,16},{14,18},{16,12},{1... | collective-permute-start | bytes 786440 | tf_op jit(solution)/shard_map/ppermute | solution.py:73
  21.8 5.1 %collective-permute-start.10 = (bf16[2,256,256]{2,1,0:T(8,128)(2,1)S(1)}, bf16[2,256,256]{2,1,0:T(8,128)(2,1)S(1)}, u32[]{:S(2)}, u32[]{:S(2)}) collective-permute-start(bf16[2,256,256]{2,1,0:T(8,128)(2,1)S(1)} %get-tuple-element.86), channel_id=1, source_target_pairs={{0,6},{2,4},{4,2},{6,0},{8,14},{10,12},{12,10},{14,8},{16,22},{18,... | collective-permute-start | bytes 786440 | tf_op jit(solution)/shard_map/ppermute | solution.py:73
  27.2 6.0 %collective-permute-start.9 = (bf16[2,256,256]{2,1,0:T(8,128)(2,1)S(1)}, bf16[2,256,256]{2,1,0:T(8,128)(2,1)S(1)}, u32[]{:S(2)}, u32[]{:S(2)}) collective-permute-start(bf16[2,256,256]{2,1,0:T(8,128)(2,1)S(1)} %relay_2.1), channel_id=1, source_target_pairs={{0,4},{2,6},{4,0},{6,2},{8,12},{10,14},{12,8},{14,10},{16,20},{18,... | collective-permute-start | bytes 786440 | tf_op jit(solution)/shard_map/ppermute | solution.py:73
  34.4 3.3 %collective-permute-start.12 = (bf16[2,256,256]{2,1,0:T(8,128)(2,1)S(1)}, bf16[2,256,256]{2,1,0:T(8,128)(2,1)S(1)}, u32[]{:S(2)}, u32[]{:S(2)}) collective-permute-start(bf16[2,256,256]{2,1,0:T(8,128)(2,1)S(1)} %get-tuple-element.89), channel_id=1, source_target_pairs={{0,30},{2,28},{4,10},{6,8},{8,6},{10,4},{12,18},{14,16},{16,14},{1... | collective-permute-start | bytes 786440 | tf_op jit(solution)/shard_map/ppermute | solution.py:73
  42.9 2.3 %collective-permute-done.13.near = bf16[2,256,256]{2,1,0:T(8,128)(2,1)S(1)} collective-permute-done((bf16[2,256,256]{2,1,0:T(8,128)(2,1)S(1)}, bf16[2,256,256]{2,1,0:T(8,128)(2,1)S(1)}, u32[]{:S(2)}, u32[]{:S(2)}) %collective-permute-start.13) | collective-permute-done | bytes 262176 | tf_op jit(solution)/shard_map/ppermute | solution.py:62
  47.2 7.3 %collective-permute-start.14 = (bf16[256,256]{1,0:T(8,128)(2,1)S(1)}, bf16[256,256]{1,0:T(8,128)(2,1)S(1)}, u32[]{:S(2)}, u32[]{:S(2)}) collective-permute-start(bf16[256,256]{1,0:T(8,128)(2,1)S(1)} %get-tuple-element.92), channel_id=1, source_target_pairs={{0,4},{2,6},{4,0},{6,2},{8,12},{10,14},{12,8},{14,10},{16,20},{18,... | collective-permute-start | bytes 393224 | tf_op jit(solution)/shard_map/ppermute | solution.py:73
  54.5 2.4 %collective-permute-done.14.got = bf16[256,256]{1,0:T(8,128)(2,1)S(1)} collective-permute-done((bf16[256,256]{1,0:T(8,128)(2,1)S(1)}, bf16[256,256]{1,0:T(8,128)(2,1)S(1)}, u32[]{:S(2)}, u32[]{:S(2)}) %collective-permute-start.14) | collective-permute-done | bytes 131104 | tf_op jit(solution)/shard_map/ppermute | solution.py:73
  57.8 2.7 %collective-permute-start.16 = (bf16[256,256]{1,0:T(8,128)(2,1)S(1)}, bf16[256,256]{1,0:T(8,128)(2,1)S(1)}, u32[]{:S(2)}, u32[]{:S(2)}) collective-permute-start(bf16[256,256]{1,0:T(8,128)(2,1)S(1)} %get-tuple-element.96.grad), channel_id=1, source_target_pairs={{0,4},{2,6},{4,0},{6,2},{8,12},{10,14},{12,8},{14,10},{16,20},{18,... | collective-permute-start | bytes 393224 | tf_op jit(solution)/shard_map/ppermute | solution.py:73
  62.9 2.3 %collective-permute-start.18 = (bf16[2,256,256]{2,1,0:T(8,128)(2,1)S(1)}, bf16[2,256,256]{2,1,0:T(8,128)(2,1)S(1)}, u32[]{:S(2)}, u32[]{:S(2)}) collective-permute-start(bf16[2,256,256]{2,1,0:T(8,128)(2,1)S(1)} %pad_maximum_fusion.rest_0_), channel_id=1, source_target_pairs={{0,30},{2,28},{4,10},{6,8},{8,6},{10,4},{12,18},{14,16},{16,14},{1... | collective-permute-start | bytes 786440 | tf_op jit(solution)/shard_map/ppermute | solution.py:73
  65.2 2.7 %collective-permute-start.17 = (bf16[2,256,256]{2,1,0:T(8,128)(2,1)S(1)}, bf16[2,256,256]{2,1,0:T(8,128)(2,1)S(1)}, u32[]{:S(2)}, u32[]{:S(2)}) collective-permute-start(bf16[2,256,256]{2,1,0:T(8,128)(2,1)S(1)} %pad_maximum_fusion.rest_0_), channel_id=1, source_target_pairs={{0,28},{2,30},{4,8},{6,10},{8,4},{10,6},{12,16},{14,18},{16,12},{1... | collective-permute-start | bytes 786440 | tf_op jit(solution)/shard_map/ppermute | solution.py:73
  67.9 3.0 %collective-permute-start.19 = (bf16[144,256]{1,0:T(8,128)(2,1)S(1)}, bf16[144,256]{1,0:T(8,128)(2,1)S(1)}, u32[]{:S(2)}, u32[]{:S(2)}) collective-permute-start(bf16[144,256]{1,0:T(8,128)(2,1)S(1)} %add_terms.5.mine), channel_id=1, source_target_pairs={{0,2},{2,0},{4,6},{6,4},{8,10},{10,8},{12,14},{14,12},{16,18},{18,... | collective-permute-start | bytes 221192 | tf_op jit(solution)/shard_map/ppermute | solution.py:62
  72.1 9.3 %collective-permute-done.19.other = bf16[144,256]{1,0:T(8,128)(2,1)S(1)} collective-permute-done((bf16[144,256]{1,0:T(8,128)(2,1)S(1)}, bf16[144,256]{1,0:T(8,128)(2,1)S(1)}, u32[]{:S(2)}, u32[]{:S(2)}) %collective-permute-start.19) | collective-permute-done | bytes 73760 | tf_op jit(solution)/shard_map/ppermute | solution.py:62
  81.4 5.5 %collective-permute-start.22 = (bf16[2,256,256]{2,1,0:T(8,128)(2,1)S(1)}, bf16[2,256,256]{2,1,0:T(8,128)(2,1)S(1)}, u32[]{:S(2)}, u32[]{:S(2)}) collective-permute-start(bf16[2,256,256]{2,1,0:T(8,128)(2,1)S(1)} %collective-permute-done.17.rest_0_), channel_id=1, source_target_pairs={{0,6},{2,4},{4,2},{6,0},{8,14},{10,12},{12,10},{14,8},{16,22},{18,... | collective-permute-start | bytes 786440 | tf_op jit(solution)/shard_map/ppermute | solution.py:73
  88.3 3.3 %collective-permute-done.23.other = bf16[144,256]{1,0:T(8,128)(2,1)S(1)} collective-permute-done((bf16[144,256]{1,0:T(8,128)(2,1)S(1)}, bf16[144,256]{1,0:T(8,128)(2,1)S(1)}, u32[]{:S(2)}, u32[]{:S(2)}) %collective-permute-start.23) | collective-permute-done | bytes 73760 | tf_op jit(solution)/shard_map/ppermute | solution.py:77
  94.1 2.6 %collective-permute-start.24 = (bf16[2,256,256]{2,1,0:T(8,128)(2,1)S(1)}, bf16[2,256,256]{2,1,0:T(8,128)(2,1)S(1)}, u32[]{:S(2)}, u32[]{:S(2)}) collective-permute-start(bf16[2,256,256]{2,1,0:T(8,128)(2,1)S(1)} %collective-permute-done.21.rest_0_), channel_id=1, source_target_pairs={{0,28},{2,30},{4,8},{6,10},{8,4},{10,6},{12,16},{14,18},{16,12},{1... | collective-permute-start | bytes 786440 | tf_op jit(solution)/shard_map/ppermute | solution.py:73
  98.0 5.2 %collective-permute-done.26.other = bf16[144,256]{1,0:T(8,128)(2,1)S(1)} collective-permute-done((bf16[144,256]{1,0:T(8,128)(2,1)S(1)}, bf16[144,256]{1,0:T(8,128)(2,1)S(1)}, u32[]{:S(2)}, u32[]{:S(2)}) %collective-permute-start.26) | collective-permute-done | bytes 73760 | tf_op jit(solution)/shard_map/ppermute | solution.py:77
  105.7 4.3 %collective-permute-start.27 = (bf16[4,256,256]{2,1,0:T(8,128)(2,1)S(1)}, bf16[4,256,256]{2,1,0:T(8,128)(2,1)S(1)}, u32[]{:S(2)}, u32[]{:S(2)}) collective-permute-start(bf16[4,256,256]{2,1,0:T(8,128)(2,1)S(1)} %get-tuple-element.126), channel_id=1, source_target_pairs={{0,32},{32,0},{64,96},{96,64},{128,160},{160,128},{192,224},{224,1... | collective-permute-start | bytes 1572872 | tf_op jit(solution)/shard_map/ppermute | solution.py:54
  110.1 3.1 %collective-permute-start.28 = (bf16[144,256]{1,0:T(8,128)(2,1)S(1)}, bf16[144,256]{1,0:T(8,128)(2,1)S(1)}, u32[]{:S(2)}, u32[]{:S(2)}) collective-permute-start(bf16[144,256]{1,0:T(8,128)(2,1)S(1)} %add_terms.8.mine), channel_id=1, source_target_pairs={{0,16},{2,18},{4,20},{6,22},{8,24},{10,26},{12,28},{14,30},{16,0},... | collective-permute-start | bytes 221192 | tf_op jit(solution)/shard_map/ppermute | solution.py:77
  113.2 4.6 %collective-permute-done.28.other = bf16[144,256]{1,0:T(8,128)(2,1)S(1)} collective-permute-done((bf16[144,256]{1,0:T(8,128)(2,1)S(1)}, bf16[144,256]{1,0:T(8,128)(2,1)S(1)}, u32[]{:S(2)}, u32[]{:S(2)}) %collective-permute-start.28) | collective-permute-done | bytes 73760 | tf_op jit(solution)/shard_map/ppermute | solution.py:77
  117.9 2.7 %collective-permute-start.29 = (bf16[400,256]{1,0:T(8,128)(2,1)S(1)}, bf16[400,256]{1,0:T(8,128)(2,1)S(1)}, u32[]{:S(2)}, u32[]{:S(2)}) collective-permute-start(bf16[400,256]{1,0:T(8,128)(2,1)S(1)} %get-tuple-element.129), channel_id=1, source_target_pairs={{0,64},{32,96},{64,128},{96,160},{128,192},{160,224},{192,0},{224,... | collective-permute-start | bytes 614408 | tf_op jit(solution)/shard_map/ppermute | solution.py:58
  123.1 3.3 %collective-permute-done.29.a = bf16[400,256]{1,0:T(8,128)(2,1)S(1)} collective-permute-done((bf16[400,256]{1,0:T(8,128)(2,1)S(1)}, bf16[400,256]{1,0:T(8,128)(2,1)S(1)}, u32[]{:S(2)}, u32[]{:S(2)}) %collective-permute-start.29) | collective-permute-done | bytes 204832 | tf_op jit(solution)/shard_map/ppermute | solution.py:58
  126.4 5.2 %collective-permute-done.30.b = bf16[400,256]{1,0:T(8,128)(2,1)S(1)} collective-permute-done((bf16[400,256]{1,0:T(8,128)(2,1)S(1)}, bf16[400,256]{1,0:T(8,128)(2,1)S(1)}, u32[]{:S(2)}, u32[]{:S(2)}) %collective-permute-start.30) | collective-permute-done | bytes 204832 | tf_op jit(solution)/shard_map/ppermute | solution.py:58
  (83 shorter events, 37.9 us)
Async XLA Ops:
  0.6 12.0 %collective-permute-start.2 = (bf16[256,256]{1,0:T(8,128)(2,1)}, bf16[256,256]{1,0:T(8,128)(2,1)S(1)}, u32[]{:S(2)}, u32[]{:S(2)}) collective-permute-start(bf16[256,256]{1,0:T(8,128)(2,1)} %refs_0_.1), channel_id=1, source_target_pairs={{0,128},{32,160},{64,192},{96,224},{128,0},{160,32},{192,64},{224,... | collective-permute-start | bytes 393224 | tf_op jit(solution)/shard_map/ppermute | solution.py:58
  4.5 8.2 %collective-permute-start.1 = (bf16[256,256]{1,0:T(8,128)(2,1)}, bf16[256,256]{1,0:T(8,128)(2,1)S(1)}, u32[]{:S(2)}, u32[]{:S(2)}) collective-permute-start(bf16[256,256]{1,0:T(8,128)(2,1)} %refs_0_.1), channel_id=1, source_target_pairs={{0,192},{32,224},{64,0},{96,32},{128,64},{160,96},{192,128},{224,1... | collective-permute-start | bytes 393224 | tf_op jit(solution)/shard_map/ppermute | solution.py:58
  5.2 7.5 %collective-permute-start = (bf16[256,256]{1,0:T(8,128)(2,1)}, bf16[256,256]{1,0:T(8,128)(2,1)S(1)}, u32[]{:S(2)}, u32[]{:S(2)}) collective-permute-start(bf16[256,256]{1,0:T(8,128)(2,1)} %refs_0_.1), channel_id=1, source_target_pairs={{0,64},{32,96},{64,128},{96,160},{128,192},{160,224},{192,0},{224,... | collective-permute-start | bytes 393224 | tf_op jit(solution)/shard_map/ppermute | solution.py:58
  5.9 8.3 %collective-permute-start.3 = (bf16[256,256]{1,0:T(8,128)(2,1)}, bf16[256,256]{1,0:T(8,128)(2,1)S(1)}, u32[]{:S(2)}, u32[]{:S(2)}) collective-permute-start(bf16[256,256]{1,0:T(8,128)(2,1)} %refs_0_.1), channel_id=1, source_target_pairs={{0,32},{32,0},{64,96},{96,64},{128,160},{160,128},{192,224},{224,1... | collective-permute-start | bytes 393224 | tf_op jit(solution)/shard_map/ppermute | solution.py:54
  16.5 10.5 %collective-permute-start.7 = (bf16[2,256,256]{2,1,0:T(8,128)(2,1)S(1)}, bf16[2,256,256]{2,1,0:T(8,128)(2,1)S(1)}, u32[]{:S(2)}, u32[]{:S(2)}) collective-permute-start(bf16[2,256,256]{2,1,0:T(8,128)(2,1)S(1)} %get-tuple-element.81), channel_id=1, source_target_pairs={{0,28},{2,30},{4,8},{6,10},{8,4},{10,6},{12,16},{14,18},{16,12},{1... | collective-permute-start | bytes 786440 | tf_op jit(solution)/shard_map/ppermute | solution.py:73
  18.9 8.2 %collective-permute-start.8 = (bf16[2,256,256]{2,1,0:T(8,128)(2,1)S(1)}, bf16[2,256,256]{2,1,0:T(8,128)(2,1)S(1)}, u32[]{:S(2)}, u32[]{:S(2)}) collective-permute-start(bf16[2,256,256]{2,1,0:T(8,128)(2,1)S(1)} %get-tuple-element.82), channel_id=1, source_target_pairs={{0,30},{2,28},{4,10},{6,8},{8,6},{10,4},{12,18},{14,16},{16,14},{1... | collective-permute-start | bytes 786440 | tf_op jit(solution)/shard_map/ppermute | solution.py:73
  21.8 17.9 %collective-permute-start.10 = (bf16[2,256,256]{2,1,0:T(8,128)(2,1)S(1)}, bf16[2,256,256]{2,1,0:T(8,128)(2,1)S(1)}, u32[]{:S(2)}, u32[]{:S(2)}) collective-permute-start(bf16[2,256,256]{2,1,0:T(8,128)(2,1)S(1)} %get-tuple-element.86), channel_id=1, source_target_pairs={{0,6},{2,4},{4,2},{6,0},{8,14},{10,12},{12,10},{14,8},{16,22},{18,... | collective-permute-start | bytes 786440 | tf_op jit(solution)/shard_map/ppermute | solution.py:73
  27.2 12.5 %collective-permute-start.9 = (bf16[2,256,256]{2,1,0:T(8,128)(2,1)S(1)}, bf16[2,256,256]{2,1,0:T(8,128)(2,1)S(1)}, u32[]{:S(2)}, u32[]{:S(2)}) collective-permute-start(bf16[2,256,256]{2,1,0:T(8,128)(2,1)S(1)} %relay_2.1), channel_id=1, source_target_pairs={{0,4},{2,6},{4,0},{6,2},{8,12},{10,14},{12,8},{14,10},{16,20},{18,... | collective-permute-start | bytes 786440 | tf_op jit(solution)/shard_map/ppermute | solution.py:73
  34.4 8.5 %collective-permute-start.12 = (bf16[2,256,256]{2,1,0:T(8,128)(2,1)S(1)}, bf16[2,256,256]{2,1,0:T(8,128)(2,1)S(1)}, u32[]{:S(2)}, u32[]{:S(2)}) collective-permute-start(bf16[2,256,256]{2,1,0:T(8,128)(2,1)S(1)} %get-tuple-element.89), channel_id=1, source_target_pairs={{0,30},{2,28},{4,10},{6,8},{8,6},{10,4},{12,18},{14,16},{16,14},{1... | collective-permute-start | bytes 786440 | tf_op jit(solution)/shard_map/ppermute | solution.py:73
  37.7 7.6 %collective-permute-start.13 = (bf16[2,256,256]{2,1,0:T(8,128)(2,1)S(1)}, bf16[2,256,256]{2,1,0:T(8,128)(2,1)S(1)}, u32[]{:S(2)}, u32[]{:S(2)}) collective-permute-start(bf16[2,256,256]{2,1,0:T(8,128)(2,1)S(1)} %get-tuple-element.90), channel_id=1, source_target_pairs={{0,2},{2,0},{4,6},{6,4},{8,10},{10,8},{12,14},{14,12},{16,18},{18,... | collective-permute-start | bytes 786440 | tf_op jit(solution)/shard_map/ppermute | solution.py:62
  39.8 7.3 %collective-permute-start.11 = (bf16[2,256,256]{2,1,0:T(8,128)(2,1)S(1)}, bf16[2,256,256]{2,1,0:T(8,128)(2,1)S(1)}, u32[]{:S(2)}, u32[]{:S(2)}) collective-permute-start(bf16[2,256,256]{2,1,0:T(8,128)(2,1)S(1)} %relay_1.1), channel_id=1, source_target_pairs={{0,28},{2,30},{4,8},{6,10},{8,4},{10,6},{12,16},{14,18},{16,12},{1... | collective-permute-start | bytes 786440 | tf_op jit(solution)/shard_map/ppermute | solution.py:73
  47.2 9.7 %collective-permute-start.14 = (bf16[256,256]{1,0:T(8,128)(2,1)S(1)}, bf16[256,256]{1,0:T(8,128)(2,1)S(1)}, u32[]{:S(2)}, u32[]{:S(2)}) collective-permute-start(bf16[256,256]{1,0:T(8,128)(2,1)S(1)} %get-tuple-element.92), channel_id=1, source_target_pairs={{0,4},{2,6},{4,0},{6,2},{8,12},{10,14},{12,8},{14,10},{16,20},{18,... | collective-permute-start | bytes 393224 | tf_op jit(solution)/shard_map/ppermute | solution.py:73
  62.9 18.5 %collective-permute-start.18 = (bf16[2,256,256]{2,1,0:T(8,128)(2,1)S(1)}, bf16[2,256,256]{2,1,0:T(8,128)(2,1)S(1)}, u32[]{:S(2)}, u32[]{:S(2)}) collective-permute-start(bf16[2,256,256]{2,1,0:T(8,128)(2,1)S(1)} %pad_maximum_fusion.rest_0_), channel_id=1, source_target_pairs={{0,30},{2,28},{4,10},{6,8},{8,6},{10,4},{12,18},{14,16},{16,14},{1... | collective-permute-start | bytes 786440 | tf_op jit(solution)/shard_map/ppermute | solution.py:73
  65.2 16.2 %collective-permute-start.17 = (bf16[2,256,256]{2,1,0:T(8,128)(2,1)S(1)}, bf16[2,256,256]{2,1,0:T(8,128)(2,1)S(1)}, u32[]{:S(2)}, u32[]{:S(2)}) collective-permute-start(bf16[2,256,256]{2,1,0:T(8,128)(2,1)S(1)} %pad_maximum_fusion.rest_0_), channel_id=1, source_target_pairs={{0,28},{2,30},{4,8},{6,10},{8,4},{10,6},{12,16},{14,18},{16,12},{1... | collective-permute-start | bytes 786440 | tf_op jit(solution)/shard_map/ppermute | solution.py:73
  67.9 19.1 %collective-permute-start.20 = (bf16[2,256,256]{2,1,0:T(8,128)(2,1)S(1)}, bf16[2,256,256]{2,1,0:T(8,128)(2,1)S(1)}, u32[]{:S(2)}, u32[]{:S(2)}) collective-permute-start(bf16[2,256,256]{2,1,0:T(8,128)(2,1)S(1)} %pad_maximum_fusion.rest_0_), channel_id=1, source_target_pairs={{0,2},{2,0},{4,6},{6,4},{8,10},{10,8},{12,14},{14,12},{16,18},{18,... | collective-permute-start | bytes 786440 | tf_op jit(solution)/shard_map/ppermute | solution.py:62
  67.9 13.5 %collective-permute-start.19 = (bf16[144,256]{1,0:T(8,128)(2,1)S(1)}, bf16[144,256]{1,0:T(8,128)(2,1)S(1)}, u32[]{:S(2)}, u32[]{:S(2)}) collective-permute-start(bf16[144,256]{1,0:T(8,128)(2,1)S(1)} %add_terms.5.mine), channel_id=1, source_target_pairs={{0,2},{2,0},{4,6},{6,4},{8,10},{10,8},{12,14},{14,12},{16,18},{18,... | collective-permute-start | bytes 221192 | tf_op jit(solution)/shard_map/ppermute | solution.py:62
  81.4 11.4 %collective-permute-start.22 = (bf16[2,256,256]{2,1,0:T(8,128)(2,1)S(1)}, bf16[2,256,256]{2,1,0:T(8,128)(2,1)S(1)}, u32[]{:S(2)}, u32[]{:S(2)}) collective-permute-start(bf16[2,256,256]{2,1,0:T(8,128)(2,1)S(1)} %collective-permute-done.17.rest_0_), channel_id=1, source_target_pairs={{0,6},{2,4},{4,2},{6,0},{8,14},{10,12},{12,10},{14,8},{16,22},{18,... | collective-permute-start | bytes 786440 | tf_op jit(solution)/shard_map/ppermute | solution.py:73
  94.0 9.2 %collective-permute-start.25 = (bf16[2,256,256]{2,1,0:T(8,128)(2,1)S(1)}, bf16[2,256,256]{2,1,0:T(8,128)(2,1)S(1)}, u32[]{:S(2)}, u32[]{:S(2)}) collective-permute-start(bf16[2,256,256]{2,1,0:T(8,128)(2,1)S(1)} %collective-permute-done.21.rest_0_), channel_id=1, source_target_pairs={{0,30},{2,28},{4,10},{6,8},{8,6},{10,4},{12,18},{14,16},{16,14},{1... | collective-permute-start | bytes 786440 | tf_op jit(solution)/shard_map/ppermute | solution.py:73
  94.1 10.3 %collective-permute-start.24 = (bf16[2,256,256]{2,1,0:T(8,128)(2,1)S(1)}, bf16[2,256,256]{2,1,0:T(8,128)(2,1)S(1)}, u32[]{:S(2)}, u32[]{:S(2)}) collective-permute-start(bf16[2,256,256]{2,1,0:T(8,128)(2,1)S(1)} %collective-permute-done.21.rest_0_), channel_id=1, source_target_pairs={{0,28},{2,30},{4,8},{6,10},{8,4},{10,6},{12,16},{14,18},{16,12},{1... | collective-permute-start | bytes 786440 | tf_op jit(solution)/shard_map/ppermute | solution.py:73
  105.7 12.1 %collective-permute-start.27 = (bf16[4,256,256]{2,1,0:T(8,128)(2,1)S(1)}, bf16[4,256,256]{2,1,0:T(8,128)(2,1)S(1)}, u32[]{:S(2)}, u32[]{:S(2)}) collective-permute-start(bf16[4,256,256]{2,1,0:T(8,128)(2,1)S(1)} %get-tuple-element.126), channel_id=1, source_target_pairs={{0,32},{32,0},{64,96},{96,64},{128,160},{160,128},{192,224},{224,1... | collective-permute-start | bytes 1572872 | tf_op jit(solution)/shard_map/ppermute | solution.py:54
  110.1 7.7 %collective-permute-start.28 = (bf16[144,256]{1,0:T(8,128)(2,1)S(1)}, bf16[144,256]{1,0:T(8,128)(2,1)S(1)}, u32[]{:S(2)}, u32[]{:S(2)}) collective-permute-start(bf16[144,256]{1,0:T(8,128)(2,1)S(1)} %add_terms.8.mine), channel_id=1, source_target_pairs={{0,16},{2,18},{4,20},{6,22},{8,24},{10,26},{12,28},{14,30},{16,0},... | collective-permute-start | bytes 221192 | tf_op jit(solution)/shard_map/ppermute | solution.py:77
  117.9 8.5 %collective-permute-start.29 = (bf16[400,256]{1,0:T(8,128)(2,1)S(1)}, bf16[400,256]{1,0:T(8,128)(2,1)S(1)}, u32[]{:S(2)}, u32[]{:S(2)}) collective-permute-start(bf16[400,256]{1,0:T(8,128)(2,1)S(1)} %get-tuple-element.129), channel_id=1, source_target_pairs={{0,64},{32,96},{64,128},{96,160},{128,192},{160,224},{192,0},{224,... | collective-permute-start | bytes 614408 | tf_op jit(solution)/shard_map/ppermute | solution.py:58
  120.6 11.1 %collective-permute-start.30 = (bf16[400,256]{1,0:T(8,128)(2,1)S(1)}, bf16[400,256]{1,0:T(8,128)(2,1)S(1)}, u32[]{:S(2)}, u32[]{:S(2)}) collective-permute-start(bf16[400,256]{1,0:T(8,128)(2,1)S(1)} %get-tuple-element.130), channel_id=1, source_target_pairs={{0,128},{32,160},{64,192},{96,224},{128,0},{160,32},{192,64},{224,... | collective-permute-start | bytes 614408 | tf_op jit(solution)/shard_map/ppermute | solution.py:58
  122.5 9.1 %collective-permute-start.31 = (bf16[400,256]{1,0:T(8,128)(2,1)S(1)}, bf16[400,256]{1,0:T(8,128)(2,1)S(1)}, u32[]{:S(2)}, u32[]{:S(2)}) collective-permute-start(bf16[400,256]{1,0:T(8,128)(2,1)S(1)} %get-tuple-element.131), channel_id=1, source_target_pairs={{0,192},{32,224},{64,0},{96,32},{128,64},{160,96},{192,128},{224,1... | collective-permute-start | bytes 614408 | tf_op jit(solution)/shard_map/ppermute | solution.py:58
  (14 other events, 89.2 us)

commit v6 on v5

--- a/solution.py
+++ b/solution.py
@@ -12,12 +12,14 @@
 UNROLL = 16
 ORDER = (
     ((0, 0), (1, 0)),
-    ((7, 0), (6, 0), (7, 1), (6, 1), (0, 1), (1, 1)),
-    ((2, 0), (3, 0), (2, 1), (3, 1)),
-    ((5, 0), (4, 0), (5, 1), (4, 1)),
+    ((7, 0), (6, 0)),
+    ((0, 1), (1, 1)),
+    ((2, 0), (3, 0)),
+    ((7, 1), (6, 1)),
+    ((2, 1), (3, 1)),
+    ((5, 0), (4, 0)),
+    ((5, 1), (4, 1)),
 )
-FIRST = (0, 2, 8, 12)
-LAST = 3
 NY = 4
 NZ = 8
 F32 = jnp.float32
@@ -73,10 +75,6 @@
     return lax.ppermute(a, ("row", "col"), pairs)
 
 
-def flip_z(a, bit):
-    return lax.ppermute(a, "col", [(i, i ^ (2 * bit)) for i in range(2 * NZ)])
-
-
 def load_body(source, out, sem):
     copy = pltpu.make_async_copy(source, out, sem)
     copy.start()
@@ -95,8 +93,8 @@
         ref[half * TILE : (half + 1) * TILE] = total[2 * first + half].astype(dtype)
 
 
-def add_tiles(group, starts, order, to_slot, product, total, dummy):
-    first, last = starts[group], starts[group + 1]
+def add_tiles(begin, end, starts, order, to_slot, product, total, dummy):
+    first, last = starts[begin], starts[end]
 
     def batch(i, carry):
         slots = [first + i * UNROLL + u for u in range(UNROLL)]
@@ -110,35 +108,39 @@
     lax.fori_loop(0, (last - first + UNROLL - 1) // UNROLL, batch, 0)
 
 
-def forward_body(group, starts, order, rows, cols, vals, source, *rest):
+def forward_body(begin, end, starts, order, rows, cols, vals, source, *rest):
     outs, total = rest[:-1], rest[-1]
-    size = 2 * len(ORDER[group])
+    size = 4 * (end - begin)
     total[...] = jnp.zeros_like(total)
     add_tiles(
-        group,
+        begin,
+        end,
         starts,
         order,
-        lambda t: jnp.clip(rows[t] - 2 * FIRST[group], 0, size - 1),
+        lambda t: jnp.clip(rows[t] - 4 * begin, 0, size - 1),
         lambda tile, t: jnp.dot(vals[tile], source[cols[t]], preferred_element_type=F32),
         total,
         size,
     )
     for k, out in enumerate(outs):
         for n in range(2):
-            place(out.at[n], total, 2 * k + n, F32 if k == 0 and group < LAST else BF16)
+            place(out.at[n], total, 2 * k + n, out.dtype)
 
 
 def wide(ref):
     return ref[...].astype(F32)
 
 
-def relay_body(kept, got, over, out):
-    out[...] = (kept[...] + wide(got) + wide(over)).astype(BF16)
-
-
-def relay_last_body(kept, got, over, near, own, out):
-    own[...] = kept[0] + wide(got.at[0]) + wide(over.at[0]) + wide(near.at[0])
-    out[...] = (kept[1] + wide(got.at[1]) + wide(over.at[1]) + wide(near.at[1])).astype(BF16)
+def relay_body(kept, *rest):
+    total = kept[...]
+    for ref in rest[:-1]:
+        total = total + wide(ref)
+    rest[-1][...] = total.astype(BF16)
+
+
+def relay_last_body(kept, over, got, own, out):
+    own[...] = kept[0] + wide(over.at[0]) + wide(got.at[0])
+    out[...] = (kept[1] + wide(over.at[1]) + wide(got.at[1])).astype(BF16)
 
 
 def activate_body(own, got, weight, bias, given, hidden, grad, high, low):
@@ -170,43 +172,59 @@
         ref[128:144] = jnp.broadcast_to(column, (16, 256)).astype(BF16)
 
 
-def add_terms_body(mine, other, out):
-    out[...] = (wide(mine) + wide(other)).astype(BF16)
-
-
-def backward_body(group, starts, order, rows, cols, vals, *rest):
-    count = (1, 3, 2, 2)[group]
-    blocks, rest = rest[:count], rest[count:]
-    if group:
+def add_rows(a, b):
+    return (a.astype(F32) + b.astype(F32)).astype(BF16)
+
+
+def pack_own_body(grad, mine, other, out):
+    out[0:256] = grad[...]
+    out[256:400] = add_rows(mine[...], other[...])
+
+
+def pack_pair_body(own, got, out):
+    out[0:256] = own[0:256]
+    out[256:512] = got[0:256]
+    out[512:656] = add_rows(own[256:400], got[256:400])
+
+
+def pack_far_body(before, got, out):
+    out[0:512] = got[0:512]
+    out[512:656] = add_rows(before[512:656], got[512:656])
+
+
+def backward_body(begin, end, starts, order, rows, cols, vals, *rest):
+    blocks, rest = rest[: end - begin], rest[end - begin :]
+    if begin:
         before, rest = rest[0], rest[1:]
-    if group == LAST:
+    if end == len(ORDER):
         own, kept, over, source, total = rest
     else:
         total, source = rest
     n = 0
     for block in blocks:
-        for half in range(4):
-            source[n] = block[half // 2, half % 2 * TILE : (half % 2 + 1) * TILE]
+        for k in range(4):
+            source[n] = block[k * TILE : (k + 1) * TILE]
             n += 1
-    if group:
+    if begin:
         total[...] = before[...]
     else:
         total[...] = jnp.zeros_like(total)
     add_tiles(
-        group,
+        begin,
+        end,
         starts,
         order,
         lambda t: cols[t],
         lambda tile, t: lax.dot_general(
             vals[tile],
-            source[jnp.clip(rows[t] - 2 * FIRST[group], 0, n - 1)],
+            source[jnp.clip(rows[t] - 4 * begin, 0, n - 1)],
             (((0,), (0,)), ((), ())),
             preferred_element_type=F32,
         ),
         total,
         16,
     )
-    if group == LAST:
+    if end == len(ORDER):
         place(own, total, 0, F32)
         for k, dy in enumerate((1, 2, 3)):
             place(kept.at[k], total, 2 * dy, F32)
@@ -214,7 +232,11 @@
         place(over.at[3], total, 1, BF16)
 
 
-def back_relay_body(kept, over, terms, out_a, out_b, out_c):
+def back_relay_body(kept, over, pair, last, far, side, near, out_a, out_b, out_c, terms):
+    sums = slice(512, 656)
+    plane = add_rows(pair[sums], last[sums]).astype(F32) + far[sums].astype(F32)
+    other = side[sums].astype(F32) + near[sums].astype(F32)
+    terms[...] = (plane + other).astype(BF16)
     for k, out in enumerate((out_a, out_b, out_c)):
         out[0:256] = (kept[k] + over[k].astype(F32)).astype(BF16)
         out[256:400] = terms[...]
@@ -254,19 +276,18 @@
     for rank, (dz, dx) in enumerate(sum(ORDER, ())):
         ranks[dz * 2 + dx] = rank
     rank = sum(jnp.where(where == k, r, 0) for k, r in enumerate(ranks))
-    group = sum((rank >= f).astype(jnp.int32) for f in FIRST[1:])
     rows = rank * 2 + tile_rows[0, 0] % 2
     rel_y = (owner_col // 2 - y) % NY
     cols = (rel_y * 2 + (owner_col + core) % 2) * 2 + tile_cols[0, 0] % 2
     slots = jnp.arange(rows.shape[0], dtype=jnp.int32)
     live = slots < tile_count[0, 0]
-    key = jnp.where(live, group, LAST + 1) * rows.shape[0] + slots
+    key = jnp.where(live, rank // 2, len(ORDER)) * rows.shape[0] + slots
     position = jnp.sum((key[None, :] < key[:, None]).astype(jnp.int32), axis=1)
     chosen = position[None, :] == slots[:, None]
     order, rows, cols = (
         jnp.sum(jnp.where(chosen, a[None, :], 0), axis=1) for a in (slots, rows, cols)
     )
-    groups = jnp.arange(8, dtype=jnp.int32)
+    groups = jnp.arange(16, dtype=jnp.int32)
     starts = jnp.sum((key[None, :] < groups[:, None] * rows.shape[0]).astype(jnp.int32), axis=1)
     plan = (starts, order, rows, cols)
 
@@ -294,43 +315,40 @@
         tuple(gathered[k // 2, k % 2] for k in range(8)),
         moved=2**21,
     )
-    work = 2 * 48 * TILE * TILE * 256
 
     one, two = shape(shard, F32), jax.ShapeDtypeStruct((2, shard, 256), F32)
     one16, two16 = shape(shard, BF16), jax.ShapeDtypeStruct((2, shard, 256), BF16)
     half = shape(144, BF16)
 
-    def forward(group, outs, source):
+    def forward(begin, end, outs, source):
         return call(
-            functools.partial(forward_body, group),
-            f"forward_{group}",
+            functools.partial(forward_body, begin, end),
+            f"forward_{begin}",
             outs,
             (*plan, vals, source),
             scalars=4,
-            scratch=(pltpu.VMEM((2 * len(ORDER[group]) + 1, TILE, 256), F32),),
-            flops=0,
-            moved=0,
+            scratch=(pltpu.VMEM((4 * (end - begin) + 1, TILE, 256), F32),),
         )
 
     def relay(body, name, outs, *args):
         return call(body, name, outs, args, moved=2**20)
 
     barrier = lax.optimization_barrier
-    moving, over = forward(3, (two16, two16), source)
-    moving, over, source = barrier((moving, over, source))
-    moving, over = swap_z(moving, -1), swap_z(over, -1, 1)
-    kept, next_over = forward(2, (two, two16), source)
-    next_over = swap_z(next_over, 1, 1)
-    moving = relay(relay_body, "relay_2", two16, kept, moving, over)
+    moving, far = forward(6, 8, (two16, two16), source)
+    moving, far, source = barrier((moving, far, source))
+    far, moving = swap_z(far, -1, 1), swap_z(moving, -1)
+    kept_b, over_c, over_b = forward(3, 6, (two, two16, two16), source)
+    over_b, over_c = to_x(over_b), to_x(over_c)
+    moving = relay(relay_body, "relay_b", two16, kept_b, moving, far, over_b)
     moving, source = barrier((moving, source))
-    moving, over = swap_z(moving, 1), next_over
-    kept, next_over, near = forward(1, (two, two16, two16), source)
-    next_over, near = swap_z(next_over, -1, 1), to_x(near)
-    moving = relay(relay_body, "relay_1", two16, kept, moving, over)
+    moving = swap_z(moving, 1)
+    kept_c, over_d = forward(1, 3, (two, two16), source)
+    over_d = to_x(over_d)
+    moving = relay(relay_body, "relay_c", two16, kept_c, moving, over_c)
     moving, source = barrier((moving, source))
-    moving, over = swap_z(moving, -1), next_over
-    (kept,) = forward(0, (two,), source)
-    own, moving = relay(relay_last_body, "relay_0", (one, one16), kept, moving, over, near)
+    moving = swap_z(moving, -1)
+    (kept_d,) = forward(0, 1, (two,), source)
+    own, moving = relay(relay_last_body, "relay_last", (one, one16), kept_d, over_d, moving)
     moving = swap_z(moving, 1)
     hidden_out, grad, high, low = call(
         activate_body,
@@ -341,29 +359,19 @@
         moved=2 * 2**20,
     )
 
-    def backward(group, blocks, before, outs):
+    def backward(begin, blocks, before, outs):
+        end = begin + len(blocks)
         return call(
-            functools.partial(backward_body, group),
-            f"backward_{group}",
+            functools.partial(backward_body, begin, end),
+            f"backward_{begin}",
             outs,
             (*plan, vals, *blocks, *before),
             scalars=4,
-            scratch=(pltpu.VMEM((2 * len(ORDER[group]), TILE, 256), BF16),)
-            + ((pltpu.VMEM((17, TILE, 256), F32),) if group == LAST else ()),
-            flops=0,
-            moved=0,
+            scratch=(pltpu.VMEM((4 * len(blocks), TILE, 256), BF16),)
+            + ((pltpu.VMEM((17, TILE, 256), F32),) if end == len(ORDER) else ()),
         )
 
     running = jax.ShapeDtypeStruct((17, TILE, 256), F32)
-    last = (
-        one,
-        jax.ShapeDtypeStruct((3, shard, 256), F32),
-        jax.ShapeDtypeStruct((4, shard, 256), BF16),
-    )
-    def add_terms(mine, other):
-        return call(add_terms_body, "add_terms", half, (mine, other), moved=2**18)
-
-    first = swap_z(grad, 1)
     terms, sent = call(
         terms_body,
         "weight_terms",
@@ -374,33 +382,41 @@
         flops=4 * 256**3,
         moved=2**20,
     )
-    terms = add_terms(terms, to_core(sent))
-    terms, first = barrier((terms, first))
-    pair_d = jnp.stack([grad, first])
-    pair, over, near = swap_z(pair_d, -1), swap_z(pair_d, -1, 1), to_x(pair_d)
-    moved_terms = to_x(terms)
+    message = shape(656, BF16)
+    own_grad = call(
+        pack_own_body, "pack_own", shape(400, BF16), (grad, terms, to_core(sent)), moved=2**19
+    )
+    first = swap_z(own_grad, 1)
+    pair_d = call(pack_pair_body, "pack_pair", message, (own_grad, first), moved=2**20)
+    pair_c, over_d = swap_z(pair_d, -1), to_x(pair_d[:512])
     total = backward(0, (pair_d,), (), running)
-    pair, over, total, moved_terms = barrier((pair, over, total, moved_terms))
-    blocks = (pair, over, near)
-    for group, way, bit in ((1, 1, 1), (2, -1, 2)):
-        next_pair, over = swap_z(pair, way), swap_z(pair, way, 1)
-        terms = add_terms(terms, moved_terms)
-        terms, blocks, total = barrier((terms, blocks, total))
-        moved_terms = flip_z(terms, bit)
-        total = backward(group, blocks, (total,), running)
-        pair, over, total, moved_terms = barrier((next_pair, over, total, moved_terms))
-        blocks = (pair, over)
-    terms = add_terms(terms, moved_terms)
-    terms, blocks, total = barrier((terms, blocks, total))
-    moved_terms = flip_z(terms, 4)
-    own, kept, over = backward(LAST, blocks, (total,), last)
-    terms = add_terms(terms, moved_terms)
+    pair_c, over_d, total = barrier((pair_c, over_d, total))
+    pair_b, over_c = swap_z(pair_c, 1), to_x(pair_c[:512])
+    total = backward(1, (pair_c, over_d), (total,), running)
+    pair_b, over_c, total = barrier((pair_b, over_c, total))
+    far = call(pack_far_body, "pack_far", message, (pair_c, pair_b), moved=2**20)
+    pair_b, far = barrier((pair_b, far))
+    side, pair_a, near = swap_z(far, -1, 1), swap_z(pair_b, -1), to_x(far)
+    total = backward(3, (pair_b, over_c), (total,), running)
+    pair_a, near, total = barrier((pair_a, near, total))
+    total = backward(5, (near, pair_a), (total,), running)
+    side, total = barrier((side, total))
+    own, kept, over = backward(
+        7,
+        (side,),
+        (total,),
+        (
+            one,
+            jax.ShapeDtypeStruct((3, shard, 256), F32),
+            jax.ShapeDtypeStruct((4, shard, 256), BF16),
+        ),
+    )
     over = to_core(over)
-    sends = call(
+    *sends, terms = call(
         back_relay_body,
         "back_relay",
-        (shape(400, BF16),) * 3,
-        (kept, over, terms),
+        (*[shape(400, BF16)] * 3, half),
+        (kept, over, pair_d, pair_a, far, side, near),
         moved=2 * 2**20,
     )
     got = [to_y(a, s) for a, s in zip(sends, (1, 2, 3))]

time: 135 us -> 129 us (0.956)
  starting transfers between devices: 69.3 us -> 52.2 us
  waiting for transfers between devices: 46.2 us -> 53.9 us
  Pallas kernels: 13.6 us -> 17.2 us
    ppermute x3 -> x6, waiting for transfers between devices: 11.6 us -> 31.7 us  [to_x(): return lax.ppermute(a, 'col', [(i, i ^ 1) for i in range(2 * NZ)])]
    ppermute x14 -> x10, starting transfers between devices: 41.7 us -> 25.3 us  [swap_z(): return lax.ppermute(a, ('row', 'col'), pairs)]
    ppermute x3 -> x0, waiting for transfers between devices: 13.1 us -> none  [flip_z(): return lax.ppermute(a, 'col', [(i, i ^ 2 * bit) for i in range(2 * NZ)])]
    pallas_call x24 -> x23, Pallas kernels: 13.6 us -> 17.2 us  [call(): pl.pallas_call(body, name=name, out_shape=out_shape, in_specs=specs or [s...]
    ppermute x3 -> x0, starting transfers between devices: 3.29 us -> none  [flip_z(): return lax.ppermute(a, 'col', [(i, i ^ 2 * bit) for i in range(2 * NZ)])]
    ppermute x6, starting transfers between devices: 10.5 us -> 12.6 us  [to_y(): lax.ppermute(a, 'row', [(i, (i + 2 * step) % (2 * NY)) for i in range(2 *...]
    ppermute x3 -> x6, starting transfers between devices: 5.04 us -> 6.71 us  [to_x(): return lax.ppermute(a, 'col', [(i, i ^ 1) for i in range(2 * NZ)])]
    ppermute x14 -> x10, waiting for transfers between devices: 10.5 us -> 11.1 us  [swap_z(): return lax.ppermute(a, ('row', 'col'), pairs)]
  transfers between devices with their start and end apart: 33 -> 29, of which waited for: 20 -> 19; matrix products, arithmetic and copies ran while one was open for 1% -> 1% of each run, Pallas kernels for 7% -> 9%
where the time goes in v6:
time: 129 us
  waiting for transfers between devices  53.9 us (42%)
  starting transfers between devices  52.2 us (40%)
  Pallas kernels  17.2 us (13%)
  local copies, waits for them, and re-layouts  2.85 us (2%)
  between operations  1.55 us (1%)
  other arithmetic  1.34 us (1%)
    ppermute x6, waiting for transfers between devices, to_x(): return lax.ppermute(a, 'col', [(i, i ^ 1) for i in range(2 * NZ)])  31.7 us
    ppermute x10, starting transfers between devices, swap_z(): return lax.ppermute(a, ('row', 'col'), pairs)  25.3 us
    pallas_call x23, Pallas kernels, call(): pl.pallas_call(body, name=name, out_shape=out_shape, in_specs=specs or [s...  17.2 us
    ppermute x6, starting transfers between devices, to_y(): lax.ppermute(a, 'row', [(i, (i + 2 * step) % (2 * NY)) for i in range(2 *...  12.6 us
    ppermute x10, waiting for transfers between devices, swap_z(): return lax.ppermute(a, ('row', 'col'), pairs)  11.1 us
    ppermute x7, starting transfers between devices, to_core(): return lax.ppermute(a, 'row', [(i, i ^ 1) for i in range(2 * NY)])  7.63 us
    ppermute x6, waiting for transfers between devices, to_y(): lax.ppermute(a, 'row', [(i, (i + 2 * step) % (2 * NY)) for i in range(2 *...  7.48 us
    ppermute x6, starting transfers between devices, to_x(): return lax.ppermute(a, 'col', [(i, i ^ 1) for i in range(2 * NZ)])  6.71 us
  transfers between devices with their start and end apart: 29, of which 19 were waited for; matrix products, arithmetic and copies ran while one was open for 1% of the time, Pallas kernels for 9%

profile of v6, /device:TPU:1, one launch (start us, length us, event | category | flops | bytes accessed | tf_op | source)
XLA Modules:
  0.0 129.0 jit_solution(6608086384280338257)
XLA Ops:
  0.6 3.8 %collective-permute-start.2 = (bf16[256,256]{1,0:T(8,128)(2,1)}, bf16[256,256]{1,0:T(8,128)(2,1)S(1)}, u32[]{:S(2)}, u32[]{:S(2)}) collective-permute-start(bf16[256,256]{1,0:T(8,128)(2,1)} %refs_0_.1), channel_id=1, source_target_pairs={{0,128},{32,160},{64,192},{96,224},{128,0},{160,32},{192,64},{224,... | collective-permute-start | bytes 393224 | tf_op jit(solution)/shard_map/ppermute | solution.py:60
  9.2 2.8 %copy-done = bf16[1,1,192,128,128]{4,3,2,1,0:T(8,128)(2,1)S(1)} copy-done((bf16[1,1,192,128,128]{4,3,2,1,0:T(8,128)(2,1)S(1)}, bf16[1,1,192,128,128]{4,3,2,1,0:T(8,128)(2,1)}, u32[]{:S(2)}) %copy-start) | copy-done | bytes 6291480
  17.6 2.6 %collective-permute-start.8 = (bf16[2,256,256]{2,1,0:T(8,128)(2,1)S(1)}, bf16[2,256,256]{2,1,0:T(8,128)(2,1)S(1)}, u32[]{:S(2)}, u32[]{:S(2)}) collective-permute-start(bf16[2,256,256]{2,1,0:T(8,128)(2,1)S(1)} %get-tuple-element.69), channel_id=1, source_target_pairs={{0,30},{2,28},{4,10},{6,8},{8,6},{10,4},{12,18},{14,16},{16,14},{1... | collective-permute-start | bytes 786440 | tf_op jit(solution)/shard_map/ppermute | solution.py:75
  20.2 2.1 %forward_3.1 = (f32[2,256,256]{2,1,0:T(8,128)S(1)}, bf16[2,256,256]{2,1,0:T(8,128)(2,1)S(1)}, bf16[2,256,256]{2,1,0:T(8,128)(2,1)S(1)}) custom-call(s32[16]{0:T(128)S(1)} %convert_reduce_fusion.1.starts, s32[192]{0:T(256)S(1)} %get-tuple-element.57.order, s32[192]{0:T(256)S(1)} %get-tuple-element.58.rows, s32[192]{0:T(256)S(1)} %get-tuple-element.59.cols, ...), custom_call_target="tpu_custom_call" | custom-call | tf_op jit(solution)/shard_map/forward_3/pallas_call | solution.py:43
  22.5 2.9 %collective-permute-start.11 = (bf16[2,256,256]{2,1,0:T(8,128)(2,1)S(1)}, bf16[2,256,256]{2,1,0:T(8,128)(2,1)S(1)}, u32[]{:S(2)}, u32[]{:S(2)}) collective-permute-start(bf16[2,256,256]{2,1,0:T(8,128)(2,1)S(1)} %get-tuple-element.74), channel_id=1, source_target_pairs={{0,2},{2,0},{4,6},{6,4},{8,10},{10,8},{12,14},{14,12},{16,18},{18,... | collective-permute-start | bytes 786440 | tf_op jit(solution)/shard_map/ppermute | solution.py:64
  26.7 6.6 %collective-permute-done.9.rest_2_ = bf16[2,256,256]{2,1,0:T(8,128)(2,1)S(1)} collective-permute-done((bf16[2,256,256]{2,1,0:T(8,128)(2,1)S(1)}, bf16[2,256,256]{2,1,0:T(8,128)(2,1)S(1)}, u32[]{:S(2)}, u32[]{:S(2)}) %collective-permute-start.9) | collective-permute-done | bytes 262176 | tf_op jit(solution)/shard_map/ppermute | solution.py:64
  33.4 7.5 %collective-permute-start.10 = (bf16[2,256,256]{2,1,0:T(8,128)(2,1)S(1)}, bf16[2,256,256]{2,1,0:T(8,128)(2,1)S(1)}, u32[]{:S(2)}, u32[]{:S(2)}) collective-permute-start(bf16[2,256,256]{2,1,0:T(8,128)(2,1)S(1)} %relay_b.1), channel_id=1, source_target_pairs={{0,4},{2,6},{4,0},{6,2},{8,12},{10,14},{12,8},{14,10},{16,20},{18,... | collective-permute-start | bytes 786440 | tf_op jit(solution)/shard_map/ppermute | solution.py:75
  43.2 1.8 %collective-permute-done.10.rest_0_ = bf16[2,256,256]{2,1,0:T(8,128)(2,1)S(1)} collective-permute-done((bf16[2,256,256]{2,1,0:T(8,128)(2,1)S(1)}, bf16[2,256,256]{2,1,0:T(8,128)(2,1)S(1)}, u32[]{:S(2)}, u32[]{:S(2)}) %collective-permute-start.10) | collective-permute-done | bytes 262176 | tf_op jit(solution)/shard_map/ppermute | solution.py:75
  46.3 2.6 %collective-permute-done.12.over = bf16[2,256,256]{2,1,0:T(8,128)(2,1)S(1)} collective-permute-done((bf16[2,256,256]{2,1,0:T(8,128)(2,1)S(1)}, bf16[2,256,256]{2,1,0:T(8,128)(2,1)S(1)}, u32[]{:S(2)}, u32[]{:S(2)}) %collective-permute-start.12) | collective-permute-done | bytes 262176 | tf_op jit(solution)/shard_map/ppermute | solution.py:64
  48.9 1.8 %collective-permute-done.13.got = bf16[2,256,256]{2,1,0:T(8,128)(2,1)S(1)} collective-permute-done((bf16[2,256,256]{2,1,0:T(8,128)(2,1)S(1)}, bf16[2,256,256]{2,1,0:T(8,128)(2,1)S(1)}, u32[]{:S(2)}, u32[]{:S(2)}) %collective-permute-start.13) | collective-permute-done | bytes 262176 | tf_op jit(solution)/shard_map/ppermute | solution.py:75
  50.7 2.6 %collective-permute-start.14 = (bf16[256,256]{1,0:T(8,128)(2,1)S(1)}, bf16[256,256]{1,0:T(8,128)(2,1)S(1)}, u32[]{:S(2)}, u32[]{:S(2)}) collective-permute-start(bf16[256,256]{1,0:T(8,128)(2,1)S(1)} %get-tuple-element.79), channel_id=1, source_target_pairs={{0,4},{2,6},{4,0},{6,2},{8,12},{10,14},{12,8},{14,10},{16,20},{18,... | collective-permute-start | bytes 393224 | tf_op jit(solution)/shard_map/ppermute | solution.py:75
  53.4 2.7 %collective-permute-done.14.got = bf16[256,256]{1,0:T(8,128)(2,1)S(1)} collective-permute-done((bf16[256,256]{1,0:T(8,128)(2,1)S(1)}, bf16[256,256]{1,0:T(8,128)(2,1)S(1)}, u32[]{:S(2)}, u32[]{:S(2)}) %collective-permute-start.14) | collective-permute-done | bytes 131104 | tf_op jit(solution)/shard_map/ppermute | solution.py:75
  57.3 2.0 %collective-permute-start.15 = (bf16[144,256]{1,0:T(8,128)(2,1)S(1)}, bf16[144,256]{1,0:T(8,128)(2,1)S(1)}, u32[]{:S(2)}, u32[]{:S(2)}) collective-permute-start(bf16[144,256]{1,0:T(8,128)(2,1)S(1)} %get-tuple-element.85), channel_id=1, source_target_pairs={{0,32},{32,0},{64,96},{96,64},{128,160},{160,128},{192,224},{224,1... | collective-permute-start | bytes 221192 | tf_op jit(solution)/shard_map/ppermute | solution.py:56
  60.3 3.0 %collective-permute-start.16 = (bf16[400,256]{1,0:T(8,128)(2,1)S(1)}, bf16[400,256]{1,0:T(8,128)(2,1)S(1)}, u32[]{:S(2)}, u32[]{:S(2)}) collective-permute-start(bf16[400,256]{1,0:T(8,128)(2,1)S(1)} %pack_own.1.own), channel_id=1, source_target_pairs={{0,4},{2,6},{4,0},{6,2},{8,12},{10,14},{12,8},{14,10},{16,20},{18,... | collective-permute-start | bytes 614408 | tf_op jit(solution)/shard_map/ppermute | solution.py:75
  63.3 3.1 %collective-permute-done.16.got = bf16[400,256]{1,0:T(8,128)(2,1)S(1)} collective-permute-done((bf16[400,256]{1,0:T(8,128)(2,1)S(1)}, bf16[400,256]{1,0:T(8,128)(2,1)S(1)}, u32[]{:S(2)}, u32[]{:S(2)}) %collective-permute-start.16) | collective-permute-done | bytes 204832 | tf_op jit(solution)/shard_map/ppermute | solution.py:75
  69.3 4.2 %collective-permute-done.18.rest_1_ = bf16[512,256]{1,0:T(8,128)(2,1)S(1)} collective-permute-done((bf16[512,256]{1,0:T(8,128)(2,1)S(1)}, bf16[512,256]{1,0:T(8,128)(2,1)S(1)}, u32[]{:S(2)}, u32[]{:S(2)}) %collective-permute-start.18) | collective-permute-done | bytes 262176 | tf_op jit(solution)/shard_map/ppermute | solution.py:64
  73.4 5.1 %collective-permute-start.19 = (bf16[656,256]{1,0:T(8,128)(2,1)S(1)}, bf16[656,256]{1,0:T(8,128)(2,1)S(1)}, u32[]{:S(2)}, u32[]{:S(2)}) collective-permute-start(bf16[656,256]{1,0:T(8,128)(2,1)S(1)} %collective-permute-done.17.rest_0_.before), channel_id=1, source_target_pairs={{0,4},{2,6},{4,0},{6,2},{8,12},{10,14},{12,8},{14,10},{16,20},{18,... | collective-permute-start | bytes 1007624 | tf_op jit(solution)/shard_map/ppermute | solution.py:75
  80.3 7.6 %collective-permute-done.20.rest_1_ = bf16[512,256]{1,0:T(8,128)(2,1)S(1)} collective-permute-done((bf16[512,256]{1,0:T(8,128)(2,1)S(1)}, bf16[512,256]{1,0:T(8,128)(2,1)S(1)}, u32[]{:S(2)}, u32[]{:S(2)}) %collective-permute-start.20) | collective-permute-done | bytes 262176 | tf_op jit(solution)/shard_map/ppermute | solution.py:64
  88.6 3.5 %collective-permute-start.21 = (bf16[656,256]{1,0:T(8,128)(2,1)S(1)}, bf16[656,256]{1,0:T(8,128)(2,1)S(1)}, u32[]{:S(2)}, u32[]{:S(2)}) collective-permute-start(bf16[656,256]{1,0:T(8,128)(2,1)S(1)} %pack_far.1.far), channel_id=1, source_target_pairs={{0,30},{2,28},{4,10},{6,8},{8,6},{10,4},{12,18},{14,16},{16,14},{1... | collective-permute-start | bytes 1007624 | tf_op jit(solution)/shard_map/ppermute | solution.py:75
  92.1 1.7 %backward_3.1.rest_2_ = f32[17,128,256]{2,1,0:T(8,128)S(1)} custom-call(s32[16]{0:T(128)S(1)} %convert_reduce_fusion.1.starts, s32[192]{0:T(256)S(1)} %get-tuple-element.57.order, s32[192]{0:T(256)S(1)} %get-tuple-element.58.rows, s32[192]{0:T(256)S(1)} %get-tuple-element.59.cols, bf16[192,128,128]{2,1,0:T(8,128)(2,1)S(1)} %load_tiles.1.vals, ...), custom_call_target="tpu_custom_call" | custom-call | tf_op jit(solution)/shard_map/backward_3/pallas_call | solution.py:43
  94.3 10.8 %collective-permute-done.23.rest_0_.near = bf16[656,256]{1,0:T(8,128)(2,1)S(1)} collective-permute-done((bf16[656,256]{1,0:T(8,128)(2,1)S(1)}, bf16[656,256]{1,0:T(8,128)(2,1)S(1)}, u32[]{:S(2)}, u32[]{:S(2)}) %collective-permute-start.23) | collective-permute-done | bytes 335904 | tf_op jit(solution)/shard_map/ppermute | solution.py:64
  111.9 4.9 %collective-permute-start.26 = (bf16[400,256]{1,0:T(8,128)(2,1)S(1)}, bf16[400,256]{1,0:T(8,128)(2,1)S(1)}, u32[]{:S(2)}, u32[]{:S(2)}) collective-permute-start(bf16[400,256]{1,0:T(8,128)(2,1)S(1)} %get-tuple-element.103), channel_id=1, source_target_pairs={{0,128},{32,160},{64,192},{96,224},{128,0},{160,32},{192,64},{224,... | collective-permute-start | bytes 614408 | tf_op jit(solution)/shard_map/ppermute | solution.py:60
  116.8 2.0 %collective-permute-start.27 = (bf16[400,256]{1,0:T(8,128)(2,1)S(1)}, bf16[400,256]{1,0:T(8,128)(2,1)S(1)}, u32[]{:S(2)}, u32[]{:S(2)}) collective-permute-start(bf16[400,256]{1,0:T(8,128)(2,1)S(1)} %get-tuple-element.104), channel_id=1, source_target_pairs={{0,192},{32,224},{64,0},{96,32},{128,64},{160,96},{192,128},{224,1... | collective-permute-start | bytes 614408 | tf_op jit(solution)/shard_map/ppermute | solution.py:60
  119.1 7.2 %collective-permute-done.26.b = bf16[400,256]{1,0:T(8,128)(2,1)S(1)} collective-permute-done((bf16[400,256]{1,0:T(8,128)(2,1)S(1)}, bf16[400,256]{1,0:T(8,128)(2,1)S(1)}, u32[]{:S(2)}, u32[]{:S(2)}) %collective-permute-start.26) | collective-permute-done | bytes 204832 | tf_op jit(solution)/shard_map/ppermute | solution.py:60
  (75 shorter events, 32.7 us)
Async XLA Ops:
  0.6 12.1 %collective-permute-start.2 = (bf16[256,256]{1,0:T(8,128)(2,1)}, bf16[256,256]{1,0:T(8,128)(2,1)S(1)}, u32[]{:S(2)}, u32[]{:S(2)}) collective-permute-start(bf16[256,256]{1,0:T(8,128)(2,1)} %refs_0_.1), channel_id=1, source_target_pairs={{0,128},{32,160},{64,192},{96,224},{128,0},{160,32},{192,64},{224,... | collective-permute-start | bytes 393224 | tf_op jit(solution)/shard_map/ppermute | solution.py:60
  4.5 8.2 %collective-permute-start.1 = (bf16[256,256]{1,0:T(8,128)(2,1)}, bf16[256,256]{1,0:T(8,128)(2,1)S(1)}, u32[]{:S(2)}, u32[]{:S(2)}) collective-permute-start(bf16[256,256]{1,0:T(8,128)(2,1)} %refs_0_.1), channel_id=1, source_target_pairs={{0,192},{32,224},{64,0},{96,32},{128,64},{160,96},{192,128},{224,1... | collective-permute-start | bytes 393224 | tf_op jit(solution)/shard_map/ppermute | solution.py:60
  5.2 7.5 %collective-permute-start = (bf16[256,256]{1,0:T(8,128)(2,1)}, bf16[256,256]{1,0:T(8,128)(2,1)S(1)}, u32[]{:S(2)}, u32[]{:S(2)}) collective-permute-start(bf16[256,256]{1,0:T(8,128)(2,1)} %refs_0_.1), channel_id=1, source_target_pairs={{0,64},{32,96},{64,128},{96,160},{128,192},{160,224},{192,0},{224,... | collective-permute-start | bytes 393224 | tf_op jit(solution)/shard_map/ppermute | solution.py:60
  5.9 8.3 %collective-permute-start.3 = (bf16[256,256]{1,0:T(8,128)(2,1)}, bf16[256,256]{1,0:T(8,128)(2,1)S(1)}, u32[]{:S(2)}, u32[]{:S(2)}) collective-permute-start(bf16[256,256]{1,0:T(8,128)(2,1)} %refs_0_.1), channel_id=1, source_target_pairs={{0,32},{32,0},{64,96},{96,64},{128,160},{160,128},{192,224},{224,1... | collective-permute-start | bytes 393224 | tf_op jit(solution)/shard_map/ppermute | solution.py:56
  16.9 8.4 %collective-permute-start.7 = (bf16[2,256,256]{2,1,0:T(8,128)(2,1)S(1)}, bf16[2,256,256]{2,1,0:T(8,128)(2,1)S(1)}, u32[]{:S(2)}, u32[]{:S(2)}) collective-permute-start(bf16[2,256,256]{2,1,0:T(8,128)(2,1)S(1)} %get-tuple-element.68), channel_id=1, source_target_pairs={{0,28},{2,30},{4,8},{6,10},{8,4},{10,6},{12,16},{14,18},{16,12},{1... | collective-permute-start | bytes 786440 | tf_op jit(solution)/shard_map/ppermute | solution.py:75
  17.6 9.1 %collective-permute-start.8 = (bf16[2,256,256]{2,1,0:T(8,128)(2,1)S(1)}, bf16[2,256,256]{2,1,0:T(8,128)(2,1)S(1)}, u32[]{:S(2)}, u32[]{:S(2)}) collective-permute-start(bf16[2,256,256]{2,1,0:T(8,128)(2,1)S(1)} %get-tuple-element.69), channel_id=1, source_target_pairs={{0,30},{2,28},{4,10},{6,8},{8,6},{10,4},{12,18},{14,16},{16,14},{1... | collective-permute-start | bytes 786440 | tf_op jit(solution)/shard_map/ppermute | solution.py:75
  22.3 11.0 %collective-permute-start.9 = (bf16[2,256,256]{2,1,0:T(8,128)(2,1)S(1)}, bf16[2,256,256]{2,1,0:T(8,128)(2,1)S(1)}, u32[]{:S(2)}, u32[]{:S(2)}) collective-permute-start(bf16[2,256,256]{2,1,0:T(8,128)(2,1)S(1)} %get-tuple-element.70), channel_id=1, source_target_pairs={{0,2},{2,0},{4,6},{6,4},{8,10},{10,8},{12,14},{14,12},{16,18},{18,... | collective-permute-start | bytes 786440 | tf_op jit(solution)/shard_map/ppermute | solution.py:64
  22.5 20.7 %collective-permute-start.11 = (bf16[2,256,256]{2,1,0:T(8,128)(2,1)S(1)}, bf16[2,256,256]{2,1,0:T(8,128)(2,1)S(1)}, u32[]{:S(2)}, u32[]{:S(2)}) collective-permute-start(bf16[2,256,256]{2,1,0:T(8,128)(2,1)S(1)} %get-tuple-element.74), channel_id=1, source_target_pairs={{0,2},{2,0},{4,6},{6,4},{8,10},{10,8},{12,14},{14,12},{16,18},{18,... | collective-permute-start | bytes 786440 | tf_op jit(solution)/shard_map/ppermute | solution.py:64
  33.4 11.6 %collective-permute-start.10 = (bf16[2,256,256]{2,1,0:T(8,128)(2,1)S(1)}, bf16[2,256,256]{2,1,0:T(8,128)(2,1)S(1)}, u32[]{:S(2)}, u32[]{:S(2)}) collective-permute-start(bf16[2,256,256]{2,1,0:T(8,128)(2,1)S(1)} %relay_b.1), channel_id=1, source_target_pairs={{0,4},{2,6},{4,0},{6,2},{8,12},{10,14},{12,8},{14,10},{16,20},{18,... | collective-permute-start | bytes 786440 | tf_op jit(solution)/shard_map/ppermute | solution.py:75
  42.1 6.8 %collective-permute-start.12 = (bf16[2,256,256]{2,1,0:T(8,128)(2,1)S(1)}, bf16[2,256,256]{2,1,0:T(8,128)(2,1)S(1)}, u32[]{:S(2)}, u32[]{:S(2)}) collective-permute-start(bf16[2,256,256]{2,1,0:T(8,128)(2,1)S(1)} %get-tuple-element.76), channel_id=1, source_target_pairs={{0,2},{2,0},{4,6},{6,4},{8,10},{10,8},{12,14},{14,12},{16,18},{18,... | collective-permute-start | bytes 786440 | tf_op jit(solution)/shard_map/ppermute | solution.py:64
  45.1 5.6 %collective-permute-start.13 = (bf16[2,256,256]{2,1,0:T(8,128)(2,1)S(1)}, bf16[2,256,256]{2,1,0:T(8,128)(2,1)S(1)}, u32[]{:S(2)}, u32[]{:S(2)}) collective-permute-start(bf16[2,256,256]{2,1,0:T(8,128)(2,1)S(1)} %relay_c.1), channel_id=1, source_target_pairs={{0,28},{2,30},{4,8},{6,10},{8,4},{10,6},{12,16},{14,18},{16,12},{1... | collective-permute-start | bytes 786440 | tf_op jit(solution)/shard_map/ppermute | solution.py:75
  50.7 5.3 %collective-permute-start.14 = (bf16[256,256]{1,0:T(8,128)(2,1)S(1)}, bf16[256,256]{1,0:T(8,128)(2,1)S(1)}, u32[]{:S(2)}, u32[]{:S(2)}) collective-permute-start(bf16[256,256]{1,0:T(8,128)(2,1)S(1)} %get-tuple-element.79), channel_id=1, source_target_pairs={{0,4},{2,6},{4,0},{6,2},{8,12},{10,14},{12,8},{14,10},{16,20},{18,... | collective-permute-start | bytes 393224 | tf_op jit(solution)/shard_map/ppermute | solution.py:75
  60.3 6.2 %collective-permute-start.16 = (bf16[400,256]{1,0:T(8,128)(2,1)S(1)}, bf16[400,256]{1,0:T(8,128)(2,1)S(1)}, u32[]{:S(2)}, u32[]{:S(2)}) collective-permute-start(bf16[400,256]{1,0:T(8,128)(2,1)S(1)} %pack_own.1.own), channel_id=1, source_target_pairs={{0,4},{2,6},{4,0},{6,2},{8,12},{10,14},{12,8},{14,10},{16,20},{18,... | collective-permute-start | bytes 614408 | tf_op jit(solution)/shard_map/ppermute | solution.py:75
  66.5 6.9 %collective-permute-start.17 = (bf16[656,256]{1,0:T(8,128)(2,1)S(1)}, bf16[656,256]{1,0:T(8,128)(2,1)S(1)}, u32[]{:S(2)}, u32[]{:S(2)}) collective-permute-start(bf16[656,256]{1,0:T(8,128)(2,1)S(1)} %pack_pair.1.rest_0_.pair), channel_id=1, source_target_pairs={{0,28},{2,30},{4,8},{6,10},{8,4},{10,6},{12,16},{14,18},{16,12},{1... | collective-permute-start | bytes 1007624 | tf_op jit(solution)/shard_map/ppermute | solution.py:75
  66.6 6.8 %collective-permute-start.18 = (bf16[512,256]{1,0:T(8,128)(2,1)S(1)}, bf16[512,256]{1,0:T(8,128)(2,1)S(1)}, u32[]{:S(2)}, u32[]{:S(2)}) collective-permute-start(bf16[512,256]{1,0:T(8,128)(2,1)S(1)} %slice.8), channel_id=1, source_target_pairs={{0,2},{2,0},{4,6},{6,4},{8,10},{10,8},{12,14},{14,12},{16,18},{18,... | collective-permute-start | bytes 786440 | tf_op jit(solution)/shard_map/ppermute | solution.py:64
  73.4 14.4 %collective-permute-start.19 = (bf16[656,256]{1,0:T(8,128)(2,1)S(1)}, bf16[656,256]{1,0:T(8,128)(2,1)S(1)}, u32[]{:S(2)}, u32[]{:S(2)}) collective-permute-start(bf16[656,256]{1,0:T(8,128)(2,1)S(1)} %collective-permute-done.17.rest_0_.before), channel_id=1, source_target_pairs={{0,4},{2,6},{4,0},{6,2},{8,12},{10,14},{12,8},{14,10},{16,20},{18,... | collective-permute-start | bytes 1007624 | tf_op jit(solution)/shard_map/ppermute | solution.py:75
  78.5 9.3 %collective-permute-start.20 = (bf16[512,256]{1,0:T(8,128)(2,1)S(1)}, bf16[512,256]{1,0:T(8,128)(2,1)S(1)}, u32[]{:S(2)}, u32[]{:S(2)}) collective-permute-start(bf16[512,256]{1,0:T(8,128)(2,1)S(1)} %slice.7), channel_id=1, source_target_pairs={{0,2},{2,0},{4,6},{6,4},{8,10},{10,8},{12,14},{14,12},{16,18},{18,... | collective-permute-start | bytes 786440 | tf_op jit(solution)/shard_map/ppermute | solution.py:64
  87.9 6.4 %collective-permute-start.22 = (bf16[656,256]{1,0:T(8,128)(2,1)S(1)}, bf16[656,256]{1,0:T(8,128)(2,1)S(1)}, u32[]{:S(2)}, u32[]{:S(2)}) collective-permute-start(bf16[656,256]{1,0:T(8,128)(2,1)S(1)} %collective-permute-done.19.got.rest_0_), channel_id=1, source_target_pairs={{0,28},{2,30},{4,8},{6,10},{8,4},{10,6},{12,16},{14,18},{16,12},{1... | collective-permute-start | bytes 1007624 | tf_op jit(solution)/shard_map/ppermute | solution.py:75
  88.0 17.1 %collective-permute-start.23 = (bf16[656,256]{1,0:T(8,128)(2,1)S(1)}, bf16[656,256]{1,0:T(8,128)(2,1)S(1)}, u32[]{:S(2)}, u32[]{:S(2)}) collective-permute-start(bf16[656,256]{1,0:T(8,128)(2,1)S(1)} %pack_far.1.far), channel_id=1, source_target_pairs={{0,2},{2,0},{4,6},{6,4},{8,10},{10,8},{12,14},{14,12},{16,18},{18,... | collective-permute-start | bytes 1007624 | tf_op jit(solution)/shard_map/ppermute | solution.py:64
  88.6 18.2 %collective-permute-start.21 = (bf16[656,256]{1,0:T(8,128)(2,1)S(1)}, bf16[656,256]{1,0:T(8,128)(2,1)S(1)}, u32[]{:S(2)}, u32[]{:S(2)}) collective-permute-start(bf16[656,256]{1,0:T(8,128)(2,1)S(1)} %pack_far.1.far), channel_id=1, source_target_pairs={{0,30},{2,28},{4,10},{6,8},{8,6},{10,4},{12,18},{14,16},{16,14},{1... | collective-permute-start | bytes 1007624 | tf_op jit(solution)/shard_map/ppermute | solution.py:75
  108.2 3.1 %collective-permute-start.24 = (bf16[4,256,256]{2,1,0:T(8,128)(2,1)S(1)}, bf16[4,256,256]{2,1,0:T(8,128)(2,1)S(1)}, u32[]{:S(2)}, u32[]{:S(2)}) collective-permute-start(bf16[4,256,256]{2,1,0:T(8,128)(2,1)S(1)} %get-tuple-element.100), channel_id=1, source_target_pairs={{0,32},{32,0},{64,96},{96,64},{128,160},{160,128},{192,224},{224,1... | collective-permute-start | bytes 1572872 | tf_op jit(solution)/shard_map/ppermute | solution.py:56
  111.5 7.6 %collective-permute-start.25 = (bf16[400,256]{1,0:T(8,128)(2,1)S(1)}, bf16[400,256]{1,0:T(8,128)(2,1)S(1)}, u32[]{:S(2)}, u32[]{:S(2)}) collective-permute-start(bf16[400,256]{1,0:T(8,128)(2,1)S(1)} %get-tuple-element.102), channel_id=1, source_target_pairs={{0,64},{32,96},{64,128},{96,160},{128,192},{160,224},{192,0},{224,... | collective-permute-start | bytes 614408 | tf_op jit(solution)/shard_map/ppermute | solution.py:60
  111.9 14.4 %collective-permute-start.26 = (bf16[400,256]{1,0:T(8,128)(2,1)S(1)}, bf16[400,256]{1,0:T(8,128)(2,1)S(1)}, u32[]{:S(2)}, u32[]{:S(2)}) collective-permute-start(bf16[400,256]{1,0:T(8,128)(2,1)S(1)} %get-tuple-element.103), channel_id=1, source_target_pairs={{0,128},{32,160},{64,192},{96,224},{128,0},{160,32},{192,64},{224,... | collective-permute-start | bytes 614408 | tf_op jit(solution)/shard_map/ppermute | solution.py:60
  116.8 9.4 %collective-permute-start.27 = (bf16[400,256]{1,0:T(8,128)(2,1)S(1)}, bf16[400,256]{1,0:T(8,128)(2,1)S(1)}, u32[]{:S(2)}, u32[]{:S(2)}) collective-permute-start(bf16[400,256]{1,0:T(8,128)(2,1)S(1)} %get-tuple-element.104), channel_id=1, source_target_pairs={{0,192},{32,224},{64,0},{96,32},{128,64},{160,96},{192,128},{224,1... | collective-permute-start | bytes 614408 | tf_op jit(solution)/shard_map/ppermute | solution.py:60
  (10 other events, 48.8 us)

commit v7 on v6

--- a/solution.py
+++ b/solution.py
@@ -15,8 +15,8 @@
     ((7, 0), (6, 0)),
     ((0, 1), (1, 1)),
     ((2, 0), (3, 0)),
+    ((2, 1), (3, 1)),
     ((7, 1), (6, 1)),
-    ((2, 1), (3, 1)),
     ((5, 0), (4, 0)),
     ((5, 1), (4, 1)),
 )
@@ -122,13 +122,20 @@
         total,
         size,
     )
-    for k, out in enumerate(outs):
-        for n in range(2):
-            place(out.at[n], total, 2 * k + n, out.dtype)
+    first = 0
+    for out in outs:
+        for n in range(out.shape[0]):
+            place(out.at[n], total, first + n, out.dtype)
+        first += out.shape[0]
 
 
 def wide(ref):
     return ref[...].astype(F32)
+
+
+def relay_first_body(kept, side, got, out, out_side):
+    out[...] = (kept[...] + wide(got.at[0:2])).astype(BF16)
+    out_side[...] = (side[...] + wide(got.at[2:4])).astype(BF16)
 
 
 def relay_body(kept, *rest):
@@ -185,11 +192,6 @@
     out[0:256] = own[0:256]
     out[256:512] = got[0:256]
     out[512:656] = add_rows(own[256:400], got[256:400])
-
-
-def pack_far_body(before, got, out):
-    out[0:512] = got[0:512]
-    out[512:656] = add_rows(before[512:656], got[512:656])
 
 
 def backward_body(begin, end, starts, order, rows, cols, vals, *rest):
@@ -232,10 +234,10 @@
         place(over.at[3], total, 1, BF16)
 
 
-def back_relay_body(kept, over, pair, last, far, side, near, out_a, out_b, out_c, terms):
+def back_relay_body(kept, over, pd, pa, pc, pb, sd, sa, sc, sb, out_a, out_b, out_c, terms):
     sums = slice(512, 656)
-    plane = add_rows(pair[sums], last[sums]).astype(F32) + far[sums].astype(F32)
-    other = side[sums].astype(F32) + near[sums].astype(F32)
+    plane = add_rows(pd[sums], pa[sums]).astype(F32) + add_rows(pc[sums], pb[sums]).astype(F32)
+    other = add_rows(sd[sums], sa[sums]).astype(F32) + add_rows(sc[sums], sb[sums]).astype(F32)
     terms[...] = (plane + other).astype(BF16)
     for k, out in enumerate((out_a, out_b, out_c)):
         out[0:256] = (kept[k] + over[k].astype(F32)).astype(BF16)
@@ -334,21 +336,22 @@
         return call(body, name, outs, args, moved=2**20)
 
     barrier = lax.optimization_barrier
-    moving, far = forward(6, 8, (two16, two16), source)
-    moving, far, source = barrier((moving, far, source))
-    far, moving = swap_z(far, -1, 1), swap_z(moving, -1)
-    kept_b, over_c, over_b = forward(3, 6, (two, two16, two16), source)
-    over_b, over_c = to_x(over_b), to_x(over_c)
-    moving = relay(relay_body, "relay_b", two16, kept_b, moving, far, over_b)
+    (moving,) = forward(6, 8, (jax.ShapeDtypeStruct((4, shard, 256), BF16),), source)
     moving, source = barrier((moving, source))
-    moving = swap_z(moving, 1)
-    kept_c, over_d = forward(1, 3, (two, two16), source)
-    over_d = to_x(over_d)
-    moving = relay(relay_body, "relay_c", two16, kept_c, moving, over_c)
+    moving = swap_z(moving, -1)
+    kept_b, side_b, side_c = forward(3, 6, (two, two, two16), source)
+    side_c = swap_z(side_c, -1)
+    moving, side = relay(relay_first_body, "relay_b", (two16, two16), kept_b, side_b, moving)
+    moving, side, source = barrier((moving, side, source))
+    side, moving = swap_z(side, 1, 1), swap_z(moving, 1)
+    kept_c, side_d = forward(1, 3, (two, two), source)
+    side_d = relay(relay_body, "relay_side", two16, side_d, side_c)
+    side_d = to_x(side_d)
+    moving = relay(relay_body, "relay_c", two16, kept_c, moving, side)
     moving, source = barrier((moving, source))
     moving = swap_z(moving, -1)
     (kept_d,) = forward(0, 1, (two,), source)
-    own, moving = relay(relay_last_body, "relay_last", (one, one16), kept_d, over_d, moving)
+    own, moving = relay(relay_last_body, "relay_last", (one, one16), kept_d, side_d, moving)
     moving = swap_z(moving, 1)
     hidden_out, grad, high, low = call(
         activate_body,
@@ -388,22 +391,20 @@
     )
     first = swap_z(own_grad, 1)
     pair_d = call(pack_pair_body, "pack_pair", message, (own_grad, first), moved=2**20)
-    pair_c, over_d = swap_z(pair_d, -1), to_x(pair_d[:512])
+    pair_c, side_d = swap_z(pair_d, -1), to_x(pair_d)
     total = backward(0, (pair_d,), (), running)
-    pair_c, over_d, total = barrier((pair_c, over_d, total))
-    pair_b, over_c = swap_z(pair_c, 1), to_x(pair_c[:512])
-    total = backward(1, (pair_c, over_d), (total,), running)
-    pair_b, over_c, total = barrier((pair_b, over_c, total))
-    far = call(pack_far_body, "pack_far", message, (pair_c, pair_b), moved=2**20)
-    pair_b, far = barrier((pair_b, far))
-    side, pair_a, near = swap_z(far, -1, 1), swap_z(pair_b, -1), to_x(far)
-    total = backward(3, (pair_b, over_c), (total,), running)
-    pair_a, near, total = barrier((pair_a, near, total))
-    total = backward(5, (near, pair_a), (total,), running)
-    side, total = barrier((side, total))
+    pair_c, side_d, total = barrier((pair_c, side_d, total))
+    side_b, pair_b, side_c = swap_z(pair_c, 1, 1), swap_z(pair_c, 1), swap_z(side_d, -1)
+    total = backward(1, (pair_c, side_d), (total,), running)
+    pair_b, side_b, total = barrier((pair_b, side_b, total))
+    pair_a, side_a = swap_z(pair_b, -1), swap_z(side_b, -1)
+    total = backward(3, (pair_b, side_b), (total,), running)
+    pair_a, side_c, total = barrier((pair_a, side_c, total))
+    total = backward(5, (side_c, pair_a), (total,), running)
+    side_a, total = barrier((side_a, total))
     own, kept, over = backward(
         7,
-        (side,),
+        (side_a,),
         (total,),
         (
             one,
@@ -416,7 +417,7 @@
         back_relay_body,
         "back_relay",
         (*[shape(400, BF16)] * 3, half),
-        (kept, over, pair_d, pair_a, far, side, near),
+        (kept, over, pair_d, pair_a, pair_c, pair_b, side_d, side_a, side_c, side_b),
         moved=2 * 2**20,
     )
     got = [to_y(a, s) for a, s in zip(sends, (1, 2, 3))]

time: 129 us -> 123 us (0.953)
  starting transfers between devices: 52.2 us -> 46.4 us
  Pallas kernels: 17.2 us -> 15.3 us
  waiting for transfers between devices: 53.9 us -> 55.4 us
    ppermute x10 -> x13, waiting for transfers between devices: 11.1 us -> 37 us  [swap_z(): return lax.ppermute(a, ('row', 'col'), pairs)]
    ppermute x6 -> x2, waiting for transfers between devices: 31.7 us -> 7.08 us  [to_x(): return lax.ppermute(a, 'col', [(i, i ^ 1) for i in range(2 * NZ)])]
    ppermute x6 -> x2, starting transfers between devices: 6.71 us -> 1.47 us  [to_x(): return lax.ppermute(a, 'col', [(i, i ^ 1) for i in range(2 * NZ)])]
    ppermute x7, starting transfers between devices: 7.63 us -> 11.1 us  [to_core(): return lax.ppermute(a, 'row', [(i, i ^ 1) for i in range(2 * NY)])]
    ppermute x6, starting transfers between devices: 12.6 us -> 9.8 us  [to_y(): lax.ppermute(a, 'row', [(i, (i + 2 * step) % (2 * NY)) for i in range(2 *...]
    pallas_call x23, Pallas kernels: 17.2 us -> 15.3 us  [call(): pl.pallas_call(body, name=name, out_shape=out_shape, in_specs=specs or [s...]
    ppermute x10 -> x13, starting transfers between devices: 25.3 us -> 24.1 us  [swap_z(): return lax.ppermute(a, ('row', 'col'), pairs)]
  transfers between devices with their start and end apart: 29 -> 28, of which waited for: 19 -> 21; matrix products, arithmetic and copies ran while one was open for 1% -> 1% of each run, Pallas kernels for 9% -> 8%
where the time goes in v7:
time: 123 us
  waiting for transfers between devices  55.4 us (45%)
  starting transfers between devices  46.4 us (38%)
  Pallas kernels  15.3 us (12%)
  local copies, waits for them, and re-layouts  2.81 us (2%)
  between operations  1.54 us (1%)
  other arithmetic  1.34 us (1%)
    ppermute x13, waiting for transfers between devices, swap_z(): return lax.ppermute(a, ('row', 'col'), pairs)  37 us
    ppermute x13, starting transfers between devices, swap_z(): return lax.ppermute(a, ('row', 'col'), pairs)  24.1 us
    pallas_call x23, Pallas kernels, call(): pl.pallas_call(body, name=name, out_shape=out_shape, in_specs=specs or [s...  15.3 us
    ppermute x7, starting transfers between devices, to_core(): return lax.ppermute(a, 'row', [(i, i ^ 1) for i in range(2 * NY)])  11.1 us
    ppermute x6, starting transfers between devices, to_y(): lax.ppermute(a, 'row', [(i, (i + 2 * step) % (2 * NY)) for i in range(2 *...  9.8 us
    ppermute x6, waiting for transfers between devices, to_y(): lax.ppermute(a, 'row', [(i, (i + 2 * step) % (2 * NY)) for i in range(2 *...  7.75 us
    ppermute x2, waiting for transfers between devices, to_x(): return lax.ppermute(a, 'col', [(i, i ^ 1) for i in range(2 * NZ)])  7.08 us
    ppermute x7, waiting for transfers between devices, to_core(): return lax.ppermute(a, 'row', [(i, i ^ 1) for i in range(2 * NY)])  3.58 us
  transfers between devices with their start and end apart: 28, of which 21 were waited for; matrix products, arithmetic and copies ran while one was open for 1% of the time, Pallas kernels for 8%

profile of v7, /device:TPU:1, one launch (start us, length us, event | category | flops | bytes accessed | tf_op | source)
XLA Modules:
  0.0 122.8 jit_solution(17606439041640084202)
XLA Ops:
  0.6 2.2 %collective-permute-start = (bf16[256,256]{1,0:T(8,128)(2,1)}, bf16[256,256]{1,0:T(8,128)(2,1)S(1)}, u32[]{:S(2)}, u32[]{:S(2)}) collective-permute-start(bf16[256,256]{1,0:T(8,128)(2,1)} %refs_0_.1), channel_id=1, source_target_pairs={{0,64},{32,96},{64,128},{96,160},{128,192},{160,224},{192,0},{224,... | collective-permute-start | bytes 393224 | tf_op jit(solution)/shard_map/ppermute | solution.py:60
  9.2 2.8 %copy-done = bf16[1,1,192,128,128]{4,3,2,1,0:T(8,128)(2,1)S(1)} copy-done((bf16[1,1,192,128,128]{4,3,2,1,0:T(8,128)(2,1)S(1)}, bf16[1,1,192,128,128]{4,3,2,1,0:T(8,128)(2,1)}, u32[]{:S(2)}) %copy-start) | copy-done | bytes 6291480
  15.5 1.6 %forward_6.1 = bf16[4,256,256]{2,1,0:T(8,128)(2,1)S(1)} custom-call(s32[16]{0:T(128)S(1)} %convert_reduce_fusion.1.starts, s32[192]{0:T(256)S(1)} %get-tuple-element.55.order, s32[192]{0:T(256)S(1)} %get-tuple-element.56.rows, s32[192]{0:T(256)S(1)} %get-tuple-element.57.cols, bf16[192,128,128]{2,1,0:T(8,128)(2,1)S(1)} %load_tiles.1.vals, ...), custom_call_target="tpu_custom_call" | custom-call | tf_op jit(solution)/shard_map/forward_6/pallas_call | solution.py:43
  20.4 5.1 %collective-permute-done.7.got = bf16[4,256,256]{2,1,0:T(8,128)(2,1)S(1)} collective-permute-done((bf16[4,256,256]{2,1,0:T(8,128)(2,1)S(1)}, bf16[4,256,256]{2,1,0:T(8,128)(2,1)S(1)}, u32[]{:S(2)}, u32[]{:S(2)}) %collective-permute-start.7) | collective-permute-done | bytes 524320 | tf_op jit(solution)/shard_map/ppermute | solution.py:75
  25.6 4.9 %collective-permute-start.8 = (bf16[2,256,256]{2,1,0:T(8,128)(2,1)S(1)}, bf16[2,256,256]{2,1,0:T(8,128)(2,1)S(1)}, u32[]{:S(2)}, u32[]{:S(2)}) collective-permute-start(bf16[2,256,256]{2,1,0:T(8,128)(2,1)S(1)} %get-tuple-element.70), channel_id=1, source_target_pairs={{0,4},{2,6},{4,0},{6,2},{8,12},{10,14},{12,8},{14,10},{16,20},{18,... | collective-permute-start | bytes 786440 | tf_op jit(solution)/shard_map/ppermute | solution.py:75
  30.5 2.3 %collective-permute-start.9 = (bf16[2,256,256]{2,1,0:T(8,128)(2,1)S(1)}, bf16[2,256,256]{2,1,0:T(8,128)(2,1)S(1)}, u32[]{:S(2)}, u32[]{:S(2)}) collective-permute-start(bf16[2,256,256]{2,1,0:T(8,128)(2,1)S(1)} %get-tuple-element.71), channel_id=1, source_target_pairs={{0,6},{2,4},{4,2},{6,0},{8,14},{10,12},{12,10},{14,8},{16,22},{18,... | collective-permute-start | bytes 786440 | tf_op jit(solution)/shard_map/ppermute | solution.py:75
  34.5 6.4 %collective-permute-done.9.rest_1_ = bf16[2,256,256]{2,1,0:T(8,128)(2,1)S(1)} collective-permute-done((bf16[2,256,256]{2,1,0:T(8,128)(2,1)S(1)}, bf16[2,256,256]{2,1,0:T(8,128)(2,1)S(1)}, u32[]{:S(2)}, u32[]{:S(2)}) %collective-permute-start.9) | collective-permute-done | bytes 262176 | tf_op jit(solution)/shard_map/ppermute | solution.py:75
  42.2 5.8 %collective-permute-done.11.over = bf16[2,256,256]{2,1,0:T(8,128)(2,1)S(1)} collective-permute-done((bf16[2,256,256]{2,1,0:T(8,128)(2,1)S(1)}, bf16[2,256,256]{2,1,0:T(8,128)(2,1)S(1)}, u32[]{:S(2)}, u32[]{:S(2)}) %collective-permute-start.11) | collective-permute-done | bytes 262176 | tf_op jit(solution)/shard_map/ppermute | solution.py:64
  48.1 3.0 %collective-permute-start.13 = (bf16[256,256]{1,0:T(8,128)(2,1)S(1)}, bf16[256,256]{1,0:T(8,128)(2,1)S(1)}, u32[]{:S(2)}, u32[]{:S(2)}) collective-permute-start(bf16[256,256]{1,0:T(8,128)(2,1)S(1)} %get-tuple-element.77), channel_id=1, source_target_pairs={{0,4},{2,6},{4,0},{6,2},{8,12},{10,14},{12,8},{14,10},{16,20},{18,... | collective-permute-start | bytes 393224 | tf_op jit(solution)/shard_map/ppermute | solution.py:75
  51.1 2.4 %collective-permute-done.13.got = bf16[256,256]{1,0:T(8,128)(2,1)S(1)} collective-permute-done((bf16[256,256]{1,0:T(8,128)(2,1)S(1)}, bf16[256,256]{1,0:T(8,128)(2,1)S(1)}, u32[]{:S(2)}, u32[]{:S(2)}) %collective-permute-start.13) | collective-permute-done | bytes 131104 | tf_op jit(solution)/shard_map/ppermute | solution.py:75
  54.7 2.7 %collective-permute-start.14 = (bf16[144,256]{1,0:T(8,128)(2,1)S(1)}, bf16[144,256]{1,0:T(8,128)(2,1)S(1)}, u32[]{:S(2)}, u32[]{:S(2)}) collective-permute-start(bf16[144,256]{1,0:T(8,128)(2,1)S(1)} %get-tuple-element.83), channel_id=1, source_target_pairs={{0,32},{32,0},{64,96},{96,64},{128,160},{160,128},{192,224},{224,1... | collective-permute-start | bytes 221192 | tf_op jit(solution)/shard_map/ppermute | solution.py:56
  58.3 3.0 %collective-permute-start.15 = (bf16[400,256]{1,0:T(8,128)(2,1)S(1)}, bf16[400,256]{1,0:T(8,128)(2,1)S(1)}, u32[]{:S(2)}, u32[]{:S(2)}) collective-permute-start(bf16[400,256]{1,0:T(8,128)(2,1)S(1)} %pack_own.1.own), channel_id=1, source_target_pairs={{0,4},{2,6},{4,0},{6,2},{8,12},{10,14},{12,8},{14,10},{16,20},{18,... | collective-permute-start | bytes 614408 | tf_op jit(solution)/shard_map/ppermute | solution.py:75
  61.4 3.1 %collective-permute-done.15.got = bf16[400,256]{1,0:T(8,128)(2,1)S(1)} collective-permute-done((bf16[400,256]{1,0:T(8,128)(2,1)S(1)}, bf16[400,256]{1,0:T(8,128)(2,1)S(1)}, u32[]{:S(2)}, u32[]{:S(2)}) %collective-permute-start.15) | collective-permute-done | bytes 204832 | tf_op jit(solution)/shard_map/ppermute | solution.py:75
  67.2 3.8 %collective-permute-done.16.rest_0_.pc = bf16[656,256]{1,0:T(8,128)(2,1)S(1)} collective-permute-done((bf16[656,256]{1,0:T(8,128)(2,1)S(1)}, bf16[656,256]{1,0:T(8,128)(2,1)S(1)}, u32[]{:S(2)}, u32[]{:S(2)}) %collective-permute-start.16) | collective-permute-done | bytes 335904 | tf_op jit(solution)/shard_map/ppermute | solution.py:75
  72.3 5.8 %collective-permute-start.18 = (bf16[656,256]{1,0:T(8,128)(2,1)S(1)}, bf16[656,256]{1,0:T(8,128)(2,1)S(1)}, u32[]{:S(2)}, u32[]{:S(2)}) collective-permute-start(bf16[656,256]{1,0:T(8,128)(2,1)S(1)} %collective-permute-done.16.rest_0_.pc), channel_id=1, source_target_pairs={{0,4},{2,6},{4,0},{6,2},{8,12},{10,14},{12,8},{14,10},{16,20},{18,... | collective-permute-start | bytes 1007624 | tf_op jit(solution)/shard_map/ppermute | solution.py:75
  80.6 2.0 %collective-permute-done.18.rest_0_.pb = bf16[656,256]{1,0:T(8,128)(2,1)S(1)} collective-permute-done((bf16[656,256]{1,0:T(8,128)(2,1)S(1)}, bf16[656,256]{1,0:T(8,128)(2,1)S(1)}, u32[]{:S(2)}, u32[]{:S(2)}) %collective-permute-start.18) | collective-permute-done | bytes 335904 | tf_op jit(solution)/shard_map/ppermute | solution.py:75
  82.7 7.9 %collective-permute-done.19.rest_1_.sb = bf16[656,256]{1,0:T(8,128)(2,1)S(1)} collective-permute-done((bf16[656,256]{1,0:T(8,128)(2,1)S(1)}, bf16[656,256]{1,0:T(8,128)(2,1)S(1)}, u32[]{:S(2)}, u32[]{:S(2)}) %collective-permute-start.19) | collective-permute-done | bytes 335904 | tf_op jit(solution)/shard_map/ppermute | solution.py:75
  93.3 3.6 %collective-permute-done.21.rest_1_.pa = bf16[656,256]{1,0:T(8,128)(2,1)S(1)} collective-permute-done((bf16[656,256]{1,0:T(8,128)(2,1)S(1)}, bf16[656,256]{1,0:T(8,128)(2,1)S(1)}, u32[]{:S(2)}, u32[]{:S(2)}) %collective-permute-start.21) | collective-permute-done | bytes 335904 | tf_op jit(solution)/shard_map/ppermute | solution.py:75
  98.2 2.3 %collective-permute-done.20.rest_0_.sa = bf16[656,256]{1,0:T(8,128)(2,1)S(1)} collective-permute-done((bf16[656,256]{1,0:T(8,128)(2,1)S(1)}, bf16[656,256]{1,0:T(8,128)(2,1)S(1)}, u32[]{:S(2)}, u32[]{:S(2)}) %collective-permute-start.20) | collective-permute-done | bytes 335904 | tf_op jit(solution)/shard_map/ppermute | solution.py:75
  101.9 3.6 %collective-permute-start.23 = (bf16[4,256,256]{2,1,0:T(8,128)(2,1)S(1)}, bf16[4,256,256]{2,1,0:T(8,128)(2,1)S(1)}, u32[]{:S(2)}, u32[]{:S(2)}) collective-permute-start(bf16[4,256,256]{2,1,0:T(8,128)(2,1)S(1)} %get-tuple-element.96), channel_id=1, source_target_pairs={{0,32},{32,0},{64,96},{96,64},{128,160},{160,128},{192,224},{224,1... | collective-permute-start | bytes 1572872 | tf_op jit(solution)/shard_map/ppermute | solution.py:56
  107.2 2.0 %collective-permute-start.24 = (bf16[400,256]{1,0:T(8,128)(2,1)S(1)}, bf16[400,256]{1,0:T(8,128)(2,1)S(1)}, u32[]{:S(2)}, u32[]{:S(2)}) collective-permute-start(bf16[400,256]{1,0:T(8,128)(2,1)S(1)} %get-tuple-element.98), channel_id=1, source_target_pairs={{0,64},{32,96},{64,128},{96,160},{128,192},{160,224},{192,0},{224,... | collective-permute-start | bytes 614408 | tf_op jit(solution)/shard_map/ppermute | solution.py:60
  111.7 3.1 %collective-permute-done.24.a = bf16[400,256]{1,0:T(8,128)(2,1)S(1)} collective-permute-done((bf16[400,256]{1,0:T(8,128)(2,1)S(1)}, bf16[400,256]{1,0:T(8,128)(2,1)S(1)}, u32[]{:S(2)}, u32[]{:S(2)}) %collective-permute-start.24) | collective-permute-done | bytes 204832 | tf_op jit(solution)/shard_map/ppermute | solution.py:60
  114.8 4.6 %collective-permute-done.25.b = bf16[400,256]{1,0:T(8,128)(2,1)S(1)} collective-permute-done((bf16[400,256]{1,0:T(8,128)(2,1)S(1)}, bf16[400,256]{1,0:T(8,128)(2,1)S(1)}, u32[]{:S(2)}, u32[]{:S(2)}) %collective-permute-start.25) | collective-permute-done | bytes 204832 | tf_op jit(solution)/shard_map/ppermute | solution.py:60
  119.5 1.6 %collective-permute-start.27 = (f32[136,256]{1,0:T(8,128)S(1)}, f32[136,256]{1,0:T(8,128)S(1)}, u32[]{:S(2)}, u32[]{:S(2)}) collective-permute-start(f32[136,256]{1,0:T(8,128)S(1)} %sum_terms.1.mine), channel_id=1, source_target_pairs={{0,32},{32,0},{64,96},{96,64},{128,160},{160,128},{192,224},{224,1... | collective-permute-start | bytes 417800 | tf_op jit(solution)/shard_map/ppermute | solution.py:56
  (71 shorter events, 35.7 us)
Async XLA Ops:
  0.6 12.0 %collective-permute-start = (bf16[256,256]{1,0:T(8,128)(2,1)}, bf16[256,256]{1,0:T(8,128)(2,1)S(1)}, u32[]{:S(2)}, u32[]{:S(2)}) collective-permute-start(bf16[256,256]{1,0:T(8,128)(2,1)} %refs_0_.1), channel_id=1, source_target_pairs={{0,64},{32,96},{64,128},{96,160},{128,192},{160,224},{192,0},{224,... | collective-permute-start | bytes 393224 | tf_op jit(solution)/shard_map/ppermute | solution.py:60
  2.8 9.8 %collective-permute-start.1 = (bf16[256,256]{1,0:T(8,128)(2,1)}, bf16[256,256]{1,0:T(8,128)(2,1)S(1)}, u32[]{:S(2)}, u32[]{:S(2)}) collective-permute-start(bf16[256,256]{1,0:T(8,128)(2,1)} %refs_0_.1), channel_id=1, source_target_pairs={{0,192},{32,224},{64,0},{96,32},{128,64},{160,96},{192,128},{224,1... | collective-permute-start | bytes 393224 | tf_op jit(solution)/shard_map/ppermute | solution.py:60
  4.4 8.3 %collective-permute-start.2 = (bf16[256,256]{1,0:T(8,128)(2,1)}, bf16[256,256]{1,0:T(8,128)(2,1)S(1)}, u32[]{:S(2)}, u32[]{:S(2)}) collective-permute-start(bf16[256,256]{1,0:T(8,128)(2,1)} %refs_0_.1), channel_id=1, source_target_pairs={{0,128},{32,160},{64,192},{96,224},{128,0},{160,32},{192,64},{224,... | collective-permute-start | bytes 393224 | tf_op jit(solution)/shard_map/ppermute | solution.py:60
  5.9 8.5 %collective-permute-start.3 = (bf16[256,256]{1,0:T(8,128)(2,1)}, bf16[256,256]{1,0:T(8,128)(2,1)S(1)}, u32[]{:S(2)}, u32[]{:S(2)}) collective-permute-start(bf16[256,256]{1,0:T(8,128)(2,1)} %refs_0_.1), channel_id=1, source_target_pairs={{0,32},{32,0},{64,96},{96,64},{128,160},{160,128},{192,224},{224,1... | collective-permute-start | bytes 393224 | tf_op jit(solution)/shard_map/ppermute | solution.py:56
  17.1 8.4 %collective-permute-start.7 = (bf16[4,256,256]{2,1,0:T(8,128)(2,1)S(1)}, bf16[4,256,256]{2,1,0:T(8,128)(2,1)S(1)}, u32[]{:S(2)}, u32[]{:S(2)}) collective-permute-start(bf16[4,256,256]{2,1,0:T(8,128)(2,1)S(1)} %forward_6.1), channel_id=1, source_target_pairs={{0,28},{2,30},{4,8},{6,10},{8,4},{10,6},{12,16},{14,18},{16,12},{1... | collective-permute-start | bytes 1572872 | tf_op jit(solution)/shard_map/ppermute | solution.py:75
  19.3 14.7 %collective-permute-start.10 = (bf16[2,256,256]{2,1,0:T(8,128)(2,1)S(1)}, bf16[2,256,256]{2,1,0:T(8,128)(2,1)S(1)}, u32[]{:S(2)}, u32[]{:S(2)}) collective-permute-start(bf16[2,256,256]{2,1,0:T(8,128)(2,1)S(1)} %get-tuple-element.74), channel_id=1, source_target_pairs={{0,28},{2,30},{4,8},{6,10},{8,4},{10,6},{12,16},{14,18},{16,12},{1... | collective-permute-start | bytes 786440 | tf_op jit(solution)/shard_map/ppermute | solution.py:75
  25.6 9.0 %collective-permute-start.8 = (bf16[2,256,256]{2,1,0:T(8,128)(2,1)S(1)}, bf16[2,256,256]{2,1,0:T(8,128)(2,1)S(1)}, u32[]{:S(2)}, u32[]{:S(2)}) collective-permute-start(bf16[2,256,256]{2,1,0:T(8,128)(2,1)S(1)} %get-tuple-element.70), channel_id=1, source_target_pairs={{0,4},{2,6},{4,0},{6,2},{8,12},{10,14},{12,8},{14,10},{16,20},{18,... | collective-permute-start | bytes 786440 | tf_op jit(solution)/shard_map/ppermute | solution.py:75
  30.5 10.4 %collective-permute-start.9 = (bf16[2,256,256]{2,1,0:T(8,128)(2,1)S(1)}, bf16[2,256,256]{2,1,0:T(8,128)(2,1)S(1)}, u32[]{:S(2)}, u32[]{:S(2)}) collective-permute-start(bf16[2,256,256]{2,1,0:T(8,128)(2,1)S(1)} %get-tuple-element.71), channel_id=1, source_target_pairs={{0,6},{2,4},{4,2},{6,0},{8,14},{10,12},{12,10},{14,8},{16,22},{18,... | collective-permute-start | bytes 786440 | tf_op jit(solution)/shard_map/ppermute | solution.py:75
  34.0 14.0 %collective-permute-start.11 = (bf16[2,256,256]{2,1,0:T(8,128)(2,1)S(1)}, bf16[2,256,256]{2,1,0:T(8,128)(2,1)S(1)}, u32[]{:S(2)}, u32[]{:S(2)}) collective-permute-start(bf16[2,256,256]{2,1,0:T(8,128)(2,1)S(1)} %relay_side.1), channel_id=1, source_target_pairs={{0,2},{2,0},{4,6},{6,4},{8,10},{10,8},{12,14},{14,12},{16,18},{18,... | collective-permute-start | bytes 786440 | tf_op jit(solution)/shard_map/ppermute | solution.py:64
  41.0 7.0 %collective-permute-start.12 = (bf16[2,256,256]{2,1,0:T(8,128)(2,1)S(1)}, bf16[2,256,256]{2,1,0:T(8,128)(2,1)S(1)}, u32[]{:S(2)}, u32[]{:S(2)}) collective-permute-start(bf16[2,256,256]{2,1,0:T(8,128)(2,1)S(1)} %relay_c.1), channel_id=1, source_target_pairs={{0,28},{2,30},{4,8},{6,10},{8,4},{10,6},{12,16},{14,18},{16,12},{1... | collective-permute-start | bytes 786440 | tf_op jit(solution)/shard_map/ppermute | solution.py:75
  48.1 5.4 %collective-permute-start.13 = (bf16[256,256]{1,0:T(8,128)(2,1)S(1)}, bf16[256,256]{1,0:T(8,128)(2,1)S(1)}, u32[]{:S(2)}, u32[]{:S(2)}) collective-permute-start(bf16[256,256]{1,0:T(8,128)(2,1)S(1)} %get-tuple-element.77), channel_id=1, source_target_pairs={{0,4},{2,6},{4,0},{6,2},{8,12},{10,14},{12,8},{14,10},{16,20},{18,... | collective-permute-start | bytes 393224 | tf_op jit(solution)/shard_map/ppermute | solution.py:75
  54.7 3.6 %collective-permute-start.14 = (bf16[144,256]{1,0:T(8,128)(2,1)S(1)}, bf16[144,256]{1,0:T(8,128)(2,1)S(1)}, u32[]{:S(2)}, u32[]{:S(2)}) collective-permute-start(bf16[144,256]{1,0:T(8,128)(2,1)S(1)} %get-tuple-element.83), channel_id=1, source_target_pairs={{0,32},{32,0},{64,96},{96,64},{128,160},{160,128},{192,224},{224,1... | collective-permute-start | bytes 221192 | tf_op jit(solution)/shard_map/ppermute | solution.py:56
  58.3 6.2 %collective-permute-start.15 = (bf16[400,256]{1,0:T(8,128)(2,1)S(1)}, bf16[400,256]{1,0:T(8,128)(2,1)S(1)}, u32[]{:S(2)}, u32[]{:S(2)}) collective-permute-start(bf16[400,256]{1,0:T(8,128)(2,1)S(1)} %pack_own.1.own), channel_id=1, source_target_pairs={{0,4},{2,6},{4,0},{6,2},{8,12},{10,14},{12,8},{14,10},{16,20},{18,... | collective-permute-start | bytes 614408 | tf_op jit(solution)/shard_map/ppermute | solution.py:75
  64.6 6.4 %collective-permute-start.16 = (bf16[656,256]{1,0:T(8,128)(2,1)S(1)}, bf16[656,256]{1,0:T(8,128)(2,1)S(1)}, u32[]{:S(2)}, u32[]{:S(2)}) collective-permute-start(bf16[656,256]{1,0:T(8,128)(2,1)S(1)} %pack_pair.1.rest_0_.pd), channel_id=1, source_target_pairs={{0,28},{2,30},{4,8},{6,10},{8,4},{10,6},{12,16},{14,18},{16,12},{1... | collective-permute-start | bytes 1007624 | tf_op jit(solution)/shard_map/ppermute | solution.py:75
  64.7 7.6 %collective-permute-start.17 = (bf16[656,256]{1,0:T(8,128)(2,1)S(1)}, bf16[656,256]{1,0:T(8,128)(2,1)S(1)}, u32[]{:S(2)}, u32[]{:S(2)}) collective-permute-start(bf16[656,256]{1,0:T(8,128)(2,1)S(1)} %pack_pair.1.rest_0_.pd), channel_id=1, source_target_pairs={{0,2},{2,0},{4,6},{6,4},{8,10},{10,8},{12,14},{14,12},{16,18},{18,... | collective-permute-start | bytes 1007624 | tf_op jit(solution)/shard_map/ppermute | solution.py:64
  72.3 10.4 %collective-permute-start.18 = (bf16[656,256]{1,0:T(8,128)(2,1)S(1)}, bf16[656,256]{1,0:T(8,128)(2,1)S(1)}, u32[]{:S(2)}, u32[]{:S(2)}) collective-permute-start(bf16[656,256]{1,0:T(8,128)(2,1)S(1)} %collective-permute-done.16.rest_0_.pc), channel_id=1, source_target_pairs={{0,4},{2,6},{4,0},{6,2},{8,12},{10,14},{12,8},{14,10},{16,20},{18,... | collective-permute-start | bytes 1007624 | tf_op jit(solution)/shard_map/ppermute | solution.py:75
  78.1 12.5 %collective-permute-start.19 = (bf16[656,256]{1,0:T(8,128)(2,1)S(1)}, bf16[656,256]{1,0:T(8,128)(2,1)S(1)}, u32[]{:S(2)}, u32[]{:S(2)}) collective-permute-start(bf16[656,256]{1,0:T(8,128)(2,1)S(1)} %collective-permute-done.16.rest_0_.pc), channel_id=1, source_target_pairs={{0,6},{2,4},{4,2},{6,0},{8,14},{10,12},{12,10},{14,8},{16,22},{18,... | collective-permute-start | bytes 1007624 | tf_op jit(solution)/shard_map/ppermute | solution.py:75
  78.1 15.2 %collective-permute-start.22 = (bf16[656,256]{1,0:T(8,128)(2,1)S(1)}, bf16[656,256]{1,0:T(8,128)(2,1)S(1)}, u32[]{:S(2)}, u32[]{:S(2)}) collective-permute-start(bf16[656,256]{1,0:T(8,128)(2,1)S(1)} %collective-permute-done.17.rest_1_.sd), channel_id=1, source_target_pairs={{0,28},{2,30},{4,8},{6,10},{8,4},{10,6},{12,16},{14,18},{16,12},{1... | collective-permute-start | bytes 1007624 | tf_op jit(solution)/shard_map/ppermute | solution.py:75
  90.6 6.3 %collective-permute-start.21 = (bf16[656,256]{1,0:T(8,128)(2,1)S(1)}, bf16[656,256]{1,0:T(8,128)(2,1)S(1)}, u32[]{:S(2)}, u32[]{:S(2)}) collective-permute-start(bf16[656,256]{1,0:T(8,128)(2,1)S(1)} %collective-permute-done.18.rest_0_.pb), channel_id=1, source_target_pairs={{0,28},{2,30},{4,8},{6,10},{8,4},{10,6},{12,16},{14,18},{16,12},{1... | collective-permute-start | bytes 1007624 | tf_op jit(solution)/shard_map/ppermute | solution.py:75
  90.6 9.9 %collective-permute-start.20 = (bf16[656,256]{1,0:T(8,128)(2,1)S(1)}, bf16[656,256]{1,0:T(8,128)(2,1)S(1)}, u32[]{:S(2)}, u32[]{:S(2)}) collective-permute-start(bf16[656,256]{1,0:T(8,128)(2,1)S(1)} %collective-permute-done.19.rest_1_.sb), channel_id=1, source_target_pairs={{0,28},{2,30},{4,8},{6,10},{8,4},{10,6},{12,16},{14,18},{16,12},{1... | collective-permute-start | bytes 1007624 | tf_op jit(solution)/shard_map/ppermute | solution.py:75
  101.9 5.1 %collective-permute-start.23 = (bf16[4,256,256]{2,1,0:T(8,128)(2,1)S(1)}, bf16[4,256,256]{2,1,0:T(8,128)(2,1)S(1)}, u32[]{:S(2)}, u32[]{:S(2)}) collective-permute-start(bf16[4,256,256]{2,1,0:T(8,128)(2,1)S(1)} %get-tuple-element.96), channel_id=1, source_target_pairs={{0,32},{32,0},{64,96},{96,64},{128,160},{160,128},{192,224},{224,1... | collective-permute-start | bytes 1572872 | tf_op jit(solution)/shard_map/ppermute | solution.py:56
  107.2 7.6 %collective-permute-start.24 = (bf16[400,256]{1,0:T(8,128)(2,1)S(1)}, bf16[400,256]{1,0:T(8,128)(2,1)S(1)}, u32[]{:S(2)}, u32[]{:S(2)}) collective-permute-start(bf16[400,256]{1,0:T(8,128)(2,1)S(1)} %get-tuple-element.98), channel_id=1, source_target_pairs={{0,64},{32,96},{64,128},{96,160},{128,192},{160,224},{192,0},{224,... | collective-permute-start | bytes 614408 | tf_op jit(solution)/shard_map/ppermute | solution.py:60
  109.2 10.1 %collective-permute-start.25 = (bf16[400,256]{1,0:T(8,128)(2,1)S(1)}, bf16[400,256]{1,0:T(8,128)(2,1)S(1)}, u32[]{:S(2)}, u32[]{:S(2)}) collective-permute-start(bf16[400,256]{1,0:T(8,128)(2,1)S(1)} %get-tuple-element.99), channel_id=1, source_target_pairs={{0,128},{32,160},{64,192},{96,224},{128,0},{160,32},{192,64},{224,... | collective-permute-start | bytes 614408 | tf_op jit(solution)/shard_map/ppermute | solution.py:60
  110.2 9.3 %collective-permute-start.26 = (bf16[400,256]{1,0:T(8,128)(2,1)S(1)}, bf16[400,256]{1,0:T(8,128)(2,1)S(1)}, u32[]{:S(2)}, u32[]{:S(2)}) collective-permute-start(bf16[400,256]{1,0:T(8,128)(2,1)S(1)} %get-tuple-element.100), channel_id=1, source_target_pairs={{0,192},{32,224},{64,0},{96,32},{128,64},{160,96},{192,128},{224,1... | collective-permute-start | bytes 614408 | tf_op jit(solution)/shard_map/ppermute | solution.py:60
  (9 other events, 51.3 us)

commit v8 on v7

--- a/solution.py
+++ b/solution.py
@@ -15,8 +15,8 @@
     ((7, 0), (6, 0)),
     ((0, 1), (1, 1)),
     ((2, 0), (3, 0)),
+    ((7, 1), (6, 1)),
     ((2, 1), (3, 1)),
-    ((7, 1), (6, 1)),
     ((5, 0), (4, 0)),
     ((5, 1), (4, 1)),
 )
@@ -145,13 +145,13 @@
     rest[-1][...] = total.astype(BF16)
 
 
-def relay_last_body(kept, over, got, own, out):
-    own[...] = kept[0] + wide(over.at[0]) + wide(got.at[0])
-    out[...] = (kept[1] + wide(over.at[1]) + wide(got.at[1])).astype(BF16)
-
-
-def activate_body(own, got, weight, bias, given, hidden, grad, high, low):
-    summed = own[...] + wide(got)
+def relay_last_body(kept, got, own, out):
+    own[...] = kept[0] + wide(got.at[0])
+    out[...] = (kept[1] + wide(got.at[1])).astype(BF16)
+
+
+def activate_body(own, got, near, side, weight, bias, given, hidden, grad, high, low):
+    summed = own[...] + wide(got) + wide(near) + wide(side)
     top = summed.astype(BF16)
     rest = (summed - top.astype(F32)).astype(BF16)
     high[...] = top
@@ -339,25 +339,24 @@
     (moving,) = forward(6, 8, (jax.ShapeDtypeStruct((4, shard, 256), BF16),), source)
     moving, source = barrier((moving, source))
     moving = swap_z(moving, -1)
-    kept_b, side_b, side_c = forward(3, 6, (two, two, two16), source)
+    kept_b, side_c, side_b = forward(3, 6, (two, two16, two), source)
     side_c = swap_z(side_c, -1)
     moving, side = relay(relay_first_body, "relay_b", (two16, two16), kept_b, side_b, moving)
     moving, side, source = barrier((moving, side, source))
     side, moving = swap_z(side, 1, 1), swap_z(moving, 1)
     kept_c, side_d = forward(1, 3, (two, two), source)
     side_d = relay(relay_body, "relay_side", two16, side_d, side_c)
-    side_d = to_x(side_d)
     moving = relay(relay_body, "relay_c", two16, kept_c, moving, side)
-    moving, source = barrier((moving, source))
-    moving = swap_z(moving, -1)
+    moving, source, side_d = barrier((moving, source, side_d))
+    moving, near, side = swap_z(moving, -1), to_x(side_d[0]), swap_z(side_d[1], 1, 1)
     (kept_d,) = forward(0, 1, (two,), source)
-    own, moving = relay(relay_last_body, "relay_last", (one, one16), kept_d, side_d, moving)
+    own, moving = relay(relay_last_body, "relay_last", (one, one16), kept_d, moving)
     moving = swap_z(moving, 1)
     hidden_out, grad, high, low = call(
         activate_body,
         "activate",
         (one16, one16, one16, one16),
-        (own, moving, weight, bias[None, :], grad_out),
+        (own, moving, near, side, weight, bias[None, :], grad_out),
         flops=4 * 256**3,
         moved=2 * 2**20,
     )
@@ -391,16 +390,19 @@
     )
     first = swap_z(own_grad, 1)
     pair_d = call(pack_pair_body, "pack_pair", message, (own_grad, first), moved=2**20)
-    pair_c, side_d = swap_z(pair_d, -1), to_x(pair_d)
+    side_d = to_x(pair_d)
     total = backward(0, (pair_d,), (), running)
+    pair_d, total = barrier((pair_d, total))
+    pair_c = swap_z(pair_d, -1)
     pair_c, side_d, total = barrier((pair_c, side_d, total))
-    side_b, pair_b, side_c = swap_z(pair_c, 1, 1), swap_z(pair_c, 1), swap_z(side_d, -1)
+    pair_b, side_c = swap_z(pair_c, 1), swap_z(side_d, -1)
     total = backward(1, (pair_c, side_d), (total,), running)
-    pair_b, side_b, total = barrier((pair_b, side_b, total))
-    pair_a, side_a = swap_z(pair_b, -1), swap_z(side_b, -1)
-    total = backward(3, (pair_b, side_b), (total,), running)
-    pair_a, side_c, total = barrier((pair_a, side_c, total))
-    total = backward(5, (side_c, pair_a), (total,), running)
+    pair_b, side_c, total = barrier((pair_b, side_c, total))
+    pair_a, side_b = swap_z(pair_b, -1), swap_z(side_c, 1)
+    total = backward(3, (pair_b, side_c), (total,), running)
+    pair_a, side_b, total = barrier((pair_a, side_b, total))
+    side_a = swap_z(side_b, -1)
+    total = backward(5, (side_b, pair_a), (total,), running)
     side_a, total = barrier((side_a, total))
     own, kept, over = backward(
         7,

time: 123 us -> 127 us (1.033)
  waiting for transfers between devices: 55.4 us -> 59.3 us
  Pallas kernels: 15.3 us -> 19 us
  starting transfers between devices: 46.4 us -> 43.4 us
    ppermute x13 -> x14, starting transfers between devices: 24.1 us -> 17.8 us  [swap_z(): return lax.ppermute(a, ('row', 'col'), pairs)]
    pallas_call x23, Pallas kernels: 15.3 us -> 19 us  [call(): pl.pallas_call(body, name=name, out_shape=out_shape, in_specs=specs or [s...]
    ppermute x2, starting transfers between devices: 1.47 us -> 4.02 us  [to_x(): return lax.ppermute(a, 'col', [(i, i ^ 1) for i in range(2 * NZ)])]
    ppermute x2, waiting for transfers between devices: 7.08 us -> 9.41 us  [to_x(): return lax.ppermute(a, 'col', [(i, i ^ 1) for i in range(2 * NZ)])]
    ppermute x13 -> x14, waiting for transfers between devices: 37 us -> 38.5 us  [swap_z(): return lax.ppermute(a, ('row', 'col'), pairs)]
  transfers between devices with their start and end apart: 28 -> 29, of which waited for: 21 -> 22; matrix products, arithmetic and copies ran while one was open for 1% -> 1% of each run, Pallas kernels for 8% -> 11%
where the time goes in v8:
time: 127 us
  waiting for transfers between devices  59.3 us (47%)
  starting transfers between devices  43.4 us (34%)
  Pallas kernels  19 us (15%)
  local copies, waits for them, and re-layouts  2.83 us (2%)
  between operations  1.55 us (1%)
  other arithmetic  1.34 us (1%)
    ppermute x14, waiting for transfers between devices, swap_z(): return lax.ppermute(a, ('row', 'col'), pairs)  38.5 us
    pallas_call x23, Pallas kernels, call(): pl.pallas_call(body, name=name, out_shape=out_shape, in_specs=specs or [s...  19 us
    ppermute x14, starting transfers between devices, swap_z(): return lax.ppermute(a, ('row', 'col'), pairs)  17.8 us
    ppermute x7, starting transfers between devices, to_core(): return lax.ppermute(a, 'row', [(i, i ^ 1) for i in range(2 * NY)])  11.8 us
    ppermute x6, starting transfers between devices, to_y(): lax.ppermute(a, 'row', [(i, (i + 2 * step) % (2 * NY)) for i in range(2 *...  9.75 us
    ppermute x2, waiting for transfers between devices, to_x(): return lax.ppermute(a, 'col', [(i, i ^ 1) for i in range(2 * NZ)])  9.41 us
    ppermute x6, waiting for transfers between devices, to_y(): lax.ppermute(a, 'row', [(i, (i + 2 * step) % (2 * NY)) for i in range(2 *...  7.82 us
    ppermute x2, starting transfers between devices, to_x(): return lax.ppermute(a, 'col', [(i, i ^ 1) for i in range(2 * NZ)])  4.02 us
  transfers between devices with their start and end apart: 29, of which 22 were waited for; matrix products, arithmetic and copies ran while one was open for 1% of the time, Pallas kernels for 11%

profile of v8, /device:TPU:1, one launch (start us, length us, event | category | flops | bytes accessed | tf_op | source)
XLA Modules:
  0.0 127.4 jit_solution(16400024998429145629)
XLA Ops:
  0.6 3.8 %collective-permute-start.2 = (bf16[256,256]{1,0:T(8,128)(2,1)}, bf16[256,256]{1,0:T(8,128)(2,1)S(1)}, u32[]{:S(2)}, u32[]{:S(2)}) collective-permute-start(bf16[256,256]{1,0:T(8,128)(2,1)} %refs_0_.1), channel_id=1, source_target_pairs={{0,128},{32,160},{64,192},{96,224},{128,0},{160,32},{192,64},{224,... | collective-permute-start | bytes 393224 | tf_op jit(solution)/shard_map/ppermute | solution.py:60
  9.2 2.8 %copy-done = bf16[1,1,192,128,128]{4,3,2,1,0:T(8,128)(2,1)S(1)} copy-done((bf16[1,1,192,128,128]{4,3,2,1,0:T(8,128)(2,1)S(1)}, bf16[1,1,192,128,128]{4,3,2,1,0:T(8,128)(2,1)}, u32[]{:S(2)}) %copy-start) | copy-done | bytes 6291480
  17.6 2.5 %forward_3.1 = (f32[2,256,256]{2,1,0:T(8,128)S(1)}, bf16[2,256,256]{2,1,0:T(8,128)(2,1)S(1)}, f32[2,256,256]{2,1,0:T(8,128)S(1)}) custom-call(s32[16]{0:T(128)S(1)} %convert_reduce_fusion.1.starts, s32[192]{0:T(256)S(1)} %get-tuple-element.58.order, s32[192]{0:T(256)S(1)} %get-tuple-element.59.rows, s32[192]{0:T(256)S(1)} %get-tuple-element.60.cols, ...), custom_call_target="tpu_custom_call" | custom-call | tf_op jit(solution)/shard_map/forward_3/pallas_call | solution.py:43
  20.3 5.1 %collective-permute-done.7.got = bf16[4,256,256]{2,1,0:T(8,128)(2,1)S(1)} collective-permute-done((bf16[4,256,256]{2,1,0:T(8,128)(2,1)S(1)}, bf16[4,256,256]{2,1,0:T(8,128)(2,1)S(1)}, u32[]{:S(2)}, u32[]{:S(2)}) %collective-permute-start.7) | collective-permute-done | bytes 524320 | tf_op jit(solution)/shard_map/ppermute | solution.py:75
  25.4 4.6 %collective-permute-start.8 = (bf16[2,256,256]{2,1,0:T(8,128)(2,1)S(1)}, bf16[2,256,256]{2,1,0:T(8,128)(2,1)S(1)}, u32[]{:S(2)}, u32[]{:S(2)}) collective-permute-start(bf16[2,256,256]{2,1,0:T(8,128)(2,1)S(1)} %get-tuple-element.73), channel_id=1, source_target_pairs={{0,4},{2,6},{4,0},{6,2},{8,12},{10,14},{12,8},{14,10},{16,20},{18,... | collective-permute-start | bytes 786440 | tf_op jit(solution)/shard_map/ppermute | solution.py:75
  30.1 2.6 %collective-permute-start.9 = (bf16[2,256,256]{2,1,0:T(8,128)(2,1)S(1)}, bf16[2,256,256]{2,1,0:T(8,128)(2,1)S(1)}, u32[]{:S(2)}, u32[]{:S(2)}) collective-permute-start(bf16[2,256,256]{2,1,0:T(8,128)(2,1)S(1)} %get-tuple-element.74), channel_id=1, source_target_pairs={{0,6},{2,4},{4,2},{6,0},{8,14},{10,12},{12,10},{14,8},{16,22},{18,... | collective-permute-start | bytes 786440 | tf_op jit(solution)/shard_map/ppermute | solution.py:75
  35.4 6.3 %collective-permute-done.9.rest_1_ = bf16[2,256,256]{2,1,0:T(8,128)(2,1)S(1)} collective-permute-done((bf16[2,256,256]{2,1,0:T(8,128)(2,1)S(1)}, bf16[2,256,256]{2,1,0:T(8,128)(2,1)S(1)}, u32[]{:S(2)}, u32[]{:S(2)}) %collective-permute-start.9) | collective-permute-done | bytes 262176 | tf_op jit(solution)/shard_map/ppermute | solution.py:75
  43.1 3.4 %collective-permute-start.14 = (bf16[256,256]{1,0:T(8,128)(2,1)S(1)}, bf16[256,256]{1,0:T(8,128)(2,1)S(1)}, u32[]{:S(2)}, u32[]{:S(2)}) collective-permute-start(bf16[256,256]{1,0:T(8,128)(2,1)S(1)} %get-tuple-element.115), channel_id=1, source_target_pairs={{0,6},{2,4},{4,2},{6,0},{8,14},{10,12},{12,10},{14,8},{16,22},{18,... | collective-permute-start | bytes 393224 | tf_op jit(solution)/shard_map/ppermute | solution.py:75
  46.5 2.3 %collective-permute-start.13 = (bf16[256,256]{1,0:T(8,128)(2,1)S(1)}, bf16[256,256]{1,0:T(8,128)(2,1)S(1)}, u32[]{:S(2)}, u32[]{:S(2)}) collective-permute-start(bf16[256,256]{1,0:T(8,128)(2,1)S(1)} %get-tuple-element.116), channel_id=1, source_target_pairs={{0,2},{2,0},{4,6},{6,4},{8,10},{10,8},{12,14},{14,12},{16,18},{18,... | collective-permute-start | bytes 393224 | tf_op jit(solution)/shard_map/ppermute | solution.py:64
  55.7 3.9 %collective-permute-start.15 = (bf16[144,256]{1,0:T(8,128)(2,1)S(1)}, bf16[144,256]{1,0:T(8,128)(2,1)S(1)}, u32[]{:S(2)}, u32[]{:S(2)}) collective-permute-start(bf16[144,256]{1,0:T(8,128)(2,1)S(1)} %get-tuple-element.87), channel_id=1, source_target_pairs={{0,32},{32,0},{64,96},{96,64},{128,160},{160,128},{192,224},{224,1... | collective-permute-start | bytes 221192 | tf_op jit(solution)/shard_map/ppermute | solution.py:56
  60.5 2.4 %collective-permute-start.16 = (bf16[400,256]{1,0:T(8,128)(2,1)S(1)}, bf16[400,256]{1,0:T(8,128)(2,1)S(1)}, u32[]{:S(2)}, u32[]{:S(2)}) collective-permute-start(bf16[400,256]{1,0:T(8,128)(2,1)S(1)} %pack_own.1.own), channel_id=1, source_target_pairs={{0,4},{2,6},{4,0},{6,2},{8,12},{10,14},{12,8},{14,10},{16,20},{18,... | collective-permute-start | bytes 614408 | tf_op jit(solution)/shard_map/ppermute | solution.py:75
  62.9 3.5 %collective-permute-done.16.got = bf16[400,256]{1,0:T(8,128)(2,1)S(1)} collective-permute-done((bf16[400,256]{1,0:T(8,128)(2,1)S(1)}, bf16[400,256]{1,0:T(8,128)(2,1)S(1)}, u32[]{:S(2)}, u32[]{:S(2)}) %collective-permute-start.16) | collective-permute-done | bytes 204832 | tf_op jit(solution)/shard_map/ppermute | solution.py:75
  69.5 7.7 %collective-permute-done.18.rest_1_.sd = bf16[656,256]{1,0:T(8,128)(2,1)S(1)} collective-permute-done((bf16[656,256]{1,0:T(8,128)(2,1)S(1)}, bf16[656,256]{1,0:T(8,128)(2,1)S(1)}, u32[]{:S(2)}, u32[]{:S(2)}) %collective-permute-start.18) | collective-permute-done | bytes 335904 | tf_op jit(solution)/shard_map/ppermute | solution.py:64
  77.2 2.3 %collective-permute-start.19 = (bf16[656,256]{1,0:T(8,128)(2,1)S(1)}, bf16[656,256]{1,0:T(8,128)(2,1)S(1)}, u32[]{:S(2)}, u32[]{:S(2)}) collective-permute-start(bf16[656,256]{1,0:T(8,128)(2,1)S(1)} %collective-permute-done.17.rest_0_.pc), channel_id=1, source_target_pairs={{0,4},{2,6},{4,0},{6,2},{8,12},{10,14},{12,8},{14,10},{16,20},{18,... | collective-permute-start | bytes 1007624 | tf_op jit(solution)/shard_map/ppermute | solution.py:75
  81.3 5.2 %collective-permute-done.19.rest_0_.pb = bf16[656,256]{1,0:T(8,128)(2,1)S(1)} collective-permute-done((bf16[656,256]{1,0:T(8,128)(2,1)S(1)}, bf16[656,256]{1,0:T(8,128)(2,1)S(1)}, u32[]{:S(2)}, u32[]{:S(2)}) %collective-permute-start.19) | collective-permute-done | bytes 335904 | tf_op jit(solution)/shard_map/ppermute | solution.py:75
  86.4 2.3 %collective-permute-done.20.rest_1_.sc = bf16[656,256]{1,0:T(8,128)(2,1)S(1)} collective-permute-done((bf16[656,256]{1,0:T(8,128)(2,1)S(1)}, bf16[656,256]{1,0:T(8,128)(2,1)S(1)}, u32[]{:S(2)}, u32[]{:S(2)}) %collective-permute-start.20) | collective-permute-done | bytes 335904 | tf_op jit(solution)/shard_map/ppermute | solution.py:75
  90.4 5.0 %collective-permute-done.21.rest_1_.pa = bf16[656,256]{1,0:T(8,128)(2,1)S(1)} collective-permute-done((bf16[656,256]{1,0:T(8,128)(2,1)S(1)}, bf16[656,256]{1,0:T(8,128)(2,1)S(1)}, u32[]{:S(2)}, u32[]{:S(2)}) %collective-permute-start.21) | collective-permute-done | bytes 335904 | tf_op jit(solution)/shard_map/ppermute | solution.py:75
  95.5 3.6 %collective-permute-done.22.rest_0_.sb = bf16[656,256]{1,0:T(8,128)(2,1)S(1)} collective-permute-done((bf16[656,256]{1,0:T(8,128)(2,1)S(1)}, bf16[656,256]{1,0:T(8,128)(2,1)S(1)}, u32[]{:S(2)}, u32[]{:S(2)}) %collective-permute-start.22) | collective-permute-done | bytes 335904 | tf_op jit(solution)/shard_map/ppermute | solution.py:75
  99.1 2.2 %backward_5.1.rest_1_ = f32[17,128,256]{2,1,0:T(8,128)S(1)} custom-call(s32[16]{0:T(128)S(1)} %convert_reduce_fusion.1.starts, s32[192]{0:T(256)S(1)} %get-tuple-element.58.order, s32[192]{0:T(256)S(1)} %get-tuple-element.59.rows, s32[192]{0:T(256)S(1)} %get-tuple-element.60.cols, bf16[192,128,128]{2,1,0:T(8,128)(2,1)S(1)} %load_tiles.1.vals, ...), custom_call_target="tpu_custom_call" | custom-call | tf_op jit(solution)/shard_map/backward_5/pallas_call | solution.py:43
  101.3 4.1 %collective-permute-done.23.rest_0_.sa = bf16[656,256]{1,0:T(8,128)(2,1)S(1)} collective-permute-done((bf16[656,256]{1,0:T(8,128)(2,1)S(1)}, bf16[656,256]{1,0:T(8,128)(2,1)S(1)}, u32[]{:S(2)}, u32[]{:S(2)}) %collective-permute-start.23) | collective-permute-done | bytes 335904 | tf_op jit(solution)/shard_map/ppermute | solution.py:75
  106.7 3.3 %collective-permute-start.24 = (bf16[4,256,256]{2,1,0:T(8,128)(2,1)S(1)}, bf16[4,256,256]{2,1,0:T(8,128)(2,1)S(1)}, u32[]{:S(2)}, u32[]{:S(2)}) collective-permute-start(bf16[4,256,256]{2,1,0:T(8,128)(2,1)S(1)} %get-tuple-element.102), channel_id=1, source_target_pairs={{0,32},{32,0},{64,96},{96,64},{128,160},{160,128},{192,224},{224,1... | collective-permute-start | bytes 1572872 | tf_op jit(solution)/shard_map/ppermute | solution.py:56
  112.0 2.3 %collective-permute-start.26 = (bf16[400,256]{1,0:T(8,128)(2,1)S(1)}, bf16[400,256]{1,0:T(8,128)(2,1)S(1)}, u32[]{:S(2)}, u32[]{:S(2)}) collective-permute-start(bf16[400,256]{1,0:T(8,128)(2,1)S(1)} %get-tuple-element.105), channel_id=1, source_target_pairs={{0,128},{32,160},{64,192},{96,224},{128,0},{160,32},{192,64},{224,... | collective-permute-start | bytes 614408 | tf_op jit(solution)/shard_map/ppermute | solution.py:60
  116.3 3.4 %collective-permute-done.25.a = bf16[400,256]{1,0:T(8,128)(2,1)S(1)} collective-permute-done((bf16[400,256]{1,0:T(8,128)(2,1)S(1)}, bf16[400,256]{1,0:T(8,128)(2,1)S(1)}, u32[]{:S(2)}, u32[]{:S(2)}) %collective-permute-start.25) | collective-permute-done | bytes 204832 | tf_op jit(solution)/shard_map/ppermute | solution.py:60
  119.6 3.9 %collective-permute-done.26.b = bf16[400,256]{1,0:T(8,128)(2,1)S(1)} collective-permute-done((bf16[400,256]{1,0:T(8,128)(2,1)S(1)}, bf16[400,256]{1,0:T(8,128)(2,1)S(1)}, u32[]{:S(2)}, u32[]{:S(2)}) %collective-permute-start.26) | collective-permute-done | bytes 204832 | tf_op jit(solution)/shard_map/ppermute | solution.py:60
  (74 shorter events, 37.4 us)
Async XLA Ops:
  0.6 12.1 %collective-permute-start.2 = (bf16[256,256]{1,0:T(8,128)(2,1)}, bf16[256,256]{1,0:T(8,128)(2,1)S(1)}, u32[]{:S(2)}, u32[]{:S(2)}) collective-permute-start(bf16[256,256]{1,0:T(8,128)(2,1)} %refs_0_.1), channel_id=1, source_target_pairs={{0,128},{32,160},{64,192},{96,224},{128,0},{160,32},{192,64},{224,... | collective-permute-start | bytes 393224 | tf_op jit(solution)/shard_map/ppermute | solution.py:60
  4.5 8.2 %collective-permute-start.1 = (bf16[256,256]{1,0:T(8,128)(2,1)}, bf16[256,256]{1,0:T(8,128)(2,1)S(1)}, u32[]{:S(2)}, u32[]{:S(2)}) collective-permute-start(bf16[256,256]{1,0:T(8,128)(2,1)} %refs_0_.1), channel_id=1, source_target_pairs={{0,192},{32,224},{64,0},{96,32},{128,64},{160,96},{192,128},{224,1... | collective-permute-start | bytes 393224 | tf_op jit(solution)/shard_map/ppermute | solution.py:60
  5.2 7.5 %collective-permute-start = (bf16[256,256]{1,0:T(8,128)(2,1)}, bf16[256,256]{1,0:T(8,128)(2,1)S(1)}, u32[]{:S(2)}, u32[]{:S(2)}) collective-permute-start(bf16[256,256]{1,0:T(8,128)(2,1)} %refs_0_.1), channel_id=1, source_target_pairs={{0,64},{32,96},{64,128},{96,160},{128,192},{160,224},{192,0},{224,... | collective-permute-start | bytes 393224 | tf_op jit(solution)/shard_map/ppermute | solution.py:60
  5.9 8.3 %collective-permute-start.3 = (bf16[256,256]{1,0:T(8,128)(2,1)}, bf16[256,256]{1,0:T(8,128)(2,1)S(1)}, u32[]{:S(2)}, u32[]{:S(2)}) collective-permute-start(bf16[256,256]{1,0:T(8,128)(2,1)} %refs_0_.1), channel_id=1, source_target_pairs={{0,32},{32,0},{64,96},{96,64},{128,160},{160,128},{192,224},{224,1... | collective-permute-start | bytes 393224 | tf_op jit(solution)/shard_map/ppermute | solution.py:56
  16.9 8.4 %collective-permute-start.7 = (bf16[4,256,256]{2,1,0:T(8,128)(2,1)S(1)}, bf16[4,256,256]{2,1,0:T(8,128)(2,1)S(1)}, u32[]{:S(2)}, u32[]{:S(2)}) collective-permute-start(bf16[4,256,256]{2,1,0:T(8,128)(2,1)S(1)} %forward_6.1), channel_id=1, source_target_pairs={{0,28},{2,30},{4,8},{6,10},{8,4},{10,6},{12,16},{14,18},{16,12},{1... | collective-permute-start | bytes 1572872 | tf_op jit(solution)/shard_map/ppermute | solution.py:75
  20.2 14.1 %collective-permute-start.10 = (bf16[2,256,256]{2,1,0:T(8,128)(2,1)S(1)}, bf16[2,256,256]{2,1,0:T(8,128)(2,1)S(1)}, u32[]{:S(2)}, u32[]{:S(2)}) collective-permute-start(bf16[2,256,256]{2,1,0:T(8,128)(2,1)S(1)} %get-tuple-element.76), channel_id=1, source_target_pairs={{0,28},{2,30},{4,8},{6,10},{8,4},{10,6},{12,16},{14,18},{16,12},{1... | collective-permute-start | bytes 786440 | tf_op jit(solution)/shard_map/ppermute | solution.py:75
  25.4 10.0 %collective-permute-start.8 = (bf16[2,256,256]{2,1,0:T(8,128)(2,1)S(1)}, bf16[2,256,256]{2,1,0:T(8,128)(2,1)S(1)}, u32[]{:S(2)}, u32[]{:S(2)}) collective-permute-start(bf16[2,256,256]{2,1,0:T(8,128)(2,1)S(1)} %get-tuple-element.73), channel_id=1, source_target_pairs={{0,4},{2,6},{4,0},{6,2},{8,12},{10,14},{12,8},{14,10},{16,20},{18,... | collective-permute-start | bytes 786440 | tf_op jit(solution)/shard_map/ppermute | solution.py:75
  30.1 11.6 %collective-permute-start.9 = (bf16[2,256,256]{2,1,0:T(8,128)(2,1)S(1)}, bf16[2,256,256]{2,1,0:T(8,128)(2,1)S(1)}, u32[]{:S(2)}, u32[]{:S(2)}) collective-permute-start(bf16[2,256,256]{2,1,0:T(8,128)(2,1)S(1)} %get-tuple-element.74), channel_id=1, source_target_pairs={{0,6},{2,4},{4,2},{6,0},{8,14},{10,12},{12,10},{14,8},{16,22},{18,... | collective-permute-start | bytes 786440 | tf_op jit(solution)/shard_map/ppermute | solution.py:75
  41.8 7.0 %collective-permute-start.11 = (bf16[2,256,256]{2,1,0:T(8,128)(2,1)S(1)}, bf16[2,256,256]{2,1,0:T(8,128)(2,1)S(1)}, u32[]{:S(2)}, u32[]{:S(2)}) collective-permute-start(bf16[2,256,256]{2,1,0:T(8,128)(2,1)S(1)} %relay_c.1), channel_id=1, source_target_pairs={{0,28},{2,30},{4,8},{6,10},{8,4},{10,6},{12,16},{14,18},{16,12},{1... | collective-permute-start | bytes 786440 | tf_op jit(solution)/shard_map/ppermute | solution.py:75
  43.1 8.9 %collective-permute-start.14 = (bf16[256,256]{1,0:T(8,128)(2,1)S(1)}, bf16[256,256]{1,0:T(8,128)(2,1)S(1)}, u32[]{:S(2)}, u32[]{:S(2)}) collective-permute-start(bf16[256,256]{1,0:T(8,128)(2,1)S(1)} %get-tuple-element.115), channel_id=1, source_target_pairs={{0,6},{2,4},{4,2},{6,0},{8,14},{10,12},{12,10},{14,8},{16,22},{18,... | collective-permute-start | bytes 393224 | tf_op jit(solution)/shard_map/ppermute | solution.py:75
  46.5 7.2 %collective-permute-start.13 = (bf16[256,256]{1,0:T(8,128)(2,1)S(1)}, bf16[256,256]{1,0:T(8,128)(2,1)S(1)}, u32[]{:S(2)}, u32[]{:S(2)}) collective-permute-start(bf16[256,256]{1,0:T(8,128)(2,1)S(1)} %get-tuple-element.116), channel_id=1, source_target_pairs={{0,2},{2,0},{4,6},{6,4},{8,10},{10,8},{12,14},{14,12},{16,18},{18,... | collective-permute-start | bytes 393224 | tf_op jit(solution)/shard_map/ppermute | solution.py:64
  48.8 5.6 %collective-permute-start.12 = (bf16[256,256]{1,0:T(8,128)(2,1)S(1)}, bf16[256,256]{1,0:T(8,128)(2,1)S(1)}, u32[]{:S(2)}, u32[]{:S(2)}) collective-permute-start(bf16[256,256]{1,0:T(8,128)(2,1)S(1)} %get-tuple-element.80), channel_id=1, source_target_pairs={{0,4},{2,6},{4,0},{6,2},{8,12},{10,14},{12,8},{14,10},{16,20},{18,... | collective-permute-start | bytes 393224 | tf_op jit(solution)/shard_map/ppermute | solution.py:75
  60.5 5.9 %collective-permute-start.16 = (bf16[400,256]{1,0:T(8,128)(2,1)S(1)}, bf16[400,256]{1,0:T(8,128)(2,1)S(1)}, u32[]{:S(2)}, u32[]{:S(2)}) collective-permute-start(bf16[400,256]{1,0:T(8,128)(2,1)S(1)} %pack_own.1.own), channel_id=1, source_target_pairs={{0,4},{2,6},{4,0},{6,2},{8,12},{10,14},{12,8},{14,10},{16,20},{18,... | collective-permute-start | bytes 614408 | tf_op jit(solution)/shard_map/ppermute | solution.py:75
  66.5 10.8 %collective-permute-start.18 = (bf16[656,256]{1,0:T(8,128)(2,1)S(1)}, bf16[656,256]{1,0:T(8,128)(2,1)S(1)}, u32[]{:S(2)}, u32[]{:S(2)}) collective-permute-start(bf16[656,256]{1,0:T(8,128)(2,1)S(1)} %pack_pair.1.rest_0_.pd), channel_id=1, source_target_pairs={{0,2},{2,0},{4,6},{6,4},{8,10},{10,8},{12,14},{14,12},{16,18},{18,... | collective-permute-start | bytes 1007624 | tf_op jit(solution)/shard_map/ppermute | solution.py:64
  69.4 7.8 %collective-permute-start.17 = (bf16[656,256]{1,0:T(8,128)(2,1)S(1)}, bf16[656,256]{1,0:T(8,128)(2,1)S(1)}, u32[]{:S(2)}, u32[]{:S(2)}) collective-permute-start(bf16[656,256]{1,0:T(8,128)(2,1)S(1)} %pack_pair.1.rest_0_.pd), channel_id=1, source_target_pairs={{0,28},{2,30},{4,8},{6,10},{8,4},{10,6},{12,16},{14,18},{16,12},{1... | collective-permute-start | bytes 1007624 | tf_op jit(solution)/shard_map/ppermute | solution.py:75
  77.2 9.2 %collective-permute-start.19 = (bf16[656,256]{1,0:T(8,128)(2,1)S(1)}, bf16[656,256]{1,0:T(8,128)(2,1)S(1)}, u32[]{:S(2)}, u32[]{:S(2)}) collective-permute-start(bf16[656,256]{1,0:T(8,128)(2,1)S(1)} %collective-permute-done.17.rest_0_.pc), channel_id=1, source_target_pairs={{0,4},{2,6},{4,0},{6,2},{8,12},{10,14},{12,8},{14,10},{16,20},{18,... | collective-permute-start | bytes 1007624 | tf_op jit(solution)/shard_map/ppermute | solution.py:75
  79.5 9.2 %collective-permute-start.20 = (bf16[656,256]{1,0:T(8,128)(2,1)S(1)}, bf16[656,256]{1,0:T(8,128)(2,1)S(1)}, u32[]{:S(2)}, u32[]{:S(2)}) collective-permute-start(bf16[656,256]{1,0:T(8,128)(2,1)S(1)} %collective-permute-done.18.rest_1_.sd), channel_id=1, source_target_pairs={{0,28},{2,30},{4,8},{6,10},{8,4},{10,6},{12,16},{14,18},{16,12},{1... | collective-permute-start | bytes 1007624 | tf_op jit(solution)/shard_map/ppermute | solution.py:75
  88.7 6.8 %collective-permute-start.21 = (bf16[656,256]{1,0:T(8,128)(2,1)S(1)}, bf16[656,256]{1,0:T(8,128)(2,1)S(1)}, u32[]{:S(2)}, u32[]{:S(2)}) collective-permute-start(bf16[656,256]{1,0:T(8,128)(2,1)S(1)} %collective-permute-done.19.rest_0_.pb), channel_id=1, source_target_pairs={{0,28},{2,30},{4,8},{6,10},{8,4},{10,6},{12,16},{14,18},{16,12},{1... | collective-permute-start | bytes 1007624 | tf_op jit(solution)/shard_map/ppermute | solution.py:75
  88.7 10.3 %collective-permute-start.22 = (bf16[656,256]{1,0:T(8,128)(2,1)S(1)}, bf16[656,256]{1,0:T(8,128)(2,1)S(1)}, u32[]{:S(2)}, u32[]{:S(2)}) collective-permute-start(bf16[656,256]{1,0:T(8,128)(2,1)S(1)} %collective-permute-done.20.rest_1_.sc), channel_id=1, source_target_pairs={{0,4},{2,6},{4,0},{6,2},{8,12},{10,14},{12,8},{14,10},{16,20},{18,... | collective-permute-start | bytes 1007624 | tf_op jit(solution)/shard_map/ppermute | solution.py:75
  99.1 6.3 %collective-permute-start.23 = (bf16[656,256]{1,0:T(8,128)(2,1)S(1)}, bf16[656,256]{1,0:T(8,128)(2,1)S(1)}, u32[]{:S(2)}, u32[]{:S(2)}) collective-permute-start(bf16[656,256]{1,0:T(8,128)(2,1)S(1)} %collective-permute-done.22.rest_0_.sb), channel_id=1, source_target_pairs={{0,28},{2,30},{4,8},{6,10},{8,4},{10,6},{12,16},{14,18},{16,12},{1... | collective-permute-start | bytes 1007624 | tf_op jit(solution)/shard_map/ppermute | solution.py:75
  106.7 4.9 %collective-permute-start.24 = (bf16[4,256,256]{2,1,0:T(8,128)(2,1)S(1)}, bf16[4,256,256]{2,1,0:T(8,128)(2,1)S(1)}, u32[]{:S(2)}, u32[]{:S(2)}) collective-permute-start(bf16[4,256,256]{2,1,0:T(8,128)(2,1)S(1)} %get-tuple-element.102), channel_id=1, source_target_pairs={{0,32},{32,0},{64,96},{96,64},{128,160},{160,128},{192,224},{224,1... | collective-permute-start | bytes 1572872 | tf_op jit(solution)/shard_map/ppermute | solution.py:56
  111.8 7.8 %collective-permute-start.25 = (bf16[400,256]{1,0:T(8,128)(2,1)S(1)}, bf16[400,256]{1,0:T(8,128)(2,1)S(1)}, u32[]{:S(2)}, u32[]{:S(2)}) collective-permute-start(bf16[400,256]{1,0:T(8,128)(2,1)S(1)} %get-tuple-element.104), channel_id=1, source_target_pairs={{0,64},{32,96},{64,128},{96,160},{128,192},{160,224},{192,0},{224,... | collective-permute-start | bytes 614408 | tf_op jit(solution)/shard_map/ppermute | solution.py:60
  112.0 11.5 %collective-permute-start.26 = (bf16[400,256]{1,0:T(8,128)(2,1)S(1)}, bf16[400,256]{1,0:T(8,128)(2,1)S(1)}, u32[]{:S(2)}, u32[]{:S(2)}) collective-permute-start(bf16[400,256]{1,0:T(8,128)(2,1)S(1)} %get-tuple-element.105), channel_id=1, source_target_pairs={{0,128},{32,160},{64,192},{96,224},{128,0},{160,32},{192,64},{224,... | collective-permute-start | bytes 614408 | tf_op jit(solution)/shard_map/ppermute | solution.py:60
  114.3 9.8 %collective-permute-start.27 = (bf16[400,256]{1,0:T(8,128)(2,1)S(1)}, bf16[400,256]{1,0:T(8,128)(2,1)S(1)}, u32[]{:S(2)}, u32[]{:S(2)}) collective-permute-start(bf16[400,256]{1,0:T(8,128)(2,1)S(1)} %get-tuple-element.106), channel_id=1, source_target_pairs={{0,192},{32,224},{64,0},{96,32},{128,64},{160,96},{192,128},{224,1... | collective-permute-start | bytes 614408 | tf_op jit(solution)/shard_map/ppermute | solution.py:60
  (10 other events, 56.2 us)

commit v9 on v7

--- a/solution.py
+++ b/solution.py
@@ -9,7 +9,6 @@
 from jax.sharding import PartitionSpec as P
 
 TILE = 128
-UNROLL = 16
 ORDER = (
     ((0, 0), (1, 0)),
     ((7, 0), (6, 0)),
@@ -96,16 +95,26 @@
 def add_tiles(begin, end, starts, order, to_slot, product, total, dummy):
     first, last = starts[begin], starts[end]
 
-    def batch(i, carry):
-        slots = [first + i * UNROLL + u for u in range(UNROLL)]
+    def step(start, count):
+        slots = [start + u for u in range(count)]
         safe = [jnp.minimum(t, 191) for t in slots]
         terms = [product(order[t], t) for t in safe]
         for slot, t, term in zip(slots, safe, terms):
             place_at = jnp.where(slot < last, to_slot(t), dummy)
             total[place_at] = total[place_at] + term
+
+    size = last - first
+    full = (size + 7) // 16
+
+    def batch(i, carry):
+        step(first + 16 * i, 16)
         return carry
 
-    lax.fori_loop(0, (last - first + UNROLL - 1) // UNROLL, batch, 0)
+    lax.fori_loop(0, full, batch, 0)
+
+    @pl.when(16 * full < size)
+    def _():
+        step(first + 16 * full, 8)
 
 
 def forward_body(begin, end, starts, order, rows, cols, vals, source, *rest):
@@ -234,11 +243,14 @@
         place(over.at[3], total, 1, BF16)
 
 
-def back_relay_body(kept, over, pd, pa, pc, pb, sd, sa, sc, sb, out_a, out_b, out_c, terms):
+def plane_terms_body(pd, pa, pc, pb, out):
     sums = slice(512, 656)
     plane = add_rows(pd[sums], pa[sums]).astype(F32) + add_rows(pc[sums], pb[sums]).astype(F32)
-    other = add_rows(sd[sums], sa[sums]).astype(F32) + add_rows(sc[sums], sb[sums]).astype(F32)
-    terms[...] = (plane + other).astype(BF16)
+    out[...] = plane.astype(BF16)
+
+
+def back_relay_body(kept, over, plane, other, out_a, out_b, out_c, terms):
+    terms[...] = add_rows(plane[...], other[...])
     for k, out in enumerate((out_a, out_b, out_c)):
         out[0:256] = (kept[k] + over[k].astype(F32)).astype(BF16)
         out[256:400] = terms[...]
@@ -343,8 +355,10 @@
     side_c = swap_z(side_c, -1)
     moving, side = relay(relay_first_body, "relay_b", (two16, two16), kept_b, side_b, moving)
     moving, side, source = barrier((moving, side, source))
-    side, moving = swap_z(side, 1, 1), swap_z(moving, 1)
+    side = swap_z(side, 1, 1)
     kept_c, side_d = forward(1, 3, (two, two), source)
+    moving, kept_c = barrier((moving, kept_c))
+    moving = swap_z(moving, 1)
     side_d = relay(relay_body, "relay_side", two16, side_d, side_c)
     side_d = to_x(side_d)
     moving = relay(relay_body, "relay_c", two16, kept_c, moving, side)
@@ -391,17 +405,21 @@
     )
     first = swap_z(own_grad, 1)
     pair_d = call(pack_pair_body, "pack_pair", message, (own_grad, first), moved=2**20)
-    pair_c, side_d = swap_z(pair_d, -1), to_x(pair_d)
+    pair_c, side_d = swap_z(pair_d, -1), to_x(pair_d[:512])
     total = backward(0, (pair_d,), (), running)
     pair_c, side_d, total = barrier((pair_c, side_d, total))
-    side_b, pair_b, side_c = swap_z(pair_c, 1, 1), swap_z(pair_c, 1), swap_z(side_d, -1)
+    side_b, pair_b, side_c = swap_z(pair_c[:512], 1, 1), swap_z(pair_c, 1), swap_z(side_d, -1)
     total = backward(1, (pair_c, side_d), (total,), running)
     pair_b, side_b, total = barrier((pair_b, side_b, total))
     pair_a, side_a = swap_z(pair_b, -1), swap_z(side_b, -1)
     total = backward(3, (pair_b, side_b), (total,), running)
     pair_a, side_c, total = barrier((pair_a, side_c, total))
+    plane = call(
+        plane_terms_body, "plane_terms", half, (pair_d, pair_a, pair_c, pair_b), moved=2**19
+    )
+    other = to_x(plane)
     total = backward(5, (side_c, pair_a), (total,), running)
-    side_a, total = barrier((side_a, total))
+    side_a, total, other = barrier((side_a, total, other))
     own, kept, over = backward(
         7,
         (side_a,),
@@ -417,7 +435,7 @@
         back_relay_body,
         "back_relay",
         (*[shape(400, BF16)] * 3, half),
-        (kept, over, pair_d, pair_a, pair_c, pair_b, side_d, side_a, side_c, side_b),
+        (kept, over, plane, other),
         moved=2 * 2**20,
     )
     got = [to_y(a, s) for a, s in zip(sends, (1, 2, 3))]

time: 123 us -> 125 us (1.016)
  waiting for transfers between devices: 55.4 us -> 57.7 us
  starting transfers between devices: 46.4 us -> 47.7 us
  Pallas kernels: 15.3 us -> 14 us
    ppermute x2 -> x3, waiting for transfers between devices: 7.08 us -> 10.6 us  [to_x(): return lax.ppermute(a, 'col', [(i, i ^ 1) for i in range(2 * NZ)])]
    ppermute x7, starting transfers between devices: 11.1 us -> 14.1 us  [to_core(): return lax.ppermute(a, 'row', [(i, i ^ 1) for i in range(2 * NY)])]
    ppermute x13, waiting for transfers between devices: 37 us -> 35.5 us  [swap_z(): return lax.ppermute(a, ('row', 'col'), pairs)]
    pallas_call x23 -> x24, Pallas kernels: 15.3 us -> 14 us  [call(): pl.pallas_call(body, name=name, out_shape=out_shape, in_specs=specs or [s...]
  transfers between devices with their start and end apart: 28 -> 29, of which waited for: 21 -> 21; matrix products, arithmetic and copies ran while one was open for 1% -> 1% of each run, Pallas kernels for 8% -> 8%
where the time goes in v9:
time: 125 us
  waiting for transfers between devices  57.7 us (46%)
  starting transfers between devices  47.7 us (38%)
  Pallas kernels  14 us (11%)
  local copies, waits for them, and re-layouts  2.85 us (2%)
  between operations  1.57 us (1%)
  other arithmetic  1.34 us (1%)
    ppermute x13, waiting for transfers between devices, swap_z(): return lax.ppermute(a, ('row', 'col'), pairs)  35.5 us
    ppermute x13, starting transfers between devices, swap_z(): return lax.ppermute(a, ('row', 'col'), pairs)  23 us
    ppermute x7, starting transfers between devices, to_core(): return lax.ppermute(a, 'row', [(i, i ^ 1) for i in range(2 * NY)])  14.1 us
    pallas_call x24, Pallas kernels, call(): pl.pallas_call(body, name=name, out_shape=out_shape, in_specs=specs or [s...  14 us
    ppermute x3, waiting for transfers between devices, to_x(): return lax.ppermute(a, 'col', [(i, i ^ 1) for i in range(2 * NZ)])  10.6 us
    ppermute x6, starting transfers between devices, to_y(): lax.ppermute(a, 'row', [(i, (i + 2 * step) % (2 * NY)) for i in range(2 *...  9.49 us
    ppermute x6, waiting for transfers between devices, to_y(): lax.ppermute(a, 'row', [(i, (i + 2 * step) % (2 * NY)) for i in range(2 *...  8.07 us
    ppermute x7, waiting for transfers between devices, to_core(): return lax.ppermute(a, 'row', [(i, i ^ 1) for i in range(2 * NY)])  3.58 us
  transfers between devices with their start and end apart: 29, of which 21 were waited for; matrix products, arithmetic and copies ran while one was open for 1% of the time, Pallas kernels for 8%

profile of v9, /device:TPU:1, one launch (start us, length us, event | category | flops | bytes accessed | tf_op | source)
XLA Modules:
  0.0 125.2 jit_solution(18008897083047027110)
XLA Ops:
  0.6 3.8 %collective-permute-start.2 = (bf16[256,256]{1,0:T(8,128)(2,1)}, bf16[256,256]{1,0:T(8,128)(2,1)S(1)}, u32[]{:S(2)}, u32[]{:S(2)}) collective-permute-start(bf16[256,256]{1,0:T(8,128)(2,1)} %refs_0_.1), channel_id=1, source_target_pairs={{0,128},{32,160},{64,192},{96,224},{128,0},{160,32},{192,64},{224,... | collective-permute-start | bytes 393224 | tf_op jit(solution)/shard_map/ppermute | solution.py:59
  9.2 2.8 %copy-done = bf16[1,1,192,128,128]{4,3,2,1,0:T(8,128)(2,1)S(1)} copy-done((bf16[1,1,192,128,128]{4,3,2,1,0:T(8,128)(2,1)S(1)}, bf16[1,1,192,128,128]{4,3,2,1,0:T(8,128)(2,1)}, u32[]{:S(2)}) %copy-start) | copy-done | bytes 6291480
  16.3 1.8 %collective-permute-start.7 = (bf16[4,256,256]{2,1,0:T(8,128)(2,1)S(1)}, bf16[4,256,256]{2,1,0:T(8,128)(2,1)S(1)}, u32[]{:S(2)}, u32[]{:S(2)}) collective-permute-start(bf16[4,256,256]{2,1,0:T(8,128)(2,1)S(1)} %forward_6.1), channel_id=1, source_target_pairs={{0,28},{2,30},{4,8},{6,10},{8,4},{10,6},{12,16},{14,18},{16,12},{1... | collective-permute-start | bytes 1572872 | tf_op jit(solution)/shard_map/ppermute | solution.py:74
  19.8 5.2 %collective-permute-done.7.got = bf16[4,256,256]{2,1,0:T(8,128)(2,1)S(1)} collective-permute-done((bf16[4,256,256]{2,1,0:T(8,128)(2,1)S(1)}, bf16[4,256,256]{2,1,0:T(8,128)(2,1)S(1)}, u32[]{:S(2)}, u32[]{:S(2)}) %collective-permute-start.7) | collective-permute-done | bytes 524320 | tf_op jit(solution)/shard_map/ppermute | solution.py:74
  25.1 7.8 %collective-permute-start.9 = (bf16[2,256,256]{2,1,0:T(8,128)(2,1)S(1)}, bf16[2,256,256]{2,1,0:T(8,128)(2,1)S(1)}, u32[]{:S(2)}, u32[]{:S(2)}) collective-permute-start(bf16[2,256,256]{2,1,0:T(8,128)(2,1)S(1)} %get-tuple-element.76), channel_id=1, source_target_pairs={{0,6},{2,4},{4,2},{6,0},{8,14},{10,12},{12,10},{14,8},{16,22},{18,... | collective-permute-start | bytes 786440 | tf_op jit(solution)/shard_map/ppermute | solution.py:74
  34.6 4.5 %collective-permute-done.9.rest_1_ = bf16[2,256,256]{2,1,0:T(8,128)(2,1)S(1)} collective-permute-done((bf16[2,256,256]{2,1,0:T(8,128)(2,1)S(1)}, bf16[2,256,256]{2,1,0:T(8,128)(2,1)S(1)}, u32[]{:S(2)}, u32[]{:S(2)}) %collective-permute-start.9) | collective-permute-done | bytes 262176 | tf_op jit(solution)/shard_map/ppermute | solution.py:74
  41.6 3.1 %collective-permute-done.11.over = bf16[2,256,256]{2,1,0:T(8,128)(2,1)S(1)} collective-permute-done((bf16[2,256,256]{2,1,0:T(8,128)(2,1)S(1)}, bf16[2,256,256]{2,1,0:T(8,128)(2,1)S(1)}, u32[]{:S(2)}, u32[]{:S(2)}) %collective-permute-start.11) | collective-permute-done | bytes 262176 | tf_op jit(solution)/shard_map/ppermute | solution.py:63
  45.9 2.6 %collective-permute-start.13 = (bf16[256,256]{1,0:T(8,128)(2,1)S(1)}, bf16[256,256]{1,0:T(8,128)(2,1)S(1)}, u32[]{:S(2)}, u32[]{:S(2)}) collective-permute-start(bf16[256,256]{1,0:T(8,128)(2,1)S(1)} %get-tuple-element.82), channel_id=1, source_target_pairs={{0,4},{2,6},{4,0},{6,2},{8,12},{10,14},{12,8},{14,10},{16,20},{18,... | collective-permute-start | bytes 393224 | tf_op jit(solution)/shard_map/ppermute | solution.py:74
  48.5 2.7 %collective-permute-done.13.got = bf16[256,256]{1,0:T(8,128)(2,1)S(1)} collective-permute-done((bf16[256,256]{1,0:T(8,128)(2,1)S(1)}, bf16[256,256]{1,0:T(8,128)(2,1)S(1)}, u32[]{:S(2)}, u32[]{:S(2)}) %collective-permute-start.13) | collective-permute-done | bytes 131104 | tf_op jit(solution)/shard_map/ppermute | solution.py:74
  52.5 4.7 %collective-permute-start.14 = (bf16[144,256]{1,0:T(8,128)(2,1)S(1)}, bf16[144,256]{1,0:T(8,128)(2,1)S(1)}, u32[]{:S(2)}, u32[]{:S(2)}) collective-permute-start(bf16[144,256]{1,0:T(8,128)(2,1)S(1)} %get-tuple-element.88), channel_id=1, source_target_pairs={{0,32},{32,0},{64,96},{96,64},{128,160},{160,128},{192,224},{224,1... | collective-permute-start | bytes 221192 | tf_op jit(solution)/shard_map/ppermute | solution.py:55
  58.1 3.5 %collective-permute-start.15 = (bf16[400,256]{1,0:T(8,128)(2,1)S(1)}, bf16[400,256]{1,0:T(8,128)(2,1)S(1)}, u32[]{:S(2)}, u32[]{:S(2)}) collective-permute-start(bf16[400,256]{1,0:T(8,128)(2,1)S(1)} %pack_own.1.own), channel_id=1, source_target_pairs={{0,4},{2,6},{4,0},{6,2},{8,12},{10,14},{12,8},{14,10},{16,20},{18,... | collective-permute-start | bytes 614408 | tf_op jit(solution)/shard_map/ppermute | solution.py:74
  61.6 3.1 %collective-permute-done.15.got = bf16[400,256]{1,0:T(8,128)(2,1)S(1)} collective-permute-done((bf16[400,256]{1,0:T(8,128)(2,1)S(1)}, bf16[400,256]{1,0:T(8,128)(2,1)S(1)}, u32[]{:S(2)}, u32[]{:S(2)}) %collective-permute-start.15) | collective-permute-done | bytes 204832 | tf_op jit(solution)/shard_map/ppermute | solution.py:74
  66.2 5.5 %collective-permute-done.17.rest_1_ = bf16[512,256]{1,0:T(8,128)(2,1)S(1)} collective-permute-done((bf16[512,256]{1,0:T(8,128)(2,1)S(1)}, bf16[512,256]{1,0:T(8,128)(2,1)S(1)}, u32[]{:S(2)}, u32[]{:S(2)}) %collective-permute-start.17) | collective-permute-done | bytes 262176 | tf_op jit(solution)/shard_map/ppermute | solution.py:63
  71.7 5.1 %collective-permute-start.18 = (bf16[656,256]{1,0:T(8,128)(2,1)S(1)}, bf16[656,256]{1,0:T(8,128)(2,1)S(1)}, u32[]{:S(2)}, u32[]{:S(2)}) collective-permute-start(bf16[656,256]{1,0:T(8,128)(2,1)S(1)} %collective-permute-done.16.rest_0_.pc), channel_id=1, source_target_pairs={{0,4},{2,6},{4,0},{6,2},{8,12},{10,14},{12,8},{14,10},{16,20},{18,... | collective-permute-start | bytes 1007624 | tf_op jit(solution)/shard_map/ppermute | solution.py:74
  78.0 9.8 %collective-permute-done.19.rest_1_ = bf16[512,256]{1,0:T(8,128)(2,1)S(1)} collective-permute-done((bf16[512,256]{1,0:T(8,128)(2,1)S(1)}, bf16[512,256]{1,0:T(8,128)(2,1)S(1)}, u32[]{:S(2)}, u32[]{:S(2)}) %collective-permute-start.19) | collective-permute-done | bytes 262176 | tf_op jit(solution)/shard_map/ppermute | solution.py:74
  90.5 6.5 %collective-permute-done.22.rest_0_ = bf16[512,256]{1,0:T(8,128)(2,1)S(1)} collective-permute-done((bf16[512,256]{1,0:T(8,128)(2,1)S(1)}, bf16[512,256]{1,0:T(8,128)(2,1)S(1)}, u32[]{:S(2)}, u32[]{:S(2)}) %collective-permute-start.22) | collective-permute-done | bytes 262176 | tf_op jit(solution)/shard_map/ppermute | solution.py:74
  99.8 2.0 %collective-permute-done.23.other = bf16[144,256]{1,0:T(8,128)(2,1)S(1)} collective-permute-done((bf16[144,256]{1,0:T(8,128)(2,1)S(1)}, bf16[144,256]{1,0:T(8,128)(2,1)S(1)}, u32[]{:S(2)}, u32[]{:S(2)}) %collective-permute-start.23) | collective-permute-done | bytes 73760 | tf_op jit(solution)/shard_map/ppermute | solution.py:63
  103.1 4.8 %collective-permute-start.24 = (bf16[4,256,256]{2,1,0:T(8,128)(2,1)S(1)}, bf16[4,256,256]{2,1,0:T(8,128)(2,1)S(1)}, u32[]{:S(2)}, u32[]{:S(2)}) collective-permute-start(bf16[4,256,256]{2,1,0:T(8,128)(2,1)S(1)} %get-tuple-element.101), channel_id=1, source_target_pairs={{0,32},{32,0},{64,96},{96,64},{128,160},{160,128},{192,224},{224,1... | collective-permute-start | bytes 1572872 | tf_op jit(solution)/shard_map/ppermute | solution.py:55
  107.9 1.5 %collective-permute-done.24.over = bf16[4,256,256]{2,1,0:T(8,128)(2,1)S(1)} collective-permute-done((bf16[4,256,256]{2,1,0:T(8,128)(2,1)S(1)}, bf16[4,256,256]{2,1,0:T(8,128)(2,1)S(1)}, u32[]{:S(2)}, u32[]{:S(2)}) %collective-permute-start.24) | collective-permute-done | bytes 524320 | tf_op jit(solution)/shard_map/ppermute | solution.py:55
  109.6 2.2 %collective-permute-start.26 = (bf16[400,256]{1,0:T(8,128)(2,1)S(1)}, bf16[400,256]{1,0:T(8,128)(2,1)S(1)}, u32[]{:S(2)}, u32[]{:S(2)}) collective-permute-start(bf16[400,256]{1,0:T(8,128)(2,1)S(1)} %get-tuple-element.105), channel_id=1, source_target_pairs={{0,128},{32,160},{64,192},{96,224},{128,0},{160,32},{192,64},{224,... | collective-permute-start | bytes 614408 | tf_op jit(solution)/shard_map/ppermute | solution.py:59
  111.8 1.9 %collective-permute-start.27 = (bf16[400,256]{1,0:T(8,128)(2,1)S(1)}, bf16[400,256]{1,0:T(8,128)(2,1)S(1)}, u32[]{:S(2)}, u32[]{:S(2)}) collective-permute-start(bf16[400,256]{1,0:T(8,128)(2,1)S(1)} %get-tuple-element.106), channel_id=1, source_target_pairs={{0,192},{32,224},{64,0},{96,32},{128,64},{160,96},{192,128},{224,1... | collective-permute-start | bytes 614408 | tf_op jit(solution)/shard_map/ppermute | solution.py:59
  113.8 3.8 %collective-permute-done.25.a = bf16[400,256]{1,0:T(8,128)(2,1)S(1)} collective-permute-done((bf16[400,256]{1,0:T(8,128)(2,1)S(1)}, bf16[400,256]{1,0:T(8,128)(2,1)S(1)}, u32[]{:S(2)}, u32[]{:S(2)}) %collective-permute-start.25) | collective-permute-done | bytes 204832 | tf_op jit(solution)/shard_map/ppermute | solution.py:59
  117.6 3.5 %collective-permute-done.26.b = bf16[400,256]{1,0:T(8,128)(2,1)S(1)} collective-permute-done((bf16[400,256]{1,0:T(8,128)(2,1)S(1)}, bf16[400,256]{1,0:T(8,128)(2,1)S(1)}, u32[]{:S(2)}, u32[]{:S(2)}) %collective-permute-start.26) | collective-permute-done | bytes 204832 | tf_op jit(solution)/shard_map/ppermute | solution.py:59
  121.9 1.6 %collective-permute-start.28 = (f32[136,256]{1,0:T(8,128)S(1)}, f32[136,256]{1,0:T(8,128)S(1)}, u32[]{:S(2)}, u32[]{:S(2)}) collective-permute-start(f32[136,256]{1,0:T(8,128)S(1)} %sum_terms.1.mine), channel_id=1, source_target_pairs={{0,32},{32,0},{64,96},{96,64},{128,160},{160,128},{192,224},{224,1... | collective-permute-start | bytes 417800 | tf_op jit(solution)/shard_map/ppermute | solution.py:55
  (76 shorter events, 29.8 us)
Async XLA Ops:
  0.6 12.1 %collective-permute-start.2 = (bf16[256,256]{1,0:T(8,128)(2,1)}, bf16[256,256]{1,0:T(8,128)(2,1)S(1)}, u32[]{:S(2)}, u32[]{:S(2)}) collective-permute-start(bf16[256,256]{1,0:T(8,128)(2,1)} %refs_0_.1), channel_id=1, source_target_pairs={{0,128},{32,160},{64,192},{96,224},{128,0},{160,32},{192,64},{224,... | collective-permute-start | bytes 393224 | tf_op jit(solution)/shard_map/ppermute | solution.py:59
  4.5 8.2 %collective-permute-start.1 = (bf16[256,256]{1,0:T(8,128)(2,1)}, bf16[256,256]{1,0:T(8,128)(2,1)S(1)}, u32[]{:S(2)}, u32[]{:S(2)}) collective-permute-start(bf16[256,256]{1,0:T(8,128)(2,1)} %refs_0_.1), channel_id=1, source_target_pairs={{0,192},{32,224},{64,0},{96,32},{128,64},{160,96},{192,128},{224,1... | collective-permute-start | bytes 393224 | tf_op jit(solution)/shard_map/ppermute | solution.py:59
  5.2 7.5 %collective-permute-start = (bf16[256,256]{1,0:T(8,128)(2,1)}, bf16[256,256]{1,0:T(8,128)(2,1)S(1)}, u32[]{:S(2)}, u32[]{:S(2)}) collective-permute-start(bf16[256,256]{1,0:T(8,128)(2,1)} %refs_0_.1), channel_id=1, source_target_pairs={{0,64},{32,96},{64,128},{96,160},{128,192},{160,224},{192,0},{224,... | collective-permute-start | bytes 393224 | tf_op jit(solution)/shard_map/ppermute | solution.py:59
  5.9 8.3 %collective-permute-start.3 = (bf16[256,256]{1,0:T(8,128)(2,1)}, bf16[256,256]{1,0:T(8,128)(2,1)S(1)}, u32[]{:S(2)}, u32[]{:S(2)}) collective-permute-start(bf16[256,256]{1,0:T(8,128)(2,1)} %refs_0_.1), channel_id=1, source_target_pairs={{0,32},{32,0},{64,96},{96,64},{128,160},{160,128},{192,224},{224,1... | collective-permute-start | bytes 393224 | tf_op jit(solution)/shard_map/ppermute | solution.py:55
  16.3 8.6 %collective-permute-start.7 = (bf16[4,256,256]{2,1,0:T(8,128)(2,1)S(1)}, bf16[4,256,256]{2,1,0:T(8,128)(2,1)S(1)}, u32[]{:S(2)}, u32[]{:S(2)}) collective-permute-start(bf16[4,256,256]{2,1,0:T(8,128)(2,1)S(1)} %forward_6.1), channel_id=1, source_target_pairs={{0,28},{2,30},{4,8},{6,10},{8,4},{10,6},{12,16},{14,18},{16,12},{1... | collective-permute-start | bytes 1572872 | tf_op jit(solution)/shard_map/ppermute | solution.py:74
  19.4 14.6 %collective-permute-start.10 = (bf16[2,256,256]{2,1,0:T(8,128)(2,1)S(1)}, bf16[2,256,256]{2,1,0:T(8,128)(2,1)S(1)}, u32[]{:S(2)}, u32[]{:S(2)}) collective-permute-start(bf16[2,256,256]{2,1,0:T(8,128)(2,1)S(1)} %get-tuple-element.79), channel_id=1, source_target_pairs={{0,28},{2,30},{4,8},{6,10},{8,4},{10,6},{12,16},{14,18},{16,12},{1... | collective-permute-start | bytes 786440 | tf_op jit(solution)/shard_map/ppermute | solution.py:74
  25.1 14.0 %collective-permute-start.9 = (bf16[2,256,256]{2,1,0:T(8,128)(2,1)S(1)}, bf16[2,256,256]{2,1,0:T(8,128)(2,1)S(1)}, u32[]{:S(2)}, u32[]{:S(2)}) collective-permute-start(bf16[2,256,256]{2,1,0:T(8,128)(2,1)S(1)} %get-tuple-element.76), channel_id=1, source_target_pairs={{0,6},{2,4},{4,2},{6,0},{8,14},{10,12},{12,10},{14,8},{16,22},{18,... | collective-permute-start | bytes 786440 | tf_op jit(solution)/shard_map/ppermute | solution.py:74
  33.9 6.5 %collective-permute-start.8 = (bf16[2,256,256]{2,1,0:T(8,128)(2,1)S(1)}, bf16[2,256,256]{2,1,0:T(8,128)(2,1)S(1)}, u32[]{:S(2)}, u32[]{:S(2)}) collective-permute-start(bf16[2,256,256]{2,1,0:T(8,128)(2,1)S(1)} %get-tuple-element.75), channel_id=1, source_target_pairs={{0,4},{2,6},{4,0},{6,2},{8,12},{10,14},{12,8},{14,10},{16,20},{18,... | collective-permute-start | bytes 786440 | tf_op jit(solution)/shard_map/ppermute | solution.py:74
  34.1 10.6 %collective-permute-start.11 = (bf16[2,256,256]{2,1,0:T(8,128)(2,1)S(1)}, bf16[2,256,256]{2,1,0:T(8,128)(2,1)S(1)}, u32[]{:S(2)}, u32[]{:S(2)}) collective-permute-start(bf16[2,256,256]{2,1,0:T(8,128)(2,1)S(1)} %relay_side.1), channel_id=1, source_target_pairs={{0,2},{2,0},{4,6},{6,4},{8,10},{10,8},{12,14},{14,12},{16,18},{18,... | collective-permute-start | bytes 786440 | tf_op jit(solution)/shard_map/ppermute | solution.py:63
  40.6 5.3 %collective-permute-start.12 = (bf16[2,256,256]{2,1,0:T(8,128)(2,1)S(1)}, bf16[2,256,256]{2,1,0:T(8,128)(2,1)S(1)}, u32[]{:S(2)}, u32[]{:S(2)}) collective-permute-start(bf16[2,256,256]{2,1,0:T(8,128)(2,1)S(1)} %relay_c.1), channel_id=1, source_target_pairs={{0,28},{2,30},{4,8},{6,10},{8,4},{10,6},{12,16},{14,18},{16,12},{1... | collective-permute-start | bytes 786440 | tf_op jit(solution)/shard_map/ppermute | solution.py:74
  45.9 5.3 %collective-permute-start.13 = (bf16[256,256]{1,0:T(8,128)(2,1)S(1)}, bf16[256,256]{1,0:T(8,128)(2,1)S(1)}, u32[]{:S(2)}, u32[]{:S(2)}) collective-permute-start(bf16[256,256]{1,0:T(8,128)(2,1)S(1)} %get-tuple-element.82), channel_id=1, source_target_pairs={{0,4},{2,6},{4,0},{6,2},{8,12},{10,14},{12,8},{14,10},{16,20},{18,... | collective-permute-start | bytes 393224 | tf_op jit(solution)/shard_map/ppermute | solution.py:74
  52.5 5.6 %collective-permute-start.14 = (bf16[144,256]{1,0:T(8,128)(2,1)S(1)}, bf16[144,256]{1,0:T(8,128)(2,1)S(1)}, u32[]{:S(2)}, u32[]{:S(2)}) collective-permute-start(bf16[144,256]{1,0:T(8,128)(2,1)S(1)} %get-tuple-element.88), channel_id=1, source_target_pairs={{0,32},{32,0},{64,96},{96,64},{128,160},{160,128},{192,224},{224,1... | collective-permute-start | bytes 221192 | tf_op jit(solution)/shard_map/ppermute | solution.py:55
  58.1 6.6 %collective-permute-start.15 = (bf16[400,256]{1,0:T(8,128)(2,1)S(1)}, bf16[400,256]{1,0:T(8,128)(2,1)S(1)}, u32[]{:S(2)}, u32[]{:S(2)}) collective-permute-start(bf16[400,256]{1,0:T(8,128)(2,1)S(1)} %pack_own.1.own), channel_id=1, source_target_pairs={{0,4},{2,6},{4,0},{6,2},{8,12},{10,14},{12,8},{14,10},{16,20},{18,... | collective-permute-start | bytes 614408 | tf_op jit(solution)/shard_map/ppermute | solution.py:74
  64.8 6.9 %collective-permute-start.16 = (bf16[656,256]{1,0:T(8,128)(2,1)S(1)}, bf16[656,256]{1,0:T(8,128)(2,1)S(1)}, u32[]{:S(2)}, u32[]{:S(2)}) collective-permute-start(bf16[656,256]{1,0:T(8,128)(2,1)S(1)} %pack_pair.1.rest_0_.pd), channel_id=1, source_target_pairs={{0,28},{2,30},{4,8},{6,10},{8,4},{10,6},{12,16},{14,18},{16,12},{1... | collective-permute-start | bytes 1007624 | tf_op jit(solution)/shard_map/ppermute | solution.py:74
  64.9 6.8 %collective-permute-start.17 = (bf16[512,256]{1,0:T(8,128)(2,1)S(1)}, bf16[512,256]{1,0:T(8,128)(2,1)S(1)}, u32[]{:S(2)}, u32[]{:S(2)}) collective-permute-start(bf16[512,256]{1,0:T(8,128)(2,1)S(1)} %slice.8), channel_id=1, source_target_pairs={{0,2},{2,0},{4,6},{6,4},{8,10},{10,8},{12,14},{14,12},{16,18},{18,... | collective-permute-start | bytes 786440 | tf_op jit(solution)/shard_map/ppermute | solution.py:63
  71.7 16.1 %collective-permute-start.18 = (bf16[656,256]{1,0:T(8,128)(2,1)S(1)}, bf16[656,256]{1,0:T(8,128)(2,1)S(1)}, u32[]{:S(2)}, u32[]{:S(2)}) collective-permute-start(bf16[656,256]{1,0:T(8,128)(2,1)S(1)} %collective-permute-done.16.rest_0_.pc), channel_id=1, source_target_pairs={{0,4},{2,6},{4,0},{6,2},{8,12},{10,14},{12,8},{14,10},{16,20},{18,... | collective-permute-start | bytes 1007624 | tf_op jit(solution)/shard_map/ppermute | solution.py:74
  76.8 11.0 %collective-permute-start.19 = (bf16[512,256]{1,0:T(8,128)(2,1)S(1)}, bf16[512,256]{1,0:T(8,128)(2,1)S(1)}, u32[]{:S(2)}, u32[]{:S(2)}) collective-permute-start(bf16[512,256]{1,0:T(8,128)(2,1)S(1)} %slice.7), channel_id=1, source_target_pairs={{0,6},{2,4},{4,2},{6,0},{8,14},{10,12},{12,10},{14,8},{16,22},{18,... | collective-permute-start | bytes 786440 | tf_op jit(solution)/shard_map/ppermute | solution.py:74
  87.9 9.1 %collective-permute-start.21 = (bf16[656,256]{1,0:T(8,128)(2,1)S(1)}, bf16[656,256]{1,0:T(8,128)(2,1)S(1)}, u32[]{:S(2)}, u32[]{:S(2)}) collective-permute-start(bf16[656,256]{1,0:T(8,128)(2,1)S(1)} %collective-permute-done.18.rest_0_.pb), channel_id=1, source_target_pairs={{0,28},{2,30},{4,8},{6,10},{8,4},{10,6},{12,16},{14,18},{16,12},{1... | collective-permute-start | bytes 1007624 | tf_op jit(solution)/shard_map/ppermute | solution.py:74
  87.9 9.1 %collective-permute-start.22 = (bf16[512,256]{1,0:T(8,128)(2,1)S(1)}, bf16[512,256]{1,0:T(8,128)(2,1)S(1)}, u32[]{:S(2)}, u32[]{:S(2)}) collective-permute-start(bf16[512,256]{1,0:T(8,128)(2,1)S(1)} %collective-permute-done.17.rest_1_), channel_id=1, source_target_pairs={{0,28},{2,30},{4,8},{6,10},{8,4},{10,6},{12,16},{14,18},{16,12},{1... | collective-permute-start | bytes 786440 | tf_op jit(solution)/shard_map/ppermute | solution.py:74
  89.3 10.5 %collective-permute-start.20 = (bf16[512,256]{1,0:T(8,128)(2,1)S(1)}, bf16[512,256]{1,0:T(8,128)(2,1)S(1)}, u32[]{:S(2)}, u32[]{:S(2)}) collective-permute-start(bf16[512,256]{1,0:T(8,128)(2,1)S(1)} %collective-permute-done.19.rest_1_), channel_id=1, source_target_pairs={{0,28},{2,30},{4,8},{6,10},{8,4},{10,6},{12,16},{14,18},{16,12},{1... | collective-permute-start | bytes 786440 | tf_op jit(solution)/shard_map/ppermute | solution.py:74
  103.1 6.4 %collective-permute-start.24 = (bf16[4,256,256]{2,1,0:T(8,128)(2,1)S(1)}, bf16[4,256,256]{2,1,0:T(8,128)(2,1)S(1)}, u32[]{:S(2)}, u32[]{:S(2)}) collective-permute-start(bf16[4,256,256]{2,1,0:T(8,128)(2,1)S(1)} %get-tuple-element.101), channel_id=1, source_target_pairs={{0,32},{32,0},{64,96},{96,64},{128,160},{160,128},{192,224},{224,1... | collective-permute-start | bytes 1572872 | tf_op jit(solution)/shard_map/ppermute | solution.py:55
  109.5 8.0 %collective-permute-start.25 = (bf16[400,256]{1,0:T(8,128)(2,1)S(1)}, bf16[400,256]{1,0:T(8,128)(2,1)S(1)}, u32[]{:S(2)}, u32[]{:S(2)}) collective-permute-start(bf16[400,256]{1,0:T(8,128)(2,1)S(1)} %get-tuple-element.104), channel_id=1, source_target_pairs={{0,64},{32,96},{64,128},{96,160},{128,192},{160,224},{192,0},{224,... | collective-permute-start | bytes 614408 | tf_op jit(solution)/shard_map/ppermute | solution.py:59
  109.6 11.5 %collective-permute-start.26 = (bf16[400,256]{1,0:T(8,128)(2,1)S(1)}, bf16[400,256]{1,0:T(8,128)(2,1)S(1)}, u32[]{:S(2)}, u32[]{:S(2)}) collective-permute-start(bf16[400,256]{1,0:T(8,128)(2,1)S(1)} %get-tuple-element.105), channel_id=1, source_target_pairs={{0,128},{32,160},{64,192},{96,224},{128,0},{160,32},{192,64},{224,... | collective-permute-start | bytes 614408 | tf_op jit(solution)/shard_map/ppermute | solution.py:59
  111.8 10.0 %collective-permute-start.27 = (bf16[400,256]{1,0:T(8,128)(2,1)S(1)}, bf16[400,256]{1,0:T(8,128)(2,1)S(1)}, u32[]{:S(2)}, u32[]{:S(2)}) collective-permute-start(bf16[400,256]{1,0:T(8,128)(2,1)S(1)} %get-tuple-element.106), channel_id=1, source_target_pairs={{0,192},{32,224},{64,0},{96,32},{128,64},{160,96},{192,128},{224,1... | collective-permute-start | bytes 614408 | tf_op jit(solution)/shard_map/ppermute | solution.py:59
  (10 other events, 50.4 us)

commit v10 on v9

--- a/solution.py
+++ b/solution.py
@@ -410,10 +410,10 @@
     pair_c, side_d, total = barrier((pair_c, side_d, total))
     side_b, pair_b, side_c = swap_z(pair_c[:512], 1, 1), swap_z(pair_c, 1), swap_z(side_d, -1)
     total = backward(1, (pair_c, side_d), (total,), running)
-    pair_b, side_b, total = barrier((pair_b, side_b, total))
+    pair_b, side_b, side_c, total = barrier((pair_b, side_b, side_c, total))
     pair_a, side_a = swap_z(pair_b, -1), swap_z(side_b, -1)
     total = backward(3, (pair_b, side_b), (total,), running)
-    pair_a, side_c, total = barrier((pair_a, side_c, total))
+    pair_a, total = barrier((pair_a, total))
     plane = call(
         plane_terms_body, "plane_terms", half, (pair_d, pair_a, pair_c, pair_b), moved=2**19
     )

time: 125 us -> 124 us (level)
  waiting for transfers between devices: 57.7 us -> 54.8 us
    ppermute x13, starting transfers between devices: 23 us -> 19.5 us  [swap_z(): return lax.ppermute(a, ('row', 'col'), pairs)]
    ppermute x13, waiting for transfers between devices: 35.5 us -> 32.1 us  [swap_z(): return lax.ppermute(a, ('row', 'col'), pairs)]
    ppermute x3, starting transfers between devices: 1.08 us -> 4.39 us  [to_x(): return lax.ppermute(a, 'col', [(i, i ^ 1) for i in range(2 * NZ)])]
  transfers between devices with their start and end apart: 29 -> 29, of which waited for: 21 -> 22; matrix products, arithmetic and copies ran while one was open for 1% -> 1% of each run, Pallas kernels for 8% -> 8%
where the time goes in v10:
time: 124 us
  waiting for transfers between devices  54.8 us (44%)
  starting transfers between devices  48.4 us (39%)
  Pallas kernels  14.9 us (12%)
  local copies, waits for them, and re-layouts  2.85 us (2%)
  between operations  1.54 us (1%)
  other arithmetic  1.34 us (1%)
    ppermute x13, waiting for transfers between devices, swap_z(): return lax.ppermute(a, ('row', 'col'), pairs)  32.1 us
    ppermute x13, starting transfers between devices, swap_z(): return lax.ppermute(a, ('row', 'col'), pairs)  19.5 us
    ppermute x7, starting transfers between devices, to_core(): return lax.ppermute(a, 'row', [(i, i ^ 1) for i in range(2 * NY)])  15.1 us
    pallas_call x24, Pallas kernels, call(): pl.pallas_call(body, name=name, out_shape=out_shape, in_specs=specs or [s...  14.9 us
    ppermute x3, waiting for transfers between devices, to_x(): return lax.ppermute(a, 'col', [(i, i ^ 1) for i in range(2 * NZ)])  11 us
    ppermute x6, starting transfers between devices, to_y(): lax.ppermute(a, 'row', [(i, (i + 2 * step) % (2 * NY)) for i in range(2 *...  9.43 us
    ppermute x6, waiting for transfers between devices, to_y(): lax.ppermute(a, 'row', [(i, (i + 2 * step) % (2 * NY)) for i in range(2 *...  8.13 us
    ppermute x3, starting transfers between devices, to_x(): return lax.ppermute(a, 'col', [(i, i ^ 1) for i in range(2 * NZ)])  4.39 us
  transfers between devices with their start and end apart: 29, of which 22 were waited for; matrix products, arithmetic and copies ran while one was open for 1% of the time, Pallas kernels for 8%

profile of v10, /device:TPU:1, one launch (start us, length us, event | category | flops | bytes accessed | tf_op | source)
XLA Modules:
  0.0 123.8 jit_solution(15917284107372656082)
XLA Ops:
  0.6 2.2 %collective-permute-start = (bf16[256,256]{1,0:T(8,128)(2,1)}, bf16[256,256]{1,0:T(8,128)(2,1)S(1)}, u32[]{:S(2)}, u32[]{:S(2)}) collective-permute-start(bf16[256,256]{1,0:T(8,128)(2,1)} %refs_0_.1), channel_id=1, source_target_pairs={{0,64},{32,96},{64,128},{96,160},{128,192},{160,224},{192,0},{224,... | collective-permute-start | bytes 393224 | tf_op jit(solution)/shard_map/ppermute | solution.py:59
  9.2 2.8 %copy-done = bf16[1,1,192,128,128]{4,3,2,1,0:T(8,128)(2,1)S(1)} copy-done((bf16[1,1,192,128,128]{4,3,2,1,0:T(8,128)(2,1)S(1)}, bf16[1,1,192,128,128]{4,3,2,1,0:T(8,128)(2,1)}, u32[]{:S(2)}) %copy-start) | copy-done | bytes 6291480
  19.4 5.7 %collective-permute-done.7.got = bf16[4,256,256]{2,1,0:T(8,128)(2,1)S(1)} collective-permute-done((bf16[4,256,256]{2,1,0:T(8,128)(2,1)S(1)}, bf16[4,256,256]{2,1,0:T(8,128)(2,1)S(1)}, u32[]{:S(2)}, u32[]{:S(2)}) %collective-permute-start.7) | collective-permute-done | bytes 524320 | tf_op jit(solution)/shard_map/ppermute | solution.py:74
  26.4 7.0 %collective-permute-start.8 = (bf16[2,256,256]{2,1,0:T(8,128)(2,1)S(1)}, bf16[2,256,256]{2,1,0:T(8,128)(2,1)S(1)}, u32[]{:S(2)}, u32[]{:S(2)}) collective-permute-start(bf16[2,256,256]{2,1,0:T(8,128)(2,1)S(1)} %get-tuple-element.75), channel_id=1, source_target_pairs={{0,4},{2,6},{4,0},{6,2},{8,12},{10,14},{12,8},{14,10},{16,20},{18,... | collective-permute-start | bytes 786440 | tf_op jit(solution)/shard_map/ppermute | solution.py:74
  33.8 2.6 %collective-permute-start.11 = (bf16[2,256,256]{2,1,0:T(8,128)(2,1)S(1)}, bf16[2,256,256]{2,1,0:T(8,128)(2,1)S(1)}, u32[]{:S(2)}, u32[]{:S(2)}) collective-permute-start(bf16[2,256,256]{2,1,0:T(8,128)(2,1)S(1)} %relay_side.1), channel_id=1, source_target_pairs={{0,2},{2,0},{4,6},{6,4},{8,10},{10,8},{12,14},{14,12},{16,18},{18,... | collective-permute-start | bytes 786440 | tf_op jit(solution)/shard_map/ppermute | solution.py:63
  37.2 6.7 %collective-permute-done.9.rest_1_ = bf16[2,256,256]{2,1,0:T(8,128)(2,1)S(1)} collective-permute-done((bf16[2,256,256]{2,1,0:T(8,128)(2,1)S(1)}, bf16[2,256,256]{2,1,0:T(8,128)(2,1)S(1)}, u32[]{:S(2)}, u32[]{:S(2)}) %collective-permute-start.9) | collective-permute-done | bytes 262176 | tf_op jit(solution)/shard_map/ppermute | solution.py:74
  45.1 2.6 %collective-permute-done.11.over = bf16[2,256,256]{2,1,0:T(8,128)(2,1)S(1)} collective-permute-done((bf16[2,256,256]{2,1,0:T(8,128)(2,1)S(1)}, bf16[2,256,256]{2,1,0:T(8,128)(2,1)S(1)}, u32[]{:S(2)}, u32[]{:S(2)}) %collective-permute-start.11) | collective-permute-done | bytes 262176 | tf_op jit(solution)/shard_map/ppermute | solution.py:63
  49.4 2.4 %collective-permute-start.13 = (bf16[256,256]{1,0:T(8,128)(2,1)S(1)}, bf16[256,256]{1,0:T(8,128)(2,1)S(1)}, u32[]{:S(2)}, u32[]{:S(2)}) collective-permute-start(bf16[256,256]{1,0:T(8,128)(2,1)S(1)} %get-tuple-element.82), channel_id=1, source_target_pairs={{0,4},{2,6},{4,0},{6,2},{8,12},{10,14},{12,8},{14,10},{16,20},{18,... | collective-permute-start | bytes 393224 | tf_op jit(solution)/shard_map/ppermute | solution.py:74
  51.8 2.8 %collective-permute-done.13.got = bf16[256,256]{1,0:T(8,128)(2,1)S(1)} collective-permute-done((bf16[256,256]{1,0:T(8,128)(2,1)S(1)}, bf16[256,256]{1,0:T(8,128)(2,1)S(1)}, u32[]{:S(2)}, u32[]{:S(2)}) %collective-permute-start.13) | collective-permute-done | bytes 131104 | tf_op jit(solution)/shard_map/ppermute | solution.py:74
  55.9 4.4 %collective-permute-start.14 = (bf16[144,256]{1,0:T(8,128)(2,1)S(1)}, bf16[144,256]{1,0:T(8,128)(2,1)S(1)}, u32[]{:S(2)}, u32[]{:S(2)}) collective-permute-start(bf16[144,256]{1,0:T(8,128)(2,1)S(1)} %get-tuple-element.88), channel_id=1, source_target_pairs={{0,32},{32,0},{64,96},{96,64},{128,160},{160,128},{192,224},{224,1... | collective-permute-start | bytes 221192 | tf_op jit(solution)/shard_map/ppermute | solution.py:55
  61.9 5.3 %collective-permute-done.15.got = bf16[400,256]{1,0:T(8,128)(2,1)S(1)} collective-permute-done((bf16[400,256]{1,0:T(8,128)(2,1)S(1)}, bf16[400,256]{1,0:T(8,128)(2,1)S(1)}, u32[]{:S(2)}, u32[]{:S(2)}) %collective-permute-start.15) | collective-permute-done | bytes 204832 | tf_op jit(solution)/shard_map/ppermute | solution.py:74
  69.0 6.6 %collective-permute-done.17.rest_1_ = bf16[512,256]{1,0:T(8,128)(2,1)S(1)} collective-permute-done((bf16[512,256]{1,0:T(8,128)(2,1)S(1)}, bf16[512,256]{1,0:T(8,128)(2,1)S(1)}, u32[]{:S(2)}, u32[]{:S(2)}) %collective-permute-start.17) | collective-permute-done | bytes 262176 | tf_op jit(solution)/shard_map/ppermute | solution.py:63
  75.6 2.2 %collective-permute-start.19 = (bf16[512,256]{1,0:T(8,128)(2,1)S(1)}, bf16[512,256]{1,0:T(8,128)(2,1)S(1)}, u32[]{:S(2)}, u32[]{:S(2)}) collective-permute-start(bf16[512,256]{1,0:T(8,128)(2,1)S(1)} %slice.7), channel_id=1, source_target_pairs={{0,6},{2,4},{4,2},{6,0},{8,14},{10,12},{12,10},{14,8},{16,22},{18,... | collective-permute-start | bytes 786440 | tf_op jit(solution)/shard_map/ppermute | solution.py:74
  77.9 2.2 %collective-permute-start.20 = (bf16[512,256]{1,0:T(8,128)(2,1)S(1)}, bf16[512,256]{1,0:T(8,128)(2,1)S(1)}, u32[]{:S(2)}, u32[]{:S(2)}) collective-permute-start(bf16[512,256]{1,0:T(8,128)(2,1)S(1)} %collective-permute-done.17.rest_1_), channel_id=1, source_target_pairs={{0,28},{2,30},{4,8},{6,10},{8,4},{10,6},{12,16},{14,18},{16,12},{1... | collective-permute-start | bytes 786440 | tf_op jit(solution)/shard_map/ppermute | solution.py:74
  81.3 3.8 %collective-permute-done.19.rest_1_ = bf16[512,256]{1,0:T(8,128)(2,1)S(1)} collective-permute-done((bf16[512,256]{1,0:T(8,128)(2,1)S(1)}, bf16[512,256]{1,0:T(8,128)(2,1)S(1)}, u32[]{:S(2)}, u32[]{:S(2)}) %collective-permute-start.19) | collective-permute-done | bytes 262176 | tf_op jit(solution)/shard_map/ppermute | solution.py:74
  85.1 1.7 %collective-permute-done.20.rest_0_ = bf16[512,256]{1,0:T(8,128)(2,1)S(1)} collective-permute-done((bf16[512,256]{1,0:T(8,128)(2,1)S(1)}, bf16[512,256]{1,0:T(8,128)(2,1)S(1)}, u32[]{:S(2)}, u32[]{:S(2)}) %collective-permute-start.20) | collective-permute-done | bytes 262176 | tf_op jit(solution)/shard_map/ppermute | solution.py:74
  86.8 3.2 %collective-permute-start.22 = (bf16[656,256]{1,0:T(8,128)(2,1)S(1)}, bf16[656,256]{1,0:T(8,128)(2,1)S(1)}, u32[]{:S(2)}, u32[]{:S(2)}) collective-permute-start(bf16[656,256]{1,0:T(8,128)(2,1)S(1)} %collective-permute-done.18.rest_0_.pb), channel_id=1, source_target_pairs={{0,28},{2,30},{4,8},{6,10},{8,4},{10,6},{12,16},{14,18},{16,12},{1... | collective-permute-start | bytes 1007624 | tf_op jit(solution)/shard_map/ppermute | solution.py:74
  91.4 3.2 %collective-permute-done.22.rest_1_.pa = bf16[656,256]{1,0:T(8,128)(2,1)S(1)} collective-permute-done((bf16[656,256]{1,0:T(8,128)(2,1)S(1)}, bf16[656,256]{1,0:T(8,128)(2,1)S(1)}, u32[]{:S(2)}, u32[]{:S(2)}) %collective-permute-start.22) | collective-permute-done | bytes 335904 | tf_op jit(solution)/shard_map/ppermute | solution.py:74
  97.7 1.7 %collective-permute-done.23.other = bf16[144,256]{1,0:T(8,128)(2,1)S(1)} collective-permute-done((bf16[144,256]{1,0:T(8,128)(2,1)S(1)}, bf16[144,256]{1,0:T(8,128)(2,1)S(1)}, u32[]{:S(2)}, u32[]{:S(2)}) %collective-permute-start.23) | collective-permute-done | bytes 73760 | tf_op jit(solution)/shard_map/ppermute | solution.py:63
  100.6 5.9 %collective-permute-start.24 = (bf16[4,256,256]{2,1,0:T(8,128)(2,1)S(1)}, bf16[4,256,256]{2,1,0:T(8,128)(2,1)S(1)}, u32[]{:S(2)}, u32[]{:S(2)}) collective-permute-start(bf16[4,256,256]{2,1,0:T(8,128)(2,1)S(1)} %get-tuple-element.101), channel_id=1, source_target_pairs={{0,32},{32,0},{64,96},{96,64},{128,160},{160,128},{192,224},{224,1... | collective-permute-start | bytes 1572872 | tf_op jit(solution)/shard_map/ppermute | solution.py:55
  110.4 2.0 %collective-permute-start.27 = (bf16[400,256]{1,0:T(8,128)(2,1)S(1)}, bf16[400,256]{1,0:T(8,128)(2,1)S(1)}, u32[]{:S(2)}, u32[]{:S(2)}) collective-permute-start(bf16[400,256]{1,0:T(8,128)(2,1)S(1)} %get-tuple-element.106), channel_id=1, source_target_pairs={{0,192},{32,224},{64,0},{96,32},{128,64},{160,96},{192,128},{224,1... | collective-permute-start | bytes 614408 | tf_op jit(solution)/shard_map/ppermute | solution.py:59
  112.3 3.8 %collective-permute-done.25.a = bf16[400,256]{1,0:T(8,128)(2,1)S(1)} collective-permute-done((bf16[400,256]{1,0:T(8,128)(2,1)S(1)}, bf16[400,256]{1,0:T(8,128)(2,1)S(1)}, u32[]{:S(2)}, u32[]{:S(2)}) %collective-permute-start.25) | collective-permute-done | bytes 204832 | tf_op jit(solution)/shard_map/ppermute | solution.py:59
  116.2 3.6 %collective-permute-done.26.b = bf16[400,256]{1,0:T(8,128)(2,1)S(1)} collective-permute-done((bf16[400,256]{1,0:T(8,128)(2,1)S(1)}, bf16[400,256]{1,0:T(8,128)(2,1)S(1)}, u32[]{:S(2)}, u32[]{:S(2)}) %collective-permute-start.26) | collective-permute-done | bytes 204832 | tf_op jit(solution)/shard_map/ppermute | solution.py:59
  120.5 1.6 %collective-permute-start.28 = (f32[136,256]{1,0:T(8,128)S(1)}, f32[136,256]{1,0:T(8,128)S(1)}, u32[]{:S(2)}, u32[]{:S(2)}) collective-permute-start(f32[136,256]{1,0:T(8,128)S(1)} %sum_terms.1.mine), channel_id=1, source_target_pairs={{0,32},{32,0},{64,96},{96,64},{128,160},{160,128},{192,224},{224,1... | collective-permute-start | bytes 417800 | tf_op jit(solution)/shard_map/ppermute | solution.py:55
  (76 shorter events, 36.2 us)
Async XLA Ops:
  0.6 12.0 %collective-permute-start = (bf16[256,256]{1,0:T(8,128)(2,1)}, bf16[256,256]{1,0:T(8,128)(2,1)S(1)}, u32[]{:S(2)}, u32[]{:S(2)}) collective-permute-start(bf16[256,256]{1,0:T(8,128)(2,1)} %refs_0_.1), channel_id=1, source_target_pairs={{0,64},{32,96},{64,128},{96,160},{128,192},{160,224},{192,0},{224,... | collective-permute-start | bytes 393224 | tf_op jit(solution)/shard_map/ppermute | solution.py:59
  2.8 9.8 %collective-permute-start.1 = (bf16[256,256]{1,0:T(8,128)(2,1)}, bf16[256,256]{1,0:T(8,128)(2,1)S(1)}, u32[]{:S(2)}, u32[]{:S(2)}) collective-permute-start(bf16[256,256]{1,0:T(8,128)(2,1)} %refs_0_.1), channel_id=1, source_target_pairs={{0,192},{32,224},{64,0},{96,32},{128,64},{160,96},{192,128},{224,1... | collective-permute-start | bytes 393224 | tf_op jit(solution)/shard_map/ppermute | solution.py:59
  4.4 8.3 %collective-permute-start.2 = (bf16[256,256]{1,0:T(8,128)(2,1)}, bf16[256,256]{1,0:T(8,128)(2,1)S(1)}, u32[]{:S(2)}, u32[]{:S(2)}) collective-permute-start(bf16[256,256]{1,0:T(8,128)(2,1)} %refs_0_.1), channel_id=1, source_target_pairs={{0,128},{32,160},{64,192},{96,224},{128,0},{160,32},{192,64},{224,... | collective-permute-start | bytes 393224 | tf_op jit(solution)/shard_map/ppermute | solution.py:59
  5.9 8.5 %collective-permute-start.3 = (bf16[256,256]{1,0:T(8,128)(2,1)}, bf16[256,256]{1,0:T(8,128)(2,1)S(1)}, u32[]{:S(2)}, u32[]{:S(2)}) collective-permute-start(bf16[256,256]{1,0:T(8,128)(2,1)} %refs_0_.1), channel_id=1, source_target_pairs={{0,32},{32,0},{64,96},{96,64},{128,160},{160,128},{192,224},{224,1... | collective-permute-start | bytes 393224 | tf_op jit(solution)/shard_map/ppermute | solution.py:55
  16.7 8.4 %collective-permute-start.7 = (bf16[4,256,256]{2,1,0:T(8,128)(2,1)S(1)}, bf16[4,256,256]{2,1,0:T(8,128)(2,1)S(1)}, u32[]{:S(2)}, u32[]{:S(2)}) collective-permute-start(bf16[4,256,256]{2,1,0:T(8,128)(2,1)S(1)} %forward_6.1), channel_id=1, source_target_pairs={{0,28},{2,30},{4,8},{6,10},{8,4},{10,6},{12,16},{14,18},{16,12},{1... | collective-permute-start | bytes 1572872 | tf_op jit(solution)/shard_map/ppermute | solution.py:74
  18.8 14.9 %collective-permute-start.10 = (bf16[2,256,256]{2,1,0:T(8,128)(2,1)S(1)}, bf16[2,256,256]{2,1,0:T(8,128)(2,1)S(1)}, u32[]{:S(2)}, u32[]{:S(2)}) collective-permute-start(bf16[2,256,256]{2,1,0:T(8,128)(2,1)S(1)} %get-tuple-element.79), channel_id=1, source_target_pairs={{0,28},{2,30},{4,8},{6,10},{8,4},{10,6},{12,16},{14,18},{16,12},{1... | collective-permute-start | bytes 786440 | tf_op jit(solution)/shard_map/ppermute | solution.py:74
  26.4 10.8 %collective-permute-start.8 = (bf16[2,256,256]{2,1,0:T(8,128)(2,1)S(1)}, bf16[2,256,256]{2,1,0:T(8,128)(2,1)S(1)}, u32[]{:S(2)}, u32[]{:S(2)}) collective-permute-start(bf16[2,256,256]{2,1,0:T(8,128)(2,1)S(1)} %get-tuple-element.75), channel_id=1, source_target_pairs={{0,4},{2,6},{4,0},{6,2},{8,12},{10,14},{12,8},{14,10},{16,20},{18,... | collective-permute-start | bytes 786440 | tf_op jit(solution)/shard_map/ppermute | solution.py:74
  33.4 10.4 %collective-permute-start.9 = (bf16[2,256,256]{2,1,0:T(8,128)(2,1)S(1)}, bf16[2,256,256]{2,1,0:T(8,128)(2,1)S(1)}, u32[]{:S(2)}, u32[]{:S(2)}) collective-permute-start(bf16[2,256,256]{2,1,0:T(8,128)(2,1)S(1)} %get-tuple-element.76), channel_id=1, source_target_pairs={{0,6},{2,4},{4,2},{6,0},{8,14},{10,12},{12,10},{14,8},{16,22},{18,... | collective-permute-start | bytes 786440 | tf_op jit(solution)/shard_map/ppermute | solution.py:74
  33.8 13.9 %collective-permute-start.11 = (bf16[2,256,256]{2,1,0:T(8,128)(2,1)S(1)}, bf16[2,256,256]{2,1,0:T(8,128)(2,1)S(1)}, u32[]{:S(2)}, u32[]{:S(2)}) collective-permute-start(bf16[2,256,256]{2,1,0:T(8,128)(2,1)S(1)} %relay_side.1), channel_id=1, source_target_pairs={{0,2},{2,0},{4,6},{6,4},{8,10},{10,8},{12,14},{14,12},{16,18},{18,... | collective-permute-start | bytes 786440 | tf_op jit(solution)/shard_map/ppermute | solution.py:63
  44.0 5.3 %collective-permute-start.12 = (bf16[2,256,256]{2,1,0:T(8,128)(2,1)S(1)}, bf16[2,256,256]{2,1,0:T(8,128)(2,1)S(1)}, u32[]{:S(2)}, u32[]{:S(2)}) collective-permute-start(bf16[2,256,256]{2,1,0:T(8,128)(2,1)S(1)} %relay_c.1), channel_id=1, source_target_pairs={{0,28},{2,30},{4,8},{6,10},{8,4},{10,6},{12,16},{14,18},{16,12},{1... | collective-permute-start | bytes 786440 | tf_op jit(solution)/shard_map/ppermute | solution.py:74
  49.4 5.3 %collective-permute-start.13 = (bf16[256,256]{1,0:T(8,128)(2,1)S(1)}, bf16[256,256]{1,0:T(8,128)(2,1)S(1)}, u32[]{:S(2)}, u32[]{:S(2)}) collective-permute-start(bf16[256,256]{1,0:T(8,128)(2,1)S(1)} %get-tuple-element.82), channel_id=1, source_target_pairs={{0,4},{2,6},{4,0},{6,2},{8,12},{10,14},{12,8},{14,10},{16,20},{18,... | collective-permute-start | bytes 393224 | tf_op jit(solution)/shard_map/ppermute | solution.py:74
  55.9 5.3 %collective-permute-start.14 = (bf16[144,256]{1,0:T(8,128)(2,1)S(1)}, bf16[144,256]{1,0:T(8,128)(2,1)S(1)}, u32[]{:S(2)}, u32[]{:S(2)}) collective-permute-start(bf16[144,256]{1,0:T(8,128)(2,1)S(1)} %get-tuple-element.88), channel_id=1, source_target_pairs={{0,32},{32,0},{64,96},{96,64},{128,160},{160,128},{192,224},{224,1... | collective-permute-start | bytes 221192 | tf_op jit(solution)/shard_map/ppermute | solution.py:55
  61.2 5.9 %collective-permute-start.15 = (bf16[400,256]{1,0:T(8,128)(2,1)S(1)}, bf16[400,256]{1,0:T(8,128)(2,1)S(1)}, u32[]{:S(2)}, u32[]{:S(2)}) collective-permute-start(bf16[400,256]{1,0:T(8,128)(2,1)S(1)} %pack_own.1.own), channel_id=1, source_target_pairs={{0,4},{2,6},{4,0},{6,2},{8,12},{10,14},{12,8},{14,10},{16,20},{18,... | collective-permute-start | bytes 614408 | tf_op jit(solution)/shard_map/ppermute | solution.py:74
  67.2 8.4 %collective-permute-start.16 = (bf16[656,256]{1,0:T(8,128)(2,1)S(1)}, bf16[656,256]{1,0:T(8,128)(2,1)S(1)}, u32[]{:S(2)}, u32[]{:S(2)}) collective-permute-start(bf16[656,256]{1,0:T(8,128)(2,1)S(1)} %pack_pair.1.rest_0_.pd), channel_id=1, source_target_pairs={{0,28},{2,30},{4,8},{6,10},{8,4},{10,6},{12,16},{14,18},{16,12},{1... | collective-permute-start | bytes 1007624 | tf_op jit(solution)/shard_map/ppermute | solution.py:74
  67.3 8.3 %collective-permute-start.17 = (bf16[512,256]{1,0:T(8,128)(2,1)S(1)}, bf16[512,256]{1,0:T(8,128)(2,1)S(1)}, u32[]{:S(2)}, u32[]{:S(2)}) collective-permute-start(bf16[512,256]{1,0:T(8,128)(2,1)S(1)} %slice.8), channel_id=1, source_target_pairs={{0,2},{2,0},{4,6},{6,4},{8,10},{10,8},{12,14},{14,12},{16,18},{18,... | collective-permute-start | bytes 786440 | tf_op jit(solution)/shard_map/ppermute | solution.py:63
  75.6 11.2 %collective-permute-start.18 = (bf16[656,256]{1,0:T(8,128)(2,1)S(1)}, bf16[656,256]{1,0:T(8,128)(2,1)S(1)}, u32[]{:S(2)}, u32[]{:S(2)}) collective-permute-start(bf16[656,256]{1,0:T(8,128)(2,1)S(1)} %collective-permute-done.16.rest_0_.pc), channel_id=1, source_target_pairs={{0,4},{2,6},{4,0},{6,2},{8,12},{10,14},{12,8},{14,10},{16,20},{18,... | collective-permute-start | bytes 1007624 | tf_op jit(solution)/shard_map/ppermute | solution.py:74
  75.6 9.5 %collective-permute-start.19 = (bf16[512,256]{1,0:T(8,128)(2,1)S(1)}, bf16[512,256]{1,0:T(8,128)(2,1)S(1)}, u32[]{:S(2)}, u32[]{:S(2)}) collective-permute-start(bf16[512,256]{1,0:T(8,128)(2,1)S(1)} %slice.7), channel_id=1, source_target_pairs={{0,6},{2,4},{4,2},{6,0},{8,14},{10,12},{12,10},{14,8},{16,22},{18,... | collective-permute-start | bytes 786440 | tf_op jit(solution)/shard_map/ppermute | solution.py:74
  77.9 8.9 %collective-permute-start.20 = (bf16[512,256]{1,0:T(8,128)(2,1)S(1)}, bf16[512,256]{1,0:T(8,128)(2,1)S(1)}, u32[]{:S(2)}, u32[]{:S(2)}) collective-permute-start(bf16[512,256]{1,0:T(8,128)(2,1)S(1)} %collective-permute-done.17.rest_1_), channel_id=1, source_target_pairs={{0,28},{2,30},{4,8},{6,10},{8,4},{10,6},{12,16},{14,18},{16,12},{1... | collective-permute-start | bytes 786440 | tf_op jit(solution)/shard_map/ppermute | solution.py:74
  86.8 7.7 %collective-permute-start.22 = (bf16[656,256]{1,0:T(8,128)(2,1)S(1)}, bf16[656,256]{1,0:T(8,128)(2,1)S(1)}, u32[]{:S(2)}, u32[]{:S(2)}) collective-permute-start(bf16[656,256]{1,0:T(8,128)(2,1)S(1)} %collective-permute-done.18.rest_0_.pb), channel_id=1, source_target_pairs={{0,28},{2,30},{4,8},{6,10},{8,4},{10,6},{12,16},{14,18},{16,12},{1... | collective-permute-start | bytes 1007624 | tf_op jit(solution)/shard_map/ppermute | solution.py:74
  90.0 7.7 %collective-permute-start.21 = (bf16[512,256]{1,0:T(8,128)(2,1)S(1)}, bf16[512,256]{1,0:T(8,128)(2,1)S(1)}, u32[]{:S(2)}, u32[]{:S(2)}) collective-permute-start(bf16[512,256]{1,0:T(8,128)(2,1)S(1)} %collective-permute-done.19.rest_1_), channel_id=1, source_target_pairs={{0,28},{2,30},{4,8},{6,10},{8,4},{10,6},{12,16},{14,18},{16,12},{1... | collective-permute-start | bytes 786440 | tf_op jit(solution)/shard_map/ppermute | solution.py:74
  100.6 7.4 %collective-permute-start.24 = (bf16[4,256,256]{2,1,0:T(8,128)(2,1)S(1)}, bf16[4,256,256]{2,1,0:T(8,128)(2,1)S(1)}, u32[]{:S(2)}, u32[]{:S(2)}) collective-permute-start(bf16[4,256,256]{2,1,0:T(8,128)(2,1)S(1)} %get-tuple-element.101), channel_id=1, source_target_pairs={{0,32},{32,0},{64,96},{96,64},{128,160},{160,128},{192,224},{224,1... | collective-permute-start | bytes 1572872 | tf_op jit(solution)/shard_map/ppermute | solution.py:55
  108.2 8.0 %collective-permute-start.25 = (bf16[400,256]{1,0:T(8,128)(2,1)S(1)}, bf16[400,256]{1,0:T(8,128)(2,1)S(1)}, u32[]{:S(2)}, u32[]{:S(2)}) collective-permute-start(bf16[400,256]{1,0:T(8,128)(2,1)S(1)} %get-tuple-element.104), channel_id=1, source_target_pairs={{0,64},{32,96},{64,128},{96,160},{128,192},{160,224},{192,0},{224,... | collective-permute-start | bytes 614408 | tf_op jit(solution)/shard_map/ppermute | solution.py:59
  109.0 10.8 %collective-permute-start.26 = (bf16[400,256]{1,0:T(8,128)(2,1)S(1)}, bf16[400,256]{1,0:T(8,128)(2,1)S(1)}, u32[]{:S(2)}, u32[]{:S(2)}) collective-permute-start(bf16[400,256]{1,0:T(8,128)(2,1)S(1)} %get-tuple-element.105), channel_id=1, source_target_pairs={{0,128},{32,160},{64,192},{96,224},{128,0},{160,32},{192,64},{224,... | collective-permute-start | bytes 614408 | tf_op jit(solution)/shard_map/ppermute | solution.py:59
  110.4 10.1 %collective-permute-start.27 = (bf16[400,256]{1,0:T(8,128)(2,1)S(1)}, bf16[400,256]{1,0:T(8,128)(2,1)S(1)}, u32[]{:S(2)}, u32[]{:S(2)}) collective-permute-start(bf16[400,256]{1,0:T(8,128)(2,1)S(1)} %get-tuple-element.106), channel_id=1, source_target_pairs={{0,192},{32,224},{64,0},{96,32},{128,64},{160,96},{192,128},{224,1... | collective-permute-start | bytes 614408 | tf_op jit(solution)/shard_map/ppermute | solution.py:59
  (10 other events, 50.8 us)

commit v11 on v10

--- a/solution.py
+++ b/solution.py
@@ -61,6 +61,15 @@
 
 def to_x(a):
     return lax.ppermute(a, "col", [(i, i ^ 1) for i in range(2 * NZ)])
+
+
+def swap_y(a, side):
+    pairs = []
+    for row in range(2 * NY):
+        y, core = divmod(row, 2)
+        step = side if (y + core) % 2 == 0 else -side
+        pairs.append((row, (y + step) % NY * 2 + core))
+    return lax.ppermute(a, "row", pairs)
 
 
 def swap_z(a, side, across=0):
@@ -243,30 +252,31 @@
         place(over.at[3], total, 1, BF16)
 
 
-def plane_terms_body(pd, pa, pc, pb, out):
-    sums = slice(512, 656)
-    plane = add_rows(pd[sums], pa[sums]).astype(F32) + add_rows(pc[sums], pb[sums]).astype(F32)
-    out[...] = plane.astype(BF16)
-
-
-def back_relay_body(kept, over, plane, other, out_a, out_b, out_c, terms):
-    terms[...] = add_rows(plane[...], other[...])
-    for k, out in enumerate((out_a, out_b, out_c)):
-        out[0:256] = (kept[k] + over[k].astype(F32)).astype(BF16)
-        out[256:400] = terms[...]
-
-
-def sum_terms_body(scale, own, a, b, c, out):
-    total = (wide(own) + b[256:400].astype(F32)) + (
-        a[256:400].astype(F32) + c[256:400].astype(F32)
-    )
+def far_terms_body(pc, pb, out):
+    out[...] = add_rows(pc[512:656], pb[512:656])
+
+
+def back_relay_body(kept, over, pd, pa, far, side, near, out):
+    out[0:256] = (kept[2] + over[0].astype(F32)).astype(BF16)
+    out[256:512] = (kept[1] + over[1].astype(F32)).astype(BF16)
+    plane = add_rows(pd[512:656], pa[512:656]).astype(F32) + wide(far)
+    out[512:656] = (plane + (wide(side) + wide(near))).astype(BF16)
+
+
+def back_last_body(kept, over, sent, got, out):
+    total = kept[0] + over[2].astype(F32) + got[256:512].astype(F32)
+    out[0:256] = total.astype(BF16)
+    out[256:400] = add_rows(sent[512:656], got[512:656])
+
+
+def sum_terms_body(scale, sent, got, out):
+    total = sent[256:400].astype(F32) + got[256:400].astype(F32)
     out[...] = total[0:136] * scale
 
 
-def finish_body(own, over, a, b, c, weight, out):
+def finish_body(own, over, first, second, weight, out):
     back = own[...] + over[3].astype(F32)
-    for ref in (a, b, c):
-        back = back + ref[0:256].astype(F32)
+    back = back + first[0:256].astype(F32) + second[0:256].astype(F32)
     out[...] = lax.dot_general(
         back.astype(BF16), weight[...], (((1,), (1,)), ((), ())), preferred_element_type=F32
     ).astype(BF16)
@@ -293,17 +303,20 @@
     rows = rank * 2 + tile_rows[0, 0] % 2
     rel_y = (owner_col // 2 - y) % NY
     cols = (rel_y * 2 + (owner_col + core) % 2) * 2 + tile_cols[0, 0] % 2
+    toward_y = 1 - 2 * ((y + core) % 2)
+    sink_y = (owner_col // 2 - y) * toward_y % NY
+    sinks = (sink_y * 2 + (owner_col + core) % 2) * 2 + tile_cols[0, 0] % 2
     slots = jnp.arange(rows.shape[0], dtype=jnp.int32)
     live = slots < tile_count[0, 0]
     key = jnp.where(live, rank // 2, len(ORDER)) * rows.shape[0] + slots
     position = jnp.sum((key[None, :] < key[:, None]).astype(jnp.int32), axis=1)
     chosen = position[None, :] == slots[:, None]
-    order, rows, cols = (
-        jnp.sum(jnp.where(chosen, a[None, :], 0), axis=1) for a in (slots, rows, cols)
+    order, rows, cols, sinks = (
+        jnp.sum(jnp.where(chosen, a[None, :], 0), axis=1) for a in (slots, rows, cols, sinks)
     )
     groups = jnp.arange(16, dtype=jnp.int32)
     starts = jnp.sum((key[None, :] < groups[:, None] * rows.shape[0]).astype(jnp.int32), axis=1)
-    plan = (starts, order, rows, cols)
+    plan = (starts, order, rows, cols, sinks)
 
     tiles = tile_vals[0, 0]
     vals = call(
@@ -339,7 +352,7 @@
             functools.partial(forward_body, begin, end),
             f"forward_{begin}",
             outs,
-            (*plan, vals, source),
+            (*plan[:4], vals, source),
             scalars=4,
             scratch=(pltpu.VMEM((4 * (end - begin) + 1, TILE, 256), F32),),
         )
@@ -382,7 +395,7 @@
             functools.partial(backward_body, begin, end),
             f"backward_{begin}",
             outs,
-            (*plan, vals, *blocks, *before),
+            (*plan[:3], plan[4], vals, *blocks, *before),
             scalars=4,
             scratch=(pltpu.VMEM((4 * len(blocks), TILE, 256), BF16),)
             + ((pltpu.VMEM((17, TILE, 256), F32),) if end == len(ORDER) else ()),
@@ -412,14 +425,12 @@
     total = backward(1, (pair_c, side_d), (total,), running)
     pair_b, side_b, side_c, total = barrier((pair_b, side_b, side_c, total))
     pair_a, side_a = swap_z(pair_b, -1), swap_z(side_b, -1)
+    far_terms = call(far_terms_body, "far_terms", half, (pair_c, pair_b), moved=2**18)
+    side_terms, near_terms = swap_z(far_terms, -1, 1), to_x(far_terms)
     total = backward(3, (pair_b, side_b), (total,), running)
-    pair_a, total = barrier((pair_a, total))
-    plane = call(
-        plane_terms_body, "plane_terms", half, (pair_d, pair_a, pair_c, pair_b), moved=2**19
-    )
-    other = to_x(plane)
+    pair_a, side_terms, near_terms, total = barrier((pair_a, side_terms, near_terms, total))
     total = backward(5, (side_c, pair_a), (total,), running)
-    side_a, total, other = barrier((side_a, total, other))
+    side_a, total = barrier((side_a, total))
     own, kept, over = backward(
         7,
         (side_a,),
@@ -431,19 +442,23 @@
         ),
     )
     over = to_core(over)
-    *sends, terms = call(
+    sent = call(
         back_relay_body,
         "back_relay",
-        (*[shape(400, BF16)] * 3, half),
-        (kept, over, plane, other),
+        message,
+        (kept, over, pair_d, pair_a, far_terms, side_terms, near_terms),
         moved=2 * 2**20,
     )
-    got = [to_y(a, s) for a, s in zip(sends, (1, 2, 3))]
+    first = swap_y(sent, -1)
+    sent = call(
+        back_last_body, "back_last", shape(400, BF16), (kept, over, sent, first), moved=2**20
+    )
+    second = swap_y(sent, 1)
     mine = call(
         functools.partial(sum_terms_body, scale),
         "sum_terms",
         shape(136, F32),
-        (terms, *got),
+        (sent, second),
         moved=2**19,
     )
     other = to_core(mine)
@@ -451,7 +466,7 @@
         finish_body,
         "finish",
         one16,
-        (own, over, *got, weight),
+        (own, over, first, second, weight),
         flops=2 * 256**3,
         moved=2 * 2**20,
     )

time: 124 us -> 127 us (1.024)
  waiting for transfers between devices: 54.8 us -> 59.2 us
  Pallas kernels: 14.9 us -> 12.7 us
    ppermute x0 -> x2, waiting for transfers between devices: none -> 11.5 us  [swap_y(): return lax.ppermute(a, 'row', pairs)]
    ppermute x13 -> x14, starting transfers between devices: 19.5 us -> 27.9 us  [swap_z(): return lax.ppermute(a, ('row', 'col'), pairs)]
    ppermute x6 -> x3, waiting for transfers between devices: 8.13 us -> 0.01 us  [to_y(): lax.ppermute(a, 'row', [(i, (i + 2 * step) % (2 * NY)) for i in range(2 *...]
    ppermute x6 -> x3, starting transfers between devices: 9.43 us -> 5.29 us  [to_y(): lax.ppermute(a, 'row', [(i, (i + 2 * step) % (2 * NY)) for i in range(2 *...]
    ppermute x3, starting transfers between devices: 4.39 us -> 1.03 us  [to_x(): return lax.ppermute(a, 'col', [(i, i ^ 1) for i in range(2 * NZ)])]
    pallas_call x24 -> x25, Pallas kernels: 14.9 us -> 12.7 us  [call(): pl.pallas_call(body, name=name, out_shape=out_shape, in_specs=specs or [s...]
    ppermute x13 -> x14, waiting for transfers between devices: 32.1 us -> 33.2 us  [swap_z(): return lax.ppermute(a, ('row', 'col'), pairs)]
  transfers between devices with their start and end apart: 29 -> 29, of which waited for: 22 -> 16; matrix products, arithmetic and copies ran while one was open for 1% -> 2% of each run, Pallas kernels for 8% -> 7%
where the time goes in v11:
time: 127 us; the launch traced here: 128 us
  waiting for transfers between devices  59.2 us (47%)
  starting transfers between devices  49.3 us (39%)
  Pallas kernels  12.7 us (10%)
  local copies, waits for them, and re-layouts  2.85 us (2%)
  other arithmetic  2.07 us (2%)
  between operations  1.55 us (1%)
    ppermute x14, waiting for transfers between devices, swap_z(): return lax.ppermute(a, ('row', 'col'), pairs)  33.2 us
    ppermute x14, starting transfers between devices, swap_z(): return lax.ppermute(a, ('row', 'col'), pairs)  27.9 us
    ppermute x7, starting transfers between devices, to_core(): return lax.ppermute(a, 'row', [(i, i ^ 1) for i in range(2 * NY)])  14.2 us
    pallas_call x25, Pallas kernels, call(): pl.pallas_call(body, name=name, out_shape=out_shape, in_specs=specs or [s...  12.7 us
    ppermute x2, waiting for transfers between devices, swap_y(): return lax.ppermute(a, 'row', pairs)  11.5 us
    ppermute x3, waiting for transfers between devices, to_x(): return lax.ppermute(a, 'col', [(i, i ^ 1) for i in range(2 * NZ)])  10.9 us
    ppermute x3, starting transfers between devices, to_y(): lax.ppermute(a, 'row', [(i, (i + 2 * step) % (2 * NY)) for i in range(2 *...  5.29 us
    ppermute x7, waiting for transfers between devices, to_core(): return lax.ppermute(a, 'row', [(i, i ^ 1) for i in range(2 * NY)])  3.58 us
  transfers between devices with their start and end apart: 29, of which 16 were waited for; matrix products, arithmetic and copies ran while one was open for 2% of the time, Pallas kernels for 7%

profile of v11, /device:TPU:1, one launch (start us, length us, event | category | flops | bytes accessed | tf_op | source)
XLA Modules:
  0.0 127.7 jit_solution(7422128308592971875)
XLA Ops:
  0.6 2.2 %collective-permute-start = (bf16[256,256]{1,0:T(8,128)(2,1)}, bf16[256,256]{1,0:T(8,128)(2,1)S(1)}, u32[]{:S(2)}, u32[]{:S(2)}) collective-permute-start(bf16[256,256]{1,0:T(8,128)(2,1)} %refs_0_.1), channel_id=1, source_target_pairs={{0,64},{32,96},{64,128},{96,160},{128,192},{160,224},{192,0},{224,... | collective-permute-start | bytes 393224 | tf_op jit(solution)/shard_map/ppermute | solution.py:59
  4.4 1.6 %collective-permute-start.2 = (bf16[256,256]{1,0:T(8,128)(2,1)}, bf16[256,256]{1,0:T(8,128)(2,1)S(1)}, u32[]{:S(2)}, u32[]{:S(2)}) collective-permute-start(bf16[256,256]{1,0:T(8,128)(2,1)} %refs_0_.1), channel_id=1, source_target_pairs={{0,128},{32,160},{64,192},{96,224},{128,0},{160,32},{192,64},{224,... | collective-permute-start | bytes 393224 | tf_op jit(solution)/shard_map/ppermute | solution.py:59
  9.9 2.8 %copy-done = bf16[1,1,192,128,128]{4,3,2,1,0:T(8,128)(2,1)S(1)} copy-done((bf16[1,1,192,128,128]{4,3,2,1,0:T(8,128)(2,1)S(1)}, bf16[1,1,192,128,128]{4,3,2,1,0:T(8,128)(2,1)}, u32[]{:S(2)}) %copy-start) | copy-done | bytes 6291480
  16.5 1.7 %collective-permute-start.7 = (bf16[4,256,256]{2,1,0:T(8,128)(2,1)S(1)}, bf16[4,256,256]{2,1,0:T(8,128)(2,1)S(1)}, u32[]{:S(2)}, u32[]{:S(2)}) collective-permute-start(bf16[4,256,256]{2,1,0:T(8,128)(2,1)S(1)} %forward_6.1), channel_id=1, source_target_pairs={{0,28},{2,30},{4,8},{6,10},{8,4},{10,6},{12,16},{14,18},{16,12},{1... | collective-permute-start | bytes 1572872 | tf_op jit(solution)/shard_map/ppermute | solution.py:83
  19.9 5.2 %collective-permute-done.7.got = bf16[4,256,256]{2,1,0:T(8,128)(2,1)S(1)} collective-permute-done((bf16[4,256,256]{2,1,0:T(8,128)(2,1)S(1)}, bf16[4,256,256]{2,1,0:T(8,128)(2,1)S(1)}, u32[]{:S(2)}, u32[]{:S(2)}) %collective-permute-start.7) | collective-permute-done | bytes 524320 | tf_op jit(solution)/shard_map/ppermute | solution.py:83
  26.2 6.4 %collective-permute-start.8 = (bf16[2,256,256]{2,1,0:T(8,128)(2,1)S(1)}, bf16[2,256,256]{2,1,0:T(8,128)(2,1)S(1)}, u32[]{:S(2)}, u32[]{:S(2)}) collective-permute-start(bf16[2,256,256]{2,1,0:T(8,128)(2,1)S(1)} %get-tuple-element.73), channel_id=1, source_target_pairs={{0,4},{2,6},{4,0},{6,2},{8,12},{10,14},{12,8},{14,10},{16,20},{18,... | collective-permute-start | bytes 786440 | tf_op jit(solution)/shard_map/ppermute | solution.py:83
  32.6 3.9 %collective-permute-start.9 = (bf16[2,256,256]{2,1,0:T(8,128)(2,1)S(1)}, bf16[2,256,256]{2,1,0:T(8,128)(2,1)S(1)}, u32[]{:S(2)}, u32[]{:S(2)}) collective-permute-start(bf16[2,256,256]{2,1,0:T(8,128)(2,1)S(1)} %get-tuple-element.74), channel_id=1, source_target_pairs={{0,6},{2,4},{4,2},{6,0},{8,14},{10,12},{12,10},{14,8},{16,22},{18,... | collective-permute-start | bytes 786440 | tf_op jit(solution)/shard_map/ppermute | solution.py:83
  36.9 8.3 %collective-permute-done.9.rest_1_ = bf16[2,256,256]{2,1,0:T(8,128)(2,1)S(1)} collective-permute-done((bf16[2,256,256]{2,1,0:T(8,128)(2,1)S(1)}, bf16[2,256,256]{2,1,0:T(8,128)(2,1)S(1)}, u32[]{:S(2)}, u32[]{:S(2)}) %collective-permute-start.9) | collective-permute-done | bytes 262176 | tf_op jit(solution)/shard_map/ppermute | solution.py:83
  46.4 5.3 %collective-permute-done.11.over = bf16[2,256,256]{2,1,0:T(8,128)(2,1)S(1)} collective-permute-done((bf16[2,256,256]{2,1,0:T(8,128)(2,1)S(1)}, bf16[2,256,256]{2,1,0:T(8,128)(2,1)S(1)}, u32[]{:S(2)}, u32[]{:S(2)}) %collective-permute-start.11) | collective-permute-done | bytes 262176 | tf_op jit(solution)/shard_map/ppermute | solution.py:63
  51.8 2.9 %collective-permute-start.13 = (bf16[256,256]{1,0:T(8,128)(2,1)S(1)}, bf16[256,256]{1,0:T(8,128)(2,1)S(1)}, u32[]{:S(2)}, u32[]{:S(2)}) collective-permute-start(bf16[256,256]{1,0:T(8,128)(2,1)S(1)} %get-tuple-element.80), channel_id=1, source_target_pairs={{0,4},{2,6},{4,0},{6,2},{8,12},{10,14},{12,8},{14,10},{16,20},{18,... | collective-permute-start | bytes 393224 | tf_op jit(solution)/shard_map/ppermute | solution.py:83
  54.7 2.4 %collective-permute-done.13.got = bf16[256,256]{1,0:T(8,128)(2,1)S(1)} collective-permute-done((bf16[256,256]{1,0:T(8,128)(2,1)S(1)}, bf16[256,256]{1,0:T(8,128)(2,1)S(1)}, u32[]{:S(2)}, u32[]{:S(2)}) %collective-permute-start.13) | collective-permute-done | bytes 131104 | tf_op jit(solution)/shard_map/ppermute | solution.py:83
  58.3 2.7 %collective-permute-start.14 = (bf16[144,256]{1,0:T(8,128)(2,1)S(1)}, bf16[144,256]{1,0:T(8,128)(2,1)S(1)}, u32[]{:S(2)}, u32[]{:S(2)}) collective-permute-start(bf16[144,256]{1,0:T(8,128)(2,1)S(1)} %get-tuple-element.87), channel_id=1, source_target_pairs={{0,32},{32,0},{64,96},{96,64},{128,160},{160,128},{192,224},{224,1... | collective-permute-start | bytes 221192 | tf_op jit(solution)/shard_map/ppermute | solution.py:55
  62.0 2.8 %collective-permute-start.15 = (bf16[400,256]{1,0:T(8,128)(2,1)S(1)}, bf16[400,256]{1,0:T(8,128)(2,1)S(1)}, u32[]{:S(2)}, u32[]{:S(2)}) collective-permute-start(bf16[400,256]{1,0:T(8,128)(2,1)S(1)} %pack_own.1.own), channel_id=1, source_target_pairs={{0,4},{2,6},{4,0},{6,2},{8,12},{10,14},{12,8},{14,10},{16,20},{18,... | collective-permute-start | bytes 614408 | tf_op jit(solution)/shard_map/ppermute | solution.py:83
  64.8 3.1 %collective-permute-done.15.got = bf16[400,256]{1,0:T(8,128)(2,1)S(1)} collective-permute-done((bf16[400,256]{1,0:T(8,128)(2,1)S(1)}, bf16[400,256]{1,0:T(8,128)(2,1)S(1)}, u32[]{:S(2)}, u32[]{:S(2)}) %collective-permute-start.15) | collective-permute-done | bytes 204832 | tf_op jit(solution)/shard_map/ppermute | solution.py:83
  69.3 5.6 %collective-permute-done.17.rest_1_ = bf16[512,256]{1,0:T(8,128)(2,1)S(1)} collective-permute-done((bf16[512,256]{1,0:T(8,128)(2,1)S(1)}, bf16[512,256]{1,0:T(8,128)(2,1)S(1)}, u32[]{:S(2)}, u32[]{:S(2)}) %collective-permute-start.17) | collective-permute-done | bytes 262176 | tf_op jit(solution)/shard_map/ppermute | solution.py:63
  74.9 4.8 %collective-permute-start.18 = (bf16[656,256]{1,0:T(8,128)(2,1)S(1)}, bf16[656,256]{1,0:T(8,128)(2,1)S(1)}, u32[]{:S(2)}, u32[]{:S(2)}) collective-permute-start(bf16[656,256]{1,0:T(8,128)(2,1)S(1)} %collective-permute-done.16.rest_0_.pc), channel_id=1, source_target_pairs={{0,4},{2,6},{4,0},{6,2},{8,12},{10,14},{12,8},{14,10},{16,20},{18,... | collective-permute-start | bytes 1007624 | tf_op jit(solution)/shard_map/ppermute | solution.py:83
  81.6 8.5 %collective-permute-done.19.rest_1_ = bf16[512,256]{1,0:T(8,128)(2,1)S(1)} collective-permute-done((bf16[512,256]{1,0:T(8,128)(2,1)S(1)}, bf16[512,256]{1,0:T(8,128)(2,1)S(1)}, u32[]{:S(2)}, u32[]{:S(2)}) %collective-permute-start.19) | collective-permute-done | bytes 262176 | tf_op jit(solution)/shard_map/ppermute | solution.py:83
  91.6 2.2 %collective-permute-start.23 = (bf16[144,256]{1,0:T(8,128)(2,1)S(1)}, bf16[144,256]{1,0:T(8,128)(2,1)S(1)}, u32[]{:S(2)}, u32[]{:S(2)}) collective-permute-start(bf16[144,256]{1,0:T(8,128)(2,1)S(1)} %far_terms.1.far), channel_id=1, source_target_pairs={{0,30},{2,28},{4,10},{6,8},{8,6},{10,4},{12,18},{14,16},{16,14},{1... | collective-permute-start | bytes 221192 | tf_op jit(solution)/shard_map/ppermute | solution.py:83
  95.3 5.7 %collective-permute-done.23.side = bf16[144,256]{1,0:T(8,128)(2,1)S(1)} collective-permute-done((bf16[144,256]{1,0:T(8,128)(2,1)S(1)}, bf16[144,256]{1,0:T(8,128)(2,1)S(1)}, u32[]{:S(2)}, u32[]{:S(2)}) %collective-permute-start.23) | collective-permute-done | bytes 73760 | tf_op jit(solution)/shard_map/ppermute | solution.py:83
  102.9 6.5 %collective-permute-start.25 = (bf16[4,256,256]{2,1,0:T(8,128)(2,1)S(1)}, bf16[4,256,256]{2,1,0:T(8,128)(2,1)S(1)}, u32[]{:S(2)}, u32[]{:S(2)}) collective-permute-start(bf16[4,256,256]{2,1,0:T(8,128)(2,1)S(1)} %get-tuple-element.100), channel_id=1, source_target_pairs={{0,32},{32,0},{64,96},{96,64},{128,160},{160,128},{192,224},{224,1... | collective-permute-start | bytes 1572872 | tf_op jit(solution)/shard_map/ppermute | solution.py:55
  109.5 1.5 %collective-permute-done.25.over = bf16[4,256,256]{2,1,0:T(8,128)(2,1)S(1)} collective-permute-done((bf16[4,256,256]{2,1,0:T(8,128)(2,1)S(1)}, bf16[4,256,256]{2,1,0:T(8,128)(2,1)S(1)}, u32[]{:S(2)}, u32[]{:S(2)}) %collective-permute-start.25) | collective-permute-done | bytes 524320 | tf_op jit(solution)/shard_map/ppermute | solution.py:55
  111.4 6.1 %collective-permute-done.26.got.first = bf16[656,256]{1,0:T(8,128)(2,1)S(1)} collective-permute-done((bf16[656,256]{1,0:T(8,128)(2,1)S(1)}, bf16[656,256]{1,0:T(8,128)(2,1)S(1)}, u32[]{:S(2)}, u32[]{:S(2)}) %collective-permute-start.26) | collective-permute-done | bytes 335904 | tf_op jit(solution)/shard_map/ppermute | solution.py:72
  118.1 5.4 %collective-permute-done.27.second.got = bf16[400,256]{1,0:T(8,128)(2,1)S(1)} collective-permute-done((bf16[400,256]{1,0:T(8,128)(2,1)S(1)}, bf16[400,256]{1,0:T(8,128)(2,1)S(1)}, u32[]{:S(2)}, u32[]{:S(2)}) %collective-permute-start.27) | collective-permute-done | bytes 204832 | tf_op jit(solution)/shard_map/ppermute | solution.py:72
  123.5 2.5 %collective-permute-start.28 = (f32[136,256]{1,0:T(8,128)S(1)}, f32[136,256]{1,0:T(8,128)S(1)}, u32[]{:S(2)}, u32[]{:S(2)}) collective-permute-start(f32[136,256]{1,0:T(8,128)S(1)} %sum_terms.1.mine), channel_id=1, source_target_pairs={{0,32},{32,0},{64,96},{96,64},{128,160},{160,128},{192,224},{224,1... | collective-permute-start | bytes 417800 | tf_op jit(solution)/shard_map/ppermute | solution.py:55
  (78 shorter events, 26.1 us)
Async XLA Ops:
  0.6 12.8 %collective-permute-start = (bf16[256,256]{1,0:T(8,128)(2,1)}, bf16[256,256]{1,0:T(8,128)(2,1)S(1)}, u32[]{:S(2)}, u32[]{:S(2)}) collective-permute-start(bf16[256,256]{1,0:T(8,128)(2,1)} %refs_0_.1), channel_id=1, source_target_pairs={{0,64},{32,96},{64,128},{96,160},{128,192},{160,224},{192,0},{224,... | collective-permute-start | bytes 393224 | tf_op jit(solution)/shard_map/ppermute | solution.py:59
  2.8 10.6 %collective-permute-start.1 = (bf16[256,256]{1,0:T(8,128)(2,1)}, bf16[256,256]{1,0:T(8,128)(2,1)S(1)}, u32[]{:S(2)}, u32[]{:S(2)}) collective-permute-start(bf16[256,256]{1,0:T(8,128)(2,1)} %refs_0_.1), channel_id=1, source_target_pairs={{0,192},{32,224},{64,0},{96,32},{128,64},{160,96},{192,128},{224,1... | collective-permute-start | bytes 393224 | tf_op jit(solution)/shard_map/ppermute | solution.py:59
  4.4 9.1 %collective-permute-start.2 = (bf16[256,256]{1,0:T(8,128)(2,1)}, bf16[256,256]{1,0:T(8,128)(2,1)S(1)}, u32[]{:S(2)}, u32[]{:S(2)}) collective-permute-start(bf16[256,256]{1,0:T(8,128)(2,1)} %refs_0_.1), channel_id=1, source_target_pairs={{0,128},{32,160},{64,192},{96,224},{128,0},{160,32},{192,64},{224,... | collective-permute-start | bytes 393224 | tf_op jit(solution)/shard_map/ppermute | solution.py:59
  5.9 8.5 %collective-permute-start.3 = (bf16[256,256]{1,0:T(8,128)(2,1)}, bf16[256,256]{1,0:T(8,128)(2,1)S(1)}, u32[]{:S(2)}, u32[]{:S(2)}) collective-permute-start(bf16[256,256]{1,0:T(8,128)(2,1)} %refs_0_.1), channel_id=1, source_target_pairs={{0,32},{32,0},{64,96},{96,64},{128,160},{160,128},{192,224},{224,1... | collective-permute-start | bytes 393224 | tf_op jit(solution)/shard_map/ppermute | solution.py:55
  16.5 8.6 %collective-permute-start.7 = (bf16[4,256,256]{2,1,0:T(8,128)(2,1)S(1)}, bf16[4,256,256]{2,1,0:T(8,128)(2,1)S(1)}, u32[]{:S(2)}, u32[]{:S(2)}) collective-permute-start(bf16[4,256,256]{2,1,0:T(8,128)(2,1)S(1)} %forward_6.1), channel_id=1, source_target_pairs={{0,28},{2,30},{4,8},{6,10},{8,4},{10,6},{12,16},{14,18},{16,12},{1... | collective-permute-start | bytes 1572872 | tf_op jit(solution)/shard_map/ppermute | solution.py:83
  19.0 17.6 %collective-permute-start.10 = (bf16[2,256,256]{2,1,0:T(8,128)(2,1)S(1)}, bf16[2,256,256]{2,1,0:T(8,128)(2,1)S(1)}, u32[]{:S(2)}, u32[]{:S(2)}) collective-permute-start(bf16[2,256,256]{2,1,0:T(8,128)(2,1)S(1)} %get-tuple-element.77), channel_id=1, source_target_pairs={{0,28},{2,30},{4,8},{6,10},{8,4},{10,6},{12,16},{14,18},{16,12},{1... | collective-permute-start | bytes 786440 | tf_op jit(solution)/shard_map/ppermute | solution.py:83
  26.2 10.7 %collective-permute-start.8 = (bf16[2,256,256]{2,1,0:T(8,128)(2,1)S(1)}, bf16[2,256,256]{2,1,0:T(8,128)(2,1)S(1)}, u32[]{:S(2)}, u32[]{:S(2)}) collective-permute-start(bf16[2,256,256]{2,1,0:T(8,128)(2,1)S(1)} %get-tuple-element.73), channel_id=1, source_target_pairs={{0,4},{2,6},{4,0},{6,2},{8,12},{10,14},{12,8},{14,10},{16,20},{18,... | collective-permute-start | bytes 786440 | tf_op jit(solution)/shard_map/ppermute | solution.py:83
  32.6 12.5 %collective-permute-start.9 = (bf16[2,256,256]{2,1,0:T(8,128)(2,1)S(1)}, bf16[2,256,256]{2,1,0:T(8,128)(2,1)S(1)}, u32[]{:S(2)}, u32[]{:S(2)}) collective-permute-start(bf16[2,256,256]{2,1,0:T(8,128)(2,1)S(1)} %get-tuple-element.74), channel_id=1, source_target_pairs={{0,6},{2,4},{4,2},{6,0},{8,14},{10,12},{12,10},{14,8},{16,22},{18,... | collective-permute-start | bytes 786440 | tf_op jit(solution)/shard_map/ppermute | solution.py:83
  36.6 15.1 %collective-permute-start.11 = (bf16[2,256,256]{2,1,0:T(8,128)(2,1)S(1)}, bf16[2,256,256]{2,1,0:T(8,128)(2,1)S(1)}, u32[]{:S(2)}, u32[]{:S(2)}) collective-permute-start(bf16[2,256,256]{2,1,0:T(8,128)(2,1)S(1)} %relay_side.1), channel_id=1, source_target_pairs={{0,2},{2,0},{4,6},{6,4},{8,10},{10,8},{12,14},{14,12},{16,18},{18,... | collective-permute-start | bytes 786440 | tf_op jit(solution)/shard_map/ppermute | solution.py:63
  45.3 6.4 %collective-permute-start.12 = (bf16[2,256,256]{2,1,0:T(8,128)(2,1)S(1)}, bf16[2,256,256]{2,1,0:T(8,128)(2,1)S(1)}, u32[]{:S(2)}, u32[]{:S(2)}) collective-permute-start(bf16[2,256,256]{2,1,0:T(8,128)(2,1)S(1)} %relay_c.1), channel_id=1, source_target_pairs={{0,28},{2,30},{4,8},{6,10},{8,4},{10,6},{12,16},{14,18},{16,12},{1... | collective-permute-start | bytes 786440 | tf_op jit(solution)/shard_map/ppermute | solution.py:83
  51.8 5.3 %collective-permute-start.13 = (bf16[256,256]{1,0:T(8,128)(2,1)S(1)}, bf16[256,256]{1,0:T(8,128)(2,1)S(1)}, u32[]{:S(2)}, u32[]{:S(2)}) collective-permute-start(bf16[256,256]{1,0:T(8,128)(2,1)S(1)} %get-tuple-element.80), channel_id=1, source_target_pairs={{0,4},{2,6},{4,0},{6,2},{8,12},{10,14},{12,8},{14,10},{16,20},{18,... | collective-permute-start | bytes 393224 | tf_op jit(solution)/shard_map/ppermute | solution.py:83
  62.0 5.9 %collective-permute-start.15 = (bf16[400,256]{1,0:T(8,128)(2,1)S(1)}, bf16[400,256]{1,0:T(8,128)(2,1)S(1)}, u32[]{:S(2)}, u32[]{:S(2)}) collective-permute-start(bf16[400,256]{1,0:T(8,128)(2,1)S(1)} %pack_own.1.own), channel_id=1, source_target_pairs={{0,4},{2,6},{4,0},{6,2},{8,12},{10,14},{12,8},{14,10},{16,20},{18,... | collective-permute-start | bytes 614408 | tf_op jit(solution)/shard_map/ppermute | solution.py:83
  68.0 6.9 %collective-permute-start.16 = (bf16[656,256]{1,0:T(8,128)(2,1)S(1)}, bf16[656,256]{1,0:T(8,128)(2,1)S(1)}, u32[]{:S(2)}, u32[]{:S(2)}) collective-permute-start(bf16[656,256]{1,0:T(8,128)(2,1)S(1)} %pack_pair.1.rest_0_.pd), channel_id=1, source_target_pairs={{0,28},{2,30},{4,8},{6,10},{8,4},{10,6},{12,16},{14,18},{16,12},{1... | collective-permute-start | bytes 1007624 | tf_op jit(solution)/shard_map/ppermute | solution.py:83
  68.1 6.8 %collective-permute-start.17 = (bf16[512,256]{1,0:T(8,128)(2,1)S(1)}, bf16[512,256]{1,0:T(8,128)(2,1)S(1)}, u32[]{:S(2)}, u32[]{:S(2)}) collective-permute-start(bf16[512,256]{1,0:T(8,128)(2,1)S(1)} %slice.8), channel_id=1, source_target_pairs={{0,2},{2,0},{4,6},{6,4},{8,10},{10,8},{12,14},{14,12},{16,18},{18,... | collective-permute-start | bytes 786440 | tf_op jit(solution)/shard_map/ppermute | solution.py:63
  74.9 15.2 %collective-permute-start.18 = (bf16[656,256]{1,0:T(8,128)(2,1)S(1)}, bf16[656,256]{1,0:T(8,128)(2,1)S(1)}, u32[]{:S(2)}, u32[]{:S(2)}) collective-permute-start(bf16[656,256]{1,0:T(8,128)(2,1)S(1)} %collective-permute-done.16.rest_0_.pc), channel_id=1, source_target_pairs={{0,4},{2,6},{4,0},{6,2},{8,12},{10,14},{12,8},{14,10},{16,20},{18,... | collective-permute-start | bytes 1007624 | tf_op jit(solution)/shard_map/ppermute | solution.py:83
  79.7 10.4 %collective-permute-start.19 = (bf16[512,256]{1,0:T(8,128)(2,1)S(1)}, bf16[512,256]{1,0:T(8,128)(2,1)S(1)}, u32[]{:S(2)}, u32[]{:S(2)}) collective-permute-start(bf16[512,256]{1,0:T(8,128)(2,1)S(1)} %slice.7), channel_id=1, source_target_pairs={{0,6},{2,4},{4,2},{6,0},{8,14},{10,12},{12,10},{14,8},{16,22},{18,... | collective-permute-start | bytes 786440 | tf_op jit(solution)/shard_map/ppermute | solution.py:83
  79.8 10.3 %collective-permute-start.20 = (bf16[512,256]{1,0:T(8,128)(2,1)S(1)}, bf16[512,256]{1,0:T(8,128)(2,1)S(1)}, u32[]{:S(2)}, u32[]{:S(2)}) collective-permute-start(bf16[512,256]{1,0:T(8,128)(2,1)S(1)} %collective-permute-done.17.rest_1_), channel_id=1, source_target_pairs={{0,28},{2,30},{4,8},{6,10},{8,4},{10,6},{12,16},{14,18},{16,12},{1... | collective-permute-start | bytes 786440 | tf_op jit(solution)/shard_map/ppermute | solution.py:83
  90.1 10.8 %collective-permute-start.22 = (bf16[656,256]{1,0:T(8,128)(2,1)S(1)}, bf16[656,256]{1,0:T(8,128)(2,1)S(1)}, u32[]{:S(2)}, u32[]{:S(2)}) collective-permute-start(bf16[656,256]{1,0:T(8,128)(2,1)S(1)} %collective-permute-done.18.pb.rest_0_), channel_id=1, source_target_pairs={{0,28},{2,30},{4,8},{6,10},{8,4},{10,6},{12,16},{14,18},{16,12},{1... | collective-permute-start | bytes 1007624 | tf_op jit(solution)/shard_map/ppermute | solution.py:83
  90.1 11.9 %collective-permute-start.21 = (bf16[512,256]{1,0:T(8,128)(2,1)S(1)}, bf16[512,256]{1,0:T(8,128)(2,1)S(1)}, u32[]{:S(2)}, u32[]{:S(2)}) collective-permute-start(bf16[512,256]{1,0:T(8,128)(2,1)S(1)} %collective-permute-done.19.rest_1_), channel_id=1, source_target_pairs={{0,28},{2,30},{4,8},{6,10},{8,4},{10,6},{12,16},{14,18},{16,12},{1... | collective-permute-start | bytes 786440 | tf_op jit(solution)/shard_map/ppermute | solution.py:83
  91.6 9.3 %collective-permute-start.23 = (bf16[144,256]{1,0:T(8,128)(2,1)S(1)}, bf16[144,256]{1,0:T(8,128)(2,1)S(1)}, u32[]{:S(2)}, u32[]{:S(2)}) collective-permute-start(bf16[144,256]{1,0:T(8,128)(2,1)S(1)} %far_terms.1.far), channel_id=1, source_target_pairs={{0,30},{2,28},{4,10},{6,8},{8,6},{10,4},{12,18},{14,16},{16,14},{1... | collective-permute-start | bytes 221192 | tf_op jit(solution)/shard_map/ppermute | solution.py:83
  93.8 7.1 %collective-permute-start.24 = (bf16[144,256]{1,0:T(8,128)(2,1)S(1)}, bf16[144,256]{1,0:T(8,128)(2,1)S(1)}, u32[]{:S(2)}, u32[]{:S(2)}) collective-permute-start(bf16[144,256]{1,0:T(8,128)(2,1)S(1)} %far_terms.1.far), channel_id=1, source_target_pairs={{0,2},{2,0},{4,6},{6,4},{8,10},{10,8},{12,14},{14,12},{16,18},{18,... | collective-permute-start | bytes 221192 | tf_op jit(solution)/shard_map/ppermute | solution.py:63
  102.9 8.1 %collective-permute-start.25 = (bf16[4,256,256]{2,1,0:T(8,128)(2,1)S(1)}, bf16[4,256,256]{2,1,0:T(8,128)(2,1)S(1)}, u32[]{:S(2)}, u32[]{:S(2)}) collective-permute-start(bf16[4,256,256]{2,1,0:T(8,128)(2,1)S(1)} %get-tuple-element.100), channel_id=1, source_target_pairs={{0,32},{32,0},{64,96},{96,64},{128,160},{160,128},{192,224},{224,1... | collective-permute-start | bytes 1572872 | tf_op jit(solution)/shard_map/ppermute | solution.py:55
  111.1 6.4 %collective-permute-start.26 = (bf16[656,256]{1,0:T(8,128)(2,1)S(1)}, bf16[656,256]{1,0:T(8,128)(2,1)S(1)}, u32[]{:S(2)}, u32[]{:S(2)}) collective-permute-start(bf16[656,256]{1,0:T(8,128)(2,1)S(1)} %back_relay.1.sent), channel_id=1, source_target_pairs={{0,192},{32,96},{64,128},{96,32},{128,64},{160,224},{192,0},{224,1... | collective-permute-start | bytes 1007624 | tf_op jit(solution)/shard_map/ppermute | solution.py:72
  117.6 5.9 %collective-permute-start.27 = (bf16[400,256]{1,0:T(8,128)(2,1)S(1)}, bf16[400,256]{1,0:T(8,128)(2,1)S(1)}, u32[]{:S(2)}, u32[]{:S(2)}) collective-permute-start(bf16[400,256]{1,0:T(8,128)(2,1)S(1)} %back_last.1.sent), channel_id=1, source_target_pairs={{0,64},{32,224},{64,0},{96,160},{128,192},{160,96},{192,128},{224,... | collective-permute-start | bytes 614408 | tf_op jit(solution)/shard_map/ppermute | solution.py:72
  (10 other events, 52.3 us)

commit v12 on v10

--- a/solution.py
+++ b/solution.py
@@ -103,18 +103,11 @@
             place_at = jnp.where(slot < last, to_slot(t), dummy)
             total[place_at] = total[place_at] + term
 
-    size = last - first
-    full = (size + 7) // 16
-
     def batch(i, carry):
         step(first + 16 * i, 16)
         return carry
 
-    lax.fori_loop(0, full, batch, 0)
-
-    @pl.when(16 * full < size)
-    def _():
-        step(first + 16 * full, 8)
+    lax.fori_loop(0, (last - first + 15) // 16, batch, 0)
 
 
 def forward_body(begin, end, starts, order, rows, cols, vals, source, *rest):
@@ -142,9 +135,9 @@
     return ref[...].astype(F32)
 
 
-def relay_first_body(kept, side, got, out, out_side):
-    out[...] = (kept[...] + wide(got.at[0:2])).astype(BF16)
-    out_side[...] = (side[...] + wide(got.at[2:4])).astype(BF16)
+def relay_first_body(kept, side, got, got_side, out, out_side):
+    out[...] = (kept[...] + wide(got)).astype(BF16)
+    out_side[...] = (side[...] + wide(got_side)).astype(BF16)
 
 
 def relay_body(kept, *rest):
@@ -348,17 +341,17 @@
         return call(body, name, outs, args, moved=2**20)
 
     barrier = lax.optimization_barrier
-    (moving,) = forward(6, 8, (jax.ShapeDtypeStruct((4, shard, 256), BF16),), source)
-    moving, source = barrier((moving, source))
-    moving = swap_z(moving, -1)
+    moving, side = forward(6, 8, (two16, two16), source)
+    moving, side, source = barrier((moving, side, source))
+    side, moving = swap_z(side, -1), swap_z(moving, -1)
     kept_b, side_b, side_c = forward(3, 6, (two, two, two16), source)
     side_c = swap_z(side_c, -1)
-    moving, side = relay(relay_first_body, "relay_b", (two16, two16), kept_b, side_b, moving)
+    moving, side = relay(
+        relay_first_body, "relay_b", (two16, two16), kept_b, side_b, moving, side
+    )
     moving, side, source = barrier((moving, side, source))
-    side = swap_z(side, 1, 1)
+    side, moving = swap_z(side, 1, 1), swap_z(moving, 1)
     kept_c, side_d = forward(1, 3, (two, two), source)
-    moving, kept_c = barrier((moving, kept_c))
-    moving = swap_z(moving, 1)
     side_d = relay(relay_body, "relay_side", two16, side_d, side_c)
     side_d = to_x(side_d)
     moving = relay(relay_body, "relay_c", two16, kept_c, moving, side)

time: 124 us -> 123 us (level)
  waiting for transfers between devices: 54.8 us -> 42.7 us
  Pallas kernels: 14.9 us -> 24.9 us
    pallas_call x24, Pallas kernels: 14.9 us -> 24.9 us  [call(): pl.pallas_call(body, name=name, out_shape=out_shape, in_specs=specs or [s...]
    ppermute x13 -> x14, waiting for transfers between devices: 32.1 us -> 22.9 us  [swap_z(): return lax.ppermute(a, ('row', 'col'), pairs)]
    ppermute x3, waiting for transfers between devices: 11 us -> 8.25 us  [to_x(): return lax.ppermute(a, 'col', [(i, i ^ 1) for i in range(2 * NZ)])]
    ppermute x13 -> x14, starting transfers between devices: 19.5 us -> 21.5 us  [swap_z(): return lax.ppermute(a, ('row', 'col'), pairs)]
    ppermute x7, starting transfers between devices: 15.1 us -> 13.8 us  [to_core(): return lax.ppermute(a, 'row', [(i, i ^ 1) for i in range(2 * NY)])]
  transfers between devices with their start and end apart: 29 -> 30, of which waited for: 22 -> 17; matrix products, arithmetic and copies ran while one was open for 1% -> 1% of each run, Pallas kernels for 8% -> 15%
where the time goes in v12:
time: 123 us; the launch traced here: 122 us
  starting transfers between devices  48.5 us (39%)
  waiting for transfers between devices  42.7 us (35%)
  Pallas kernels  24.9 us (20%)
  local copies, waits for them, and re-layouts  2.85 us (2%)
  between operations  1.58 us (1%)
  other arithmetic  1.34 us (1%)
    pallas_call x24, Pallas kernels, call(): pl.pallas_call(body, name=name, out_shape=out_shape, in_specs=specs or [s...  24.9 us
    ppermute x14, waiting for transfers between devices, swap_z(): return lax.ppermute(a, ('row', 'col'), pairs)  22.9 us
    ppermute x14, starting transfers between devices, swap_z(): return lax.ppermute(a, ('row', 'col'), pairs)  21.5 us
    ppermute x7, starting transfers between devices, to_core(): return lax.ppermute(a, 'row', [(i, i ^ 1) for i in range(2 * NY)])  13.8 us
    ppermute x6, starting transfers between devices, to_y(): lax.ppermute(a, 'row', [(i, (i + 2 * step) % (2 * NY)) for i in range(2 *...  9.89 us
    ppermute x3, waiting for transfers between devices, to_x(): return lax.ppermute(a, 'col', [(i, i ^ 1) for i in range(2 * NZ)])  8.25 us
    ppermute x6, waiting for transfers between devices, to_y(): lax.ppermute(a, 'row', [(i, (i + 2 * step) % (2 * NY)) for i in range(2 *...  7.98 us
    ppermute x7, waiting for transfers between devices, to_core(): return lax.ppermute(a, 'row', [(i, i ^ 1) for i in range(2 * NY)])  3.58 us
  transfers between devices with their start and end apart: 30, of which 17 were waited for; matrix products, arithmetic and copies ran while one was open for 1% of the time, Pallas kernels for 15%

profile of v12, /device:TPU:1, one launch (start us, length us, event | category | flops | bytes accessed | tf_op | source)
XLA Modules:
  0.0 121.8 jit_solution(4374784304040975387)
XLA Ops:
  9.2 2.8 %copy-done = bf16[1,1,192,128,128]{4,3,2,1,0:T(8,128)(2,1)S(1)} copy-done((bf16[1,1,192,128,128]{4,3,2,1,0:T(8,128)(2,1)S(1)}, bf16[1,1,192,128,128]{4,3,2,1,0:T(8,128)(2,1)}, u32[]{:S(2)}) %copy-start) | copy-done | bytes 6291480
  15.5 2.6 %forward_6.1 = (bf16[2,256,256]{2,1,0:T(8,128)(2,1)S(1)}, bf16[2,256,256]{2,1,0:T(8,128)(2,1)S(1)}) custom-call(s32[16]{0:T(128)S(1)} %convert_reduce_fusion.1.starts, s32[192]{0:T(256)S(1)} %get-tuple-element.59.order, s32[192]{0:T(256)S(1)} %get-tuple-element.60.rows, s32[192]{0:T(256)S(1)} %get-tuple-element.61.cols, ...), custom_call_target="tpu_custom_call" | custom-call | tf_op jit(solution)/shard_map/forward_6/pallas_call | solution.py:42
  19.6 3.1 %forward_3.1 = (f32[2,256,256]{2,1,0:T(8,128)S(1)}, f32[2,256,256]{2,1,0:T(8,128)S(1)}, bf16[2,256,256]{2,1,0:T(8,128)(2,1)S(1)}) custom-call(s32[16]{0:T(128)S(1)} %convert_reduce_fusion.1.starts, s32[192]{0:T(256)S(1)} %get-tuple-element.59.order, s32[192]{0:T(256)S(1)} %get-tuple-element.60.rows, s32[192]{0:T(256)S(1)} %get-tuple-element.61.cols, ...), custom_call_target="tpu_custom_call" | custom-call | tf_op jit(solution)/shard_map/forward_3/pallas_call | solution.py:42
  23.6 2.8 %collective-permute-done.8.got_side = bf16[2,256,256]{2,1,0:T(8,128)(2,1)S(1)} collective-permute-done((bf16[2,256,256]{2,1,0:T(8,128)(2,1)S(1)}, bf16[2,256,256]{2,1,0:T(8,128)(2,1)S(1)}, u32[]{:S(2)}, u32[]{:S(2)}) %collective-permute-start.8) | collective-permute-done | bytes 262176 | tf_op jit(solution)/shard_map/ppermute | solution.py:74
  26.5 5.7 %collective-permute-start.10 = (bf16[2,256,256]{2,1,0:T(8,128)(2,1)S(1)}, bf16[2,256,256]{2,1,0:T(8,128)(2,1)S(1)}, u32[]{:S(2)}, u32[]{:S(2)}) collective-permute-start(bf16[2,256,256]{2,1,0:T(8,128)(2,1)S(1)} %get-tuple-element.78), channel_id=1, source_target_pairs={{0,6},{2,4},{4,2},{6,0},{8,14},{10,12},{12,10},{14,8},{16,22},{18,... | collective-permute-start | bytes 786440 | tf_op jit(solution)/shard_map/ppermute | solution.py:74
  32.3 2.6 %forward_1.1 = (f32[2,256,256]{2,1,0:T(8,128)S(1)}, f32[2,256,256]{2,1,0:T(8,128)S(1)}) custom-call(s32[16]{0:T(128)S(1)} %convert_reduce_fusion.1.starts, s32[192]{0:T(256)S(1)} %get-tuple-element.59.order, s32[192]{0:T(256)S(1)} %get-tuple-element.60.rows, s32[192]{0:T(256)S(1)} %get-tuple-element.61.cols, bf16[192,128,128]{2,1,0:T(8,128)(2,1)S(1)} %load_tiles.1.vals, ...), custom_call_target="tpu_custom_call" | custom-call | tf_op jit(solution)/shard_map/forward_1/pallas_call | solution.py:42
  35.0 4.2 %collective-permute-done.10.rest_1_ = bf16[2,256,256]{2,1,0:T(8,128)(2,1)S(1)} collective-permute-done((bf16[2,256,256]{2,1,0:T(8,128)(2,1)S(1)}, bf16[2,256,256]{2,1,0:T(8,128)(2,1)S(1)}, u32[]{:S(2)}, u32[]{:S(2)}) %collective-permute-start.10) | collective-permute-done | bytes 262176 | tf_op jit(solution)/shard_map/ppermute | solution.py:74
  41.6 3.8 %collective-permute-done.12.over = bf16[2,256,256]{2,1,0:T(8,128)(2,1)S(1)} collective-permute-done((bf16[2,256,256]{2,1,0:T(8,128)(2,1)S(1)}, bf16[2,256,256]{2,1,0:T(8,128)(2,1)S(1)}, u32[]{:S(2)}, u32[]{:S(2)}) %collective-permute-start.12) | collective-permute-done | bytes 262176 | tf_op jit(solution)/shard_map/ppermute | solution.py:63
  45.5 2.4 %collective-permute-start.14 = (bf16[256,256]{1,0:T(8,128)(2,1)S(1)}, bf16[256,256]{1,0:T(8,128)(2,1)S(1)}, u32[]{:S(2)}, u32[]{:S(2)}) collective-permute-start(bf16[256,256]{1,0:T(8,128)(2,1)S(1)} %get-tuple-element.84), channel_id=1, source_target_pairs={{0,4},{2,6},{4,0},{6,2},{8,12},{10,14},{12,8},{14,10},{16,20},{18,... | collective-permute-start | bytes 393224 | tf_op jit(solution)/shard_map/ppermute | solution.py:74
  47.9 2.9 %collective-permute-done.14.got = bf16[256,256]{1,0:T(8,128)(2,1)S(1)} collective-permute-done((bf16[256,256]{1,0:T(8,128)(2,1)S(1)}, bf16[256,256]{1,0:T(8,128)(2,1)S(1)}, u32[]{:S(2)}, u32[]{:S(2)}) %collective-permute-start.14) | collective-permute-done | bytes 131104 | tf_op jit(solution)/shard_map/ppermute | solution.py:74
  52.0 4.6 %collective-permute-start.15 = (bf16[144,256]{1,0:T(8,128)(2,1)S(1)}, bf16[144,256]{1,0:T(8,128)(2,1)S(1)}, u32[]{:S(2)}, u32[]{:S(2)}) collective-permute-start(bf16[144,256]{1,0:T(8,128)(2,1)S(1)} %get-tuple-element.90), channel_id=1, source_target_pairs={{0,32},{32,0},{64,96},{96,64},{128,160},{160,128},{192,224},{224,1... | collective-permute-start | bytes 221192 | tf_op jit(solution)/shard_map/ppermute | solution.py:55
  57.6 3.5 %collective-permute-start.16 = (bf16[400,256]{1,0:T(8,128)(2,1)S(1)}, bf16[400,256]{1,0:T(8,128)(2,1)S(1)}, u32[]{:S(2)}, u32[]{:S(2)}) collective-permute-start(bf16[400,256]{1,0:T(8,128)(2,1)S(1)} %pack_own.1.own), channel_id=1, source_target_pairs={{0,4},{2,6},{4,0},{6,2},{8,12},{10,14},{12,8},{14,10},{16,20},{18,... | collective-permute-start | bytes 614408 | tf_op jit(solution)/shard_map/ppermute | solution.py:74
  61.1 3.1 %collective-permute-done.16.got = bf16[400,256]{1,0:T(8,128)(2,1)S(1)} collective-permute-done((bf16[400,256]{1,0:T(8,128)(2,1)S(1)}, bf16[400,256]{1,0:T(8,128)(2,1)S(1)}, u32[]{:S(2)}, u32[]{:S(2)}) %collective-permute-start.16) | collective-permute-done | bytes 204832 | tf_op jit(solution)/shard_map/ppermute | solution.py:74
  66.8 4.4 %collective-permute-done.18.rest_1_ = bf16[512,256]{1,0:T(8,128)(2,1)S(1)} collective-permute-done((bf16[512,256]{1,0:T(8,128)(2,1)S(1)}, bf16[512,256]{1,0:T(8,128)(2,1)S(1)}, u32[]{:S(2)}, u32[]{:S(2)}) %collective-permute-start.18) | collective-permute-done | bytes 262176 | tf_op jit(solution)/shard_map/ppermute | solution.py:63
  71.2 5.1 %collective-permute-start.19 = (bf16[656,256]{1,0:T(8,128)(2,1)S(1)}, bf16[656,256]{1,0:T(8,128)(2,1)S(1)}, u32[]{:S(2)}, u32[]{:S(2)}) collective-permute-start(bf16[656,256]{1,0:T(8,128)(2,1)S(1)} %collective-permute-done.17.rest_0_.pc), channel_id=1, source_target_pairs={{0,4},{2,6},{4,0},{6,2},{8,12},{10,14},{12,8},{14,10},{16,20},{18,... | collective-permute-start | bytes 1007624 | tf_op jit(solution)/shard_map/ppermute | solution.py:74
  77.2 2.7 %backward_1.1.rest_2_ = f32[17,128,256]{2,1,0:T(8,128)S(1)} custom-call(s32[16]{0:T(128)S(1)} %convert_reduce_fusion.1.starts, s32[192]{0:T(256)S(1)} %get-tuple-element.59.order, s32[192]{0:T(256)S(1)} %get-tuple-element.60.rows, s32[192]{0:T(256)S(1)} %get-tuple-element.61.cols, bf16[192,128,128]{2,1,0:T(8,128)(2,1)S(1)} %load_tiles.1.vals, ...), custom_call_target="tpu_custom_call" | custom-call | tf_op jit(solution)/shard_map/backward_1/pallas_call | solution.py:42
  79.9 6.7 %collective-permute-done.20.rest_1_ = bf16[512,256]{1,0:T(8,128)(2,1)S(1)} collective-permute-done((bf16[512,256]{1,0:T(8,128)(2,1)S(1)}, bf16[512,256]{1,0:T(8,128)(2,1)S(1)}, u32[]{:S(2)}, u32[]{:S(2)}) %collective-permute-start.20) | collective-permute-done | bytes 262176 | tf_op jit(solution)/shard_map/ppermute | solution.py:74
  88.1 2.3 %backward_3.1.rest_2_ = f32[17,128,256]{2,1,0:T(8,128)S(1)} custom-call(s32[16]{0:T(128)S(1)} %convert_reduce_fusion.1.starts, s32[192]{0:T(256)S(1)} %get-tuple-element.59.order, s32[192]{0:T(256)S(1)} %get-tuple-element.60.rows, s32[192]{0:T(256)S(1)} %get-tuple-element.61.cols, bf16[192,128,128]{2,1,0:T(8,128)(2,1)S(1)} %load_tiles.1.vals, ...), custom_call_target="tpu_custom_call" | custom-call | tf_op jit(solution)/shard_map/backward_3/pallas_call | solution.py:42
  90.3 2.3 %collective-permute-done.23.rest_1_.pa = bf16[656,256]{1,0:T(8,128)(2,1)S(1)} collective-permute-done((bf16[656,256]{1,0:T(8,128)(2,1)S(1)}, bf16[656,256]{1,0:T(8,128)(2,1)S(1)}, u32[]{:S(2)}, u32[]{:S(2)}) %collective-permute-start.23) | collective-permute-done | bytes 335904 | tf_op jit(solution)/shard_map/ppermute | solution.py:74
  92.7 2.6 %collective-permute-start.24 = (bf16[144,256]{1,0:T(8,128)(2,1)S(1)}, bf16[144,256]{1,0:T(8,128)(2,1)S(1)}, u32[]{:S(2)}, u32[]{:S(2)}) collective-permute-start(bf16[144,256]{1,0:T(8,128)(2,1)S(1)} %plane_terms.1.plane), channel_id=1, source_target_pairs={{0,2},{2,0},{4,6},{6,4},{8,10},{10,8},{12,14},{14,12},{16,18},{18,... | collective-permute-start | bytes 221192 | tf_op jit(solution)/shard_map/ppermute | solution.py:63
  95.2 2.7 %backward_5.1.rest_1_ = f32[17,128,256]{2,1,0:T(8,128)S(1)} custom-call(s32[16]{0:T(128)S(1)} %convert_reduce_fusion.1.starts, s32[192]{0:T(256)S(1)} %get-tuple-element.59.order, s32[192]{0:T(256)S(1)} %get-tuple-element.60.rows, s32[192]{0:T(256)S(1)} %get-tuple-element.61.cols, bf16[192,128,128]{2,1,0:T(8,128)(2,1)S(1)} %load_tiles.1.vals, ...), custom_call_target="tpu_custom_call" | custom-call | tf_op jit(solution)/shard_map/backward_5/pallas_call | solution.py:42
  99.8 4.7 %collective-permute-start.25 = (bf16[4,256,256]{2,1,0:T(8,128)(2,1)S(1)}, bf16[4,256,256]{2,1,0:T(8,128)(2,1)S(1)}, u32[]{:S(2)}, u32[]{:S(2)}) collective-permute-start(bf16[4,256,256]{2,1,0:T(8,128)(2,1)S(1)} %get-tuple-element.103), channel_id=1, source_target_pairs={{0,32},{32,0},{64,96},{96,64},{128,160},{160,128},{192,224},{224,1... | collective-permute-start | bytes 1572872 | tf_op jit(solution)/shard_map/ppermute | solution.py:55
  110.8 3.0 %collective-permute-done.26.a = bf16[400,256]{1,0:T(8,128)(2,1)S(1)} collective-permute-done((bf16[400,256]{1,0:T(8,128)(2,1)S(1)}, bf16[400,256]{1,0:T(8,128)(2,1)S(1)}, u32[]{:S(2)}, u32[]{:S(2)}) %collective-permute-start.26) | collective-permute-done | bytes 204832 | tf_op jit(solution)/shard_map/ppermute | solution.py:59
  113.8 5.0 %collective-permute-done.27.b = bf16[400,256]{1,0:T(8,128)(2,1)S(1)} collective-permute-done((bf16[400,256]{1,0:T(8,128)(2,1)S(1)}, bf16[400,256]{1,0:T(8,128)(2,1)S(1)}, u32[]{:S(2)}, u32[]{:S(2)}) %collective-permute-start.27) | collective-permute-done | bytes 204832 | tf_op jit(solution)/shard_map/ppermute | solution.py:59
  (78 shorter events, 34.8 us)
Async XLA Ops:
  0.6 12.0 %collective-permute-start = (bf16[256,256]{1,0:T(8,128)(2,1)}, bf16[256,256]{1,0:T(8,128)(2,1)S(1)}, u32[]{:S(2)}, u32[]{:S(2)}) collective-permute-start(bf16[256,256]{1,0:T(8,128)(2,1)} %refs_0_.1), channel_id=1, source_target_pairs={{0,64},{32,96},{64,128},{96,160},{128,192},{160,224},{192,0},{224,... | collective-permute-start | bytes 393224 | tf_op jit(solution)/shard_map/ppermute | solution.py:59
  2.8 9.8 %collective-permute-start.1 = (bf16[256,256]{1,0:T(8,128)(2,1)}, bf16[256,256]{1,0:T(8,128)(2,1)S(1)}, u32[]{:S(2)}, u32[]{:S(2)}) collective-permute-start(bf16[256,256]{1,0:T(8,128)(2,1)} %refs_0_.1), channel_id=1, source_target_pairs={{0,192},{32,224},{64,0},{96,32},{128,64},{160,96},{192,128},{224,1... | collective-permute-start | bytes 393224 | tf_op jit(solution)/shard_map/ppermute | solution.py:59
  4.4 8.3 %collective-permute-start.2 = (bf16[256,256]{1,0:T(8,128)(2,1)}, bf16[256,256]{1,0:T(8,128)(2,1)S(1)}, u32[]{:S(2)}, u32[]{:S(2)}) collective-permute-start(bf16[256,256]{1,0:T(8,128)(2,1)} %refs_0_.1), channel_id=1, source_target_pairs={{0,128},{32,160},{64,192},{96,224},{128,0},{160,32},{192,64},{224,... | collective-permute-start | bytes 393224 | tf_op jit(solution)/shard_map/ppermute | solution.py:59
  5.9 8.5 %collective-permute-start.3 = (bf16[256,256]{1,0:T(8,128)(2,1)}, bf16[256,256]{1,0:T(8,128)(2,1)S(1)}, u32[]{:S(2)}, u32[]{:S(2)}) collective-permute-start(bf16[256,256]{1,0:T(8,128)(2,1)} %refs_0_.1), channel_id=1, source_target_pairs={{0,32},{32,0},{64,96},{96,64},{128,160},{160,128},{192,224},{224,1... | collective-permute-start | bytes 393224 | tf_op jit(solution)/shard_map/ppermute | solution.py:55
  18.0 5.6 %collective-permute-start.7 = (bf16[2,256,256]{2,1,0:T(8,128)(2,1)S(1)}, bf16[2,256,256]{2,1,0:T(8,128)(2,1)S(1)}, u32[]{:S(2)}, u32[]{:S(2)}) collective-permute-start(bf16[2,256,256]{2,1,0:T(8,128)(2,1)S(1)} %get-tuple-element.71), channel_id=1, source_target_pairs={{0,28},{2,30},{4,8},{6,10},{8,4},{10,6},{12,16},{14,18},{16,12},{1... | collective-permute-start | bytes 786440 | tf_op jit(solution)/shard_map/ppermute | solution.py:74
  18.1 8.3 %collective-permute-start.8 = (bf16[2,256,256]{2,1,0:T(8,128)(2,1)S(1)}, bf16[2,256,256]{2,1,0:T(8,128)(2,1)S(1)}, u32[]{:S(2)}, u32[]{:S(2)}) collective-permute-start(bf16[2,256,256]{2,1,0:T(8,128)(2,1)S(1)} %get-tuple-element.72), channel_id=1, source_target_pairs={{0,28},{2,30},{4,8},{6,10},{8,4},{10,6},{12,16},{14,18},{16,12},{1... | collective-permute-start | bytes 786440 | tf_op jit(solution)/shard_map/ppermute | solution.py:74
  22.7 12.2 %collective-permute-start.11 = (bf16[2,256,256]{2,1,0:T(8,128)(2,1)S(1)}, bf16[2,256,256]{2,1,0:T(8,128)(2,1)S(1)}, u32[]{:S(2)}, u32[]{:S(2)}) collective-permute-start(bf16[2,256,256]{2,1,0:T(8,128)(2,1)S(1)} %get-tuple-element.81), channel_id=1, source_target_pairs={{0,28},{2,30},{4,8},{6,10},{8,4},{10,6},{12,16},{14,18},{16,12},{1... | collective-permute-start | bytes 786440 | tf_op jit(solution)/shard_map/ppermute | solution.py:74
  26.5 12.7 %collective-permute-start.10 = (bf16[2,256,256]{2,1,0:T(8,128)(2,1)S(1)}, bf16[2,256,256]{2,1,0:T(8,128)(2,1)S(1)}, u32[]{:S(2)}, u32[]{:S(2)}) collective-permute-start(bf16[2,256,256]{2,1,0:T(8,128)(2,1)S(1)} %get-tuple-element.78), channel_id=1, source_target_pairs={{0,6},{2,4},{4,2},{6,0},{8,14},{10,12},{12,10},{14,8},{16,22},{18,... | collective-permute-start | bytes 786440 | tf_op jit(solution)/shard_map/ppermute | solution.py:74
  32.3 6.9 %collective-permute-start.9 = (bf16[2,256,256]{2,1,0:T(8,128)(2,1)S(1)}, bf16[2,256,256]{2,1,0:T(8,128)(2,1)S(1)}, u32[]{:S(2)}, u32[]{:S(2)}) collective-permute-start(bf16[2,256,256]{2,1,0:T(8,128)(2,1)S(1)} %get-tuple-element.77), channel_id=1, source_target_pairs={{0,4},{2,6},{4,0},{6,2},{8,12},{10,14},{12,8},{14,10},{16,20},{18,... | collective-permute-start | bytes 786440 | tf_op jit(solution)/shard_map/ppermute | solution.py:74
  34.9 10.5 %collective-permute-start.12 = (bf16[2,256,256]{2,1,0:T(8,128)(2,1)S(1)}, bf16[2,256,256]{2,1,0:T(8,128)(2,1)S(1)}, u32[]{:S(2)}, u32[]{:S(2)}) collective-permute-start(bf16[2,256,256]{2,1,0:T(8,128)(2,1)S(1)} %relay_side.1), channel_id=1, source_target_pairs={{0,2},{2,0},{4,6},{6,4},{8,10},{10,8},{12,14},{14,12},{16,18},{18,... | collective-permute-start | bytes 786440 | tf_op jit(solution)/shard_map/ppermute | solution.py:63
  39.3 6.1 %collective-permute-start.13 = (bf16[2,256,256]{2,1,0:T(8,128)(2,1)S(1)}, bf16[2,256,256]{2,1,0:T(8,128)(2,1)S(1)}, u32[]{:S(2)}, u32[]{:S(2)}) collective-permute-start(bf16[2,256,256]{2,1,0:T(8,128)(2,1)S(1)} %relay_c.1), channel_id=1, source_target_pairs={{0,28},{2,30},{4,8},{6,10},{8,4},{10,6},{12,16},{14,18},{16,12},{1... | collective-permute-start | bytes 786440 | tf_op jit(solution)/shard_map/ppermute | solution.py:74
  52.0 5.5 %collective-permute-start.15 = (bf16[144,256]{1,0:T(8,128)(2,1)S(1)}, bf16[144,256]{1,0:T(8,128)(2,1)S(1)}, u32[]{:S(2)}, u32[]{:S(2)}) collective-permute-start(bf16[144,256]{1,0:T(8,128)(2,1)S(1)} %get-tuple-element.90), channel_id=1, source_target_pairs={{0,32},{32,0},{64,96},{96,64},{128,160},{160,128},{192,224},{224,1... | collective-permute-start | bytes 221192 | tf_op jit(solution)/shard_map/ppermute | solution.py:55
  57.6 6.6 %collective-permute-start.16 = (bf16[400,256]{1,0:T(8,128)(2,1)S(1)}, bf16[400,256]{1,0:T(8,128)(2,1)S(1)}, u32[]{:S(2)}, u32[]{:S(2)}) collective-permute-start(bf16[400,256]{1,0:T(8,128)(2,1)S(1)} %pack_own.1.own), channel_id=1, source_target_pairs={{0,4},{2,6},{4,0},{6,2},{8,12},{10,14},{12,8},{14,10},{16,20},{18,... | collective-permute-start | bytes 614408 | tf_op jit(solution)/shard_map/ppermute | solution.py:74
  64.3 6.9 %collective-permute-start.17 = (bf16[656,256]{1,0:T(8,128)(2,1)S(1)}, bf16[656,256]{1,0:T(8,128)(2,1)S(1)}, u32[]{:S(2)}, u32[]{:S(2)}) collective-permute-start(bf16[656,256]{1,0:T(8,128)(2,1)S(1)} %pack_pair.1.rest_0_.pd), channel_id=1, source_target_pairs={{0,28},{2,30},{4,8},{6,10},{8,4},{10,6},{12,16},{14,18},{16,12},{1... | collective-permute-start | bytes 1007624 | tf_op jit(solution)/shard_map/ppermute | solution.py:74
  64.4 6.8 %collective-permute-start.18 = (bf16[512,256]{1,0:T(8,128)(2,1)S(1)}, bf16[512,256]{1,0:T(8,128)(2,1)S(1)}, u32[]{:S(2)}, u32[]{:S(2)}) collective-permute-start(bf16[512,256]{1,0:T(8,128)(2,1)S(1)} %slice.8), channel_id=1, source_target_pairs={{0,2},{2,0},{4,6},{6,4},{8,10},{10,8},{12,14},{14,12},{16,18},{18,... | collective-permute-start | bytes 786440 | tf_op jit(solution)/shard_map/ppermute | solution.py:63
  71.2 15.4 %collective-permute-start.19 = (bf16[656,256]{1,0:T(8,128)(2,1)S(1)}, bf16[656,256]{1,0:T(8,128)(2,1)S(1)}, u32[]{:S(2)}, u32[]{:S(2)}) collective-permute-start(bf16[656,256]{1,0:T(8,128)(2,1)S(1)} %collective-permute-done.17.rest_0_.pc), channel_id=1, source_target_pairs={{0,4},{2,6},{4,0},{6,2},{8,12},{10,14},{12,8},{14,10},{16,20},{18,... | collective-permute-start | bytes 1007624 | tf_op jit(solution)/shard_map/ppermute | solution.py:74
  76.3 10.3 %collective-permute-start.20 = (bf16[512,256]{1,0:T(8,128)(2,1)S(1)}, bf16[512,256]{1,0:T(8,128)(2,1)S(1)}, u32[]{:S(2)}, u32[]{:S(2)}) collective-permute-start(bf16[512,256]{1,0:T(8,128)(2,1)S(1)} %slice.7), channel_id=1, source_target_pairs={{0,6},{2,4},{4,2},{6,0},{8,14},{10,12},{12,10},{14,8},{16,22},{18,... | collective-permute-start | bytes 786440 | tf_op jit(solution)/shard_map/ppermute | solution.py:74
  76.6 10.0 %collective-permute-start.21 = (bf16[512,256]{1,0:T(8,128)(2,1)S(1)}, bf16[512,256]{1,0:T(8,128)(2,1)S(1)}, u32[]{:S(2)}, u32[]{:S(2)}) collective-permute-start(bf16[512,256]{1,0:T(8,128)(2,1)S(1)} %collective-permute-done.18.rest_1_), channel_id=1, source_target_pairs={{0,28},{2,30},{4,8},{6,10},{8,4},{10,6},{12,16},{14,18},{16,12},{1... | collective-permute-start | bytes 786440 | tf_op jit(solution)/shard_map/ppermute | solution.py:74
  86.6 6.0 %collective-permute-start.23 = (bf16[656,256]{1,0:T(8,128)(2,1)S(1)}, bf16[656,256]{1,0:T(8,128)(2,1)S(1)}, u32[]{:S(2)}, u32[]{:S(2)}) collective-permute-start(bf16[656,256]{1,0:T(8,128)(2,1)S(1)} %collective-permute-done.19.rest_0_.pb), channel_id=1, source_target_pairs={{0,28},{2,30},{4,8},{6,10},{8,4},{10,6},{12,16},{14,18},{16,12},{1... | collective-permute-start | bytes 1007624 | tf_op jit(solution)/shard_map/ppermute | solution.py:74
  87.2 10.7 %collective-permute-start.22 = (bf16[512,256]{1,0:T(8,128)(2,1)S(1)}, bf16[512,256]{1,0:T(8,128)(2,1)S(1)}, u32[]{:S(2)}, u32[]{:S(2)}) collective-permute-start(bf16[512,256]{1,0:T(8,128)(2,1)S(1)} %collective-permute-done.20.rest_1_), channel_id=1, source_target_pairs={{0,28},{2,30},{4,8},{6,10},{8,4},{10,6},{12,16},{14,18},{16,12},{1... | collective-permute-start | bytes 786440 | tf_op jit(solution)/shard_map/ppermute | solution.py:74
  99.8 6.2 %collective-permute-start.25 = (bf16[4,256,256]{2,1,0:T(8,128)(2,1)S(1)}, bf16[4,256,256]{2,1,0:T(8,128)(2,1)S(1)}, u32[]{:S(2)}, u32[]{:S(2)}) collective-permute-start(bf16[4,256,256]{2,1,0:T(8,128)(2,1)S(1)} %get-tuple-element.103), channel_id=1, source_target_pairs={{0,32},{32,0},{64,96},{96,64},{128,160},{160,128},{192,224},{224,1... | collective-permute-start | bytes 1572872 | tf_op jit(solution)/shard_map/ppermute | solution.py:55
  106.2 7.6 %collective-permute-start.26 = (bf16[400,256]{1,0:T(8,128)(2,1)S(1)}, bf16[400,256]{1,0:T(8,128)(2,1)S(1)}, u32[]{:S(2)}, u32[]{:S(2)}) collective-permute-start(bf16[400,256]{1,0:T(8,128)(2,1)S(1)} %get-tuple-element.106), channel_id=1, source_target_pairs={{0,64},{32,96},{64,128},{96,160},{128,192},{160,224},{192,0},{224,... | collective-permute-start | bytes 614408 | tf_op jit(solution)/shard_map/ppermute | solution.py:59
  107.5 11.2 %collective-permute-start.27 = (bf16[400,256]{1,0:T(8,128)(2,1)S(1)}, bf16[400,256]{1,0:T(8,128)(2,1)S(1)}, u32[]{:S(2)}, u32[]{:S(2)}) collective-permute-start(bf16[400,256]{1,0:T(8,128)(2,1)S(1)} %get-tuple-element.107), channel_id=1, source_target_pairs={{0,128},{32,160},{64,192},{96,224},{128,0},{160,32},{192,64},{224,... | collective-permute-start | bytes 614408 | tf_op jit(solution)/shard_map/ppermute | solution.py:59
  109.6 9.2 %collective-permute-start.28 = (bf16[400,256]{1,0:T(8,128)(2,1)S(1)}, bf16[400,256]{1,0:T(8,128)(2,1)S(1)}, u32[]{:S(2)}, u32[]{:S(2)}) collective-permute-start(bf16[400,256]{1,0:T(8,128)(2,1)S(1)} %get-tuple-element.108), channel_id=1, source_target_pairs={{0,192},{32,224},{64,0},{96,32},{128,64},{160,96},{192,128},{224,1... | collective-permute-start | bytes 614408 | tf_op jit(solution)/shard_map/ppermute | solution.py:59
  (11 other events, 58.6 us)

commit v13 on v12

--- a/solution.py
+++ b/solution.py
@@ -95,7 +95,9 @@
 def add_tiles(begin, end, starts, order, to_slot, product, total, dummy):
     first, last = starts[begin], starts[end]
 
-    def step(start, count):
+    count = min(24, 12 * (end - begin))
+
+    def step(start):
         slots = [start + u for u in range(count)]
         safe = [jnp.minimum(t, 191) for t in slots]
         terms = [product(order[t], t) for t in safe]
@@ -104,10 +106,10 @@
             total[place_at] = total[place_at] + term
 
     def batch(i, carry):
-        step(first + 16 * i, 16)
+        step(first + count * i)
         return carry
 
-    lax.fori_loop(0, (last - first + 15) // 16, batch, 0)
+    lax.fori_loop(0, (last - first + count - 1) // count, batch, 0)
 
 
 def forward_body(begin, end, starts, order, rows, cols, vals, source, *rest):

time: 123 us -> 123 us (level)
  Pallas kernels: 24.9 us -> 21.3 us
  waiting for transfers between devices: 42.7 us -> 45.1 us
  starting transfers between devices: 48.5 us -> 50.1 us
    pallas_call x24, Pallas kernels: 24.9 us -> 21.3 us  [call(): pl.pallas_call(body, name=name, out_shape=out_shape, in_specs=specs or [s...]
    ppermute x14, starting transfers between devices: 21.5 us -> 23.9 us  [swap_z(): return lax.ppermute(a, ('row', 'col'), pairs)]
    ppermute x3, waiting for transfers between devices: 8.25 us -> 9.83 us  [to_x(): return lax.ppermute(a, 'col', [(i, i ^ 1) for i in range(2 * NZ)])]
  transfers between devices with their start and end apart: 30 -> 30, of which waited for: 17 -> 19; matrix products, arithmetic and copies ran while one was open for 1% -> 1% of each run, Pallas kernels for 15% -> 13%
where the time goes in v13:
time: 123 us; the launch traced here: 122 us
  starting transfers between devices  50.1 us (41%)
  waiting for transfers between devices  45.1 us (37%)
  Pallas kernels  21.3 us (17%)
  local copies, waits for them, and re-layouts  2.85 us (2%)
  between operations  1.57 us (1%)
  other arithmetic  1.34 us (1%)
    ppermute x14, starting transfers between devices, swap_z(): return lax.ppermute(a, ('row', 'col'), pairs)  23.9 us
    ppermute x14, waiting for transfers between devices, swap_z(): return lax.ppermute(a, ('row', 'col'), pairs)  23 us
    pallas_call x24, Pallas kernels, call(): pl.pallas_call(body, name=name, out_shape=out_shape, in_specs=specs or [s...  21.3 us
    ppermute x7, starting transfers between devices, to_core(): return lax.ppermute(a, 'row', [(i, i ^ 1) for i in range(2 * NY)])  14.3 us
    ppermute x3, waiting for transfers between devices, to_x(): return lax.ppermute(a, 'col', [(i, i ^ 1) for i in range(2 * NZ)])  9.83 us
    ppermute x6, starting transfers between devices, to_y(): lax.ppermute(a, 'row', [(i, (i + 2 * step) % (2 * NY)) for i in range(2 *...  8.86 us
    ppermute x6, waiting for transfers between devices, to_y(): lax.ppermute(a, 'row', [(i, (i + 2 * step) % (2 * NY)) for i in range(2 *...  8.69 us
    ppermute x7, waiting for transfers between devices, to_core(): return lax.ppermute(a, 'row', [(i, i ^ 1) for i in range(2 * NY)])  3.58 us
  transfers between devices with their start and end apart: 30, of which 19 were waited for; matrix products, arithmetic and copies ran while one was open for 1% of the time, Pallas kernels for 13%

profile of v13, /device:TPU:1, one launch (start us, length us, event | category | flops | bytes accessed | tf_op | source)
XLA Modules:
  0.0 122.2 jit_solution(2342244963230367976)
XLA Ops:
  0.6 2.2 %collective-permute-start = (bf16[256,256]{1,0:T(8,128)(2,1)}, bf16[256,256]{1,0:T(8,128)(2,1)S(1)}, u32[]{:S(2)}, u32[]{:S(2)}) collective-permute-start(bf16[256,256]{1,0:T(8,128)(2,1)} %refs_0_.1), channel_id=1, source_target_pairs={{0,64},{32,96},{64,128},{96,160},{128,192},{160,224},{192,0},{224,... | collective-permute-start | bytes 393224 | tf_op jit(solution)/shard_map/ppermute | solution.py:59
  9.2 2.8 %copy-done = bf16[1,1,192,128,128]{4,3,2,1,0:T(8,128)(2,1)S(1)} copy-done((bf16[1,1,192,128,128]{4,3,2,1,0:T(8,128)(2,1)S(1)}, bf16[1,1,192,128,128]{4,3,2,1,0:T(8,128)(2,1)}, u32[]{:S(2)}) %copy-start) | copy-done | bytes 6291480
  19.0 2.6 %forward_3.1 = (f32[2,256,256]{2,1,0:T(8,128)S(1)}, f32[2,256,256]{2,1,0:T(8,128)S(1)}, bf16[2,256,256]{2,1,0:T(8,128)(2,1)S(1)}) custom-call(s32[16]{0:T(128)S(1)} %convert_reduce_fusion.1.starts, s32[192]{0:T(256)S(1)} %get-tuple-element.59.order, s32[192]{0:T(256)S(1)} %get-tuple-element.60.rows, s32[192]{0:T(256)S(1)} %get-tuple-element.61.cols, ...), custom_call_target="tpu_custom_call" | custom-call | tf_op jit(solution)/shard_map/forward_3/pallas_call | solution.py:42
  23.2 2.7 %collective-permute-done.8.got_side = bf16[2,256,256]{2,1,0:T(8,128)(2,1)S(1)} collective-permute-done((bf16[2,256,256]{2,1,0:T(8,128)(2,1)S(1)}, bf16[2,256,256]{2,1,0:T(8,128)(2,1)S(1)}, u32[]{:S(2)}, u32[]{:S(2)}) %collective-permute-start.8) | collective-permute-done | bytes 262176 | tf_op jit(solution)/shard_map/ppermute | solution.py:74
  25.9 6.8 %collective-permute-start.10 = (bf16[2,256,256]{2,1,0:T(8,128)(2,1)S(1)}, bf16[2,256,256]{2,1,0:T(8,128)(2,1)S(1)}, u32[]{:S(2)}, u32[]{:S(2)}) collective-permute-start(bf16[2,256,256]{2,1,0:T(8,128)(2,1)S(1)} %get-tuple-element.78), channel_id=1, source_target_pairs={{0,6},{2,4},{4,2},{6,0},{8,14},{10,12},{12,10},{14,8},{16,22},{18,... | collective-permute-start | bytes 786440 | tf_op jit(solution)/shard_map/ppermute | solution.py:74
  32.7 1.9 %forward_1.1 = (f32[2,256,256]{2,1,0:T(8,128)S(1)}, f32[2,256,256]{2,1,0:T(8,128)S(1)}) custom-call(s32[16]{0:T(128)S(1)} %convert_reduce_fusion.1.starts, s32[192]{0:T(256)S(1)} %get-tuple-element.59.order, s32[192]{0:T(256)S(1)} %get-tuple-element.60.rows, s32[192]{0:T(256)S(1)} %get-tuple-element.61.cols, bf16[192,128,128]{2,1,0:T(8,128)(2,1)S(1)} %load_tiles.1.vals, ...), custom_call_target="tpu_custom_call" | custom-call | tf_op jit(solution)/shard_map/forward_1/pallas_call | solution.py:42
  35.2 3.2 %collective-permute-done.10.rest_1_ = bf16[2,256,256]{2,1,0:T(8,128)(2,1)S(1)} collective-permute-done((bf16[2,256,256]{2,1,0:T(8,128)(2,1)S(1)}, bf16[2,256,256]{2,1,0:T(8,128)(2,1)S(1)}, u32[]{:S(2)}, u32[]{:S(2)}) %collective-permute-start.10) | collective-permute-done | bytes 262176 | tf_op jit(solution)/shard_map/ppermute | solution.py:74
  41.1 4.4 %collective-permute-done.12.over = bf16[2,256,256]{2,1,0:T(8,128)(2,1)S(1)} collective-permute-done((bf16[2,256,256]{2,1,0:T(8,128)(2,1)S(1)}, bf16[2,256,256]{2,1,0:T(8,128)(2,1)S(1)}, u32[]{:S(2)}, u32[]{:S(2)}) %collective-permute-start.12) | collective-permute-done | bytes 262176 | tf_op jit(solution)/shard_map/ppermute | solution.py:63
  45.5 2.7 %collective-permute-start.14 = (bf16[256,256]{1,0:T(8,128)(2,1)S(1)}, bf16[256,256]{1,0:T(8,128)(2,1)S(1)}, u32[]{:S(2)}, u32[]{:S(2)}) collective-permute-start(bf16[256,256]{1,0:T(8,128)(2,1)S(1)} %get-tuple-element.84), channel_id=1, source_target_pairs={{0,4},{2,6},{4,0},{6,2},{8,12},{10,14},{12,8},{14,10},{16,20},{18,... | collective-permute-start | bytes 393224 | tf_op jit(solution)/shard_map/ppermute | solution.py:74
  48.3 2.7 %collective-permute-done.14.got = bf16[256,256]{1,0:T(8,128)(2,1)S(1)} collective-permute-done((bf16[256,256]{1,0:T(8,128)(2,1)S(1)}, bf16[256,256]{1,0:T(8,128)(2,1)S(1)}, u32[]{:S(2)}, u32[]{:S(2)}) %collective-permute-start.14) | collective-permute-done | bytes 131104 | tf_op jit(solution)/shard_map/ppermute | solution.py:74
  52.3 4.8 %collective-permute-start.15 = (bf16[144,256]{1,0:T(8,128)(2,1)S(1)}, bf16[144,256]{1,0:T(8,128)(2,1)S(1)}, u32[]{:S(2)}, u32[]{:S(2)}) collective-permute-start(bf16[144,256]{1,0:T(8,128)(2,1)S(1)} %get-tuple-element.90), channel_id=1, source_target_pairs={{0,32},{32,0},{64,96},{96,64},{128,160},{160,128},{192,224},{224,1... | collective-permute-start | bytes 221192 | tf_op jit(solution)/shard_map/ppermute | solution.py:55
  58.0 3.5 %collective-permute-start.16 = (bf16[400,256]{1,0:T(8,128)(2,1)S(1)}, bf16[400,256]{1,0:T(8,128)(2,1)S(1)}, u32[]{:S(2)}, u32[]{:S(2)}) collective-permute-start(bf16[400,256]{1,0:T(8,128)(2,1)S(1)} %pack_own.1.own), channel_id=1, source_target_pairs={{0,4},{2,6},{4,0},{6,2},{8,12},{10,14},{12,8},{14,10},{16,20},{18,... | collective-permute-start | bytes 614408 | tf_op jit(solution)/shard_map/ppermute | solution.py:74
  61.5 3.1 %collective-permute-done.16.got = bf16[400,256]{1,0:T(8,128)(2,1)S(1)} collective-permute-done((bf16[400,256]{1,0:T(8,128)(2,1)S(1)}, bf16[400,256]{1,0:T(8,128)(2,1)S(1)}, u32[]{:S(2)}, u32[]{:S(2)}) %collective-permute-start.16) | collective-permute-done | bytes 204832 | tf_op jit(solution)/shard_map/ppermute | solution.py:74
  66.9 4.8 %collective-permute-done.18.rest_1_ = bf16[512,256]{1,0:T(8,128)(2,1)S(1)} collective-permute-done((bf16[512,256]{1,0:T(8,128)(2,1)S(1)}, bf16[512,256]{1,0:T(8,128)(2,1)S(1)}, u32[]{:S(2)}, u32[]{:S(2)}) %collective-permute-start.18) | collective-permute-done | bytes 262176 | tf_op jit(solution)/shard_map/ppermute | solution.py:63
  71.6 5.1 %collective-permute-start.19 = (bf16[656,256]{1,0:T(8,128)(2,1)S(1)}, bf16[656,256]{1,0:T(8,128)(2,1)S(1)}, u32[]{:S(2)}, u32[]{:S(2)}) collective-permute-start(bf16[656,256]{1,0:T(8,128)(2,1)S(1)} %collective-permute-done.17.rest_0_.pc), channel_id=1, source_target_pairs={{0,4},{2,6},{4,0},{6,2},{8,12},{10,14},{12,8},{14,10},{16,20},{18,... | collective-permute-start | bytes 1007624 | tf_op jit(solution)/shard_map/ppermute | solution.py:74
  77.8 2.0 %backward_1.1.rest_2_ = f32[17,128,256]{2,1,0:T(8,128)S(1)} custom-call(s32[16]{0:T(128)S(1)} %convert_reduce_fusion.1.starts, s32[192]{0:T(256)S(1)} %get-tuple-element.59.order, s32[192]{0:T(256)S(1)} %get-tuple-element.60.rows, s32[192]{0:T(256)S(1)} %get-tuple-element.61.cols, bf16[192,128,128]{2,1,0:T(8,128)(2,1)S(1)} %load_tiles.1.vals, ...), custom_call_target="tpu_custom_call" | custom-call | tf_op jit(solution)/shard_map/backward_1/pallas_call | solution.py:42
  79.9 7.4 %collective-permute-done.20.rest_1_ = bf16[512,256]{1,0:T(8,128)(2,1)S(1)} collective-permute-done((bf16[512,256]{1,0:T(8,128)(2,1)S(1)}, bf16[512,256]{1,0:T(8,128)(2,1)S(1)}, u32[]{:S(2)}, u32[]{:S(2)}) %collective-permute-start.20) | collective-permute-done | bytes 262176 | tf_op jit(solution)/shard_map/ppermute | solution.py:74
  88.8 2.1 %backward_3.1.rest_2_ = f32[17,128,256]{2,1,0:T(8,128)S(1)} custom-call(s32[16]{0:T(128)S(1)} %convert_reduce_fusion.1.starts, s32[192]{0:T(256)S(1)} %get-tuple-element.59.order, s32[192]{0:T(256)S(1)} %get-tuple-element.60.rows, s32[192]{0:T(256)S(1)} %get-tuple-element.61.cols, bf16[192,128,128]{2,1,0:T(8,128)(2,1)S(1)} %load_tiles.1.vals, ...), custom_call_target="tpu_custom_call" | custom-call | tf_op jit(solution)/shard_map/backward_3/pallas_call | solution.py:42
  90.9 2.8 %collective-permute-done.23.rest_1_.pa = bf16[656,256]{1,0:T(8,128)(2,1)S(1)} collective-permute-done((bf16[656,256]{1,0:T(8,128)(2,1)S(1)}, bf16[656,256]{1,0:T(8,128)(2,1)S(1)}, u32[]{:S(2)}, u32[]{:S(2)}) %collective-permute-start.23) | collective-permute-done | bytes 335904 | tf_op jit(solution)/shard_map/ppermute | solution.py:74
  93.7 2.1 %collective-permute-start.24 = (bf16[144,256]{1,0:T(8,128)(2,1)S(1)}, bf16[144,256]{1,0:T(8,128)(2,1)S(1)}, u32[]{:S(2)}, u32[]{:S(2)}) collective-permute-start(bf16[144,256]{1,0:T(8,128)(2,1)S(1)} %plane_terms.1.plane), channel_id=1, source_target_pairs={{0,2},{2,0},{4,6},{6,4},{8,10},{10,8},{12,14},{14,12},{16,18},{18,... | collective-permute-start | bytes 221192 | tf_op jit(solution)/shard_map/ppermute | solution.py:63
  95.8 2.0 %backward_5.1.rest_1_ = f32[17,128,256]{2,1,0:T(8,128)S(1)} custom-call(s32[16]{0:T(128)S(1)} %convert_reduce_fusion.1.starts, s32[192]{0:T(256)S(1)} %get-tuple-element.59.order, s32[192]{0:T(256)S(1)} %get-tuple-element.60.rows, s32[192]{0:T(256)S(1)} %get-tuple-element.61.cols, bf16[192,128,128]{2,1,0:T(8,128)(2,1)S(1)} %load_tiles.1.vals, ...), custom_call_target="tpu_custom_call" | custom-call | tf_op jit(solution)/shard_map/backward_5/pallas_call | solution.py:42
  100.2 4.7 %collective-permute-start.25 = (bf16[4,256,256]{2,1,0:T(8,128)(2,1)S(1)}, bf16[4,256,256]{2,1,0:T(8,128)(2,1)S(1)}, u32[]{:S(2)}, u32[]{:S(2)}) collective-permute-start(bf16[4,256,256]{2,1,0:T(8,128)(2,1)S(1)} %get-tuple-element.103), channel_id=1, source_target_pairs={{0,32},{32,0},{64,96},{96,64},{128,160},{160,128},{192,224},{224,1... | collective-permute-start | bytes 1572872 | tf_op jit(solution)/shard_map/ppermute | solution.py:55
  110.1 4.3 %collective-permute-done.26.a = bf16[400,256]{1,0:T(8,128)(2,1)S(1)} collective-permute-done((bf16[400,256]{1,0:T(8,128)(2,1)S(1)}, bf16[400,256]{1,0:T(8,128)(2,1)S(1)}, u32[]{:S(2)}, u32[]{:S(2)}) %collective-permute-start.26) | collective-permute-done | bytes 204832 | tf_op jit(solution)/shard_map/ppermute | solution.py:59
  114.4 3.9 %collective-permute-done.27.b = bf16[400,256]{1,0:T(8,128)(2,1)S(1)} collective-permute-done((bf16[400,256]{1,0:T(8,128)(2,1)S(1)}, bf16[400,256]{1,0:T(8,128)(2,1)S(1)}, u32[]{:S(2)}, u32[]{:S(2)}) %collective-permute-start.27) | collective-permute-done | bytes 204832 | tf_op jit(solution)/shard_map/ppermute | solution.py:59
  (78 shorter events, 36.1 us)
Async XLA Ops:
  0.6 12.0 %collective-permute-start = (bf16[256,256]{1,0:T(8,128)(2,1)}, bf16[256,256]{1,0:T(8,128)(2,1)S(1)}, u32[]{:S(2)}, u32[]{:S(2)}) collective-permute-start(bf16[256,256]{1,0:T(8,128)(2,1)} %refs_0_.1), channel_id=1, source_target_pairs={{0,64},{32,96},{64,128},{96,160},{128,192},{160,224},{192,0},{224,... | collective-permute-start | bytes 393224 | tf_op jit(solution)/shard_map/ppermute | solution.py:59
  2.8 9.8 %collective-permute-start.1 = (bf16[256,256]{1,0:T(8,128)(2,1)}, bf16[256,256]{1,0:T(8,128)(2,1)S(1)}, u32[]{:S(2)}, u32[]{:S(2)}) collective-permute-start(bf16[256,256]{1,0:T(8,128)(2,1)} %refs_0_.1), channel_id=1, source_target_pairs={{0,192},{32,224},{64,0},{96,32},{128,64},{160,96},{192,128},{224,1... | collective-permute-start | bytes 393224 | tf_op jit(solution)/shard_map/ppermute | solution.py:59
  4.4 8.3 %collective-permute-start.2 = (bf16[256,256]{1,0:T(8,128)(2,1)}, bf16[256,256]{1,0:T(8,128)(2,1)S(1)}, u32[]{:S(2)}, u32[]{:S(2)}) collective-permute-start(bf16[256,256]{1,0:T(8,128)(2,1)} %refs_0_.1), channel_id=1, source_target_pairs={{0,128},{32,160},{64,192},{96,224},{128,0},{160,32},{192,64},{224,... | collective-permute-start | bytes 393224 | tf_op jit(solution)/shard_map/ppermute | solution.py:59
  5.9 8.5 %collective-permute-start.3 = (bf16[256,256]{1,0:T(8,128)(2,1)}, bf16[256,256]{1,0:T(8,128)(2,1)S(1)}, u32[]{:S(2)}, u32[]{:S(2)}) collective-permute-start(bf16[256,256]{1,0:T(8,128)(2,1)} %refs_0_.1), channel_id=1, source_target_pairs={{0,32},{32,0},{64,96},{96,64},{128,160},{160,128},{192,224},{224,1... | collective-permute-start | bytes 393224 | tf_op jit(solution)/shard_map/ppermute | solution.py:55
  17.4 5.8 %collective-permute-start.7 = (bf16[2,256,256]{2,1,0:T(8,128)(2,1)S(1)}, bf16[2,256,256]{2,1,0:T(8,128)(2,1)S(1)}, u32[]{:S(2)}, u32[]{:S(2)}) collective-permute-start(bf16[2,256,256]{2,1,0:T(8,128)(2,1)S(1)} %get-tuple-element.71), channel_id=1, source_target_pairs={{0,28},{2,30},{4,8},{6,10},{8,4},{10,6},{12,16},{14,18},{16,12},{1... | collective-permute-start | bytes 786440 | tf_op jit(solution)/shard_map/ppermute | solution.py:74
  18.4 7.4 %collective-permute-start.8 = (bf16[2,256,256]{2,1,0:T(8,128)(2,1)S(1)}, bf16[2,256,256]{2,1,0:T(8,128)(2,1)S(1)}, u32[]{:S(2)}, u32[]{:S(2)}) collective-permute-start(bf16[2,256,256]{2,1,0:T(8,128)(2,1)S(1)} %get-tuple-element.72), channel_id=1, source_target_pairs={{0,28},{2,30},{4,8},{6,10},{8,4},{10,6},{12,16},{14,18},{16,12},{1... | collective-permute-start | bytes 786440 | tf_op jit(solution)/shard_map/ppermute | solution.py:74
  21.6 13.0 %collective-permute-start.11 = (bf16[2,256,256]{2,1,0:T(8,128)(2,1)S(1)}, bf16[2,256,256]{2,1,0:T(8,128)(2,1)S(1)}, u32[]{:S(2)}, u32[]{:S(2)}) collective-permute-start(bf16[2,256,256]{2,1,0:T(8,128)(2,1)S(1)} %get-tuple-element.81), channel_id=1, source_target_pairs={{0,28},{2,30},{4,8},{6,10},{8,4},{10,6},{12,16},{14,18},{16,12},{1... | collective-permute-start | bytes 786440 | tf_op jit(solution)/shard_map/ppermute | solution.py:74
  25.9 12.4 %collective-permute-start.10 = (bf16[2,256,256]{2,1,0:T(8,128)(2,1)S(1)}, bf16[2,256,256]{2,1,0:T(8,128)(2,1)S(1)}, u32[]{:S(2)}, u32[]{:S(2)}) collective-permute-start(bf16[2,256,256]{2,1,0:T(8,128)(2,1)S(1)} %get-tuple-element.78), channel_id=1, source_target_pairs={{0,6},{2,4},{4,2},{6,0},{8,14},{10,12},{12,10},{14,8},{16,22},{18,... | collective-permute-start | bytes 786440 | tf_op jit(solution)/shard_map/ppermute | solution.py:74
  32.7 6.7 %collective-permute-start.9 = (bf16[2,256,256]{2,1,0:T(8,128)(2,1)S(1)}, bf16[2,256,256]{2,1,0:T(8,128)(2,1)S(1)}, u32[]{:S(2)}, u32[]{:S(2)}) collective-permute-start(bf16[2,256,256]{2,1,0:T(8,128)(2,1)S(1)} %get-tuple-element.77), channel_id=1, source_target_pairs={{0,4},{2,6},{4,0},{6,2},{8,12},{10,14},{12,8},{14,10},{16,20},{18,... | collective-permute-start | bytes 786440 | tf_op jit(solution)/shard_map/ppermute | solution.py:74
  34.7 10.8 %collective-permute-start.12 = (bf16[2,256,256]{2,1,0:T(8,128)(2,1)S(1)}, bf16[2,256,256]{2,1,0:T(8,128)(2,1)S(1)}, u32[]{:S(2)}, u32[]{:S(2)}) collective-permute-start(bf16[2,256,256]{2,1,0:T(8,128)(2,1)S(1)} %relay_side.1), channel_id=1, source_target_pairs={{0,2},{2,0},{4,6},{6,4},{8,10},{10,8},{12,14},{14,12},{16,18},{18,... | collective-permute-start | bytes 786440 | tf_op jit(solution)/shard_map/ppermute | solution.py:63
  39.5 5.9 %collective-permute-start.13 = (bf16[2,256,256]{2,1,0:T(8,128)(2,1)S(1)}, bf16[2,256,256]{2,1,0:T(8,128)(2,1)S(1)}, u32[]{:S(2)}, u32[]{:S(2)}) collective-permute-start(bf16[2,256,256]{2,1,0:T(8,128)(2,1)S(1)} %relay_c.1), channel_id=1, source_target_pairs={{0,28},{2,30},{4,8},{6,10},{8,4},{10,6},{12,16},{14,18},{16,12},{1... | collective-permute-start | bytes 786440 | tf_op jit(solution)/shard_map/ppermute | solution.py:74
  52.3 5.7 %collective-permute-start.15 = (bf16[144,256]{1,0:T(8,128)(2,1)S(1)}, bf16[144,256]{1,0:T(8,128)(2,1)S(1)}, u32[]{:S(2)}, u32[]{:S(2)}) collective-permute-start(bf16[144,256]{1,0:T(8,128)(2,1)S(1)} %get-tuple-element.90), channel_id=1, source_target_pairs={{0,32},{32,0},{64,96},{96,64},{128,160},{160,128},{192,224},{224,1... | collective-permute-start | bytes 221192 | tf_op jit(solution)/shard_map/ppermute | solution.py:55
  58.0 6.6 %collective-permute-start.16 = (bf16[400,256]{1,0:T(8,128)(2,1)S(1)}, bf16[400,256]{1,0:T(8,128)(2,1)S(1)}, u32[]{:S(2)}, u32[]{:S(2)}) collective-permute-start(bf16[400,256]{1,0:T(8,128)(2,1)S(1)} %pack_own.1.own), channel_id=1, source_target_pairs={{0,4},{2,6},{4,0},{6,2},{8,12},{10,14},{12,8},{14,10},{16,20},{18,... | collective-permute-start | bytes 614408 | tf_op jit(solution)/shard_map/ppermute | solution.py:74
  64.7 6.9 %collective-permute-start.17 = (bf16[656,256]{1,0:T(8,128)(2,1)S(1)}, bf16[656,256]{1,0:T(8,128)(2,1)S(1)}, u32[]{:S(2)}, u32[]{:S(2)}) collective-permute-start(bf16[656,256]{1,0:T(8,128)(2,1)S(1)} %pack_pair.1.rest_0_.pd), channel_id=1, source_target_pairs={{0,28},{2,30},{4,8},{6,10},{8,4},{10,6},{12,16},{14,18},{16,12},{1... | collective-permute-start | bytes 1007624 | tf_op jit(solution)/shard_map/ppermute | solution.py:74
  64.8 6.8 %collective-permute-start.18 = (bf16[512,256]{1,0:T(8,128)(2,1)S(1)}, bf16[512,256]{1,0:T(8,128)(2,1)S(1)}, u32[]{:S(2)}, u32[]{:S(2)}) collective-permute-start(bf16[512,256]{1,0:T(8,128)(2,1)S(1)} %slice.8), channel_id=1, source_target_pairs={{0,2},{2,0},{4,6},{6,4},{8,10},{10,8},{12,14},{14,12},{16,18},{18,... | collective-permute-start | bytes 786440 | tf_op jit(solution)/shard_map/ppermute | solution.py:63
  71.6 15.7 %collective-permute-start.19 = (bf16[656,256]{1,0:T(8,128)(2,1)S(1)}, bf16[656,256]{1,0:T(8,128)(2,1)S(1)}, u32[]{:S(2)}, u32[]{:S(2)}) collective-permute-start(bf16[656,256]{1,0:T(8,128)(2,1)S(1)} %collective-permute-done.17.rest_0_.pc), channel_id=1, source_target_pairs={{0,4},{2,6},{4,0},{6,2},{8,12},{10,14},{12,8},{14,10},{16,20},{18,... | collective-permute-start | bytes 1007624 | tf_op jit(solution)/shard_map/ppermute | solution.py:74
  76.7 10.6 %collective-permute-start.20 = (bf16[512,256]{1,0:T(8,128)(2,1)S(1)}, bf16[512,256]{1,0:T(8,128)(2,1)S(1)}, u32[]{:S(2)}, u32[]{:S(2)}) collective-permute-start(bf16[512,256]{1,0:T(8,128)(2,1)S(1)} %slice.7), channel_id=1, source_target_pairs={{0,6},{2,4},{4,2},{6,0},{8,14},{10,12},{12,10},{14,8},{16,22},{18,... | collective-permute-start | bytes 786440 | tf_op jit(solution)/shard_map/ppermute | solution.py:74
  76.8 10.5 %collective-permute-start.21 = (bf16[512,256]{1,0:T(8,128)(2,1)S(1)}, bf16[512,256]{1,0:T(8,128)(2,1)S(1)}, u32[]{:S(2)}, u32[]{:S(2)}) collective-permute-start(bf16[512,256]{1,0:T(8,128)(2,1)S(1)} %collective-permute-done.18.rest_1_), channel_id=1, source_target_pairs={{0,28},{2,30},{4,8},{6,10},{8,4},{10,6},{12,16},{14,18},{16,12},{1... | collective-permute-start | bytes 786440 | tf_op jit(solution)/shard_map/ppermute | solution.py:74
  87.3 6.3 %collective-permute-start.23 = (bf16[656,256]{1,0:T(8,128)(2,1)S(1)}, bf16[656,256]{1,0:T(8,128)(2,1)S(1)}, u32[]{:S(2)}, u32[]{:S(2)}) collective-permute-start(bf16[656,256]{1,0:T(8,128)(2,1)S(1)} %collective-permute-done.19.rest_0_.pb), channel_id=1, source_target_pairs={{0,28},{2,30},{4,8},{6,10},{8,4},{10,6},{12,16},{14,18},{16,12},{1... | collective-permute-start | bytes 1007624 | tf_op jit(solution)/shard_map/ppermute | solution.py:74
  87.3 10.5 %collective-permute-start.22 = (bf16[512,256]{1,0:T(8,128)(2,1)S(1)}, bf16[512,256]{1,0:T(8,128)(2,1)S(1)}, u32[]{:S(2)}, u32[]{:S(2)}) collective-permute-start(bf16[512,256]{1,0:T(8,128)(2,1)S(1)} %collective-permute-done.20.rest_1_), channel_id=1, source_target_pairs={{0,28},{2,30},{4,8},{6,10},{8,4},{10,6},{12,16},{14,18},{16,12},{1... | collective-permute-start | bytes 786440 | tf_op jit(solution)/shard_map/ppermute | solution.py:74
  100.2 6.2 %collective-permute-start.25 = (bf16[4,256,256]{2,1,0:T(8,128)(2,1)S(1)}, bf16[4,256,256]{2,1,0:T(8,128)(2,1)S(1)}, u32[]{:S(2)}, u32[]{:S(2)}) collective-permute-start(bf16[4,256,256]{2,1,0:T(8,128)(2,1)S(1)} %get-tuple-element.103), channel_id=1, source_target_pairs={{0,32},{32,0},{64,96},{96,64},{128,160},{160,128},{192,224},{224,1... | collective-permute-start | bytes 1572872 | tf_op jit(solution)/shard_map/ppermute | solution.py:55
  106.6 7.8 %collective-permute-start.26 = (bf16[400,256]{1,0:T(8,128)(2,1)S(1)}, bf16[400,256]{1,0:T(8,128)(2,1)S(1)}, u32[]{:S(2)}, u32[]{:S(2)}) collective-permute-start(bf16[400,256]{1,0:T(8,128)(2,1)S(1)} %get-tuple-element.106), channel_id=1, source_target_pairs={{0,64},{32,96},{64,128},{96,160},{128,192},{160,224},{192,0},{224,... | collective-permute-start | bytes 614408 | tf_op jit(solution)/shard_map/ppermute | solution.py:59
  107.1 11.2 %collective-permute-start.27 = (bf16[400,256]{1,0:T(8,128)(2,1)S(1)}, bf16[400,256]{1,0:T(8,128)(2,1)S(1)}, u32[]{:S(2)}, u32[]{:S(2)}) collective-permute-start(bf16[400,256]{1,0:T(8,128)(2,1)S(1)} %get-tuple-element.107), channel_id=1, source_target_pairs={{0,128},{32,160},{64,192},{96,224},{128,0},{160,32},{192,64},{224,... | collective-permute-start | bytes 614408 | tf_op jit(solution)/shard_map/ppermute | solution.py:59
  109.0 9.8 %collective-permute-start.28 = (bf16[400,256]{1,0:T(8,128)(2,1)S(1)}, bf16[400,256]{1,0:T(8,128)(2,1)S(1)}, u32[]{:S(2)}, u32[]{:S(2)}) collective-permute-start(bf16[400,256]{1,0:T(8,128)(2,1)S(1)} %get-tuple-element.108), channel_id=1, source_target_pairs={{0,192},{32,224},{64,0},{96,32},{128,64},{160,96},{192,128},{224,1... | collective-permute-start | bytes 614408 | tf_op jit(solution)/shard_map/ppermute | solution.py:59
  (11 other events, 58.6 us)
